TPU v7x, 32 devices: a whole 2x2x4 slice. The times are simulated.
32 devices in a mesh: dp: 8 (over y, x, core), tensor: 4 (over z).
Axes of the slice: x: 2, y: 2, z: 4, core: 2. Of those that a mesh axis runs over, the one named last changes fastest.
Arguments:
- tokens: bfloat16 [640, 2048], P('dp', 'tensor'), may hold values from -6 to 6
- gate_weight: bfloat16 [2048, 8192], P('tensor', 'dp'), may hold values from -0.125 to 0.125
- up_weight: bfloat16 [2048, 8192], P('tensor', 'dp'), may hold values from -0.125 to 0.125
- down_weight: bfloat16 [8192, 2048], P('dp', 'tensor'), may hold values from -0.0625 to 0.0625
- out_grad: bfloat16 [640, 2048], P('dp', 'tensor'), may hold values from -6 to 6
Outputs:
- mixed: float32 [640, 2048], P('dp', 'tensor')
- grad_tokens: float32 [640, 2048], P('dp', 'tensor')
- grad_gate: bfloat16 [2048, 8192], P('tensor', 'dp')
- grad_up: bfloat16 [2048, 8192], P('tensor', 'dp')
- grad_down: bfloat16 [8192, 2048], P('dp', 'tensor')
All inputs are finite; a program needn't handle non-finite values.
Results may differ from a plain program's by a relative error of at most 0.0073.
Values may be sent and summed in bfloat16 or wider, within the bound.
No kernel may reach another device: no remote copies, remote signals or barrier semaphores. Data moves between devices by JAX's collectives and lax.ppermute only.
A program may use at most 64 MiB of HBM per device.

v0:
```python
import math

import jax
import jax.numpy as jnp
from jax import lax
from jax.sharding import PartitionSpec as P

D = 2048


def swapped(block, axis, apart):
    count = lax.axis_size(axis)
    route = []
    for low in range(count):
        high = low | 1 << apart
        if high != low and high < count:
            route += [(low, high), (high, low)]
    return lax.ppermute(block, axis, route)


def sylvester_table(order):
    rows = jnp.arange(order, dtype=jnp.int32)[:, None]
    cols = jnp.arange(order, dtype=jnp.int32)[None, :]
    signs = jnp.ones((order, order), jnp.float32)
    for level in range(order.bit_length() - 1):
        bit_on = jnp.bitwise_and(
            jnp.bitwise_and(jnp.right_shift(rows, level), jnp.right_shift(cols, level)), 1
        )
        signs = signs * (1.0 - 2.0 * bit_on.astype(jnp.float32))
    return signs


def rotate_rows(values):
    count = values.shape[0]
    width = values.shape[1]
    lanes = min(width, 128)
    blocks = width // lanes
    shaped = values.reshape(count, blocks, lanes)
    shaped = jnp.einsum(
        "rab,ac->rcb", shaped, sylvester_table(blocks), precision=lax.Precision.HIGHEST
    )
    shaped = jnp.einsum(
        "rcb,bd->rcd", shaped, sylvester_table(lanes), precision=lax.Precision.HIGHEST
    )
    local_rot = shaped.reshape(count, width) * (1.0 / math.sqrt(D))
    groups = lax.axis_size("tensor")
    my_index = lax.axis_index("tensor")
    current = local_rot
    for level in range(groups.bit_length() - 1):
        partner = swapped(current, "tensor", level)
        upper = jnp.bitwise_and(jnp.right_shift(my_index, level), 1) == 1
        current = jnp.where(upper, partner - current, current + partner)
    return current


def contract_last(left, right):
    return lax.dot_general(
        left, right, (((1,), (1,)), ((), ())), preferred_element_type=jnp.float32
    )


def contract_first(left, right):
    return lax.dot_general(
        left, right, (((0,), (0,)), ((), ())), preferred_element_type=jnp.float32
    )


def swiglu_grads(grad_hidden, gate, up):
    sigma = jax.nn.sigmoid(gate)
    grad_gate_act = (grad_hidden * up * sigma * (1.0 + gate * (1.0 - sigma))).astype(jnp.bfloat16)
    grad_up_act = (grad_hidden * gate * sigma).astype(jnp.bfloat16)
    return (grad_gate_act, grad_up_act)


def shards(tokens, gate_weight, up_weight, down_weight, out_grad):
    rotated = rotate_rows(tokens.astype(jnp.float32)).astype(jnp.bfloat16)
    grad_rot = rotate_rows(out_grad.astype(jnp.float32)).astype(jnp.bfloat16)
    inputs_all = lax.all_gather(rotated, "dp", axis=0, tiled=True)
    grads_all = lax.all_gather(grad_rot, "dp", axis=0, tiled=True)
    gate_part = jnp.dot(inputs_all, gate_weight, preferred_element_type=jnp.float32)
    up_part = jnp.dot(inputs_all, up_weight, preferred_element_type=jnp.float32)
    grad_part = contract_last(grads_all, down_weight)
    gate, up, grad_hidden = lax.psum((gate_part, up_part, grad_part), "tensor")
    hidden = (jax.nn.silu(gate) * up).astype(jnp.bfloat16)
    grad_gate_act, grad_up_act = swiglu_grads(grad_hidden, gate, up)
    output_sums = lax.psum_scatter(
        jnp.dot(hidden, down_weight, preferred_element_type=jnp.float32),
        "dp",
        scatter_dimension=0,
        tiled=True,
    )
    mixed = rotate_rows(output_sums)
    input_sums = lax.psum_scatter(
        contract_last(grad_gate_act, gate_weight) + contract_last(grad_up_act, up_weight),
        "dp",
        scatter_dimension=0,
        tiled=True,
    )
    grad_tokens = rotate_rows(input_sums)
    factor = 1.0 / math.sqrt(inputs_all.shape[0])
    grad_gate = (contract_first(inputs_all, grad_gate_act) * factor).astype(jnp.bfloat16)
    grad_up = (contract_first(inputs_all, grad_up_act) * factor).astype(jnp.bfloat16)
    grad_down = (contract_first(hidden, grads_all) * factor).astype(jnp.bfloat16)
    return (mixed, grad_tokens, grad_gate, grad_up, grad_down)


def solution(mesh):
    return jax.shard_map(
        shards,
        mesh=mesh,
        in_specs=(
            P("dp", "tensor"),
            P("tensor", "dp"),
            P("tensor", "dp"),
            P("dp", "tensor"),
            P("dp", "tensor"),
        ),
        out_specs=(
            P("dp", "tensor"),
            P("dp", "tensor"),
            P("tensor", "dp"),
            P("tensor", "dp"),
            P("dp", "tensor"),
        ),
        check_vma=False,
    )
```

profile of v0, /device:TPU:0, one launch (start us, length us, event | category | flops | bytes accessed | tf_op | source)
XLA Modules:
  0.0 446.0 jit_solution(5423752603800983251)
XLA Ops:
  7.3 1.0 reshape.124
  9.2 3.1 collective-permute-start
  12.3 0.9 reshape.126
  14.2 2.7 collective-permute-done
  16.9 2.7 collective-permute-start.1
  19.5 2.5 collective-permute-done.4
  22.1 1.9 collective-permute-start.5
  24.0 7.1 %collective-permute-done.1 = f32[80,512]{1,0:T(8,128)S(1)} collective-permute-done((f32[80,512]{1,0:T(8,128)S(1)}, f32[80,512]{1,0:T(8,128)S(1)}, u32[]{:S(2)}, u32[]{:S(2)}) %collective-permute-start.1) | collective-permute-done | bytes 163872 | tf_op jit(solution)/shard_map/ppermute | solution.py:18
  31.1 10.1 %all_gather.6 = bf16[640,512]{1,0:T(8,128)(2,1)S(1)} all-gather(bf16[80,512]{1,0:T(8,128)(2,1)S(1)} %select_convert_fusion.1), channel_id=1, replica_groups=mesh['dp'=8,'tensor'=4] {'dp'}, dimensions={0}, use_global_device_ids=true | all-gather | bytes 737280 | tf_op jit(solution)/shard_map/all_gather | solution.py:78
  41.3 10.1 %all_gather.7 = bf16[640,512]{1,0:T(8,128)(2,1)S(1)} all-gather(bf16[80,512]{1,0:T(8,128)(2,1)S(1)} %select_convert_fusion), channel_id=1, replica_groups=mesh['dp'=8,'tensor'=4] {'dp'}, dimensions={0}, use_global_device_ids=true | all-gather | bytes 737280 | tf_op jit(solution)/shard_map/all_gather | solution.py:79
  51.4 2.4 fusion.49
  53.8 2.4 fusion.48
  56.3 2.4 fusion.51
  58.7 274.4 %all-reduce.3.cloned.1.call-done = (f32[640,1024]{1,0:T(8,128)}, f32[640,1024]{1,0:T(8,128)}, f32[640,1024]{1,0:T(8,128)}) async-done(((f32[640,1024]{1,0:T(8,128)}, f32[640,1024]{1,0:T(8,128)}, f32[640,1024]{1,0:T(8,128)}), (f32[640,1024]{1,0:T(8,128)}, f32[640,1024]{1,0:T(8,128)}, f32[640,1024]{1,0:T(8,128)})) %all-reduce.3.cloned.1.call-update) | async-done | bytes 7864336 | tf_op jit(solution)/shard_map/psum | solution.py:83
  333.1 5.0 %multiply_convert_fusion = (bf16[640,1024]{1,0:T(8,128)(2,1)S(1)}, bf16[640,1024]{1,0:T(8,128)(2,1)}, bf16[640,1024]{1,0:T(8,128)(2,1)S(1)}) fusion(f32[640,1024]{1,0:T(8,128)} %get-tuple-element.7, f32[640,1024]{1,0:T(8,128)} %get-tuple-element.6, f32[640,1024]{1,0:T(8,128)} %get-tuple-element.5), kind=kLoop, calls=%fused_computation | loop fusion | flops 10485760 | bytes 11796480 | tf_op jit(solution)/shard_map/convert_element_type | solution.py:71
  338.1 1.1 copy-done.5
  339.2 1.9 fusion.50
  341.4 2.6 fusion.52
  344.0 2.0 convolution_add_fusion
  346.0 3.5 multiply_convert_fusion.3
  349.5 2.0 multiply_convert_fusion.4
  351.5 2.0 multiply_convert_fusion.5
  353.5 24.0 %reduce-scatter.3.cloned.1.call-done = f32[80,512]{1,0:T(8,128)} async-done(((f32[640,512]{1,0:T(8,128)}), f32[80,512]{1,0:T(8,128)}) %reduce-scatter.3.cloned.1.call-update) | async-done | bytes 163856 | tf_op jit(solution)/shard_map/reduce_scatter | solution.py:86
  377.5 1.0 reshape.125
  379.5 1.5 collective-permute-start.2
  381.1 37.0 %reduce-scatter.5.cloned.1.call-done = f32[80,512]{1,0:T(8,128)} async-done(((f32[640,512]{1,0:T(8,128)}), f32[80,512]{1,0:T(8,128)}) %reduce-scatter.5.cloned.1.call-update) | async-done | bytes 163856 | tf_op jit(solution)/shard_map/reduce_scatter | solution.py:93
  418.0 1.0 reshape.127
  420.1 1.6 collective-permute-start.6
  421.7 2.5 collective-permute-start.3
  424.2 4.9 %collective-permute-done.6 = f32[80,512]{1,0:T(8,128)S(1)} collective-permute-done((f32[80,512]{1,0:T(8,128)S(1)}, f32[80,512]{1,0:T(8,128)S(1)}, u32[]{:S(2)}, u32[]{:S(2)}) %collective-permute-start.6) | collective-permute-done | bytes 163872 | tf_op jit(solution)/shard_map/ppermute | solution.py:18
  429.8 6.1 %collective-permute-done.3 = f32[80,512]{1,0:T(8,128)S(1)} collective-permute-done((f32[80,512]{1,0:T(8,128)S(1)}, f32[80,512]{1,0:T(8,128)S(1)}, u32[]{:S(2)}, u32[]{:S(2)}) %collective-permute-start.3) | collective-permute-done | bytes 163872 | tf_op jit(solution)/shard_map/ppermute | solution.py:18
  436.6 2.2 collective-permute-done.7
  (48 shorter events, 6.5 us)
Async XLA Ops:
  7.2 49.1 %copy-start = (bf16[1024,512]{1,0:T(8,128)(2,1)S(1)}, bf16[1024,512]{1,0:T(8,128)(2,1)}, u32[]{:S(2)}) copy-start(bf16[1024,512]{1,0:T(8,128)(2,1)} %param.8) | copy-start | bytes 3145732
  7.2 325.9 %all-reduce.3.cloned.1.call-start = ((), (), s32[]{:S(2)}) async-start(), calls=%async_computation.4 | async-start | bytes 15728640 | tf_op jit(solution)/shard_map/psum | solution.py:83
  9.2 7.7 %collective-permute-start = (f32[80,512]{1,0:T(8,128)S(1)}, f32[80,512]{1,0:T(8,128)S(1)}, u32[]{:S(2)}, u32[]{:S(2)}) collective-permute-start(f32[80,512]{1,0:T(8,128)S(1)} %bitcast.81), channel_id=1, source_target_pairs={{0,1},{1,0},{2,3},{3,2},{4,5},{5,4},{6,7},{7,6},{8,9},{9,8},{10,11... | collective-permute-start | bytes 491528 | tf_op jit(solution)/shard_map/ppermute | solution.py:18
  13.6 37.8 %copy-start.1 = (bf16[512,1024]{1,0:T(8,128)(2,1)S(1)}, bf16[512,1024]{1,0:T(8,128)(2,1)}, u32[]{:S(2)}) copy-start(bf16[512,1024]{1,0:T(8,128)(2,1)} %param.7) | copy-start | bytes 3145732
  14.1 7.9 %collective-permute-start.4 = (f32[80,512]{1,0:T(8,128)S(1)}, f32[80,512]{1,0:T(8,128)S(1)}, u32[]{:S(2)}, u32[]{:S(2)}) collective-permute-start(f32[80,512]{1,0:T(8,128)S(1)} %bitcast.80), channel_id=1, source_target_pairs={{0,1},{1,0},{2,3},{3,2},{4,5},{5,4},{6,7},{7,6},{8,9},{9,8},{10,11... | collective-permute-start | bytes 491528 | tf_op jit(solution)/shard_map/ppermute | solution.py:18
  16.9 14.2 %collective-permute-start.1 = (f32[80,512]{1,0:T(8,128)S(1)}, f32[80,512]{1,0:T(8,128)S(1)}, u32[]{:S(2)}, u32[]{:S(2)}) collective-permute-start(f32[80,512]{1,0:T(8,128)S(1)} %add_select_fusion.5), channel_id=1, source_target_pairs={{0,2},{2,0},{1,3},{3,1},{4,6},{6,4},{5,7},{7,5},{8,10},{10,8},{9,1... | collective-permute-start | bytes 491528 | tf_op jit(solution)/shard_map/ppermute | solution.py:18
  22.1 19.2 %collective-permute-start.5 = (f32[80,512]{1,0:T(8,128)S(1)}, f32[80,512]{1,0:T(8,128)S(1)}, u32[]{:S(2)}, u32[]{:S(2)}) collective-permute-start(f32[80,512]{1,0:T(8,128)S(1)} %add_select_fusion.2), channel_id=1, source_target_pairs={{0,2},{2,0},{1,3},{3,1},{4,6},{6,4},{5,7},{7,5},{8,10},{10,8},{9,1... | collective-permute-start | bytes 491528 | tf_op jit(solution)/shard_map/ppermute | solution.py:18
  51.4 4.9 %copy-start.3 = (bf16[640,512]{1,0:T(8,128)(2,1)}, bf16[640,512]{1,0:T(8,128)(2,1)S(1)}, u32[]{:S(2)}) copy-start(bf16[640,512]{1,0:T(8,128)(2,1)S(1)} %all_gather.7) | copy-start | bytes 1966084
  51.4 2.4 copy-start.6
  58.7 318.8 %reduce-scatter.3.cloned.1.call-start = ((), (), s32[]{:S(2)}) async-start(), calls=%async_computation.2 | async-start | bytes 1474560 | tf_op jit(solution)/shard_map/reduce_scatter | solution.py:86
  338.1 1.1 copy-start.5
  341.1 76.9 %reduce-scatter.5.cloned.1.call-start = ((), (), s32[]{:S(2)}) async-start(), calls=%async_computation.3 | async-start | bytes 1474560 | tf_op jit(solution)/shard_map/reduce_scatter | solution.py:93
  341.4 2.6 copy-start.2
  349.5 2.0 copy-start.4
  379.5 42.1 %collective-permute-start.2 = (f32[80,512]{1,0:T(8,128)S(1)}, f32[80,512]{1,0:T(8,128)S(1)}, u32[]{:S(2)}, u32[]{:S(2)}) collective-permute-start(f32[80,512]{1,0:T(8,128)S(1)} %bitcast.82), channel_id=1, source_target_pairs={{0,1},{1,0},{2,3},{3,2},{4,5},{5,4},{6,7},{7,6},{8,9},{9,8},{10,11... | collective-permute-start | bytes 491528 | tf_op jit(solution)/shard_map/ppermute | solution.py:18
  420.1 9.0 %collective-permute-start.6 = (f32[80,512]{1,0:T(8,128)S(1)}, f32[80,512]{1,0:T(8,128)S(1)}, u32[]{:S(2)}, u32[]{:S(2)}) collective-permute-start(f32[80,512]{1,0:T(8,128)S(1)} %bitcast.83), channel_id=1, source_target_pairs={{0,1},{1,0},{2,3},{3,2},{4,5},{5,4},{6,7},{7,6},{8,9},{9,8},{10,11... | collective-permute-start | bytes 491528 | tf_op jit(solution)/shard_map/ppermute | solution.py:18
  421.7 14.2 %collective-permute-start.3 = (f32[80,512]{1,0:T(8,128)S(1)}, f32[80,512]{1,0:T(8,128)S(1)}, u32[]{:S(2)}, u32[]{:S(2)}) collective-permute-start(f32[80,512]{1,0:T(8,128)S(1)} %add_select_fusion.4), channel_id=1, source_target_pairs={{0,2},{2,0},{1,3},{3,1},{4,6},{6,4},{5,7},{7,5},{8,10},{10,8},{9,1... | collective-permute-start | bytes 491528 | tf_op jit(solution)/shard_map/ppermute | solution.py:18
  429.1 9.7 %collective-permute-start.7 = (f32[80,512]{1,0:T(8,128)S(1)}, f32[80,512]{1,0:T(8,128)S(1)}, u32[]{:S(2)}, u32[]{:S(2)}) collective-permute-start(f32[80,512]{1,0:T(8,128)S(1)} %add_select_fusion.1), channel_id=1, source_target_pairs={{0,2},{2,0},{1,3},{3,1},{4,6},{6,4},{5,7},{7,5},{8,10},{10,8},{9,1... | collective-permute-start | bytes 491528 | tf_op jit(solution)/shard_map/ppermute | solution.py:18
Sparse Core Ops, SparseCore 0:
  58.8 274.2 all-reduce.2
  341.3 36.1 reduce-scatter.2
  380.7 37.2 reduce-scatter.4
where the time goes:
time: 446 us
  waiting for transfers between devices  361 us (81%)
  matrix products  25 us (6%)
  blocking collectives  20.2 us (5%)
  starting transfers between devices  14.3 us (3%)
  between operations  14 us (3%)
  other arithmetic  6.59 us (1%)
  local copies, waits for them, and re-layouts  4.98 us (1%)
    psum x1, waiting for transfers between devices, shards(): gate, up, grad_hidden = lax.psum((gate_part, up_part, grad_part), 'tensor')  274 us
    reduce_scatter x1, waiting for transfers between devices, shards(): lax.psum_scatter(contract_last(grad_gate_act, gate_weight) + contract_las...  37 us
    ppermute x8, waiting for transfers between devices, swapped(): return lax.ppermute(block, axis, route)  25.6 us
    reduce_scatter x1, waiting for transfers between devices, shards(): lax.psum_scatter(jnp.dot(hidden, down_weight, preferred_element_type=jnp....  24 us
    ppermute x8, starting transfers between devices, swapped(): return lax.ppermute(block, axis, route)  14 us
    all_gather x1, blocking collectives, shards(): grads_all = lax.all_gather(grad_rot, 'dp', axis=0, tiled=True)  10.1 us
    all_gather x1, blocking collectives, shards(): inputs_all = lax.all_gather(rotated, 'dp', axis=0, tiled=True)  10.1 us
  transfers between devices with their start and end apart: 11, of which 9 were waited for; matrix products, arithmetic and copies ran while one was open for 4% of the time, Pallas kernels for 0%

commit v1 on v0

v1 whole, which is shorter than its diff:
```python
import math

import jax
import jax.numpy as jnp
import numpy as np
from jax import lax
from jax.sharding import PartitionSpec as P

D = 2048
BF16 = jnp.bfloat16
F32 = jnp.float32


def sylvester(order):
    table = np.ones((1, 1), np.float32)
    while table.shape[0] < order:
        table = np.block([[table, table], [table, -table]])
    return table


def dot(left, right, left_dim, right_dim):
    return lax.dot_general(
        left, right, (((left_dim,), (right_dim,)), ((), ())), preferred_element_type=F32
    )


def rotate(block):
    rows, width = block.shape
    groups = lax.axis_size("tensor")
    every = lax.all_gather(block, "tensor", axis=0, tiled=True)
    turned = dot(every, jnp.asarray(sylvester(width), BF16), 1, 0)
    signs = jnp.asarray(sylvester(groups))[lax.axis_index("tensor")] * (1.0 / math.sqrt(D))
    return jnp.sum(turned.reshape(groups, rows, width) * signs[:, None, None], axis=0)


def shards(tokens, gate_weight, up_weight, down_weight, out_grad):
    mine = tokens.shape[0]
    turned = rotate(jnp.concatenate([tokens, out_grad])).astype(BF16)
    inputs_all = lax.all_gather(turned[:mine], "dp", axis=0, tiled=True)
    grads_all = lax.all_gather(turned[mine:], "dp", axis=0, tiled=True)
    parts = jnp.stack(
        [
            dot(inputs_all, gate_weight, 1, 0).astype(BF16),
            dot(inputs_all, up_weight, 1, 0).astype(BF16),
            dot(grads_all, down_weight, 1, 1).astype(BF16),
        ]
    )
    sums = lax.psum_scatter(parts, "tensor", scatter_dimension=1, tiled=True).astype(F32)
    gate, up, grad_hidden = sums
    sigma = jax.nn.sigmoid(gate)
    acts = jnp.stack(
        [
            gate * sigma * up,
            grad_hidden * up * sigma * (1.0 + gate * (1.0 - sigma)),
            grad_hidden * gate * sigma,
        ]
    ).astype(BF16)
    hidden, grad_gate_act, grad_up_act = lax.all_gather(acts, "tensor", axis=1, tiled=True)
    output = jnp.concatenate(
        [
            dot(hidden, down_weight, 1, 0),
            dot(grad_gate_act, gate_weight, 1, 1) + dot(grad_up_act, up_weight, 1, 1),
        ],
        axis=1,
    ).astype(BF16)
    output = lax.psum_scatter(output, "dp", scatter_dimension=0, tiled=True)
    width = tokens.shape[1]
    ends = rotate(jnp.concatenate([output[:, :width], output[:, width:]]))
    factor = 1.0 / math.sqrt(inputs_all.shape[0])
    return (
        ends[:mine],
        ends[mine:],
        (dot(inputs_all, grad_gate_act, 0, 0) * factor).astype(BF16),
        (dot(inputs_all, grad_up_act, 0, 0) * factor).astype(BF16),
        (dot(hidden, grads_all, 0, 0) * factor).astype(BF16),
    )


def solution(mesh):
    return jax.shard_map(
        shards,
        mesh=mesh,
        in_specs=(
            P("dp", "tensor"),
            P("tensor", "dp"),
            P("tensor", "dp"),
            P("dp", "tensor"),
            P("dp", "tensor"),
        ),
        out_specs=(
            P("dp", "tensor"),
            P("dp", "tensor"),
            P("tensor", "dp"),
            P("tensor", "dp"),
            P("dp", "tensor"),
        ),
        check_vma=False,
    )
```

time: 446 us -> 278 us (0.62)
  waiting for transfers between devices: 361 us -> 177 us
  blocking collectives: 20.2 us -> 57.7 us
  starting transfers between devices: 14.3 us -> 0.12 us
  matrix products: 25 us -> 15.6 us
    psum x1 -> x0, waiting for transfers between devices: 274 us -> none  [shards(): gate, up, grad_hidden = lax.psum((gate_part, up_part, grad_part), 'tensor')]
    all_gather x0 -> x1, waiting for transfers between devices: none -> 76.9 us  [shards(): lax.all_gather(acts, 'tensor', axis=1, tiled=True)]
    all_gather x2 -> x4, blocking collectives: 20.2 us -> 57.7 us  [the longest x2 37.5 us: rotate(): every = lax.all_gather(block, 'tensor', axis=0, tiled=True)]
    unnamed x3 -> x4, waiting for transfers between devices: 0.05 us -> 27.6 us
    ppermute x8 -> x0, waiting for transfers between devices: 25.6 us -> none  [swapped(): return lax.ppermute(block, axis, route)]
    ppermute x8 -> x0, starting transfers between devices: 14 us -> none  [swapped(): return lax.ppermute(block, axis, route)]
    reduce_scatter x2 -> x1, waiting for transfers between devices: 61 us -> 72.1 us  [shards(): lax.psum_scatter(parts, 'tensor', scatter_dimension=1, tiled=True)]
    dot_general x17 -> x11, matrix products: 25 us -> 15.6 us  [dot(): lax.dot_general(left, right, (((left_dim,), (right_dim,)), ((), ())), pre...]
  transfers between devices with their start and end apart: 11 -> 3, of which waited for: 9 -> 3; matrix products, arithmetic and copies ran while one was open for 4% -> 3% of each run, Pallas kernels for 0% -> 0%
where the time goes in v1:
time: 278 us; the launch traced here: 277 us
  waiting for transfers between devices  177 us (64%)
  blocking collectives  57.7 us (21%)
  matrix products  15.6 us (6%)
  between operations  13.9 us (5%)
  other arithmetic  7.48 us (3%)
  local copies, waits for them, and re-layouts  6.08 us (2%)
    all_gather x1, waiting for transfers between devices, shards(): lax.all_gather(acts, 'tensor', axis=1, tiled=True)  76.9 us
    reduce_scatter x1, waiting for transfers between devices, shards(): lax.psum_scatter(parts, 'tensor', scatter_dimension=1, tiled=True)  72.1 us
    all_gather x2, blocking collectives, rotate(): every = lax.all_gather(block, 'tensor', axis=0, tiled=True)  37.5 us
    unnamed x4, waiting for transfers between devices  27.6 us
    dot_general x11, matrix products, dot(): lax.dot_general(left, right, (((left_dim,), (right_dim,)), ((), ())), pre...  15.6 us
    all_gather x1, blocking collectives, shards(): inputs_all = lax.all_gather(turned[:mine], 'dp', axis=0, tiled=True)  10.1 us
    all_gather x1, blocking collectives, shards(): grads_all = lax.all_gather(turned[mine:], 'dp', axis=0, tiled=True)  10.1 us
  transfers between devices with their start and end apart: 3, of which 3 were waited for; matrix products, arithmetic and copies ran while one was open for 3% of the time, Pallas kernels for 0%

profile of v1, /device:TPU:0, one launch (start us, length us, event | category | flops | bytes accessed | tf_op | source)
XLA Modules:
  0.0 277.4 jit_solution(8016700219420418489)
XLA Ops:
  7.2 1.1 pad_maximum_fusion.4
  8.3 19.6 %all_gather.15 = bf16[640,512]{1,0:T(8,128)(2,1)S(1)} all-gather(bf16[160,512]{1,0:T(8,128)(2,1)S(1)} %pad_maximum_fusion.4), channel_id=1, replica_groups=mesh['dp'=8,'tensor'=4] {'tensor'}, dimensions={0}, use_global_device_ids=true | all-gather | bytes 819200 | tf_op jit(solution)/shard_map/all_gather | solution.py:30
  27.9 0.7 multiply_bitcast_fusion
  28.6 0.5 fusion.8
  29.1 0.2 multiply_reduce_fusion.1
  29.4 10.1 %all_gather.16 = bf16[640,512]{1,0:T(8,128)(2,1)S(1)} all-gather(bf16[80,512]{1,0:T(8,128)(2,1)S(1)} %get-tuple-element.12), channel_id=1, replica_groups=mesh['dp'=8,'tensor'=4] {'dp'}, dimensions={0}, use_global_device_ids=true | all-gather | bytes 737280 | tf_op jit(solution)/shard_map/all_gather | solution.py:39
  39.5 0.9 fusion
  40.4 0.4 copy-done.7
  40.7 0.8 fusion.1
  41.6 10.1 %all_gather.17 = bf16[640,512]{1,0:T(8,128)(2,1)S(1)} all-gather(bf16[80,512]{1,0:T(8,128)(2,1)S(1)} %get-tuple-element.13), channel_id=1, replica_groups=mesh['dp'=8,'tensor'=4] {'dp'}, dimensions={0}, use_global_device_ids=true | all-gather | bytes 737280 | tf_op jit(solution)/shard_map/all_gather | solution.py:40
  51.7 0.8 copy-done.2
  52.5 0.9 fusion.2
  53.4 2.1 pad_maximum_fusion
  55.6 72.1 %reduce-scatter.5.cloned.1.call-done = bf16[3,160,1024]{2,1,0:T(8,128)(2,1)} async-done(((bf16[3,640,1024]{2,1,0:T(8,128)(2,1)}), bf16[3,160,1024]{2,1,0:T(8,128)(2,1)}) %reduce-scatter.5.cloned.1.call-update) | async-done | bytes 983056 | tf_op jit(solution)/shard_map/reduce_scatter | solution.py:48
  127.7 1.4 convert_element_type.30
  129.2 0.5 multiply_convert_fusion.5
  129.6 1.1 pad_maximum_fusion.2
  130.8 76.9 %all-gather.2.cloned.1.call-done = bf16[3,640,1024]{2,1,0:T(8,128)(2,1)} async-done(((bf16[3,160,1024]{2,1,0:T(8,128)(2,1)}), bf16[3,640,1024]{2,1,0:T(8,128)(2,1)}) %all-gather.2.cloned.1.call-update) | async-done | bytes 3932176 | tf_op jit(solution)/shard_map/all_gather | solution.py:58
  207.6 2.5 fusion.4
  210.2 1.1 convolution_convert_fusion.3
  211.4 1.0 fusion.3
  212.5 1.6 copy.15
  214.1 1.1 copy-done.3
  215.2 3.5 %multiply_convert_fusion = bf16[1024,512]{1,0:T(8,128)(2,1)} fusion(bf16[640,512]{1,0:T(8,128)(2,1)S(1)} %copy-done.3, bf16[3,640,1024]{2,1,0:T(8,128)(2,1)} %all-gather.2.cloned.1.call-done), kind=kOutput, calls=%fused_computation.1 | convolution fusion | flops 672137216 | bytes 3014656 | tf_op jit(solution)/shard_map/dot_general | solution.py:22
  218.6 2.0 multiply_convert_fusion.1
  220.6 2.0 multiply_convert_fusion.2
  222.6 27.5 %reduce-scatter.7.cloned.1.call-done = bf16[80,1024]{1,0:T(8,128)(2,1)} async-done(((bf16[640,1024]{1,0:T(8,128)(2,1)}), bf16[80,1024]{1,0:T(8,128)(2,1)}) %reduce-scatter.7.cloned.1.call-update) | async-done | bytes 163856
  250.1 0.9 fusion.6
  251.6 17.8 %all_gather.19 = bf16[640,512]{1,0:T(8,128)(2,1)S(1)} all-gather(bf16[160,512]{1,0:T(8,128)(2,1)S(1)} %copy.14), channel_id=1, replica_groups=mesh['dp'=8,'tensor'=4] {'tensor'}, dimensions={0}, use_global_device_ids=true | all-gather | bytes 819200 | tf_op jit(solution)/shard_map/all_gather | solution.py:30
  269.4 0.5 fusion.9
  269.9 0.2 multiply_reduce_fusion
  270.2 0.7 fusion.5
  (27 shorter events, 1.0 us)
Async XLA Ops:
  7.2 32.3 %copy-start = (bf16[512,1024]{1,0:T(8,128)(2,1)S(1)}, bf16[512,1024]{1,0:T(8,128)(2,1)}, u32[]{:S(2)}) copy-start(bf16[512,1024]{1,0:T(8,128)(2,1)} %param.10) | copy-start | bytes 3145732
  7.2 21.4 %copy-start.1 = (bf16[512,512]{1,0:T(8,128)(2,1)S(1)}, bf16[512,512]{1,0:T(8,128)(2,1)}, u32[]{:S(2)}) copy-start(bf16[512,512]{1,0:T(8,128)(2,1)} %constant.8.clone) | copy-start | bytes 1572868
  7.2 120.5 %reduce-scatter.5.cloned.1.call-start = ((), (), s32[]{:S(2)}) async-start(), calls=%async_computation.2 | async-start | bytes 4915200 | tf_op jit(solution)/shard_map/reduce_scatter | solution.py:48
  39.5 1.2 copy-start.7
  40.7 11.8 %copy-start.6 = (bf16[1024,512]{1,0:T(8,128)(2,1)S(1)}, bf16[1024,512]{1,0:T(8,128)(2,1)}, u32[]{:S(2)}) copy-start(bf16[1024,512]{1,0:T(8,128)(2,1)} %param.12) | copy-start | bytes 3145732
  51.7 0.8 copy-start.2
  55.6 152.1 %all-gather.2.cloned.1.call-start = ((), (), s32[]{:S(2)}) async-start(), calls=%async_computation.3 | async-start | bytes 4915200 | tf_op jit(solution)/shard_map/all_gather | solution.py:58
  130.7 119.4 %reduce-scatter.7.cloned.1.call-start = ((), (), s32[]{:S(2)}) async-start(), calls=%async_computation.4 | async-start | bytes 1474560
  207.6 2.5 copy-start.4
  210.2 1.2 copy-start.8
  214.1 1.1 copy-start.3
  215.2 3.5 %copy-start.5 = (bf16[3,640,1024]{2,1,0:T(8,128)(2,1)S(1)}, bf16[3,640,1024]{2,1,0:T(8,128)(2,1)}, u32[]{:S(2)}) copy-start(bf16[3,640,1024]{2,1,0:T(8,128)(2,1)} %all-gather.2.cloned.1.call-done) | copy-start | bytes 11796484
Sparse Core Ops, SparseCore 0:
  55.7 72.0 reduce-scatter.4
  130.8 76.7 all-gather.1
  214.2 35.8 reduce-scatter.6

commit v2 on v1

v2 whole, which is shorter than its diff:
```python
import math

import jax
import jax.numpy as jnp
import numpy as np
from jax import lax
from jax.sharding import PartitionSpec as P

D = 2048
BF16 = jnp.bfloat16
F32 = jnp.float32
STEP = 16


def sylvester(order):
    table = np.ones((1, 1), np.float32)
    while table.shape[0] < order:
        table = np.block([[table, table], [table, -table]])
    return table


def dot(left, right, left_dim, right_dim):
    return lax.dot_general(
        left, right, (((left_dim,), (right_dim,)), ((), ())), preferred_element_type=F32
    )


def after(block, *others):
    for other in others:
        first = other[(0,) * other.ndim]
        block = jnp.where(jnp.isnan(first), first.astype(block.dtype), block)
    return block


def exchange(block, axis, apart):
    count = lax.axis_size(axis)
    return lax.ppermute(block, axis, [(i, i ^ apart) for i in range(count)])


def spread(block):
    return [block] + [exchange(block, "tensor", k) for k in range(1, lax.axis_size("tensor"))]


def rotate(pieces):
    width = pieces[0].shape[-1]
    me = lax.axis_index("tensor").astype(jnp.int32)
    square = jnp.asarray(sylvester(width), BF16)
    total = 0.0
    for apart, piece in enumerate(pieces):
        both = me & (me ^ apart)
        odd = jnp.int32(0)
        for bit in range((len(pieces) - 1).bit_length()):
            odd = odd ^ ((both >> bit) & 1)
        turned = dot(piece, square, piece.ndim - 1, 0)
        total = total + jnp.where(odd == 1, -turned, turned)
    return total * (1.0 / math.sqrt(D))


def dp_stages():
    bits = [1 << bit for bit in reversed(range(lax.axis_size("dp").bit_length() - 1))]
    stages = []
    while len(bits) > 1:
        high, low, bits = bits[0], bits[1], bits[2:]
        stages.append([0, low, high, high | low])
    if bits:
        stages.append([0, bits[0]])
    return stages


def gather_dp(block, axis):
    stages = dp_stages()
    for stage in stages[:-1]:
        came = [exchange(block, "dp", apart) for apart in stage[1:]]
        block = jnp.concatenate([block] + came, axis=axis)
    return block, exchange(block, "dp", stages[-1][1])


def scatter_dp(low, high):
    stages = dp_stages()
    low = low + exchange(high.astype(BF16), "dp", stages[-1][1]).astype(F32)
    for stage in reversed(stages[:-1]):
        low = low.reshape(low.shape[:2] + (len(stage), -1) + low.shape[-1:])
        total = low[:, :, 0]
        for place, apart in enumerate(stage[1:], 1):
            total = total + exchange(low[:, :, place].astype(BF16), "dp", apart).astype(F32)
        low = total
    return low


def line_pairs(step):
    last = lax.axis_size("tensor") - 1
    return [(step, step + 1), (last - step, last - step - 1)]


def fold_steps():
    return range(lax.axis_size("tensor") // 2 - 1)


def inward(own):
    came, total = own, own.astype(F32)
    for step in fold_steps():
        came = lax.ppermute(total.astype(BF16), "tensor", line_pairs(step))
        total = total + came.astype(F32)
    return total, came


def outward(block):
    me = lax.axis_index("tensor")
    for step in reversed(fold_steps()):
        pairs = line_pairs(step)
        came = lax.ppermute(block, "tensor", [(b, a) for a, b in pairs])
        takes = (me == pairs[0][0]) | (me == pairs[1][0])
        block = jnp.where(takes, came, block)
    return block


def across(block):
    half = lax.axis_size("tensor") // 2
    return lax.ppermute(block, "tensor", [(half - 1, half), (half, half - 1)])


def activations(gate, up, grad_hidden):
    sigma = jax.nn.sigmoid(gate)
    silu = gate * sigma
    return jnp.stack(
        [
            silu * up,
            grad_hidden * up * sigma * (1.0 + gate * (1.0 - sigma)),
            grad_hidden * silu,
        ]
    ).astype(BF16)


def shards(tokens, gate_weight, up_weight, down_weight, out_grad):
    mine, width = tokens.shape
    peers = lax.axis_size("dp")
    step = STEP if mine % STEP == 0 else mine
    chunks = mine // step
    half = peers * step // 2
    far_side = lax.axis_index("tensor") >= lax.axis_size("tensor") // 2

    both = jnp.stack([tokens, out_grad])

    def arrive(turned):
        low, high = gather_dp(turned.reshape(2, -1, 1, step, width), 2)
        every = jnp.where(
            far_side, jnp.concatenate([low, high], axis=2), jnp.concatenate([high, low], axis=2)
        )
        return [every[:, i].reshape(2, 2 * half, width) for i in range(every.shape[1])]

    pieces = spread(both[:, :step])
    late_pieces = spread(after(both[:, step:], *pieces[1:2])) if chunks > 1 else None
    rows = arrive(rotate(pieces).astype(BF16))

    done, arrived = [], []
    for i in range(chunks):
        x, g = rows[i]
        parts = [dot(x, gate_weight, 1, 0), dot(x, up_weight, 1, 0), dot(g, down_weight, 1, 1)]
        sums = []
        for place in (slice(0, half), slice(half, 2 * half)):
            ahead = arrived[:1] if len(arrived) < 2 else arrived[-2:-1]
            message = after(jnp.stack([part[place] for part in parts]).astype(BF16), *ahead)
            if not rows[i + 1 :] and i + 1 < chunks:
                rows += arrive(rotate([after(late_pieces[0], message)] + late_pieces[1:]).astype(BF16))
            total, came = inward(message)
            arrived.append(came)
            sums.append(total)
        other, own = sums
        sums = own + across(other.astype(BF16)).astype(F32)
        own = activations(sums[0], sums[1], sums[2])
        if i == chunks - 1:
            done += [outward(across(own)), outward(own)]
        else:
            done.append(outward(jnp.concatenate([across(own), own], axis=1)))

    def leave(blocks, first, last):
        sums = []
        for acts in blocks:
            mixed = dot(acts[0], down_weight, 1, 0)
            grads = dot(acts[1], gate_weight, 1, 1) + dot(acts[2], up_weight, 1, 1)
            sums.append(jnp.stack([mixed, grads]))
        sums = jnp.concatenate(sums, axis=1).reshape(2, last - first, 2, half, width)
        low = jnp.where(far_side, sums[:, :, 0], sums[:, :, 1])
        high = jnp.where(far_side, sums[:, :, 1], sums[:, :, 0])
        if last < chunks:
            high = after(high, own)
        sums = scatter_dp(low, high).astype(BF16)
        return rotate(spread(sums.reshape(2, (last - first) * step, width)))

    ends = [leave(done[:-2], 0, chunks - 1)] if chunks > 1 else []
    ends.append(leave(done[-2:], chunks - 1, chunks))
    ends = jnp.concatenate(ends, axis=1)

    acts = jnp.concatenate(done, axis=1)
    rows = jnp.concatenate(rows, axis=1)
    factor = 1.0 / math.sqrt(rows.shape[1])
    return (
        ends[0],
        ends[1],
        (dot(rows[0], acts[1], 0, 0) * factor).astype(BF16),
        (dot(rows[0], acts[2], 0, 0) * factor).astype(BF16),
        (dot(acts[0], rows[1], 0, 0) * factor).astype(BF16),
    )


def solution(mesh):
    return jax.shard_map(
        shards,
        mesh=mesh,
        in_specs=(
            P("dp", "tensor"),
            P("tensor", "dp"),
            P("tensor", "dp"),
            P("dp", "tensor"),
            P("dp", "tensor"),
        ),
        out_specs=(
            P("dp", "tensor"),
            P("dp", "tensor"),
            P("tensor", "dp"),
            P("tensor", "dp"),
            P("dp", "tensor"),
        ),
        check_vma=False,
    )
```

time: 278 us -> 271 us (0.975)
  waiting for transfers between devices: 177 us -> 50.4 us
  starting transfers between devices: 0.12 us -> 93.6 us
  blocking collectives: 57.7 us -> 0 us
  other arithmetic: 7.48 us -> 55.6 us
  local copies, waits for them, and re-layouts: 6.08 us -> 24.8 us
  matrix products: 15.6 us -> 27.8 us
    ppermute x0 -> x54, starting transfers between devices: none -> 93.6 us  [the longest x10 40.1 us: inward(): came = lax.ppermute(total.astype(BF16), 'tensor', line_pairs(step))]
    all_gather x1 -> x0, waiting for transfers between devices: 76.9 us -> none  [shards(): lax.all_gather(acts, 'tensor', axis=1, tiled=True)]
    reduce_scatter x1 -> x0, waiting for transfers between devices: 72.1 us -> none  [shards(): lax.psum_scatter(parts, 'tensor', scatter_dimension=1, tiled=True)]
    all_gather x4 -> x0, blocking collectives: 57.7 us -> none  [the longest x2 37.5 us: rotate(): every = lax.all_gather(block, 'tensor', axis=0, tiled=True)]
    ppermute x0 -> x54, waiting for transfers between devices: none -> 50.4 us  [the longest x6 29.5 us: outward(): came = lax.ppermute(block, 'tensor', [(b, a) for a, b in pairs])]
    unnamed x4 -> x0, waiting for transfers between devices: 27.6 us -> none
    select_n x0 -> x12, other arithmetic: none -> 19.4 us  [the longest x10 19.2 us: after(): block = jnp.where(jnp.isnan(first), first.astype(block.dtype), block)]
    dot_general x11 -> x52, matrix products: 15.6 us -> 27.8 us  [dot(): lax.dot_general(left, right, (((left_dim,), (right_dim,)), ((), ())), pre...]
  transfers between devices with their start and end apart: 3 -> 54, of which waited for: 3 -> 16; matrix products, arithmetic and copies ran while one was open for 3% -> 34% of each run, Pallas kernels for 0% -> 0%
where the time goes in v2:
time: 271 us; the launch traced here: 269 us
  starting transfers between devices  93.6 us (35%)
  other arithmetic  55.6 us (21%)
  waiting for transfers between devices  50.4 us (19%)
  matrix products  27.8 us (10%)
  local copies, waits for them, and re-layouts  24.8 us (9%)
  between operations  16.6 us (6%)
    ppermute x10, starting transfers between devices, inward(): came = lax.ppermute(total.astype(BF16), 'tensor', line_pairs(step))  40.1 us
    ppermute x28, starting transfers between devices, exchange(): return lax.ppermute(block, axis, [(i, i ^ apart) for i in range(count)])  33.4 us
    ppermute x6, waiting for transfers between devices, outward(): came = lax.ppermute(block, 'tensor', [(b, a) for a, b in pairs])  29.5 us
    dot_general x52, matrix products, dot(): lax.dot_general(left, right, (((left_dim,), (right_dim,)), ((), ())), pre...  27.8 us
    select_n x10, other arithmetic, after(): block = jnp.where(jnp.isnan(first), first.astype(block.dtype), block)  19.2 us
    ppermute x28, waiting for transfers between devices, exchange(): return lax.ppermute(block, axis, [(i, i ^ apart) for i in range(count)])  19.2 us
    ppermute x10, starting transfers between devices, across(): return lax.ppermute(block, 'tensor', [(half - 1, half), (half, half - 1)])  12.3 us
    convert_element_type x5, other arithmetic, shards(): sums = own + across(other.astype(BF16)).astype(F32)  10.2 us
  transfers between devices with their start and end apart: 54, of which 16 were waited for; matrix products, arithmetic and copies ran while one was open for 34% of the time, Pallas kernels for 0%

profile of v2, /device:TPU:0, one launch (start us, length us, event | category | flops | bytes accessed | tf_op | source)
XLA Modules:
  0.0 268.8 jit_solution(15710079098415732975)
XLA Ops:
  1.5 5.0 %collective-permute-start.2 = (bf16[2,16,512]{2,1,0:T(8,128)(2,1)S(1)}, bf16[2,16,512]{2,1,0:T(8,128)(2,1)S(1)}, u32[]{:S(2)}, u32[]{:S(2)}) collective-permute-start(bf16[2,16,512]{2,1,0:T(8,128)(2,1)S(1)} %pad_maximum_fusion.10), channel_id=1, source_target_pairs={{0,3},{1,2},{2,1},{3,0},{4,7},{5,6},{6,5},{7,4},{8,11},{9,10},{10,... | collective-permute-start | bytes 98312 | tf_op jit(solution)/shard_map/ppermute | solution.py:37
  8.4 2.1 collective-permute-done
  12.2 2.5 collective-permute-start.5
  20.1 2.7 collective-permute-start.13
  22.9 3.3 %collective-permute-done.14 = bf16[2,64,512]{2,1,0:T(8,128)(2,1)S(1)} collective-permute-done((bf16[2,64,512]{2,1,0:T(8,128)(2,1)S(1)}, bf16[2,64,512]{2,1,0:T(8,128)(2,1)S(1)}, u32[]{:S(2)}, u32[]{:S(2)}) %collective-permute-start.14) | collective-permute-done | bytes 131104 | tf_op jit(solution)/shard_map/ppermute | solution.py:37
  33.5 2.4 collective-permute-start.17
  37.9 5.3 %collective-permute-start.7 = (bf16[3,64,1024]{2,1,0:T(8,128)(2,1)S(1)}, bf16[3,64,1024]{2,1,0:T(8,128)(2,1)S(1)}, u32[]{:S(2)}, u32[]{:S(2)}) collective-permute-start(bf16[3,64,1024]{2,1,0:T(8,128)(2,1)S(1)} %pad_maximum_fusion.1), channel_id=1, source_target_pairs={{0,1},{3,2},{4,5},{7,6},{8,9},{11,10},{12,13},{15,14},{16,17},{19,... | collective-permute-start | bytes 1179656 | tf_op jit(solution)/shard_map/ppermute | solution.py:102
  53.3 4.9 %collective-permute-start.8 = (bf16[3,64,1024]{2,1,0:T(8,128)(2,1)S(1)}, bf16[3,64,1024]{2,1,0:T(8,128)(2,1)S(1)}, u32[]{:S(2)}, u32[]{:S(2)}) collective-permute-start(bf16[3,64,1024]{2,1,0:T(8,128)(2,1)S(1)} %maximum_select_fusion), channel_id=1, source_target_pairs={{0,1},{3,2},{4,5},{7,6},{8,9},{11,10},{12,13},{15,14},{16,17},{19,... | collective-permute-start | bytes 1179656 | tf_op jit(solution)/shard_map/ppermute | solution.py:102
  67.3 2.1 collective-permute-start.20
  78.3 2.4 maximum_select_fusion.1
  80.7 2.1 collective-permute-start.19
  84.7 2.5 add_convert_fusion.3
  93.9 2.5 maximum_select_fusion.4
  96.4 4.7 %collective-permute-start.25 = (bf16[3,64,1024]{2,1,0:T(8,128)(2,1)}, bf16[3,64,1024]{2,1,0:T(8,128)(2,1)}, u32[]{:S(2)}, u32[]{:S(2)}) collective-permute-start(bf16[3,64,1024]{2,1,0:T(8,128)(2,1)} %maximum_select_fusion.4), channel_id=1, source_target_pairs={{0,1},{3,2},{4,5},{7,6},{8,9},{11,10},{12,13},{15,14},{16,17},{19,... | collective-permute-start | bytes 1179656 | tf_op jit(solution)/shard_map/ppermute | solution.py:102
  103.6 2.3 maximum_select_fusion.3
  106.0 2.2 collective-permute-start.24
  108.2 2.0 convert_add_fusion.3
  112.6 2.6 add_convert_fusion.2
  122.5 2.6 maximum_select_fusion.6
  125.0 6.2 %collective-permute-start.30 = (bf16[3,64,1024]{2,1,0:T(8,128)(2,1)}, bf16[3,64,1024]{2,1,0:T(8,128)(2,1)}, u32[]{:S(2)}, u32[]{:S(2)}) collective-permute-start(bf16[3,64,1024]{2,1,0:T(8,128)(2,1)} %maximum_select_fusion.6), channel_id=1, source_target_pairs={{0,1},{3,2},{4,5},{7,6},{8,9},{11,10},{12,13},{15,14},{16,17},{19,... | collective-permute-start | bytes 1179656 | tf_op jit(solution)/shard_map/ppermute | solution.py:102
  133.9 2.5 maximum_select_fusion.5
  136.3 2.0 collective-permute-start.29
  146.1 2.6 add_convert_fusion.1
  152.4 2.4 maximum_select_fusion.8
  154.9 9.2 %collective-permute-start.35 = (bf16[3,64,1024]{2,1,0:T(8,128)(2,1)}, bf16[3,64,1024]{2,1,0:T(8,128)(2,1)}, u32[]{:S(2)}, u32[]{:S(2)}) collective-permute-start(bf16[3,64,1024]{2,1,0:T(8,128)(2,1)} %maximum_select_fusion.8), channel_id=1, source_target_pairs={{0,1},{3,2},{4,5},{7,6},{8,9},{11,10},{12,13},{15,14},{16,17},{19,... | collective-permute-start | bytes 1179656 | tf_op jit(solution)/shard_map/ppermute | solution.py:102
  194.5 25.6 %collective-permute-done.33 = bf16[3,128,1024]{2,1,0:T(8,128)(2,1)S(1)} collective-permute-done((bf16[3,128,1024]{2,1,0:T(8,128)(2,1)S(1)}, bf16[3,128,1024]{2,1,0:T(8,128)(2,1)S(1)}, u32[]{:S(2)}, u32[]{:S(2)}) %collective-permute-start.33) | collective-permute-done | bytes 786464 | tf_op jit(solution)/shard_map/ppermute | solution.py:111
  220.5 3.9 %collective-permute-done.45 = bf16[3,64,1024]{2,1,0:T(8,128)(2,1)S(1)} collective-permute-done((bf16[3,64,1024]{2,1,0:T(8,128)(2,1)S(1)}, bf16[3,64,1024]{2,1,0:T(8,128)(2,1)S(1)}, u32[]{:S(2)}, u32[]{:S(2)}) %collective-permute-start.45) | collective-permute-done | bytes 393248 | tf_op jit(solution)/shard_map/ppermute | solution.py:111
  242.3 2.7 %collective-permute-start.53 = (bf16[2,16,512]{2,1,0:T(8,128)(2,1)S(1)}, bf16[2,16,512]{2,1,0:T(8,128)(2,1)S(1)}, u32[]{:S(2)}, u32[]{:S(2)}) collective-permute-start(bf16[2,16,512]{2,1,0:T(8,128)(2,1)S(1)} %fusion.55), channel_id=1, source_target_pairs={{0,3},{1,2},{2,1},{3,0},{4,7},{5,6},{6,5},{7,4},{8,11},{9,10},{10,... | collective-permute-start | bytes 98312 | tf_op jit(solution)/shard_map/ppermute | solution.py:37
  249.6 2.1 collective-permute-start.40
  253.4 2.2 collective-permute-done.40
  259.2 2.6 collective-permute-start.42
  262.0 4.2 %collective-permute-done.41 = bf16[2,64,512]{2,1,0:T(8,128)(2,1)S(1)} collective-permute-done((bf16[2,64,512]{2,1,0:T(8,128)(2,1)S(1)}, bf16[2,64,512]{2,1,0:T(8,128)(2,1)S(1)}, u32[]{:S(2)}, u32[]{:S(2)}) %collective-permute-start.41) | collective-permute-done | bytes 131104 | tf_op jit(solution)/shard_map/ppermute | solution.py:37
  (328 shorter events, 127.8 us)
Async XLA Ops:
  1.5 10.2 %collective-permute-start.2 = (bf16[2,16,512]{2,1,0:T(8,128)(2,1)S(1)}, bf16[2,16,512]{2,1,0:T(8,128)(2,1)S(1)}, u32[]{:S(2)}, u32[]{:S(2)}) collective-permute-start(bf16[2,16,512]{2,1,0:T(8,128)(2,1)S(1)} %pad_maximum_fusion.10), channel_id=1, source_target_pairs={{0,3},{1,2},{2,1},{3,0},{4,7},{5,6},{6,5},{7,4},{8,11},{9,10},{10,... | collective-permute-start | bytes 98312 | tf_op jit(solution)/shard_map/ppermute | solution.py:37
  20.1 10.2 %collective-permute-start.12 = (bf16[2,64,512]{2,1,0:T(8,128)(2,1)S(1)}, bf16[2,64,512]{2,1,0:T(8,128)(2,1)}, u32[]{:S(2)}, u32[]{:S(2)}) collective-permute-start(bf16[2,64,512]{2,1,0:T(8,128)(2,1)S(1)} %fusion.37), channel_id=1, source_target_pairs={{0,1},{1,0},{2,3},{3,2},{4,5},{5,4},{6,7},{7,6},{8,9},{9,8},{10,11... | collective-permute-start | bytes 393224 | tf_op jit(solution)/shard_map/ppermute | solution.py:37
  20.1 11.4 %collective-permute-start.13 = (bf16[2,64,512]{2,1,0:T(8,128)(2,1)S(1)}, bf16[2,64,512]{2,1,0:T(8,128)(2,1)}, u32[]{:S(2)}, u32[]{:S(2)}) collective-permute-start(bf16[2,64,512]{2,1,0:T(8,128)(2,1)S(1)} %fusion.37), channel_id=1, source_target_pairs={{0,2},{1,3},{2,0},{3,1},{4,6},{5,7},{6,4},{7,5},{8,10},{9,11},{10,... | collective-permute-start | bytes 393224 | tf_op jit(solution)/shard_map/ppermute | solution.py:37
  33.5 10.4 %collective-permute-start.17 = (bf16[2,4,1,16,512]{4,3,2,0,1:T(8,128)(2,1)S(1)}, bf16[2,4,1,16,512]{4,3,2,0,1:T(8,128)(2,1)S(1)}, u32[]{:S(2)}, u32[]{:S(2)}) collective-permute-start(bf16[2,4,1,16,512]{4,3,2,0,1:T(8,128)(2,1)S(1)} %get-tuple-element.86), channel_id=1, source_target_pairs={{0,24},{4,28},{8,16},{12,20},{16,8},{20,12},{24,0},{28,4},{1,25},{... | collective-permute-start | bytes 393224 | tf_op jit(solution)/shard_map/ppermute | solution.py:37
  37.9 10.5 %collective-permute-start.7 = (bf16[3,64,1024]{2,1,0:T(8,128)(2,1)S(1)}, bf16[3,64,1024]{2,1,0:T(8,128)(2,1)S(1)}, u32[]{:S(2)}, u32[]{:S(2)}) collective-permute-start(bf16[3,64,1024]{2,1,0:T(8,128)(2,1)S(1)} %pad_maximum_fusion.1), channel_id=1, source_target_pairs={{0,1},{3,2},{4,5},{7,6},{8,9},{11,10},{12,13},{15,14},{16,17},{19,... | collective-permute-start | bytes 1179656 | tf_op jit(solution)/shard_map/ppermute | solution.py:102
  44.9 13.4 %collective-permute-start.18 = (bf16[2,4,4,16,512]{4,3,2,0,1:T(8,128)(2,1)}, bf16[2,4,4,16,512]{4,3,2,0,1:T(8,128)(2,1)}, u32[]{:S(2)}, u32[]{:S(2)}) collective-permute-start(bf16[2,4,4,16,512]{4,3,2,0,1:T(8,128)(2,1)} %pad_maximum_fusion), channel_id=1, source_target_pairs={{0,4},{4,0},{8,12},{12,8},{16,20},{20,16},{24,28},{28,24},{1,5},{5... | collective-permute-start | bytes 1572872 | tf_op jit(solution)/shard_map/ppermute | solution.py:37
  49.4 33.4 %collective-permute-start.9 = (bf16[3,64,1024]{2,1,0:T(8,128)(2,1)}, bf16[3,64,1024]{2,1,0:T(8,128)(2,1)}, u32[]{:S(2)}, u32[]{:S(2)}) collective-permute-start(bf16[3,64,1024]{2,1,0:T(8,128)(2,1)} %add_convert_fusion.4), channel_id=1, source_target_pairs={{1,2},{2,1},{5,6},{6,5},{9,10},{10,9},{13,14},{14,13},{17,18},{18,... | collective-permute-start | bytes 1179656 | tf_op jit(solution)/shard_map/ppermute | solution.py:119
  53.3 22.2 %collective-permute-start.8 = (bf16[3,64,1024]{2,1,0:T(8,128)(2,1)S(1)}, bf16[3,64,1024]{2,1,0:T(8,128)(2,1)S(1)}, u32[]{:S(2)}, u32[]{:S(2)}) collective-permute-start(bf16[3,64,1024]{2,1,0:T(8,128)(2,1)S(1)} %maximum_select_fusion), channel_id=1, source_target_pairs={{0,1},{3,2},{4,5},{7,6},{8,9},{11,10},{12,13},{15,14},{16,17},{19,... | collective-permute-start | bytes 1179656 | tf_op jit(solution)/shard_map/ppermute | solution.py:102
  67.3 17.4 %collective-permute-start.20 = (bf16[3,64,1024]{2,1,0:T(8,128)(2,1)}, bf16[3,64,1024]{2,1,0:T(8,128)(2,1)}, u32[]{:S(2)}, u32[]{:S(2)}) collective-permute-start(bf16[3,64,1024]{2,1,0:T(8,128)(2,1)} %maximum_select_fusion.2), channel_id=1, source_target_pairs={{0,1},{3,2},{4,5},{7,6},{8,9},{11,10},{12,13},{15,14},{16,17},{19,... | collective-permute-start | bytes 1179656 | tf_op jit(solution)/shard_map/ppermute | solution.py:102
  80.7 20.4 %collective-permute-start.19 = (bf16[3,64,1024]{2,1,0:T(8,128)(2,1)}, bf16[3,64,1024]{2,1,0:T(8,128)(2,1)}, u32[]{:S(2)}, u32[]{:S(2)}) collective-permute-start(bf16[3,64,1024]{2,1,0:T(8,128)(2,1)} %maximum_select_fusion.1), channel_id=1, source_target_pairs={{0,1},{3,2},{4,5},{7,6},{8,9},{11,10},{12,13},{15,14},{16,17},{19,... | collective-permute-start | bytes 1179656 | tf_op jit(solution)/shard_map/ppermute | solution.py:102
  87.3 20.9 %collective-permute-start.21 = (bf16[3,64,1024]{2,1,0:T(8,128)(2,1)}, bf16[3,64,1024]{2,1,0:T(8,128)(2,1)}, u32[]{:S(2)}, u32[]{:S(2)}) collective-permute-start(bf16[3,64,1024]{2,1,0:T(8,128)(2,1)} %add_convert_fusion.3), channel_id=1, source_target_pairs={{1,2},{2,1},{5,6},{6,5},{9,10},{10,9},{13,14},{14,13},{17,18},{18,... | collective-permute-start | bytes 1179656 | tf_op jit(solution)/shard_map/ppermute | solution.py:119
  89.8 26.8 %collective-permute-start.10 = (bf16[3,64,1024]{2,1,0:T(8,128)(2,1)}, bf16[3,64,1024]{2,1,0:T(8,128)(2,1)}, u32[]{:S(2)}, u32[]{:S(2)}) collective-permute-start(bf16[3,64,1024]{2,1,0:T(8,128)(2,1)} %pad_maximum_fusion.2), channel_id=1, source_target_pairs={{1,2},{2,1},{5,6},{6,5},{9,10},{10,9},{13,14},{14,13},{17,18},{18,... | collective-permute-start | bytes 1179656 | tf_op jit(solution)/shard_map/ppermute | solution.py:119
  96.4 16.2 %collective-permute-start.25 = (bf16[3,64,1024]{2,1,0:T(8,128)(2,1)}, bf16[3,64,1024]{2,1,0:T(8,128)(2,1)}, u32[]{:S(2)}, u32[]{:S(2)}) collective-permute-start(bf16[3,64,1024]{2,1,0:T(8,128)(2,1)} %maximum_select_fusion.4), channel_id=1, source_target_pairs={{0,1},{3,2},{4,5},{7,6},{8,9},{11,10},{12,13},{15,14},{16,17},{19,... | collective-permute-start | bytes 1179656 | tf_op jit(solution)/shard_map/ppermute | solution.py:102
  106.0 25.3 %collective-permute-start.24 = (bf16[3,64,1024]{2,1,0:T(8,128)(2,1)}, bf16[3,64,1024]{2,1,0:T(8,128)(2,1)}, u32[]{:S(2)}, u32[]{:S(2)}) collective-permute-start(bf16[3,64,1024]{2,1,0:T(8,128)(2,1)} %maximum_select_fusion.3), channel_id=1, source_target_pairs={{0,1},{3,2},{4,5},{7,6},{8,9},{11,10},{12,13},{15,14},{16,17},{19,... | collective-permute-start | bytes 1179656 | tf_op jit(solution)/shard_map/ppermute | solution.py:102
  111.2 27.2 %collective-permute-start.22 = (bf16[3,64,1024]{2,1,0:T(8,128)(2,1)}, bf16[3,64,1024]{2,1,0:T(8,128)(2,1)}, u32[]{:S(2)}, u32[]{:S(2)}) collective-permute-start(bf16[3,64,1024]{2,1,0:T(8,128)(2,1)} %pad_maximum_fusion.3), channel_id=1, source_target_pairs={{1,2},{2,1},{5,6},{6,5},{9,10},{10,9},{13,14},{14,13},{17,18},{18,... | collective-permute-start | bytes 1179656 | tf_op jit(solution)/shard_map/ppermute | solution.py:119
  115.1 26.6 %collective-permute-start.26 = (bf16[3,64,1024]{2,1,0:T(8,128)(2,1)}, bf16[3,64,1024]{2,1,0:T(8,128)(2,1)}, u32[]{:S(2)}, u32[]{:S(2)}) collective-permute-start(bf16[3,64,1024]{2,1,0:T(8,128)(2,1)} %add_convert_fusion.2), channel_id=1, source_target_pairs={{1,2},{2,1},{5,6},{6,5},{9,10},{10,9},{13,14},{14,13},{17,18},{18,... | collective-permute-start | bytes 1179656 | tf_op jit(solution)/shard_map/ppermute | solution.py:119
  118.5 49.8 %collective-permute-start.11 = (bf16[3,128,1024]{2,1,0:T(8,128)(2,1)}, bf16[3,128,1024]{2,1,0:T(8,128)(2,1)}, u32[]{:S(2)}, u32[]{:S(2)}) collective-permute-start(bf16[3,128,1024]{2,1,0:T(8,128)(2,1)} %maximum_maximum_fusion.1), channel_id=1, source_target_pairs={{1,0},{2,3},{5,4},{6,7},{9,8},{10,11},{13,12},{14,15},{17,16},{18,... | collective-permute-start | bytes 2359304 | tf_op jit(solution)/shard_map/ppermute | solution.py:111
  125.0 21.0 %collective-permute-start.30 = (bf16[3,64,1024]{2,1,0:T(8,128)(2,1)}, bf16[3,64,1024]{2,1,0:T(8,128)(2,1)}, u32[]{:S(2)}, u32[]{:S(2)}) collective-permute-start(bf16[3,64,1024]{2,1,0:T(8,128)(2,1)} %maximum_select_fusion.6), channel_id=1, source_target_pairs={{0,1},{3,2},{4,5},{7,6},{8,9},{11,10},{12,13},{15,14},{16,17},{19,... | collective-permute-start | bytes 1179656 | tf_op jit(solution)/shard_map/ppermute | solution.py:102
  136.3 18.6 %collective-permute-start.29 = (bf16[3,64,1024]{2,1,0:T(8,128)(2,1)}, bf16[3,64,1024]{2,1,0:T(8,128)(2,1)}, u32[]{:S(2)}, u32[]{:S(2)}) collective-permute-start(bf16[3,64,1024]{2,1,0:T(8,128)(2,1)} %maximum_select_fusion.5), channel_id=1, source_target_pairs={{0,1},{3,2},{4,5},{7,6},{8,9},{11,10},{12,13},{15,14},{16,17},{19,... | collective-permute-start | bytes 1179656 | tf_op jit(solution)/shard_map/ppermute | solution.py:102
  140.3 45.6 %collective-permute-start.23 = (bf16[3,128,1024]{2,1,0:T(8,128)(2,1)}, bf16[3,128,1024]{2,1,0:T(8,128)(2,1)}, u32[]{:S(2)}, u32[]{:S(2)}) collective-permute-start(bf16[3,128,1024]{2,1,0:T(8,128)(2,1)} %maximum_maximum_fusion.2), channel_id=1, source_target_pairs={{1,0},{2,3},{5,4},{6,7},{9,8},{10,11},{13,12},{14,15},{17,16},{18,... | collective-permute-start | bytes 2359304 | tf_op jit(solution)/shard_map/ppermute | solution.py:111
  144.7 28.9 %collective-permute-start.27 = (bf16[3,64,1024]{2,1,0:T(8,128)(2,1)}, bf16[3,64,1024]{2,1,0:T(8,128)(2,1)}, u32[]{:S(2)}, u32[]{:S(2)}) collective-permute-start(bf16[3,64,1024]{2,1,0:T(8,128)(2,1)} %pad_maximum_fusion.4), channel_id=1, source_target_pairs={{1,2},{2,1},{5,6},{6,5},{9,10},{10,9},{13,14},{14,13},{17,18},{18,... | collective-permute-start | bytes 1179656 | tf_op jit(solution)/shard_map/ppermute | solution.py:119
  148.7 29.9 %collective-permute-start.31 = (bf16[3,64,1024]{2,1,0:T(8,128)(2,1)}, bf16[3,64,1024]{2,1,0:T(8,128)(2,1)}, u32[]{:S(2)}, u32[]{:S(2)}) collective-permute-start(bf16[3,64,1024]{2,1,0:T(8,128)(2,1)} %add_convert_fusion.1), channel_id=1, source_target_pairs={{1,2},{2,1},{5,6},{6,5},{9,10},{10,9},{13,14},{14,13},{17,18},{18,... | collective-permute-start | bytes 1179656 | tf_op jit(solution)/shard_map/ppermute | solution.py:119
  154.9 21.0 %collective-permute-start.35 = (bf16[3,64,1024]{2,1,0:T(8,128)(2,1)}, bf16[3,64,1024]{2,1,0:T(8,128)(2,1)}, u32[]{:S(2)}, u32[]{:S(2)}) collective-permute-start(bf16[3,64,1024]{2,1,0:T(8,128)(2,1)} %maximum_select_fusion.8), channel_id=1, source_target_pairs={{0,1},{3,2},{4,5},{7,6},{8,9},{11,10},{12,13},{15,14},{16,17},{19,... | collective-permute-start | bytes 1179656 | tf_op jit(solution)/shard_map/ppermute | solution.py:102
  168.3 13.2 %collective-permute-start.34 = (bf16[3,64,1024]{2,1,0:T(8,128)(2,1)S(1)}, bf16[3,64,1024]{2,1,0:T(8,128)(2,1)S(1)}, u32[]{:S(2)}, u32[]{:S(2)}) collective-permute-start(bf16[3,64,1024]{2,1,0:T(8,128)(2,1)S(1)} %maximum_select_fusion.7), channel_id=1, source_target_pairs={{0,1},{3,2},{4,5},{7,6},{8,9},{11,10},{12,13},{15,14},{16,17},{19,... | collective-permute-start | bytes 1179656 | tf_op jit(solution)/shard_map/ppermute | solution.py:102
  174.6 17.3 %collective-permute-start.28 = (bf16[3,128,1024]{2,1,0:T(8,128)(2,1)S(1)}, bf16[3,128,1024]{2,1,0:T(8,128)(2,1)S(1)}, u32[]{:S(2)}, u32[]{:S(2)}) collective-permute-start(bf16[3,128,1024]{2,1,0:T(8,128)(2,1)S(1)} %maximum_maximum_fusion.3), channel_id=1, source_target_pairs={{1,0},{2,3},{5,4},{6,7},{9,8},{10,11},{13,12},{14,15},{17,16},{18,... | collective-permute-start | bytes 2359304 | tf_op jit(solution)/shard_map/ppermute | solution.py:111
  182.6 8.1 %collective-permute-start.44 = (bf16[3,64,1024]{2,1,0:T(8,128)(2,1)S(1)}, bf16[3,64,1024]{2,1,0:T(8,128)(2,1)S(1)}, u32[]{:S(2)}, u32[]{:S(2)}) collective-permute-start(bf16[3,64,1024]{2,1,0:T(8,128)(2,1)S(1)} %pad_maximum_fusion.6), channel_id=1, source_target_pairs={{1,2},{2,1},{5,6},{6,5},{9,10},{10,9},{13,14},{14,13},{17,18},{18,... | collective-permute-start | bytes 1179656 | tf_op jit(solution)/shard_map/ppermute | solution.py:119
  183.3 41.2 %collective-permute-start.46 = (bf16[3,64,1024]{2,1,0:T(8,128)(2,1)S(1)}, bf16[3,64,1024]{2,1,0:T(8,128)(2,1)S(1)}, u32[]{:S(2)}, u32[]{:S(2)}) collective-permute-start(bf16[3,64,1024]{2,1,0:T(8,128)(2,1)S(1)} %pad_maximum_fusion.6), channel_id=1, source_target_pairs={{1,0},{2,3},{5,4},{6,7},{9,8},{10,11},{13,12},{14,15},{17,16},{18,... | collective-permute-start | bytes 1179656 | tf_op jit(solution)/shard_map/ppermute | solution.py:111
  184.6 35.5 %collective-permute-start.33 = (bf16[3,128,1024]{2,1,0:T(8,128)(2,1)S(1)}, bf16[3,128,1024]{2,1,0:T(8,128)(2,1)S(1)}, u32[]{:S(2)}, u32[]{:S(2)}) collective-permute-start(bf16[3,128,1024]{2,1,0:T(8,128)(2,1)S(1)} %maximum_maximum_fusion.4), channel_id=1, source_target_pairs={{1,0},{2,3},{5,4},{6,7},{9,8},{10,11},{13,12},{14,15},{17,16},{18,... | collective-permute-start | bytes 2359304 | tf_op jit(solution)/shard_map/ppermute | solution.py:111
  190.6 33.7 %collective-permute-start.45 = (bf16[3,64,1024]{2,1,0:T(8,128)(2,1)S(1)}, bf16[3,64,1024]{2,1,0:T(8,128)(2,1)S(1)}, u32[]{:S(2)}, u32[]{:S(2)}) collective-permute-start(bf16[3,64,1024]{2,1,0:T(8,128)(2,1)S(1)} %collective-permute-done.44), channel_id=1, source_target_pairs={{1,0},{2,3},{5,4},{6,7},{9,8},{10,11},{13,12},{14,15},{17,16},{18,... | collective-permute-start | bytes 1179656 | tf_op jit(solution)/shard_map/ppermute | solution.py:111
  240.1 9.1 %collective-permute-start.37 = (bf16[2,4,64,512]{3,2,1,0:T(8,128)(2,1)S(1)}, bf16[2,4,64,512]{3,2,1,0:T(8,128)(2,1)S(1)}, u32[]{:S(2)}, u32[]{:S(2)}) collective-permute-start(bf16[2,4,64,512]{3,2,1,0:T(8,128)(2,1)S(1)} %fusion.8), channel_id=1, source_target_pairs={{0,4},{4,0},{8,12},{12,8},{16,20},{20,16},{24,28},{28,24},{1,5},{5... | collective-permute-start | bytes 1572872 | tf_op jit(solution)/shard_map/ppermute | solution.py:37
  257.3 9.1 %collective-permute-start.43 = (bf16[2,64,512]{2,1,0:T(8,128)(2,1)S(1)}, bf16[2,64,512]{2,1,0:T(8,128)(2,1)S(1)}, u32[]{:S(2)}, u32[]{:S(2)}) collective-permute-start(bf16[2,64,512]{2,1,0:T(8,128)(2,1)S(1)} %bitcast.377), channel_id=1, source_target_pairs={{0,3},{1,2},{2,1},{3,0},{4,7},{5,6},{6,5},{7,4},{8,11},{9,10},{10,... | collective-permute-start | bytes 393224 | tf_op jit(solution)/shard_map/ppermute | solution.py:37
  259.2 8.7 %collective-permute-start.42 = (bf16[2,64,512]{2,1,0:T(8,128)(2,1)S(1)}, bf16[2,64,512]{2,1,0:T(8,128)(2,1)S(1)}, u32[]{:S(2)}, u32[]{:S(2)}) collective-permute-start(bf16[2,64,512]{2,1,0:T(8,128)(2,1)S(1)} %bitcast.379), channel_id=1, source_target_pairs={{0,2},{1,3},{2,0},{3,1},{4,6},{5,7},{6,4},{7,5},{8,10},{9,11},{10,... | collective-permute-start | bytes 393224 | tf_op jit(solution)/shard_map/ppermute | solution.py:37
  (70 other events, 597.2 us)

commit v3 on v2

--- a/solution.py
+++ b/solution.py
@@ -25,11 +25,25 @@
     )
 
 
-def after(block, *others):
-    for other in others:
-        first = other[(0,) * other.ndim]
-        block = jnp.where(jnp.isnan(first), first.astype(block.dtype), block)
-    return block
+def after(block, other):
+    if other.shape != block.shape:
+        row = other[(0,) * (other.ndim - 1)]
+        other = jnp.resize(row, block.shape[-1:]).astype(block.dtype)
+    return jnp.where(jnp.isnan(other), other, block)
+
+
+def my_row(length):
+    groups = lax.axis_size("tensor")
+    table = np.zeros((groups, 1 + groups, length), np.float32)
+    signs = sylvester(groups)
+    for me in range(groups):
+        table[me, 0] = me >= groups // 2
+        for apart in range(groups):
+            table[me, 1 + apart] = signs[me, me ^ apart]
+    depth = np.minimum(np.arange(groups), groups - 1 - np.arange(groups)).astype(np.float32)
+    table = np.concatenate([table, np.broadcast_to(depth[:, None, None], (groups, 1, length))], axis=1)
+    row = lax.dynamic_index_in_dim(jnp.asarray(table), lax.axis_index("tensor"), keepdims=False)
+    return row[0], row[1:-1], row[-1]
 
 
 def exchange(block, axis, apart):
@@ -41,18 +55,12 @@
     return [block] + [exchange(block, "tensor", k) for k in range(1, lax.axis_size("tensor"))]
 
 
-def rotate(pieces):
+def rotate(pieces, signs):
     width = pieces[0].shape[-1]
-    me = lax.axis_index("tensor").astype(jnp.int32)
     square = jnp.asarray(sylvester(width), BF16)
     total = 0.0
-    for apart, piece in enumerate(pieces):
-        both = me & (me ^ apart)
-        odd = jnp.int32(0)
-        for bit in range((len(pieces) - 1).bit_length()):
-            odd = odd ^ ((both >> bit) & 1)
-        turned = dot(piece, square, piece.ndim - 1, 0)
-        total = total + jnp.where(odd == 1, -turned, turned)
+    for piece, sign in zip(pieces, signs):
+        total = total + dot(piece, square, piece.ndim - 1, 0) * sign[:width]
     return total * (1.0 / math.sqrt(D))
 
 
@@ -104,13 +112,10 @@
     return total, came
 
 
-def outward(block):
-    me = lax.axis_index("tensor")
+def outward(block, depth):
     for step in reversed(fold_steps()):
-        pairs = line_pairs(step)
-        came = lax.ppermute(block, "tensor", [(b, a) for a, b in pairs])
-        takes = (me == pairs[0][0]) | (me == pairs[1][0])
-        block = jnp.where(takes, came, block)
+        came = lax.ppermute(block, "tensor", [(b, a) for a, b in line_pairs(step)])
+        block = jnp.where(depth[: block.shape[-1]] == step, came, block)
     return block
 
 
@@ -137,31 +142,33 @@
     step = STEP if mine % STEP == 0 else mine
     chunks = mine // step
     half = peers * step // 2
-    far_side = lax.axis_index("tensor") >= lax.axis_size("tensor") // 2
+    far, signs, depth = my_row(max(width, gate_weight.shape[1]))
+    far = far[:width] > 0.5
 
     both = jnp.stack([tokens, out_grad])
 
     def arrive(turned):
         low, high = gather_dp(turned.reshape(2, -1, 1, step, width), 2)
-        every = jnp.where(
-            far_side, jnp.concatenate([low, high], axis=2), jnp.concatenate([high, low], axis=2)
-        )
-        return [every[:, i].reshape(2, 2 * half, width) for i in range(every.shape[1])]
+        other, own = jnp.where(far, low, high), jnp.where(far, high, low)
+        return [part.reshape(2, -1, half, width) for part in (other, own)]
 
     pieces = spread(both[:, :step])
-    late_pieces = spread(after(both[:, step:], *pieces[1:2])) if chunks > 1 else None
-    rows = arrive(rotate(pieces).astype(BF16))
+    late_pieces = spread(after(both[:, step:], pieces[1])) if chunks > 1 else None
+    groups = [arrive(rotate(pieces, signs).astype(BF16))]
 
     done, arrived = [], []
     for i in range(chunks):
-        x, g = rows[i]
-        parts = [dot(x, gate_weight, 1, 0), dot(x, up_weight, 1, 0), dot(g, down_weight, 1, 1)]
+        group, place = (groups[0], 0) if i == 0 else (groups[1], i - 1)
         sums = []
-        for place in (slice(0, half), slice(half, 2 * half)):
+        for x, g in [(part[0, place], part[1, place]) for part in group]:
+            parts = [dot(x, gate_weight, 1, 0), dot(x, up_weight, 1, 0), dot(g, down_weight, 1, 1)]
+            message = jnp.stack(parts).astype(BF16)
             ahead = arrived[:1] if len(arrived) < 2 else arrived[-2:-1]
-            message = after(jnp.stack([part[place] for part in parts]).astype(BF16), *ahead)
-            if not rows[i + 1 :] and i + 1 < chunks:
-                rows += arrive(rotate([after(late_pieces[0], message)] + late_pieces[1:]).astype(BF16))
+            if ahead:
+                message = after(message, ahead[0])
+            if len(groups) == 1 and chunks > 1:
+                turned = rotate([after(late_pieces[0], message)] + late_pieces[1:], signs)
+                groups.append(arrive(turned.astype(BF16)))
             total, came = inward(message)
             arrived.append(came)
             sums.append(total)
@@ -169,29 +176,34 @@
         sums = own + across(other.astype(BF16)).astype(F32)
         own = activations(sums[0], sums[1], sums[2])
         if i == chunks - 1:
-            done += [outward(across(own)), outward(own)]
+            done += [outward(across(own), depth), outward(own, depth)]
         else:
-            done.append(outward(jnp.concatenate([across(own), own], axis=1)))
-
-    def leave(blocks, first, last):
+            done.append(outward(jnp.concatenate([across(own), own], axis=1), depth))
+
+    def leave(blocks, first, last, ahead):
         sums = []
         for acts in blocks:
             mixed = dot(acts[0], down_weight, 1, 0)
             grads = dot(acts[1], gate_weight, 1, 1) + dot(acts[2], up_weight, 1, 1)
             sums.append(jnp.stack([mixed, grads]))
         sums = jnp.concatenate(sums, axis=1).reshape(2, last - first, 2, half, width)
-        low = jnp.where(far_side, sums[:, :, 0], sums[:, :, 1])
-        high = jnp.where(far_side, sums[:, :, 1], sums[:, :, 0])
-        if last < chunks:
-            high = after(high, own)
+        low = jnp.where(far, sums[:, :, 0], sums[:, :, 1])
+        high = jnp.where(far, sums[:, :, 1], sums[:, :, 0])
+        if ahead is not None:
+            high = after(high, ahead)
         sums = scatter_dp(low, high).astype(BF16)
-        return rotate(spread(sums.reshape(2, (last - first) * step, width)))
-
-    ends = [leave(done[:-2], 0, chunks - 1)] if chunks > 1 else []
-    ends.append(leave(done[-2:], chunks - 1, chunks))
-    ends = jnp.concatenate(ends, axis=1)
+        pieces = spread(sums.reshape(2, (last - first) * step, width))
+        return rotate(pieces, signs), pieces[-1]
+
+    if chunks > 1:
+        first, came = leave(done[:-2], 0, chunks - 1, own)
+        last, _ = leave(done[-2:], chunks - 1, chunks, came)
+        ends = jnp.concatenate([first, last], axis=1)
+    else:
+        ends, _ = leave(done, 0, 1, None)
 
     acts = jnp.concatenate(done, axis=1)
+    rows = [jnp.stack(group, axis=2).reshape(2, -1, width) for group in groups]
     rows = jnp.concatenate(rows, axis=1)
     factor = 1.0 / math.sqrt(rows.shape[1])
     return (

time: 271 us -> 235 us (0.87)
  waiting for transfers between devices: 50.4 us -> 102 us
  other arithmetic: 55.6 us -> 9.5 us
  local copies, waits for them, and re-layouts: 24.8 us -> 1.15 us
  between operations: 16.6 us -> 1.97 us
  starting transfers between devices: 93.6 us -> 89.9 us
    ppermute x10, waiting for transfers between devices: 1.64 us -> 37.8 us  [inward(): came = lax.ppermute(total.astype(BF16), 'tensor', line_pairs(step))]
    select_n x12 -> x11, other arithmetic: 19.4 us -> 0.68 us  [the longest x9 0.54 us: after(): return jnp.where(jnp.isnan(other), other, block)]
    convert_element_type x5, other arithmetic: 10.2 us -> 0.71 us  [shards(): sums = own + across(other.astype(BF16)).astype(F32)]
    slice x12 -> x4, local copies, waits for them, and re-layouts: 10.1 us -> 0.93 us  [the longest x1 0.87 us: rotate(): total = total + dot(piece, square, piece.ndim - 1, 0) * sign[:width]]
    ppermute x28, waiting for transfers between devices: 19.2 us -> 28.3 us  [exchange(): return lax.ppermute(block, axis, [(i, i ^ apart) for i in range(count)])]
    unnamed x114 -> x12, local copies, waits for them, and re-layouts: 8.44 us -> 0.03 us
    add x5, other arithmetic: 8.72 us -> 1.18 us  [shards(): sums = own + across(other.astype(BF16)).astype(F32)]
    ppermute x6, waiting for transfers between devices: 29.5 us -> 36.2 us  [outward(): came = lax.ppermute(block, 'tensor', [(b, a) for a, b in line_pairs(step)])]
  transfers between devices with their start and end apart: 54 -> 54, of which waited for: 16 -> 28; matrix products, arithmetic and copies ran while one was open for 34% -> 13% of each run, Pallas kernels for 0% -> 0%
where the time goes in v3:
time: 235 us; the launch traced here: 234 us
  waiting for transfers between devices  102 us (43%)
  starting transfers between devices  89.9 us (38%)
  matrix products  29.4 us (13%)
  other arithmetic  9.5 us (4%)
    ppermute x10, starting transfers between devices, inward(): came = lax.ppermute(total.astype(BF16), 'tensor', line_pairs(step))  41.7 us
    ppermute x10, waiting for transfers between devices, inward(): came = lax.ppermute(total.astype(BF16), 'tensor', line_pairs(step))  37.8 us
    ppermute x6, waiting for transfers between devices, outward(): came = lax.ppermute(block, 'tensor', [(b, a) for a, b in line_pairs(step)])  36.2 us
    ppermute x28, starting transfers between devices, exchange(): return lax.ppermute(block, axis, [(i, i ^ apart) for i in range(count)])  33.6 us
    dot_general x67, matrix products, dot(): lax.dot_general(left, right, (((left_dim,), (right_dim,)), ((), ())), pre...  29.4 us
    ppermute x28, waiting for transfers between devices, exchange(): return lax.ppermute(block, axis, [(i, i ^ apart) for i in range(count)])  28.3 us
    ppermute x6, starting transfers between devices, outward(): came = lax.ppermute(block, 'tensor', [(b, a) for a, b in line_pairs(step)])  7.75 us
    ppermute x10, starting transfers between devices, across(): return lax.ppermute(block, 'tensor', [(half - 1, half), (half, half - 1)])  6.86 us
  transfers between devices with their start and end apart: 54, of which 28 were waited for; matrix products, arithmetic and copies ran while one was open for 13% of the time, Pallas kernels for 0%

profile of v3, /device:TPU:0, one launch (start us, length us, event | category | flops | bytes accessed | tf_op | source)
XLA Modules:
  0.0 234.4 jit_solution(13844721441131217996)
XLA Ops:
  1.5 5.0 %collective-permute-start.2 = (bf16[2,16,512]{2,1,0:T(8,128)(2,1)S(1)}, bf16[2,16,512]{2,1,0:T(8,128)(2,1)S(1)}, u32[]{:S(2)}, u32[]{:S(2)}) collective-permute-start(bf16[2,16,512]{2,1,0:T(8,128)(2,1)S(1)} %pad_maximum_fusion.13), channel_id=1, source_target_pairs={{0,3},{1,2},{2,1},{3,0},{4,7},{5,6},{6,5},{7,4},{8,11},{9,10},{10,... | collective-permute-start | bytes 98312 | tf_op jit(solution)/shard_map/ppermute | solution.py:51
  11.8 2.5 %collective-permute-start.5 = (bf16[2,1,1,16,512]{4,3,0,2,1:T(8,128)(2,1)S(1)}, bf16[2,1,1,16,512]{4,3,0,2,1:T(8,128)(2,1)S(1)}, u32[]{:S(2)}, u32[]{:S(2)}) collective-permute-start(bf16[2,1,1,16,512]{4,3,0,2,1:T(8,128)(2,1)S(1)} %fusion.54), channel_id=1, source_target_pairs={{0,24},{4,28},{8,16},{12,20},{16,8},{20,12},{24,0},{28,4},{1,25},{... | collective-permute-start | bytes 98312 | tf_op jit(solution)/shard_map/ppermute | solution.py:51
  15.5 3.0 %collective-permute-start.14 = (bf16[2,64,512]{2,1,0:T(8,128)(2,1)S(1)}, bf16[2,64,512]{2,1,0:T(8,128)(2,1)S(1)}, u32[]{:S(2)}, u32[]{:S(2)}) collective-permute-start(bf16[2,64,512]{2,1,0:T(8,128)(2,1)S(1)} %fusion.78), channel_id=1, source_target_pairs={{0,3},{1,2},{2,1},{3,0},{4,7},{5,6},{6,5},{7,4},{8,11},{9,10},{10,... | collective-permute-start | bytes 393224 | tf_op jit(solution)/shard_map/ppermute | solution.py:51
  23.8 4.0 %collective-permute-done.13 = bf16[2,64,512]{2,1,0:T(8,128)(2,1)S(1)} collective-permute-done((bf16[2,64,512]{2,1,0:T(8,128)(2,1)S(1)}, bf16[2,64,512]{2,1,0:T(8,128)(2,1)S(1)}, u32[]{:S(2)}, u32[]{:S(2)}) %collective-permute-start.13) | collective-permute-done | bytes 131104 | tf_op jit(solution)/shard_map/ppermute | solution.py:51
  29.0 2.5 %collective-permute-start.17 = (bf16[2,4,1,16,512]{4,3,2,1,0:T(8,128)(2,1)S(1)}, bf16[2,4,1,16,512]{4,3,2,1,0:T(8,128)(2,1)S(1)}, u32[]{:S(2)}, u32[]{:S(2)}) collective-permute-start(bf16[2,4,1,16,512]{4,3,2,1,0:T(8,128)(2,1)S(1)} %bitcast.431), channel_id=1, source_target_pairs={{0,24},{4,28},{8,16},{12,20},{16,8},{20,12},{24,0},{28,4},{1,25},{... | collective-permute-start | bytes 393224 | tf_op jit(solution)/shard_map/ppermute | solution.py:51
  33.4 2.1 collective-permute-start.7
  38.8 3.5 %collective-permute-done.7 = bf16[3,64,1024]{2,1,0:T(8,128)(2,1)S(1)} collective-permute-done((bf16[3,64,1024]{2,1,0:T(8,128)(2,1)S(1)}, bf16[3,64,1024]{2,1,0:T(8,128)(2,1)S(1)}, u32[]{:S(2)}, u32[]{:S(2)}) %collective-permute-start.7) | collective-permute-done | bytes 393248 | tf_op jit(solution)/shard_map/ppermute | solution.py:110
  50.8 6.6 %collective-permute-start.8 = (bf16[3,64,1024]{2,1,0:T(8,128)(2,1)S(1)}, bf16[3,64,1024]{2,1,0:T(8,128)(2,1)S(1)}, u32[]{:S(2)}, u32[]{:S(2)}) collective-permute-start(bf16[3,64,1024]{2,1,0:T(8,128)(2,1)S(1)} %get-tuple-element.38), channel_id=1, source_target_pairs={{0,1},{3,2},{4,5},{7,6},{8,9},{11,10},{12,13},{15,14},{16,17},{19,... | collective-permute-start | bytes 1179656 | tf_op jit(solution)/shard_map/ppermute | solution.py:110
  59.8 7.0 %collective-permute-done.8 = bf16[3,64,1024]{2,1,0:T(8,128)(2,1)S(1)} collective-permute-done((bf16[3,64,1024]{2,1,0:T(8,128)(2,1)S(1)}, bf16[3,64,1024]{2,1,0:T(8,128)(2,1)S(1)}, u32[]{:S(2)}, u32[]{:S(2)}) %collective-permute-start.8) | collective-permute-done | bytes 393248 | tf_op jit(solution)/shard_map/ppermute | solution.py:110
  67.8 3.1 %collective-permute-done.20 = bf16[3,64,1024]{2,1,0:T(8,128)(2,1)S(1)} collective-permute-done((bf16[3,64,1024]{2,1,0:T(8,128)(2,1)S(1)}, bf16[3,64,1024]{2,1,0:T(8,128)(2,1)S(1)}, u32[]{:S(2)}, u32[]{:S(2)}) %collective-permute-start.20) | collective-permute-done | bytes 393248 | tf_op jit(solution)/shard_map/ppermute | solution.py:110
  71.9 7.1 %collective-permute-start.19 = (bf16[3,64,1024]{2,1,0:T(8,128)(2,1)S(1)}, bf16[3,64,1024]{2,1,0:T(8,128)(2,1)S(1)}, u32[]{:S(2)}, u32[]{:S(2)}) collective-permute-start(bf16[3,64,1024]{2,1,0:T(8,128)(2,1)S(1)} %compare_select_fusion.8), channel_id=1, source_target_pairs={{0,1},{3,2},{4,5},{7,6},{8,9},{11,10},{12,13},{15,14},{16,17},{19,... | collective-permute-start | bytes 1179656 | tf_op jit(solution)/shard_map/ppermute | solution.py:110
  81.9 5.6 %collective-permute-done.19 = bf16[3,64,1024]{2,1,0:T(8,128)(2,1)S(1)} collective-permute-done((bf16[3,64,1024]{2,1,0:T(8,128)(2,1)S(1)}, bf16[3,64,1024]{2,1,0:T(8,128)(2,1)S(1)}, u32[]{:S(2)}, u32[]{:S(2)}) %collective-permute-start.19) | collective-permute-done | bytes 393248 | tf_op jit(solution)/shard_map/ppermute | solution.py:110
  88.6 3.6 %collective-permute-done.25 = bf16[3,64,1024]{2,1,0:T(8,128)(2,1)S(1)} collective-permute-done((bf16[3,64,1024]{2,1,0:T(8,128)(2,1)S(1)}, bf16[3,64,1024]{2,1,0:T(8,128)(2,1)S(1)}, u32[]{:S(2)}, u32[]{:S(2)}) %collective-permute-start.25) | collective-permute-done | bytes 393248 | tf_op jit(solution)/shard_map/ppermute | solution.py:110
  92.2 4.4 %collective-permute-start.30 = (bf16[3,64,1024]{2,1,0:T(8,128)(2,1)S(1)}, bf16[3,64,1024]{2,1,0:T(8,128)(2,1)S(1)}, u32[]{:S(2)}, u32[]{:S(2)}) collective-permute-start(bf16[3,64,1024]{2,1,0:T(8,128)(2,1)S(1)} %compare_select_fusion.4), channel_id=1, source_target_pairs={{0,1},{3,2},{4,5},{7,6},{8,9},{11,10},{12,13},{15,14},{16,17},{19,... | collective-permute-start | bytes 1179656 | tf_op jit(solution)/shard_map/ppermute | solution.py:110
  100.2 4.0 %collective-permute-done.30 = bf16[3,64,1024]{2,1,0:T(8,128)(2,1)S(1)} collective-permute-done((bf16[3,64,1024]{2,1,0:T(8,128)(2,1)S(1)}, bf16[3,64,1024]{2,1,0:T(8,128)(2,1)S(1)}, u32[]{:S(2)}, u32[]{:S(2)}) %collective-permute-start.30) | collective-permute-done | bytes 393248 | tf_op jit(solution)/shard_map/ppermute | solution.py:110
  105.1 4.7 %collective-permute-done.24 = bf16[3,64,1024]{2,1,0:T(8,128)(2,1)S(1)} collective-permute-done((bf16[3,64,1024]{2,1,0:T(8,128)(2,1)S(1)}, bf16[3,64,1024]{2,1,0:T(8,128)(2,1)S(1)}, u32[]{:S(2)}, u32[]{:S(2)}) %collective-permute-start.24) | collective-permute-done | bytes 393248 | tf_op jit(solution)/shard_map/ppermute | solution.py:110
  109.9 4.4 %collective-permute-start.29 = (bf16[3,64,1024]{2,1,0:T(8,128)(2,1)S(1)}, bf16[3,64,1024]{2,1,0:T(8,128)(2,1)S(1)}, u32[]{:S(2)}, u32[]{:S(2)}) collective-permute-start(bf16[3,64,1024]{2,1,0:T(8,128)(2,1)S(1)} %compare_select_fusion.5), channel_id=1, source_target_pairs={{0,1},{3,2},{4,5},{7,6},{8,9},{11,10},{12,13},{15,14},{16,17},{19,... | collective-permute-start | bytes 1179656 | tf_op jit(solution)/shard_map/ppermute | solution.py:110
  115.6 7.2 %collective-permute-start.35 = (bf16[3,64,1024]{2,1,0:T(8,128)(2,1)S(1)}, bf16[3,64,1024]{2,1,0:T(8,128)(2,1)S(1)}, u32[]{:S(2)}, u32[]{:S(2)}) collective-permute-start(bf16[3,64,1024]{2,1,0:T(8,128)(2,1)S(1)} %compare_select_fusion.2), channel_id=1, source_target_pairs={{0,1},{3,2},{4,5},{7,6},{8,9},{11,10},{12,13},{15,14},{16,17},{19,... | collective-permute-start | bytes 1179656 | tf_op jit(solution)/shard_map/ppermute | solution.py:110
  125.0 3.0 %collective-permute-done.35 = bf16[3,64,1024]{2,1,0:T(8,128)(2,1)S(1)} collective-permute-done((bf16[3,64,1024]{2,1,0:T(8,128)(2,1)S(1)}, bf16[3,64,1024]{2,1,0:T(8,128)(2,1)S(1)}, u32[]{:S(2)}, u32[]{:S(2)}) %collective-permute-start.35) | collective-permute-done | bytes 393248 | tf_op jit(solution)/shard_map/ppermute | solution.py:110
  129.0 5.9 %collective-permute-start.34 = (bf16[3,64,1024]{2,1,0:T(8,128)(2,1)S(1)}, bf16[3,64,1024]{2,1,0:T(8,128)(2,1)S(1)}, u32[]{:S(2)}, u32[]{:S(2)}) collective-permute-start(bf16[3,64,1024]{2,1,0:T(8,128)(2,1)S(1)} %compare_select_fusion.3), channel_id=1, source_target_pairs={{0,1},{3,2},{4,5},{7,6},{8,9},{11,10},{12,13},{15,14},{16,17},{19,... | collective-permute-start | bytes 1179656 | tf_op jit(solution)/shard_map/ppermute | solution.py:110
  137.5 2.6 %collective-permute-done.34 = bf16[3,64,1024]{2,1,0:T(8,128)(2,1)S(1)} collective-permute-done((bf16[3,64,1024]{2,1,0:T(8,128)(2,1)S(1)}, bf16[3,64,1024]{2,1,0:T(8,128)(2,1)S(1)}, u32[]{:S(2)}, u32[]{:S(2)}) %collective-permute-start.34) | collective-permute-done | bytes 393248 | tf_op jit(solution)/shard_map/ppermute | solution.py:110
  146.9 11.6 %collective-permute-done.28 = bf16[3,128,1024]{2,1,0:T(8,128)(2,1)S(1)} collective-permute-done((bf16[3,128,1024]{2,1,0:T(8,128)(2,1)S(1)}, bf16[3,128,1024]{2,1,0:T(8,128)(2,1)S(1)}, u32[]{:S(2)}, u32[]{:S(2)}) %collective-permute-start.28) | collective-permute-done | bytes 786464 | tf_op jit(solution)/shard_map/ppermute | solution.py:117
  160.2 21.5 %collective-permute-done.33 = bf16[3,128,1024]{2,1,0:T(8,128)(2,1)S(1)} collective-permute-done((bf16[3,128,1024]{2,1,0:T(8,128)(2,1)S(1)}, bf16[3,128,1024]{2,1,0:T(8,128)(2,1)S(1)}, u32[]{:S(2)}, u32[]{:S(2)}) %collective-permute-start.33) | collective-permute-done | bytes 786464 | tf_op jit(solution)/shard_map/ppermute | solution.py:117
  182.8 3.1 %collective-permute-done.45 = bf16[3,64,1024]{2,1,0:T(8,128)(2,1)S(1)} collective-permute-done((bf16[3,64,1024]{2,1,0:T(8,128)(2,1)S(1)}, bf16[3,64,1024]{2,1,0:T(8,128)(2,1)S(1)}, u32[]{:S(2)}, u32[]{:S(2)}) %collective-permute-start.45) | collective-permute-done | bytes 393248 | tf_op jit(solution)/shard_map/ppermute | solution.py:117
  188.2 2.0 multiply_convert_fusion
  195.2 2.5 %collective-permute-start.40 = (bf16[2,4,16,512]{3,2,1,0:T(8,128)(2,1)S(1)}, bf16[2,4,16,512]{3,2,1,0:T(8,128)(2,1)S(1)}, u32[]{:S(2)}, u32[]{:S(2)}) collective-permute-start(bf16[2,4,16,512]{3,2,1,0:T(8,128)(2,1)S(1)} %get-tuple-element.35), channel_id=1, source_target_pairs={{0,24},{4,28},{8,16},{12,20},{16,8},{20,12},{24,0},{28,4},{1,25},{... | collective-permute-start | bytes 393224 | tf_op jit(solution)/shard_map/ppermute | solution.py:51
  199.0 3.3 %collective-permute-done.40 = bf16[2,4,16,512]{3,2,1,0:T(8,128)(2,1)S(1)} collective-permute-done((bf16[2,4,16,512]{3,2,1,0:T(8,128)(2,1)S(1)}, bf16[2,4,16,512]{3,2,1,0:T(8,128)(2,1)S(1)}, u32[]{:S(2)}, u32[]{:S(2)}) %collective-permute-start.40) | collective-permute-done | bytes 131104 | tf_op jit(solution)/shard_map/ppermute | solution.py:51
  202.3 2.5 %collective-permute-done.39 = bf16[2,4,16,512]{3,2,1,0:T(8,128)(2,1)S(1)} collective-permute-done((bf16[2,4,16,512]{3,2,1,0:T(8,128)(2,1)S(1)}, bf16[2,4,16,512]{3,2,1,0:T(8,128)(2,1)S(1)}, u32[]{:S(2)}, u32[]{:S(2)}) %collective-permute-start.39) | collective-permute-done | bytes 131104 | tf_op jit(solution)/shard_map/ppermute | solution.py:51
  205.0 2.7 %collective-permute-start.43 = (bf16[2,64,512]{2,1,0:T(8,128)(2,1)S(1)}, bf16[2,64,512]{2,1,0:T(8,128)(2,1)S(1)}, u32[]{:S(2)}, u32[]{:S(2)}) collective-permute-start(bf16[2,64,512]{2,1,0:T(8,128)(2,1)S(1)} %bitcast.447), channel_id=1, source_target_pairs={{0,3},{1,2},{2,1},{3,0},{4,7},{5,6},{6,5},{7,4},{8,11},{9,10},{10,... | collective-permute-start | bytes 393224 | tf_op jit(solution)/shard_map/ppermute | solution.py:51
  209.9 3.5 %collective-permute-done.43 = bf16[2,64,512]{2,1,0:T(8,128)(2,1)S(1)} collective-permute-done((bf16[2,64,512]{2,1,0:T(8,128)(2,1)S(1)}, bf16[2,64,512]{2,1,0:T(8,128)(2,1)S(1)}, u32[]{:S(2)}, u32[]{:S(2)}) %collective-permute-start.43) | collective-permute-done | bytes 131104 | tf_op jit(solution)/shard_map/ppermute | solution.py:51
  213.7 4.1 %collective-permute-done.42 = bf16[2,64,512]{2,1,0:T(8,128)(2,1)S(1)} collective-permute-done((bf16[2,64,512]{2,1,0:T(8,128)(2,1)S(1)}, bf16[2,64,512]{2,1,0:T(8,128)(2,1)S(1)}, u32[]{:S(2)}, u32[]{:S(2)}) %collective-permute-start.42) | collective-permute-done | bytes 131104 | tf_op jit(solution)/shard_map/ppermute | solution.py:51
  225.2 2.7 %collective-permute-start.53 = (bf16[2,16,512]{2,1,0:T(8,128)(2,1)S(1)}, bf16[2,16,512]{2,1,0:T(8,128)(2,1)S(1)}, u32[]{:S(2)}, u32[]{:S(2)}) collective-permute-start(bf16[2,16,512]{2,1,0:T(8,128)(2,1)S(1)} %fusion.86), channel_id=1, source_target_pairs={{0,3},{1,2},{2,1},{3,0},{4,7},{5,6},{6,5},{7,4},{8,11},{9,10},{10,... | collective-permute-start | bytes 98312 | tf_op jit(solution)/shard_map/ppermute | solution.py:51
  (229 shorter events, 80.8 us)
Async XLA Ops:
  1.5 7.7 %collective-permute-start.2 = (bf16[2,16,512]{2,1,0:T(8,128)(2,1)S(1)}, bf16[2,16,512]{2,1,0:T(8,128)(2,1)S(1)}, u32[]{:S(2)}, u32[]{:S(2)}) collective-permute-start(bf16[2,16,512]{2,1,0:T(8,128)(2,1)S(1)} %pad_maximum_fusion.13), channel_id=1, source_target_pairs={{0,3},{1,2},{2,1},{3,0},{4,7},{5,6},{6,5},{7,4},{8,11},{9,10},{10,... | collective-permute-start | bytes 98312 | tf_op jit(solution)/shard_map/ppermute | solution.py:51
  11.8 8.3 %collective-permute-start.5 = (bf16[2,1,1,16,512]{4,3,0,2,1:T(8,128)(2,1)S(1)}, bf16[2,1,1,16,512]{4,3,0,2,1:T(8,128)(2,1)S(1)}, u32[]{:S(2)}, u32[]{:S(2)}) collective-permute-start(bf16[2,1,1,16,512]{4,3,0,2,1:T(8,128)(2,1)S(1)} %fusion.54), channel_id=1, source_target_pairs={{0,24},{4,28},{8,16},{12,20},{16,8},{20,12},{24,0},{28,4},{1,25},{... | collective-permute-start | bytes 98312 | tf_op jit(solution)/shard_map/ppermute | solution.py:51
  15.5 8.1 %collective-permute-start.14 = (bf16[2,64,512]{2,1,0:T(8,128)(2,1)S(1)}, bf16[2,64,512]{2,1,0:T(8,128)(2,1)S(1)}, u32[]{:S(2)}, u32[]{:S(2)}) collective-permute-start(bf16[2,64,512]{2,1,0:T(8,128)(2,1)S(1)} %fusion.78), channel_id=1, source_target_pairs={{0,3},{1,2},{2,1},{3,0},{4,7},{5,6},{6,5},{7,4},{8,11},{9,10},{10,... | collective-permute-start | bytes 393224 | tf_op jit(solution)/shard_map/ppermute | solution.py:51
  20.0 7.8 %collective-permute-start.13 = (bf16[2,64,512]{2,1,0:T(8,128)(2,1)S(1)}, bf16[2,64,512]{2,1,0:T(8,128)(2,1)S(1)}, u32[]{:S(2)}, u32[]{:S(2)}) collective-permute-start(bf16[2,64,512]{2,1,0:T(8,128)(2,1)S(1)} %fusion.78), channel_id=1, source_target_pairs={{0,2},{1,3},{2,0},{3,1},{4,6},{5,7},{6,4},{7,5},{8,10},{9,11},{10,... | collective-permute-start | bytes 393224 | tf_op jit(solution)/shard_map/ppermute | solution.py:51
  20.1 8.6 %collective-permute-start.12 = (bf16[2,64,512]{2,1,0:T(8,128)(2,1)S(1)}, bf16[2,64,512]{2,1,0:T(8,128)(2,1)S(1)}, u32[]{:S(2)}, u32[]{:S(2)}) collective-permute-start(bf16[2,64,512]{2,1,0:T(8,128)(2,1)S(1)} %fusion.78), channel_id=1, source_target_pairs={{0,1},{1,0},{2,3},{3,2},{4,5},{5,4},{6,7},{7,6},{8,9},{9,8},{10,11... | collective-permute-start | bytes 393224 | tf_op jit(solution)/shard_map/ppermute | solution.py:51
  33.4 8.9 %collective-permute-start.7 = (bf16[3,64,1024]{2,1,0:T(8,128)(2,1)S(1)}, bf16[3,64,1024]{2,1,0:T(8,128)(2,1)S(1)}, u32[]{:S(2)}, u32[]{:S(2)}) collective-permute-start(bf16[3,64,1024]{2,1,0:T(8,128)(2,1)S(1)} %pad_maximum_fusion.3), channel_id=1, source_target_pairs={{0,1},{3,2},{4,5},{7,6},{8,9},{11,10},{12,13},{15,14},{16,17},{19,... | collective-permute-start | bytes 1179656 | tf_op jit(solution)/shard_map/ppermute | solution.py:110
  42.4 17.4 %collective-permute-start.9 = (bf16[3,64,1024]{2,1,0:T(8,128)(2,1)S(1)}, bf16[3,64,1024]{2,1,0:T(8,128)(2,1)S(1)}, u32[]{:S(2)}, u32[]{:S(2)}) collective-permute-start(bf16[3,64,1024]{2,1,0:T(8,128)(2,1)S(1)} %add_convert_fusion.4), channel_id=1, source_target_pairs={{1,2},{2,1},{5,6},{6,5},{9,10},{10,9},{13,14},{14,13},{17,18},{18,... | collective-permute-start | bytes 1179656 | tf_op jit(solution)/shard_map/ppermute | solution.py:124
  50.8 15.9 %collective-permute-start.8 = (bf16[3,64,1024]{2,1,0:T(8,128)(2,1)S(1)}, bf16[3,64,1024]{2,1,0:T(8,128)(2,1)S(1)}, u32[]{:S(2)}, u32[]{:S(2)}) collective-permute-start(bf16[3,64,1024]{2,1,0:T(8,128)(2,1)S(1)} %get-tuple-element.38), channel_id=1, source_target_pairs={{0,1},{3,2},{4,5},{7,6},{8,9},{11,10},{12,13},{15,14},{16,17},{19,... | collective-permute-start | bytes 1179656 | tf_op jit(solution)/shard_map/ppermute | solution.py:110
  57.8 13.1 %collective-permute-start.20 = (bf16[3,64,1024]{2,1,0:T(8,128)(2,1)S(1)}, bf16[3,64,1024]{2,1,0:T(8,128)(2,1)S(1)}, u32[]{:S(2)}, u32[]{:S(2)}) collective-permute-start(bf16[3,64,1024]{2,1,0:T(8,128)(2,1)S(1)} %get-tuple-element.37), channel_id=1, source_target_pairs={{0,1},{3,2},{4,5},{7,6},{8,9},{11,10},{12,13},{15,14},{16,17},{19,... | collective-permute-start | bytes 1179656 | tf_op jit(solution)/shard_map/ppermute | solution.py:110
  67.2 13.4 %collective-permute-start.10 = (bf16[3,64,1024]{2,1,0:T(8,128)(2,1)S(1)}, bf16[3,64,1024]{2,1,0:T(8,128)(2,1)S(1)}, u32[]{:S(2)}, u32[]{:S(2)}) collective-permute-start(bf16[3,64,1024]{2,1,0:T(8,128)(2,1)S(1)} %pad_maximum_fusion.4), channel_id=1, source_target_pairs={{1,2},{2,1},{5,6},{6,5},{9,10},{10,9},{13,14},{14,13},{17,18},{18,... | collective-permute-start | bytes 1179656 | tf_op jit(solution)/shard_map/ppermute | solution.py:124
  71.1 10.8 %collective-permute-start.21 = (bf16[3,64,1024]{2,1,0:T(8,128)(2,1)S(1)}, bf16[3,64,1024]{2,1,0:T(8,128)(2,1)S(1)}, u32[]{:S(2)}, u32[]{:S(2)}) collective-permute-start(bf16[3,64,1024]{2,1,0:T(8,128)(2,1)S(1)} %add_convert_fusion.3), channel_id=1, source_target_pairs={{1,2},{2,1},{5,6},{6,5},{9,10},{10,9},{13,14},{14,13},{17,18},{18,... | collective-permute-start | bytes 1179656 | tf_op jit(solution)/shard_map/ppermute | solution.py:124
  71.9 15.6 %collective-permute-start.19 = (bf16[3,64,1024]{2,1,0:T(8,128)(2,1)S(1)}, bf16[3,64,1024]{2,1,0:T(8,128)(2,1)S(1)}, u32[]{:S(2)}, u32[]{:S(2)}) collective-permute-start(bf16[3,64,1024]{2,1,0:T(8,128)(2,1)S(1)} %compare_select_fusion.8), channel_id=1, source_target_pairs={{0,1},{3,2},{4,5},{7,6},{8,9},{11,10},{12,13},{15,14},{16,17},{19,... | collective-permute-start | bytes 1179656 | tf_op jit(solution)/shard_map/ppermute | solution.py:110
  79.2 13.0 %collective-permute-start.25 = (bf16[3,64,1024]{2,1,0:T(8,128)(2,1)S(1)}, bf16[3,64,1024]{2,1,0:T(8,128)(2,1)S(1)}, u32[]{:S(2)}, u32[]{:S(2)}) collective-permute-start(bf16[3,64,1024]{2,1,0:T(8,128)(2,1)S(1)} %compare_select_fusion.6), channel_id=1, source_target_pairs={{0,1},{3,2},{4,5},{7,6},{8,9},{11,10},{12,13},{15,14},{16,17},{19,... | collective-permute-start | bytes 1179656 | tf_op jit(solution)/shard_map/ppermute | solution.py:110
  80.6 43.3 %collective-permute-start.11 = (bf16[3,128,1024]{2,1,0:T(8,128)(2,1)S(1)}, bf16[3,128,1024]{2,1,0:T(8,128)(2,1)S(1)}, u32[]{:S(2)}, u32[]{:S(2)}) collective-permute-start(bf16[3,128,1024]{2,1,0:T(8,128)(2,1)S(1)} %maximum_maximum_fusion.1), channel_id=1, source_target_pairs={{1,0},{2,3},{5,4},{6,7},{9,8},{10,11},{13,12},{14,15},{17,16},{18,... | collective-permute-start | bytes 2359304 | tf_op jit(solution)/shard_map/ppermute | solution.py:117
  87.9 11.0 %collective-permute-start.22 = (bf16[3,64,1024]{2,1,0:T(8,128)(2,1)S(1)}, bf16[3,64,1024]{2,1,0:T(8,128)(2,1)S(1)}, u32[]{:S(2)}, u32[]{:S(2)}) collective-permute-start(bf16[3,64,1024]{2,1,0:T(8,128)(2,1)S(1)} %pad_maximum_fusion.5), channel_id=1, source_target_pairs={{1,2},{2,1},{5,6},{6,5},{9,10},{10,9},{13,14},{14,13},{17,18},{18,... | collective-permute-start | bytes 1179656 | tf_op jit(solution)/shard_map/ppermute | solution.py:124
  92.2 12.1 %collective-permute-start.30 = (bf16[3,64,1024]{2,1,0:T(8,128)(2,1)S(1)}, bf16[3,64,1024]{2,1,0:T(8,128)(2,1)S(1)}, u32[]{:S(2)}, u32[]{:S(2)}) collective-permute-start(bf16[3,64,1024]{2,1,0:T(8,128)(2,1)S(1)} %compare_select_fusion.4), channel_id=1, source_target_pairs={{0,1},{3,2},{4,5},{7,6},{8,9},{11,10},{12,13},{15,14},{16,17},{19,... | collective-permute-start | bytes 1179656 | tf_op jit(solution)/shard_map/ppermute | solution.py:110
  96.7 13.2 %collective-permute-start.24 = (bf16[3,64,1024]{2,1,0:T(8,128)(2,1)S(1)}, bf16[3,64,1024]{2,1,0:T(8,128)(2,1)S(1)}, u32[]{:S(2)}, u32[]{:S(2)}) collective-permute-start(bf16[3,64,1024]{2,1,0:T(8,128)(2,1)S(1)} %compare_select_fusion.7), channel_id=1, source_target_pairs={{0,1},{3,2},{4,5},{7,6},{8,9},{11,10},{12,13},{15,14},{16,17},{19,... | collective-permute-start | bytes 1179656 | tf_op jit(solution)/shard_map/ppermute | solution.py:110
  98.2 16.2 %collective-permute-start.26 = (bf16[3,64,1024]{2,1,0:T(8,128)(2,1)S(1)}, bf16[3,64,1024]{2,1,0:T(8,128)(2,1)S(1)}, u32[]{:S(2)}, u32[]{:S(2)}) collective-permute-start(bf16[3,64,1024]{2,1,0:T(8,128)(2,1)S(1)} %add_convert_fusion.2), channel_id=1, source_target_pairs={{1,2},{2,1},{5,6},{6,5},{9,10},{10,9},{13,14},{14,13},{17,18},{18,... | collective-permute-start | bytes 1179656 | tf_op jit(solution)/shard_map/ppermute | solution.py:124
  98.9 45.0 %collective-permute-start.23 = (bf16[3,128,1024]{2,1,0:T(8,128)(2,1)S(1)}, bf16[3,128,1024]{2,1,0:T(8,128)(2,1)S(1)}, u32[]{:S(2)}, u32[]{:S(2)}) collective-permute-start(bf16[3,128,1024]{2,1,0:T(8,128)(2,1)S(1)} %maximum_maximum_fusion.2), channel_id=1, source_target_pairs={{1,0},{2,3},{5,4},{6,7},{9,8},{10,11},{13,12},{14,15},{17,16},{18,... | collective-permute-start | bytes 2359304 | tf_op jit(solution)/shard_map/ppermute | solution.py:117
  104.4 11.1 %collective-permute-start.31 = (bf16[3,64,1024]{2,1,0:T(8,128)(2,1)S(1)}, bf16[3,64,1024]{2,1,0:T(8,128)(2,1)S(1)}, u32[]{:S(2)}, u32[]{:S(2)}) collective-permute-start(bf16[3,64,1024]{2,1,0:T(8,128)(2,1)S(1)} %add_convert_fusion.1), channel_id=1, source_target_pairs={{1,2},{2,1},{5,6},{6,5},{9,10},{10,9},{13,14},{14,13},{17,18},{18,... | collective-permute-start | bytes 1179656 | tf_op jit(solution)/shard_map/ppermute | solution.py:124
  109.9 13.6 %collective-permute-start.29 = (bf16[3,64,1024]{2,1,0:T(8,128)(2,1)S(1)}, bf16[3,64,1024]{2,1,0:T(8,128)(2,1)S(1)}, u32[]{:S(2)}, u32[]{:S(2)}) collective-permute-start(bf16[3,64,1024]{2,1,0:T(8,128)(2,1)S(1)} %compare_select_fusion.5), channel_id=1, source_target_pairs={{0,1},{3,2},{4,5},{7,6},{8,9},{11,10},{12,13},{15,14},{16,17},{19,... | collective-permute-start | bytes 1179656 | tf_op jit(solution)/shard_map/ppermute | solution.py:110
  114.8 21.3 %collective-permute-start.27 = (bf16[3,64,1024]{2,1,0:T(8,128)(2,1)S(1)}, bf16[3,64,1024]{2,1,0:T(8,128)(2,1)S(1)}, u32[]{:S(2)}, u32[]{:S(2)}) collective-permute-start(bf16[3,64,1024]{2,1,0:T(8,128)(2,1)S(1)} %pad_maximum_fusion.6), channel_id=1, source_target_pairs={{1,2},{2,1},{5,6},{6,5},{9,10},{10,9},{13,14},{14,13},{17,18},{18,... | collective-permute-start | bytes 1179656 | tf_op jit(solution)/shard_map/ppermute | solution.py:124
  115.6 12.5 %collective-permute-start.35 = (bf16[3,64,1024]{2,1,0:T(8,128)(2,1)S(1)}, bf16[3,64,1024]{2,1,0:T(8,128)(2,1)S(1)}, u32[]{:S(2)}, u32[]{:S(2)}) collective-permute-start(bf16[3,64,1024]{2,1,0:T(8,128)(2,1)S(1)} %compare_select_fusion.2), channel_id=1, source_target_pairs={{0,1},{3,2},{4,5},{7,6},{8,9},{11,10},{12,13},{15,14},{16,17},{19,... | collective-permute-start | bytes 1179656 | tf_op jit(solution)/shard_map/ppermute | solution.py:110
  128.2 9.3 %collective-permute-start.36 = (bf16[3,64,1024]{2,1,0:T(8,128)(2,1)S(1)}, bf16[3,64,1024]{2,1,0:T(8,128)(2,1)S(1)}, u32[]{:S(2)}, u32[]{:S(2)}) collective-permute-start(bf16[3,64,1024]{2,1,0:T(8,128)(2,1)S(1)} %add_convert_fusion), channel_id=1, source_target_pairs={{1,2},{2,1},{5,6},{6,5},{9,10},{10,9},{13,14},{14,13},{17,18},{18,... | collective-permute-start | bytes 1179656 | tf_op jit(solution)/shard_map/ppermute | solution.py:124
  129.0 11.2 %collective-permute-start.34 = (bf16[3,64,1024]{2,1,0:T(8,128)(2,1)S(1)}, bf16[3,64,1024]{2,1,0:T(8,128)(2,1)S(1)}, u32[]{:S(2)}, u32[]{:S(2)}) collective-permute-start(bf16[3,64,1024]{2,1,0:T(8,128)(2,1)S(1)} %compare_select_fusion.3), channel_id=1, source_target_pairs={{0,1},{3,2},{4,5},{7,6},{8,9},{11,10},{12,13},{15,14},{16,17},{19,... | collective-permute-start | bytes 1179656 | tf_op jit(solution)/shard_map/ppermute | solution.py:110
  136.2 22.4 %collective-permute-start.28 = (bf16[3,128,1024]{2,1,0:T(8,128)(2,1)S(1)}, bf16[3,128,1024]{2,1,0:T(8,128)(2,1)S(1)}, u32[]{:S(2)}, u32[]{:S(2)}) collective-permute-start(bf16[3,128,1024]{2,1,0:T(8,128)(2,1)S(1)} %maximum_maximum_fusion.3), channel_id=1, source_target_pairs={{1,0},{2,3},{5,4},{6,7},{9,8},{10,11},{13,12},{14,15},{17,16},{18,... | collective-permute-start | bytes 2359304 | tf_op jit(solution)/shard_map/ppermute | solution.py:117
  141.3 44.8 %collective-permute-start.46 = (bf16[3,64,1024]{2,1,0:T(8,128)(2,1)S(1)}, bf16[3,64,1024]{2,1,0:T(8,128)(2,1)S(1)}, u32[]{:S(2)}, u32[]{:S(2)}) collective-permute-start(bf16[3,64,1024]{2,1,0:T(8,128)(2,1)S(1)} %pad_maximum_fusion.8), channel_id=1, source_target_pairs={{1,0},{2,3},{5,4},{6,7},{9,8},{10,11},{13,12},{14,15},{17,16},{18,... | collective-permute-start | bytes 1179656 | tf_op jit(solution)/shard_map/ppermute | solution.py:117
  142.7 39.0 %collective-permute-start.33 = (bf16[3,128,1024]{2,1,0:T(8,128)(2,1)S(1)}, bf16[3,128,1024]{2,1,0:T(8,128)(2,1)S(1)}, u32[]{:S(2)}, u32[]{:S(2)}) collective-permute-start(bf16[3,128,1024]{2,1,0:T(8,128)(2,1)S(1)} %maximum_maximum_fusion.4), channel_id=1, source_target_pairs={{1,0},{2,3},{5,4},{6,7},{9,8},{10,11},{13,12},{14,15},{17,16},{18,... | collective-permute-start | bytes 2359304 | tf_op jit(solution)/shard_map/ppermute | solution.py:117
  145.6 40.3 %collective-permute-start.45 = (bf16[3,64,1024]{2,1,0:T(8,128)(2,1)S(1)}, bf16[3,64,1024]{2,1,0:T(8,128)(2,1)S(1)}, u32[]{:S(2)}, u32[]{:S(2)}) collective-permute-start(bf16[3,64,1024]{2,1,0:T(8,128)(2,1)S(1)} %collective-permute-done.44), channel_id=1, source_target_pairs={{1,0},{2,3},{5,4},{6,7},{9,8},{10,11},{13,12},{14,15},{17,16},{18,... | collective-permute-start | bytes 1179656 | tf_op jit(solution)/shard_map/ppermute | solution.py:117
  205.0 8.3 %collective-permute-start.43 = (bf16[2,64,512]{2,1,0:T(8,128)(2,1)S(1)}, bf16[2,64,512]{2,1,0:T(8,128)(2,1)S(1)}, u32[]{:S(2)}, u32[]{:S(2)}) collective-permute-start(bf16[2,64,512]{2,1,0:T(8,128)(2,1)S(1)} %bitcast.447), channel_id=1, source_target_pairs={{0,3},{1,2},{2,1},{3,0},{4,7},{5,6},{6,5},{7,4},{8,11},{9,10},{10,... | collective-permute-start | bytes 393224 | tf_op jit(solution)/shard_map/ppermute | solution.py:51
  208.1 9.8 %collective-permute-start.42 = (bf16[2,64,512]{2,1,0:T(8,128)(2,1)S(1)}, bf16[2,64,512]{2,1,0:T(8,128)(2,1)S(1)}, u32[]{:S(2)}, u32[]{:S(2)}) collective-permute-start(bf16[2,64,512]{2,1,0:T(8,128)(2,1)S(1)} %bitcast.448), channel_id=1, source_target_pairs={{0,2},{1,3},{2,0},{3,1},{4,6},{5,7},{6,4},{7,5},{8,10},{9,11},{10,... | collective-permute-start | bytes 393224 | tf_op jit(solution)/shard_map/ppermute | solution.py:51
  208.2 13.6 %collective-permute-start.41 = (bf16[2,64,512]{2,1,0:T(8,128)(2,1)S(1)}, bf16[2,64,512]{2,1,0:T(8,128)(2,1)S(1)}, u32[]{:S(2)}, u32[]{:S(2)}) collective-permute-start(bf16[2,64,512]{2,1,0:T(8,128)(2,1)S(1)} %bitcast.449), channel_id=1, source_target_pairs={{0,1},{1,0},{2,3},{3,2},{4,5},{5,4},{6,7},{7,6},{8,9},{9,8},{10,11... | collective-permute-start | bytes 393224 | tf_op jit(solution)/shard_map/ppermute | solution.py:51
  (28 other events, 208.7 us)

commit v4 on v3

--- a/solution.py
+++ b/solution.py
@@ -26,24 +26,28 @@
 
 
 def after(block, other):
-    if other.shape != block.shape:
-        row = other[(0,) * (other.ndim - 1)]
-        other = jnp.resize(row, block.shape[-1:]).astype(block.dtype)
+    other = other.reshape((-1,) + other.shape[-2:])[0]
+    if other.shape[0] < block.shape[-2]:
+        other = other[:1]
+    other = other[: block.shape[-2]]
+    wide = block.shape[-1]
+    if other.shape[-1] < wide:
+        other = jnp.concatenate([other] * (-(-wide // other.shape[-1])), axis=-1)
+    other = other[:, :wide].astype(block.dtype)
     return jnp.where(jnp.isnan(other), other, block)
 
 
 def my_row(length):
     groups = lax.axis_size("tensor")
-    table = np.zeros((groups, 1 + groups, length), np.float32)
     signs = sylvester(groups)
-    for me in range(groups):
-        table[me, 0] = me >= groups // 2
-        for apart in range(groups):
-            table[me, 1 + apart] = signs[me, me ^ apart]
-    depth = np.minimum(np.arange(groups), groups - 1 - np.arange(groups)).astype(np.float32)
-    table = np.concatenate([table, np.broadcast_to(depth[:, None, None], (groups, 1, length))], axis=1)
-    row = lax.dynamic_index_in_dim(jnp.asarray(table), lax.axis_index("tensor"), keepdims=False)
-    return row[0], row[1:-1], row[-1]
+    me = np.arange(groups)
+    columns = [me >= groups // 2, np.minimum(me, groups - 1 - me)]
+    columns += [signs[me, me ^ apart] for apart in range(groups)]
+    columns += [1 - 2 * (me >> bit & 1) for bit in range(groups.bit_length() - 1)]
+    table = np.stack(columns, axis=1).astype(np.float32)[:, :, None, None]
+    table = jnp.asarray(np.broadcast_to(table, table.shape[:3] + (length,)))
+    row = lax.dynamic_index_in_dim(table, lax.axis_index("tensor"), keepdims=False)
+    return row[0], row[1], row[2 : 2 + groups], row[2 + groups :]
 
 
 def exchange(block, axis, apart):
@@ -60,8 +64,21 @@
     square = jnp.asarray(sylvester(width), BF16)
     total = 0.0
     for piece, sign in zip(pieces, signs):
-        total = total + dot(piece, square, piece.ndim - 1, 0) * sign[:width]
+        total = total + dot(piece, square, piece.ndim - 1, 0) * sign[:, :width]
     return total * (1.0 / math.sqrt(D))
+
+
+def rotate_by_halves(block, bits):
+    width = block.shape[-1]
+    square = jnp.asarray(sylvester(width), BF16)
+    high = lax.reduce_precision(block, 8, 7)
+    low = (block - high).astype(BF16)
+    last = block.ndim - 1
+    block = dot(high.astype(BF16), square, last, 0) + dot(low, square, last, 0)
+    for level, bit in enumerate(bits):
+        came = exchange(block.astype(BF16), "tensor", 1 << level)
+        block = block * bit[:, :width] + came.astype(F32)
+    return block * (1.0 / math.sqrt(D))
 
 
 def dp_stages():
@@ -90,9 +107,10 @@
         low = low.reshape(low.shape[:2] + (len(stage), -1) + low.shape[-1:])
         total = low[:, :, 0]
         for place, apart in enumerate(stage[1:], 1):
-            total = total + exchange(low[:, :, place].astype(BF16), "dp", apart).astype(F32)
+            came = exchange(low[:, :, place].astype(BF16), "dp", apart)
+            total = total + came.astype(F32)
         low = total
-    return low
+    return low, came
 
 
 def line_pairs(step):
@@ -115,7 +133,7 @@
 def outward(block, depth):
     for step in reversed(fold_steps()):
         came = lax.ppermute(block, "tensor", [(b, a) for a, b in line_pairs(step)])
-        block = jnp.where(depth[: block.shape[-1]] == step, came, block)
+        block = jnp.where(depth[:, : block.shape[-1]] == step, came, block)
     return block
 
 
@@ -142,8 +160,8 @@
     step = STEP if mine % STEP == 0 else mine
     chunks = mine // step
     half = peers * step // 2
-    far, signs, depth = my_row(max(width, gate_weight.shape[1]))
-    far = far[:width] > 0.5
+    far, depth, signs, bits = my_row(max(width, gate_weight.shape[1]))
+    far = far[:, :width] > 0.5
 
     both = jnp.stack([tokens, out_grad])
 
@@ -156,55 +174,60 @@
     late_pieces = spread(after(both[:, step:], pieces[1])) if chunks > 1 else None
     groups = [arrive(rotate(pieces, signs).astype(BF16))]
 
-    done, arrived = [], []
+    done, arrived, crossed = [], [], []
     for i in range(chunks):
         group, place = (groups[0], 0) if i == 0 else (groups[1], i - 1)
         sums = []
-        for x, g in [(part[0, place], part[1, place]) for part in group]:
+        for which, (x, g) in enumerate([(part[0, place], part[1, place]) for part in group]):
+            if i > 0:
+                x, g = after(x, arrived[-2]), after(g, arrived[-2])
+            if i > 1 and which == 0:
+                x, g = after(x, crossed[i - 2]), after(g, crossed[i - 2])
             parts = [dot(x, gate_weight, 1, 0), dot(x, up_weight, 1, 0), dot(g, down_weight, 1, 1)]
             message = jnp.stack(parts).astype(BF16)
-            ahead = arrived[:1] if len(arrived) < 2 else arrived[-2:-1]
-            if ahead:
-                message = after(message, ahead[0])
+            if i == 0 and which == 1:
+                message = after(message, arrived[0])
             if len(groups) == 1 and chunks > 1:
-                turned = rotate([after(late_pieces[0], message)] + late_pieces[1:], signs)
-                groups.append(arrive(turned.astype(BF16)))
+                piece = late_pieces[0]
+                for part in message:
+                    piece = after(piece, part)
+                groups.append(arrive(rotate([piece] + late_pieces[1:], signs).astype(BF16)))
             total, came = inward(message)
             arrived.append(came)
             sums.append(total)
         other, own = sums
         sums = own + across(other.astype(BF16)).astype(F32)
         own = activations(sums[0], sums[1], sums[2])
-        if i == chunks - 1:
-            done += [outward(across(own), depth), outward(own, depth)]
-        else:
-            done.append(outward(jnp.concatenate([across(own), own], axis=1), depth))
-
-    def leave(blocks, first, last, ahead):
+        crossed.append(across(own))
+        if i < chunks - 1:
+            done.append(outward(jnp.concatenate([crossed[i], own], axis=1), depth))
+
+    def leave(blocks):
+        count = sum(acts.shape[1] for acts in blocks) // (2 * half)
         sums = []
         for acts in blocks:
             mixed = dot(acts[0], down_weight, 1, 0)
             grads = dot(acts[1], gate_weight, 1, 1) + dot(acts[2], up_weight, 1, 1)
             sums.append(jnp.stack([mixed, grads]))
-        sums = jnp.concatenate(sums, axis=1).reshape(2, last - first, 2, half, width)
+        sums = jnp.concatenate(sums, axis=1).reshape(2, count, 2, half, width)
         low = jnp.where(far, sums[:, :, 0], sums[:, :, 1])
-        high = jnp.where(far, sums[:, :, 1], sums[:, :, 0])
-        if ahead is not None:
-            high = after(high, ahead)
-        sums = scatter_dp(low, high).astype(BF16)
-        pieces = spread(sums.reshape(2, (last - first) * step, width))
-        return rotate(pieces, signs), pieces[-1]
-
-    if chunks > 1:
-        first, came = leave(done[:-2], 0, chunks - 1, own)
-        last, _ = leave(done[-2:], chunks - 1, chunks, came)
-        ends = jnp.concatenate([first, last], axis=1)
-    else:
-        ends, _ = leave(done, 0, 1, None)
+        high = jnp.where(far, sums[:, :, 1], sums[:, :, 0]).astype(BF16)
+        sums, came = scatter_dp(low, high)
+        return sums.reshape(2, count * step, width), high, came
+
+    split, ends = max(chunks - 2, 0), []
+    if split > 0:
+        sums, _, came = leave(done[:split])
+        ends.append(rotate_by_halves(sums, bits))
+        crossed[-1] = after(crossed[-1], came)
+    done += [outward(crossed[-1], depth), outward(own, depth)]
+    sums, message, _ = leave(done[split:])
+    ends.append(rotate(spread(sums.astype(BF16)), signs))
+    ends = jnp.concatenate(ends, axis=1)
 
     acts = jnp.concatenate(done, axis=1)
     rows = [jnp.stack(group, axis=2).reshape(2, -1, width) for group in groups]
-    rows = jnp.concatenate(rows, axis=1)
+    rows = after(jnp.concatenate(rows, axis=1), message[0, 0, :1])
     factor = 1.0 / math.sqrt(rows.shape[1])
     return (
         ends[0],

time: 235 us -> 207 us (0.88)
  waiting for transfers between devices: 102 us -> 49.9 us
  starting transfers between devices: 89.9 us -> 104 us
  matrix products: 29.4 us -> 36.6 us
    ppermute x6, waiting for transfers between devices: 36.2 us -> 1.5 us  [outward(): came = lax.ppermute(block, 'tensor', [(b, a) for a, b in line_pairs(step)])]
    ppermute x10, waiting for transfers between devices: 37.8 us -> 19.3 us  [inward(): came = lax.ppermute(total.astype(BF16), 'tensor', line_pairs(step))]
    ppermute x10, starting transfers between devices: 41.7 us -> 50.3 us  [inward(): came = lax.ppermute(total.astype(BF16), 'tensor', line_pairs(step))]
    dot_general x67 -> x65, matrix products: 29.4 us -> 36.6 us  [dot(): lax.dot_general(left, right, (((left_dim,), (right_dim,)), ((), ())), pre...]
    ppermute x28 -> x27, starting transfers between devices: 33.6 us -> 38.5 us  [exchange(): return lax.ppermute(block, axis, [(i, i ^ apart) for i in range(count)])]
    ppermute x28 -> x27, waiting for transfers between devices: 28.3 us -> 29.1 us  [exchange(): return lax.ppermute(block, axis, [(i, i ^ apart) for i in range(count)])]
  transfers between devices with their start and end apart: 54 -> 53, of which waited for: 28 -> 20; matrix products, arithmetic and copies ran while one was open for 13% -> 20% of each run, Pallas kernels for 0% -> 0%
where the time goes in v4:
time: 207 us; the launch traced here: 206 us
  starting transfers between devices  104 us (50%)
  waiting for transfers between devices  49.9 us (24%)
  matrix products  36.6 us (18%)
  other arithmetic  10.5 us (5%)
  between operations  3.48 us (2%)
  local copies, waits for them, and re-layouts  2.2 us (1%)
    ppermute x10, starting transfers between devices, inward(): came = lax.ppermute(total.astype(BF16), 'tensor', line_pairs(step))  50.3 us
    ppermute x27, starting transfers between devices, exchange(): return lax.ppermute(block, axis, [(i, i ^ apart) for i in range(count)])  38.5 us
    dot_general x65, matrix products, dot(): lax.dot_general(left, right, (((left_dim,), (right_dim,)), ((), ())), pre...  36.6 us
    ppermute x27, waiting for transfers between devices, exchange(): return lax.ppermute(block, axis, [(i, i ^ apart) for i in range(count)])  29.1 us
    ppermute x10, waiting for transfers between devices, inward(): came = lax.ppermute(total.astype(BF16), 'tensor', line_pairs(step))  19.3 us
    ppermute x6, starting transfers between devices, outward(): came = lax.ppermute(block, 'tensor', [(b, a) for a, b in line_pairs(step)])  7.96 us
    ppermute x10, starting transfers between devices, across(): return lax.ppermute(block, 'tensor', [(half - 1, half), (half, half - 1)])  7.04 us
  transfers between devices with their start and end apart: 53, of which 20 were waited for; matrix products, arithmetic and copies ran while one was open for 20% of the time, Pallas kernels for 0%

profile of v4, /device:TPU:0, one launch (start us, length us, event | category | flops | bytes accessed | tf_op | source)
XLA Modules:
  0.0 206.4 jit_solution(8438548105714531169)
XLA Ops:
  1.5 5.0 %collective-permute-start.2 = (bf16[2,16,512]{2,1,0:T(8,128)(2,1)S(1)}, bf16[2,16,512]{2,1,0:T(8,128)(2,1)S(1)}, u32[]{:S(2)}, u32[]{:S(2)}) collective-permute-start(bf16[2,16,512]{2,1,0:T(8,128)(2,1)S(1)} %pad_maximum_fusion.20), channel_id=1, source_target_pairs={{0,3},{1,2},{2,1},{3,0},{4,7},{5,6},{6,5},{7,4},{8,11},{9,10},{10,... | collective-permute-start | bytes 98312 | tf_op jit(solution)/shard_map/ppermute | solution.py:55
  8.5 1.8 convolution_multiply_fusion.11
  10.4 1.9 convolution_multiply_fusion.8
  14.0 2.7 %collective-permute-start.5 = (bf16[2,1,1,16,512]{4,3,0,2,1:T(8,128)(2,1)S(1)}, bf16[2,1,1,16,512]{4,3,0,2,1:T(8,128)(2,1)S(1)}, u32[]{:S(2)}, u32[]{:S(2)}) collective-permute-start(bf16[2,1,1,16,512]{4,3,0,2,1:T(8,128)(2,1)S(1)} %fusion.47), channel_id=1, source_target_pairs={{0,24},{4,28},{8,16},{12,20},{16,8},{20,12},{24,0},{28,4},{1,25},{... | collective-permute-start | bytes 98312 | tf_op jit(solution)/shard_map/ppermute | solution.py:55
  17.6 3.9 %collective-permute-start.14 = (bf16[2,64,512]{2,1,0:T(8,128)(2,1)S(1)}, bf16[2,64,512]{2,1,0:T(8,128)(2,1)S(1)}, u32[]{:S(2)}, u32[]{:S(2)}) collective-permute-start(bf16[2,64,512]{2,1,0:T(8,128)(2,1)S(1)} %fusion.74), channel_id=1, source_target_pairs={{0,3},{1,2},{2,1},{3,0},{4,7},{5,6},{6,5},{7,4},{8,11},{9,10},{10,... | collective-permute-start | bytes 393224 | tf_op jit(solution)/shard_map/ppermute | solution.py:55
  23.6 2.4 %collective-permute-done.14 = bf16[2,64,512]{2,1,0:T(8,128)(2,1)S(1)} collective-permute-done((bf16[2,64,512]{2,1,0:T(8,128)(2,1)S(1)}, bf16[2,64,512]{2,1,0:T(8,128)(2,1)S(1)}, u32[]{:S(2)}, u32[]{:S(2)}) %collective-permute-start.14) | collective-permute-done | bytes 131104 | tf_op jit(solution)/shard_map/ppermute | solution.py:55
  26.9 4.0 %collective-permute-done.13 = bf16[2,64,512]{2,1,0:T(8,128)(2,1)S(1)} collective-permute-done((bf16[2,64,512]{2,1,0:T(8,128)(2,1)S(1)}, bf16[2,64,512]{2,1,0:T(8,128)(2,1)S(1)}, u32[]{:S(2)}, u32[]{:S(2)}) %collective-permute-start.13) | collective-permute-done | bytes 131104 | tf_op jit(solution)/shard_map/ppermute | solution.py:55
  35.3 2.5 %collective-permute-start.17 = (bf16[2,4,1,16,512]{4,3,2,1,0:T(8,128)(2,1)S(1)}, bf16[2,4,1,16,512]{4,3,2,1,0:T(8,128)(2,1)S(1)}, u32[]{:S(2)}, u32[]{:S(2)}) collective-permute-start(bf16[2,4,1,16,512]{4,3,2,1,0:T(8,128)(2,1)S(1)} %bitcast.497), channel_id=1, source_target_pairs={{0,24},{4,28},{8,16},{12,20},{16,8},{20,12},{24,0},{28,4},{1,25},{... | collective-permute-start | bytes 393224 | tf_op jit(solution)/shard_map/ppermute | solution.py:55
  38.9 2.1 %collective-permute-start.7 = (bf16[3,64,1024]{2,1,0:T(8,128)(2,1)S(1)}, bf16[3,64,1024]{2,1,0:T(8,128)(2,1)S(1)}, u32[]{:S(2)}, u32[]{:S(2)}) collective-permute-start(bf16[3,64,1024]{2,1,0:T(8,128)(2,1)S(1)} %pad_maximum_fusion.2), channel_id=1, source_target_pairs={{0,1},{3,2},{4,5},{7,6},{8,9},{11,10},{12,13},{15,14},{16,17},{19,... | collective-permute-start | bytes 1179656 | tf_op jit(solution)/shard_map/ppermute | solution.py:128
  42.2 1.8 collective-permute-done.16
  44.2 3.5 %collective-permute-done.7 = bf16[3,64,1024]{2,1,0:T(8,128)(2,1)S(1)} collective-permute-done((bf16[3,64,1024]{2,1,0:T(8,128)(2,1)S(1)}, bf16[3,64,1024]{2,1,0:T(8,128)(2,1)S(1)}, u32[]{:S(2)}, u32[]{:S(2)}) %collective-permute-start.7) | collective-permute-done | bytes 393248 | tf_op jit(solution)/shard_map/ppermute | solution.py:128
  48.6 6.7 %collective-permute-start.8 = (bf16[3,64,1024]{2,1,0:T(8,128)(2,1)S(1)}, bf16[3,64,1024]{2,1,0:T(8,128)(2,1)S(1)}, u32[]{:S(2)}, u32[]{:S(2)}) collective-permute-start(bf16[3,64,1024]{2,1,0:T(8,128)(2,1)S(1)} %maximum_select_fusion.1), channel_id=1, source_target_pairs={{0,1},{3,2},{4,5},{7,6},{8,9},{11,10},{12,13},{15,14},{16,17},{19,... | collective-permute-start | bytes 1179656 | tf_op jit(solution)/shard_map/ppermute | solution.py:128
  58.0 6.2 %collective-permute-done.8 = bf16[3,64,1024]{2,1,0:T(8,128)(2,1)S(1)} collective-permute-done((bf16[3,64,1024]{2,1,0:T(8,128)(2,1)S(1)}, bf16[3,64,1024]{2,1,0:T(8,128)(2,1)S(1)}, u32[]{:S(2)}, u32[]{:S(2)}) %collective-permute-start.8) | collective-permute-done | bytes 393248 | tf_op jit(solution)/shard_map/ppermute | solution.py:128
  66.5 7.3 %collective-permute-start.19 = (bf16[3,64,1024]{2,1,0:T(8,128)(2,1)S(1)}, bf16[3,64,1024]{2,1,0:T(8,128)(2,1)S(1)}, u32[]{:S(2)}, u32[]{:S(2)}) collective-permute-start(bf16[3,64,1024]{2,1,0:T(8,128)(2,1)S(1)} %pad_maximum_fusion.4), channel_id=1, source_target_pairs={{0,1},{3,2},{4,5},{7,6},{8,9},{11,10},{12,13},{15,14},{16,17},{19,... | collective-permute-start | bytes 1179656 | tf_op jit(solution)/shard_map/ppermute | solution.py:128
  77.1 7.3 %collective-permute-start.25 = (bf16[3,64,1024]{2,1,0:T(8,128)(2,1)S(1)}, bf16[3,64,1024]{2,1,0:T(8,128)(2,1)S(1)}, u32[]{:S(2)}, u32[]{:S(2)}) collective-permute-start(bf16[3,64,1024]{2,1,0:T(8,128)(2,1)S(1)} %pad_maximum_fusion.8), channel_id=1, source_target_pairs={{0,1},{3,2},{4,5},{7,6},{8,9},{11,10},{12,13},{15,14},{16,17},{19,... | collective-permute-start | bytes 1179656 | tf_op jit(solution)/shard_map/ppermute | solution.py:128
  85.6 3.0 %collective-permute-start.24 = (bf16[3,64,1024]{2,1,0:T(8,128)(2,1)S(1)}, bf16[3,64,1024]{2,1,0:T(8,128)(2,1)S(1)}, u32[]{:S(2)}, u32[]{:S(2)}) collective-permute-start(bf16[3,64,1024]{2,1,0:T(8,128)(2,1)S(1)} %pad_maximum_fusion.7), channel_id=1, source_target_pairs={{0,1},{3,2},{4,5},{7,6},{8,9},{11,10},{12,13},{15,14},{16,17},{19,... | collective-permute-start | bytes 1179656 | tf_op jit(solution)/shard_map/ppermute | solution.py:128
  89.7 6.2 %collective-permute-done.24 = bf16[3,64,1024]{2,1,0:T(8,128)(2,1)S(1)} collective-permute-done((bf16[3,64,1024]{2,1,0:T(8,128)(2,1)S(1)}, bf16[3,64,1024]{2,1,0:T(8,128)(2,1)S(1)}, u32[]{:S(2)}, u32[]{:S(2)}) %collective-permute-start.24) | collective-permute-done | bytes 393248 | tf_op jit(solution)/shard_map/ppermute | solution.py:128
  97.8 6.0 %collective-permute-start.35 = (bf16[3,64,1024]{2,1,0:T(8,128)(2,1)S(1)}, bf16[3,64,1024]{2,1,0:T(8,128)(2,1)S(1)}, u32[]{:S(2)}, u32[]{:S(2)}) collective-permute-start(bf16[3,64,1024]{2,1,0:T(8,128)(2,1)S(1)} %pad_maximum_fusion.10), channel_id=1, source_target_pairs={{0,1},{3,2},{4,5},{7,6},{8,9},{11,10},{12,13},{15,14},{16,17},{19,... | collective-permute-start | bytes 1179656 | tf_op jit(solution)/shard_map/ppermute | solution.py:128
  106.4 4.6 %collective-permute-start.36 = (bf16[3,64,1024]{2,1,0:T(8,128)(2,1)S(1)}, bf16[3,64,1024]{2,1,0:T(8,128)(2,1)S(1)}, u32[]{:S(2)}, u32[]{:S(2)}) collective-permute-start(bf16[3,64,1024]{2,1,0:T(8,128)(2,1)S(1)} %pad_maximum_fusion.11), channel_id=1, source_target_pairs={{0,1},{3,2},{4,5},{7,6},{8,9},{11,10},{12,13},{15,14},{16,17},{19,... | collective-permute-start | bytes 1179656 | tf_op jit(solution)/shard_map/ppermute | solution.py:128
  114.5 4.4 %collective-permute-start.40 = (bf16[3,64,1024]{2,1,0:T(8,128)(2,1)S(1)}, bf16[3,64,1024]{2,1,0:T(8,128)(2,1)S(1)}, u32[]{:S(2)}, u32[]{:S(2)}) collective-permute-start(bf16[3,64,1024]{2,1,0:T(8,128)(2,1)S(1)} %pad_maximum_fusion.13), channel_id=1, source_target_pairs={{0,1},{3,2},{4,5},{7,6},{8,9},{11,10},{12,13},{15,14},{16,17},{19,... | collective-permute-start | bytes 1179656 | tf_op jit(solution)/shard_map/ppermute | solution.py:128
  124.0 7.6 %collective-permute-start.41 = (bf16[3,64,1024]{2,1,0:T(8,128)(2,1)S(1)}, bf16[3,64,1024]{2,1,0:T(8,128)(2,1)S(1)}, u32[]{:S(2)}, u32[]{:S(2)}) collective-permute-start(bf16[3,64,1024]{2,1,0:T(8,128)(2,1)S(1)} %pad_maximum_fusion.14), channel_id=1, source_target_pairs={{0,1},{3,2},{4,5},{7,6},{8,9},{11,10},{12,13},{15,14},{16,17},{19,... | collective-permute-start | bytes 1179656 | tf_op jit(solution)/shard_map/ppermute | solution.py:128
  134.4 2.4 %collective-permute-done.41 = bf16[3,64,1024]{2,1,0:T(8,128)(2,1)S(1)} collective-permute-done((bf16[3,64,1024]{2,1,0:T(8,128)(2,1)S(1)}, bf16[3,64,1024]{2,1,0:T(8,128)(2,1)S(1)}, u32[]{:S(2)}, u32[]{:S(2)}) %collective-permute-start.41) | collective-permute-done | bytes 393248 | tf_op jit(solution)/shard_map/ppermute | solution.py:128
  143.4 2.6 %collective-permute-start.32 = (bf16[2,3,16,512]{3,2,1,0:T(8,128)(2,1)S(1)}, bf16[2,3,16,512]{3,2,1,0:T(8,128)(2,1)S(1)}, u32[]{:S(2)}, u32[]{:S(2)}) collective-permute-start(bf16[2,3,16,512]{3,2,1,0:T(8,128)(2,1)S(1)} %get-tuple-element.35), channel_id=1, source_target_pairs={{0,24},{4,28},{8,16},{12,20},{16,8},{20,12},{24,0},{28,4},{1,25},{... | collective-permute-start | bytes 294920 | tf_op jit(solution)/shard_map/ppermute | solution.py:55
  147.7 1.6 collective-permute-done.32
  152.0 9.3 %collective-permute-start.33 = (bf16[2,48,512]{2,1,0:T(8,128)(2,1)S(1)}, bf16[2,48,512]{2,1,0:T(8,128)(2,1)S(1)}, u32[]{:S(2)}, u32[]{:S(2)}) collective-permute-start(bf16[2,48,512]{2,1,0:T(8,128)(2,1)S(1)} %get-tuple-element.60), channel_id=1, source_target_pairs={{0,1},{1,0},{2,3},{3,2},{4,5},{5,4},{6,7},{7,6},{8,9},{9,8},{10,11... | collective-permute-start | bytes 294920 | tf_op jit(solution)/shard_map/ppermute | solution.py:55
  162.9 9.8 %collective-permute-done.33 = bf16[2,48,512]{2,1,0:T(8,128)(2,1)S(1)} collective-permute-done((bf16[2,48,512]{2,1,0:T(8,128)(2,1)S(1)}, bf16[2,48,512]{2,1,0:T(8,128)(2,1)S(1)}, u32[]{:S(2)}, u32[]{:S(2)}) %collective-permute-start.33) | collective-permute-done | bytes 98336 | tf_op jit(solution)/shard_map/ppermute | solution.py:55
  175.2 3.9 %collective-permute-done.34 = bf16[2,48,512]{2,1,0:T(8,128)(2,1)S(1)} collective-permute-done((bf16[2,48,512]{2,1,0:T(8,128)(2,1)S(1)}, bf16[2,48,512]{2,1,0:T(8,128)(2,1)S(1)}, u32[]{:S(2)}, u32[]{:S(2)}) %collective-permute-start.34) | collective-permute-done | bytes 98336 | tf_op jit(solution)/shard_map/ppermute | solution.py:55
  184.8 2.0 multiply_convert_fusion
  186.8 2.0 multiply_convert_fusion.2
  188.9 2.5 %collective-permute-start.49 = (bf16[2,2,16,512]{3,2,1,0:T(8,128)(2,1)S(1)}, bf16[2,2,16,512]{3,2,1,0:T(8,128)(2,1)S(1)}, u32[]{:S(2)}, u32[]{:S(2)}) collective-permute-start(bf16[2,2,16,512]{3,2,1,0:T(8,128)(2,1)S(1)} %get-tuple-element.40), channel_id=1, source_target_pairs={{0,24},{4,28},{8,16},{12,20},{16,8},{20,12},{24,0},{28,4},{1,25},{... | collective-permute-start | bytes 196616 | tf_op jit(solution)/shard_map/ppermute | solution.py:55
  192.4 2.0 multiply_convert_fusion.1
  198.6 3.0 %collective-permute-start.51 = (bf16[2,32,512]{2,1,0:T(8,128)(2,1)S(1)}, bf16[2,32,512]{2,1,0:T(8,128)(2,1)S(1)}, u32[]{:S(2)}, u32[]{:S(2)}) collective-permute-start(bf16[2,32,512]{2,1,0:T(8,128)(2,1)S(1)} %bitcast.516), channel_id=1, source_target_pairs={{0,2},{1,3},{2,0},{3,1},{4,6},{5,7},{6,4},{7,5},{8,10},{9,11},{10,... | collective-permute-start | bytes 196616 | tf_op jit(solution)/shard_map/ppermute | solution.py:55
  (246 shorter events, 71.1 us)
Async XLA Ops:
  1.5 8.8 %collective-permute-start.2 = (bf16[2,16,512]{2,1,0:T(8,128)(2,1)S(1)}, bf16[2,16,512]{2,1,0:T(8,128)(2,1)S(1)}, u32[]{:S(2)}, u32[]{:S(2)}) collective-permute-start(bf16[2,16,512]{2,1,0:T(8,128)(2,1)S(1)} %pad_maximum_fusion.20), channel_id=1, source_target_pairs={{0,3},{1,2},{2,1},{3,0},{4,7},{5,6},{6,5},{7,4},{8,11},{9,10},{10,... | collective-permute-start | bytes 98312 | tf_op jit(solution)/shard_map/ppermute | solution.py:55
  14.0 8.9 %collective-permute-start.5 = (bf16[2,1,1,16,512]{4,3,0,2,1:T(8,128)(2,1)S(1)}, bf16[2,1,1,16,512]{4,3,0,2,1:T(8,128)(2,1)S(1)}, u32[]{:S(2)}, u32[]{:S(2)}) collective-permute-start(bf16[2,1,1,16,512]{4,3,0,2,1:T(8,128)(2,1)S(1)} %fusion.47), channel_id=1, source_target_pairs={{0,24},{4,28},{8,16},{12,20},{16,8},{20,12},{24,0},{28,4},{1,25},{... | collective-permute-start | bytes 98312 | tf_op jit(solution)/shard_map/ppermute | solution.py:55
  17.6 8.3 %collective-permute-start.14 = (bf16[2,64,512]{2,1,0:T(8,128)(2,1)S(1)}, bf16[2,64,512]{2,1,0:T(8,128)(2,1)S(1)}, u32[]{:S(2)}, u32[]{:S(2)}) collective-permute-start(bf16[2,64,512]{2,1,0:T(8,128)(2,1)S(1)} %fusion.74), channel_id=1, source_target_pairs={{0,3},{1,2},{2,1},{3,0},{4,7},{5,6},{6,5},{7,4},{8,11},{9,10},{10,... | collective-permute-start | bytes 393224 | tf_op jit(solution)/shard_map/ppermute | solution.py:55
  22.8 8.0 %collective-permute-start.13 = (bf16[2,64,512]{2,1,0:T(8,128)(2,1)S(1)}, bf16[2,64,512]{2,1,0:T(8,128)(2,1)S(1)}, u32[]{:S(2)}, u32[]{:S(2)}) collective-permute-start(bf16[2,64,512]{2,1,0:T(8,128)(2,1)S(1)} %fusion.74), channel_id=1, source_target_pairs={{0,2},{1,3},{2,0},{3,1},{4,6},{5,7},{6,4},{7,5},{8,10},{9,11},{10,... | collective-permute-start | bytes 393224 | tf_op jit(solution)/shard_map/ppermute | solution.py:55
  22.9 11.4 %collective-permute-start.12 = (bf16[2,64,512]{2,1,0:T(8,128)(2,1)S(1)}, bf16[2,64,512]{2,1,0:T(8,128)(2,1)S(1)}, u32[]{:S(2)}, u32[]{:S(2)}) collective-permute-start(bf16[2,64,512]{2,1,0:T(8,128)(2,1)S(1)} %fusion.74), channel_id=1, source_target_pairs={{0,1},{1,0},{2,3},{3,2},{4,5},{5,4},{6,7},{7,6},{8,9},{9,8},{10,11... | collective-permute-start | bytes 393224 | tf_op jit(solution)/shard_map/ppermute | solution.py:55
  23.5 8.2 %collective-permute-start.6 = (bf16[2,1,4,16,512]{4,3,0,2,1:T(8,128)(2,1)S(1)}, bf16[2,1,4,16,512]{4,3,0,2,1:T(8,128)(2,1)S(1)}, u32[]{:S(2)}, u32[]{:S(2)}) collective-permute-start(bf16[2,1,4,16,512]{4,3,0,2,1:T(8,128)(2,1)S(1)} %pad_maximum_fusion.19), channel_id=1, source_target_pairs={{0,4},{4,0},{8,12},{12,8},{16,20},{20,16},{24,28},{28,24},{1,5},{5... | collective-permute-start | bytes 393224 | tf_op jit(solution)/shard_map/ppermute | solution.py:55
  38.9 8.8 %collective-permute-start.7 = (bf16[3,64,1024]{2,1,0:T(8,128)(2,1)S(1)}, bf16[3,64,1024]{2,1,0:T(8,128)(2,1)S(1)}, u32[]{:S(2)}, u32[]{:S(2)}) collective-permute-start(bf16[3,64,1024]{2,1,0:T(8,128)(2,1)S(1)} %pad_maximum_fusion.2), channel_id=1, source_target_pairs={{0,1},{3,2},{4,5},{7,6},{8,9},{11,10},{12,13},{15,14},{16,17},{19,... | collective-permute-start | bytes 1179656 | tf_op jit(solution)/shard_map/ppermute | solution.py:128
  44.1 11.2 %collective-permute-start.18 = (bf16[2,4,4,16,512]{4,3,2,1,0:T(8,128)(2,1)S(1)}, bf16[2,4,4,16,512]{4,3,2,1,0:T(8,128)(2,1)S(1)}, u32[]{:S(2)}, u32[]{:S(2)}) collective-permute-start(bf16[2,4,4,16,512]{4,3,2,1,0:T(8,128)(2,1)S(1)} %pad_maximum_fusion.1), channel_id=1, source_target_pairs={{0,4},{4,0},{8,12},{12,8},{16,20},{20,16},{24,28},{28,24},{1,5},{5... | collective-permute-start | bytes 1572872 | tf_op jit(solution)/shard_map/ppermute | solution.py:55
  47.8 10.2 %collective-permute-start.9 = (bf16[3,64,1024]{2,1,0:T(8,128)(2,1)S(1)}, bf16[3,64,1024]{2,1,0:T(8,128)(2,1)S(1)}, u32[]{:S(2)}, u32[]{:S(2)}) collective-permute-start(bf16[3,64,1024]{2,1,0:T(8,128)(2,1)S(1)} %add_convert_fusion.4), channel_id=1, source_target_pairs={{1,2},{2,1},{5,6},{6,5},{9,10},{10,9},{13,14},{14,13},{17,18},{18,... | collective-permute-start | bytes 1179656 | tf_op jit(solution)/shard_map/ppermute | solution.py:142
  48.6 15.6 %collective-permute-start.8 = (bf16[3,64,1024]{2,1,0:T(8,128)(2,1)S(1)}, bf16[3,64,1024]{2,1,0:T(8,128)(2,1)S(1)}, u32[]{:S(2)}, u32[]{:S(2)}) collective-permute-start(bf16[3,64,1024]{2,1,0:T(8,128)(2,1)S(1)} %maximum_select_fusion.1), channel_id=1, source_target_pairs={{0,1},{3,2},{4,5},{7,6},{8,9},{11,10},{12,13},{15,14},{16,17},{19,... | collective-permute-start | bytes 1179656 | tf_op jit(solution)/shard_map/ppermute | solution.py:128
  56.6 17.2 %collective-permute-start.20 = (bf16[3,64,1024]{2,1,0:T(8,128)(2,1)S(1)}, bf16[3,64,1024]{2,1,0:T(8,128)(2,1)S(1)}, u32[]{:S(2)}, u32[]{:S(2)}) collective-permute-start(bf16[3,64,1024]{2,1,0:T(8,128)(2,1)S(1)} %pad_maximum_fusion.5), channel_id=1, source_target_pairs={{0,1},{3,2},{4,5},{7,6},{8,9},{11,10},{12,13},{15,14},{16,17},{19,... | collective-permute-start | bytes 1179656 | tf_op jit(solution)/shard_map/ppermute | solution.py:128
  64.6 10.0 %collective-permute-start.10 = (bf16[3,64,1024]{2,1,0:T(8,128)(2,1)S(1)}, bf16[3,64,1024]{2,1,0:T(8,128)(2,1)S(1)}, u32[]{:S(2)}, u32[]{:S(2)}) collective-permute-start(bf16[3,64,1024]{2,1,0:T(8,128)(2,1)S(1)} %pad_maximum_fusion.3), channel_id=1, source_target_pairs={{1,2},{2,1},{5,6},{6,5},{9,10},{10,9},{13,14},{14,13},{17,18},{18,... | collective-permute-start | bytes 1179656 | tf_op jit(solution)/shard_map/ppermute | solution.py:142
  66.5 17.9 %collective-permute-start.19 = (bf16[3,64,1024]{2,1,0:T(8,128)(2,1)S(1)}, bf16[3,64,1024]{2,1,0:T(8,128)(2,1)S(1)}, u32[]{:S(2)}, u32[]{:S(2)}) collective-permute-start(bf16[3,64,1024]{2,1,0:T(8,128)(2,1)S(1)} %pad_maximum_fusion.4), channel_id=1, source_target_pairs={{0,1},{3,2},{4,5},{7,6},{8,9},{11,10},{12,13},{15,14},{16,17},{19,... | collective-permute-start | bytes 1179656 | tf_op jit(solution)/shard_map/ppermute | solution.py:128
  73.9 14.7 %collective-permute-start.21 = (bf16[3,64,1024]{2,1,0:T(8,128)(2,1)S(1)}, bf16[3,64,1024]{2,1,0:T(8,128)(2,1)S(1)}, u32[]{:S(2)}, u32[]{:S(2)}) collective-permute-start(bf16[3,64,1024]{2,1,0:T(8,128)(2,1)S(1)} %add_convert_fusion.3), channel_id=1, source_target_pairs={{1,2},{2,1},{5,6},{6,5},{9,10},{10,9},{13,14},{14,13},{17,18},{18,... | collective-permute-start | bytes 1179656 | tf_op jit(solution)/shard_map/ppermute | solution.py:142
  74.7 44.2 %collective-permute-start.11 = (bf16[3,128,1024]{2,1,0:T(8,128)(2,1)S(1)}, bf16[3,128,1024]{2,1,0:T(8,128)(2,1)S(1)}, u32[]{:S(2)}, u32[]{:S(2)}) collective-permute-start(bf16[3,128,1024]{2,1,0:T(8,128)(2,1)S(1)} %maximum_maximum_fusion.2), channel_id=1, source_target_pairs={{1,0},{2,3},{5,4},{6,7},{9,8},{10,11},{13,12},{14,15},{17,16},{18,... | collective-permute-start | bytes 2359304 | tf_op jit(solution)/shard_map/ppermute | solution.py:135
  77.1 19.5 %collective-permute-start.25 = (bf16[3,64,1024]{2,1,0:T(8,128)(2,1)S(1)}, bf16[3,64,1024]{2,1,0:T(8,128)(2,1)S(1)}, u32[]{:S(2)}, u32[]{:S(2)}) collective-permute-start(bf16[3,64,1024]{2,1,0:T(8,128)(2,1)S(1)} %pad_maximum_fusion.8), channel_id=1, source_target_pairs={{0,1},{3,2},{4,5},{7,6},{8,9},{11,10},{12,13},{15,14},{16,17},{19,... | collective-permute-start | bytes 1179656 | tf_op jit(solution)/shard_map/ppermute | solution.py:128
  85.6 10.3 %collective-permute-start.24 = (bf16[3,64,1024]{2,1,0:T(8,128)(2,1)S(1)}, bf16[3,64,1024]{2,1,0:T(8,128)(2,1)S(1)}, u32[]{:S(2)}, u32[]{:S(2)}) collective-permute-start(bf16[3,64,1024]{2,1,0:T(8,128)(2,1)S(1)} %pad_maximum_fusion.7), channel_id=1, source_target_pairs={{0,1},{3,2},{4,5},{7,6},{8,9},{11,10},{12,13},{15,14},{16,17},{19,... | collective-permute-start | bytes 1179656 | tf_op jit(solution)/shard_map/ppermute | solution.py:128
  89.0 14.9 %collective-permute-start.22 = (bf16[3,64,1024]{2,1,0:T(8,128)(2,1)S(1)}, bf16[3,64,1024]{2,1,0:T(8,128)(2,1)S(1)}, u32[]{:S(2)}, u32[]{:S(2)}) collective-permute-start(bf16[3,64,1024]{2,1,0:T(8,128)(2,1)S(1)} %pad_maximum_fusion.6), channel_id=1, source_target_pairs={{1,2},{2,1},{5,6},{6,5},{9,10},{10,9},{13,14},{14,13},{17,18},{18,... | collective-permute-start | bytes 1179656 | tf_op jit(solution)/shard_map/ppermute | solution.py:142
  97.1 13.9 %collective-permute-start.26 = (bf16[3,64,1024]{2,1,0:T(8,128)(2,1)S(1)}, bf16[3,64,1024]{2,1,0:T(8,128)(2,1)S(1)}, u32[]{:S(2)}, u32[]{:S(2)}) collective-permute-start(bf16[3,64,1024]{2,1,0:T(8,128)(2,1)S(1)} %add_convert_fusion.2), channel_id=1, source_target_pairs={{1,2},{2,1},{5,6},{6,5},{9,10},{10,9},{13,14},{14,13},{17,18},{18,... | collective-permute-start | bytes 1179656 | tf_op jit(solution)/shard_map/ppermute | solution.py:142
  97.8 15.5 %collective-permute-start.35 = (bf16[3,64,1024]{2,1,0:T(8,128)(2,1)S(1)}, bf16[3,64,1024]{2,1,0:T(8,128)(2,1)S(1)}, u32[]{:S(2)}, u32[]{:S(2)}) collective-permute-start(bf16[3,64,1024]{2,1,0:T(8,128)(2,1)S(1)} %pad_maximum_fusion.10), channel_id=1, source_target_pairs={{0,1},{3,2},{4,5},{7,6},{8,9},{11,10},{12,13},{15,14},{16,17},{19,... | collective-permute-start | bytes 1179656 | tf_op jit(solution)/shard_map/ppermute | solution.py:128
  103.9 28.7 %collective-permute-start.23 = (bf16[3,128,1024]{2,1,0:T(8,128)(2,1)S(1)}, bf16[3,128,1024]{2,1,0:T(8,128)(2,1)S(1)}, u32[]{:S(2)}, u32[]{:S(2)}) collective-permute-start(bf16[3,128,1024]{2,1,0:T(8,128)(2,1)S(1)} %maximum_maximum_fusion.3), channel_id=1, source_target_pairs={{1,0},{2,3},{5,4},{6,7},{9,8},{10,11},{13,12},{14,15},{17,16},{18,... | collective-permute-start | bytes 2359304 | tf_op jit(solution)/shard_map/ppermute | solution.py:135
  106.4 14.2 %collective-permute-start.36 = (bf16[3,64,1024]{2,1,0:T(8,128)(2,1)S(1)}, bf16[3,64,1024]{2,1,0:T(8,128)(2,1)S(1)}, u32[]{:S(2)}, u32[]{:S(2)}) collective-permute-start(bf16[3,64,1024]{2,1,0:T(8,128)(2,1)S(1)} %pad_maximum_fusion.11), channel_id=1, source_target_pairs={{0,1},{3,2},{4,5},{7,6},{8,9},{11,10},{12,13},{15,14},{16,17},{19,... | collective-permute-start | bytes 1179656 | tf_op jit(solution)/shard_map/ppermute | solution.py:128
  111.4 10.0 %collective-permute-start.27 = (bf16[3,64,1024]{2,1,0:T(8,128)(2,1)S(1)}, bf16[3,64,1024]{2,1,0:T(8,128)(2,1)S(1)}, u32[]{:S(2)}, u32[]{:S(2)}) collective-permute-start(bf16[3,64,1024]{2,1,0:T(8,128)(2,1)S(1)} %pad_maximum_fusion.9), channel_id=1, source_target_pairs={{1,2},{2,1},{5,6},{6,5},{9,10},{10,9},{13,14},{14,13},{17,18},{18,... | collective-permute-start | bytes 1179656 | tf_op jit(solution)/shard_map/ppermute | solution.py:142
  114.5 27.0 %collective-permute-start.40 = (bf16[3,64,1024]{2,1,0:T(8,128)(2,1)S(1)}, bf16[3,64,1024]{2,1,0:T(8,128)(2,1)S(1)}, u32[]{:S(2)}, u32[]{:S(2)}) collective-permute-start(bf16[3,64,1024]{2,1,0:T(8,128)(2,1)S(1)} %pad_maximum_fusion.13), channel_id=1, source_target_pairs={{0,1},{3,2},{4,5},{7,6},{8,9},{11,10},{12,13},{15,14},{16,17},{19,... | collective-permute-start | bytes 1179656 | tf_op jit(solution)/shard_map/ppermute | solution.py:128
  120.7 10.8 %collective-permute-start.37 = (bf16[3,64,1024]{2,1,0:T(8,128)(2,1)S(1)}, bf16[3,64,1024]{2,1,0:T(8,128)(2,1)S(1)}, u32[]{:S(2)}, u32[]{:S(2)}) collective-permute-start(bf16[3,64,1024]{2,1,0:T(8,128)(2,1)S(1)} %add_convert_fusion.1), channel_id=1, source_target_pairs={{1,2},{2,1},{5,6},{6,5},{9,10},{10,9},{13,14},{14,13},{17,18},{18,... | collective-permute-start | bytes 1179656 | tf_op jit(solution)/shard_map/ppermute | solution.py:142
  122.6 16.9 %collective-permute-start.28 = (bf16[3,128,1024]{2,1,0:T(8,128)(2,1)S(1)}, bf16[3,128,1024]{2,1,0:T(8,128)(2,1)S(1)}, u32[]{:S(2)}, u32[]{:S(2)}) collective-permute-start(bf16[3,128,1024]{2,1,0:T(8,128)(2,1)S(1)} %maximum_maximum_fusion.4), channel_id=1, source_target_pairs={{1,0},{2,3},{5,4},{6,7},{9,8},{10,11},{13,12},{14,15},{17,16},{18,... | collective-permute-start | bytes 2359304 | tf_op jit(solution)/shard_map/ppermute | solution.py:135
  124.0 12.8 %collective-permute-start.41 = (bf16[3,64,1024]{2,1,0:T(8,128)(2,1)S(1)}, bf16[3,64,1024]{2,1,0:T(8,128)(2,1)S(1)}, u32[]{:S(2)}, u32[]{:S(2)}) collective-permute-start(bf16[3,64,1024]{2,1,0:T(8,128)(2,1)S(1)} %pad_maximum_fusion.14), channel_id=1, source_target_pairs={{0,1},{3,2},{4,5},{7,6},{8,9},{11,10},{12,13},{15,14},{16,17},{19,... | collective-permute-start | bytes 1179656 | tf_op jit(solution)/shard_map/ppermute | solution.py:128
  137.7 35.7 %collective-permute-start.39 = (bf16[3,128,1024]{2,1,0:T(8,128)(2,1)S(1)}, bf16[3,128,1024]{2,1,0:T(8,128)(2,1)S(1)}, u32[]{:S(2)}, u32[]{:S(2)}) collective-permute-start(bf16[3,128,1024]{2,1,0:T(8,128)(2,1)S(1)} %maximum_maximum_fusion.5), channel_id=1, source_target_pairs={{1,0},{2,3},{5,4},{6,7},{9,8},{10,11},{13,12},{14,15},{17,16},{18,... | collective-permute-start | bytes 2359304 | tf_op jit(solution)/shard_map/ppermute | solution.py:135
  147.0 14.3 %collective-permute-start.43 = (bf16[3,64,1024]{2,1,0:T(8,128)(2,1)S(1)}, bf16[3,64,1024]{2,1,0:T(8,128)(2,1)S(1)}, u32[]{:S(2)}, u32[]{:S(2)}) collective-permute-start(bf16[3,64,1024]{2,1,0:T(8,128)(2,1)S(1)} %pad_maximum_fusion.15), channel_id=1, source_target_pairs={{1,2},{2,1},{5,6},{6,5},{9,10},{10,9},{13,14},{14,13},{17,18},{18,... | collective-permute-start | bytes 1179656 | tf_op jit(solution)/shard_map/ppermute | solution.py:142
  149.3 32.4 %collective-permute-start.45 = (bf16[3,64,1024]{2,1,0:T(8,128)(2,1)S(1)}, bf16[3,64,1024]{2,1,0:T(8,128)(2,1)S(1)}, u32[]{:S(2)}, u32[]{:S(2)}) collective-permute-start(bf16[3,64,1024]{2,1,0:T(8,128)(2,1)S(1)} %pad_maximum_fusion.15), channel_id=1, source_target_pairs={{1,0},{2,3},{5,4},{6,7},{9,8},{10,11},{13,12},{14,15},{17,16},{18,... | collective-permute-start | bytes 1179656 | tf_op jit(solution)/shard_map/ppermute | solution.py:135
  152.0 20.7 %collective-permute-start.33 = (bf16[2,48,512]{2,1,0:T(8,128)(2,1)S(1)}, bf16[2,48,512]{2,1,0:T(8,128)(2,1)S(1)}, u32[]{:S(2)}, u32[]{:S(2)}) collective-permute-start(bf16[2,48,512]{2,1,0:T(8,128)(2,1)S(1)} %get-tuple-element.60), channel_id=1, source_target_pairs={{0,1},{1,0},{2,3},{3,2},{4,5},{5,4},{6,7},{7,6},{8,9},{9,8},{10,11... | collective-permute-start | bytes 294920 | tf_op jit(solution)/shard_map/ppermute | solution.py:55
  161.3 20.1 %collective-permute-start.44 = (bf16[3,64,1024]{2,1,0:T(8,128)(2,1)S(1)}, bf16[3,64,1024]{2,1,0:T(8,128)(2,1)S(1)}, u32[]{:S(2)}, u32[]{:S(2)}) collective-permute-start(bf16[3,64,1024]{2,1,0:T(8,128)(2,1)S(1)} %broadcast_select_fusion.8), channel_id=1, source_target_pairs={{1,0},{2,3},{5,4},{6,7},{9,8},{10,11},{13,12},{14,15},{17,16},{18,... | collective-permute-start | bytes 1179656 | tf_op jit(solution)/shard_map/ppermute | solution.py:135
  (27 other events, 202.9 us)

commit v5 on v4

--- a/solution.py
+++ b/solution.py
@@ -59,26 +59,26 @@
     return [block] + [exchange(block, "tensor", k) for k in range(1, lax.axis_size("tensor"))]
 
 
+def turn(block):
+    width = block.shape[-1]
+    square = jnp.asarray(sylvester(width), BF16)
+    rows = block.reshape(-1, width) * (1.0 / math.sqrt(D))
+    high = lax.reduce_precision(rows, 8, 7)
+    low = (rows - high).astype(BF16)
+    return (dot(high.astype(BF16), square, 1, 0) + dot(low, square, 1, 0)).reshape(block.shape)
+
+
 def rotate(pieces, signs):
     width = pieces[0].shape[-1]
-    square = jnp.asarray(sylvester(width), BF16)
-    total = 0.0
-    for piece, sign in zip(pieces, signs):
-        total = total + dot(piece, square, piece.ndim - 1, 0) * sign[:, :width]
-    return total * (1.0 / math.sqrt(D))
+    return turn(sum(piece.astype(F32) * sign[:, :width] for piece, sign in zip(pieces, signs)))
 
 
 def rotate_by_halves(block, bits):
-    width = block.shape[-1]
-    square = jnp.asarray(sylvester(width), BF16)
-    high = lax.reduce_precision(block, 8, 7)
-    low = (block - high).astype(BF16)
-    last = block.ndim - 1
-    block = dot(high.astype(BF16), square, last, 0) + dot(low, square, last, 0)
+    block = turn(block)
     for level, bit in enumerate(bits):
         came = exchange(block.astype(BF16), "tensor", 1 << level)
-        block = block * bit[:, :width] + came.astype(F32)
-    return block * (1.0 / math.sqrt(D))
+        block = block * bit[:, : block.shape[-1]] + came.astype(F32)
+    return block
 
 
 def dp_stages():
@@ -102,7 +102,8 @@
 
 def scatter_dp(low, high):
     stages = dp_stages()
-    low = low + exchange(high.astype(BF16), "dp", stages[-1][1]).astype(F32)
+    first = exchange(high, "dp", stages[-1][1])
+    low, came = low + first.astype(F32), first
     for stage in reversed(stages[:-1]):
         low = low.reshape(low.shape[:2] + (len(stage), -1) + low.shape[-1:])
         total = low[:, :, 0]
@@ -110,7 +111,7 @@
             came = exchange(low[:, :, place].astype(BF16), "dp", apart)
             total = total + came.astype(F32)
         low = total
-    return low, came
+    return low, first, came
 
 
 def line_pairs(step):
@@ -170,64 +171,64 @@
         other, own = jnp.where(far, low, high), jnp.where(far, high, low)
         return [part.reshape(2, -1, half, width) for part in (other, own)]
 
-    pieces = spread(both[:, :step])
-    late_pieces = spread(after(both[:, step:], pieces[1])) if chunks > 1 else None
-    groups = [arrive(rotate(pieces, signs).astype(BF16))]
+    first = min(2, chunks)
+    early = spread(both[:, : first * step])
+    late = spread(after(both[:, first * step :], early[1])) if chunks > first else None
+    groups = [arrive(rotate(early, signs).astype(BF16))]
 
     done, arrived, crossed = [], [], []
     for i in range(chunks):
-        group, place = (groups[0], 0) if i == 0 else (groups[1], i - 1)
+        group, place = (groups[0], i) if i < first else (groups[1], i - first)
         sums = []
         for which, (x, g) in enumerate([(part[0, place], part[1, place]) for part in group]):
-            if i > 0:
-                x, g = after(x, arrived[-2]), after(g, arrived[-2])
-            if i > 1 and which == 0:
-                x, g = after(x, crossed[i - 2]), after(g, crossed[i - 2])
+            ahead = arrived[max(2 * i - 4 + which, 0)] if i > 0 else message if arrived else None
+            if ahead is not None:
+                x, g = after(x, ahead), after(g, ahead)
             parts = [dot(x, gate_weight, 1, 0), dot(x, up_weight, 1, 0), dot(g, down_weight, 1, 1)]
-            message = jnp.stack(parts).astype(BF16)
-            if i == 0 and which == 1:
-                message = after(message, arrived[0])
-            if len(groups) == 1 and chunks > 1:
-                piece = late_pieces[0]
-                for part in message:
-                    piece = after(piece, part)
-                groups.append(arrive(rotate([piece] + late_pieces[1:], signs).astype(BF16)))
-            total, came = inward(message)
+            block = jnp.stack(parts).astype(BF16)
+            block = after(block, arrived[max(len(arrived) - 2, 0)]) if arrived else block
+            message = message if arrived else block[2:]
+            total, came = inward(block)
             arrived.append(came)
             sums.append(total)
+            if len(groups) == 1 and chunks > first:
+                late[0] = after(late[0], came)
+                groups.append(arrive(rotate(late, signs).astype(BF16)))
         other, own = sums
         sums = own + across(other.astype(BF16)).astype(F32)
         own = activations(sums[0], sums[1], sums[2])
         crossed.append(across(own))
         if i < chunks - 1:
-            done.append(outward(jnp.concatenate([crossed[i], own], axis=1), depth))
+            done.append([outward(crossed[i], depth), outward(own, depth)])
 
     def leave(blocks):
-        count = sum(acts.shape[1] for acts in blocks) // (2 * half)
-        sums = []
-        for acts in blocks:
-            mixed = dot(acts[0], down_weight, 1, 0)
-            grads = dot(acts[1], gate_weight, 1, 1) + dot(acts[2], up_weight, 1, 1)
-            sums.append(jnp.stack([mixed, grads]))
-        sums = jnp.concatenate(sums, axis=1).reshape(2, count, 2, half, width)
-        low = jnp.where(far, sums[:, :, 0], sums[:, :, 1])
-        high = jnp.where(far, sums[:, :, 1], sums[:, :, 0]).astype(BF16)
-        sums, came = scatter_dp(low, high)
-        return sums.reshape(2, count * step, width), high, came
+        lows, highs = [], []
+        for halves in blocks:
+            sums = []
+            for acts in halves:
+                mixed = dot(acts[0], down_weight, 1, 0)
+                grads = dot(acts[1], gate_weight, 1, 1) + dot(acts[2], up_weight, 1, 1)
+                sums.append(jnp.stack([mixed, grads]))
+            lows.append(jnp.where(far, sums[0], sums[1]))
+            highs.append(jnp.where(far, sums[1], sums[0]).astype(BF16))
+        return jnp.stack(lows, axis=1), jnp.stack(highs, axis=1)
 
     split, ends = max(chunks - 2, 0), []
     if split > 0:
-        sums, _, came = leave(done[:split])
-        ends.append(rotate_by_halves(sums, bits))
+        sums, came, last = scatter_dp(*leave(done[:split]))
+        ends.append(rotate_by_halves(sums.reshape(2, -1, width), bits))
         crossed[-1] = after(crossed[-1], came)
-    done += [outward(crossed[-1], depth), outward(own, depth)]
-    sums, message, _ = leave(done[split:])
-    ends.append(rotate(spread(sums.astype(BF16)), signs))
+    done.append([outward(crossed[-1], depth), outward(own, depth)])
+    low, high = leave(done[split:])
+    if split > 0:
+        high = after(high, last)
+    sums, _, _ = scatter_dp(low, high)
+    ends.append(rotate(spread(sums.reshape(2, -1, width).astype(BF16)), signs))
     ends = jnp.concatenate(ends, axis=1)
 
-    acts = jnp.concatenate(done, axis=1)
+    acts = jnp.concatenate([half for halves in done for half in halves], axis=1)
     rows = [jnp.stack(group, axis=2).reshape(2, -1, width) for group in groups]
-    rows = after(jnp.concatenate(rows, axis=1), message[0, 0, :1])
+    rows = after(jnp.concatenate(rows, axis=1), high[0, 0, :1])
     factor = 1.0 / math.sqrt(rows.shape[1])
     return (
         ends[0],

time: 207 us -> 229 us (1.11)
  waiting for transfers between devices: 49.9 us -> 79.9 us
  starting transfers between devices: 104 us -> 91.4 us
  other arithmetic: 10.5 us -> 18.6 us
  matrix products: 36.6 us -> 32.6 us
    ppermute x6 -> x10, waiting for transfers between devices: 1.5 us -> 42.8 us  [outward(): came = lax.ppermute(block, 'tensor', [(b, a) for a, b in line_pairs(step)])]
    ppermute x10, starting transfers between devices: 50.3 us -> 40.2 us  [inward(): came = lax.ppermute(total.astype(BF16), 'tensor', line_pairs(step))]
    ppermute x27, starting transfers between devices: 38.5 us -> 31.2 us  [exchange(): return lax.ppermute(block, axis, [(i, i ^ apart) for i in range(count)])]
    mul x1 -> x4, other arithmetic: 1.34 us -> 8.59 us  [turn(): rows = block.reshape(-1, width) * (1.0 / math.sqrt(D))]
    ppermute x10, waiting for transfers between devices: 19.3 us -> 12.8 us  [inward(): came = lax.ppermute(total.astype(BF16), 'tensor', line_pairs(step))]
    ppermute x6 -> x10, starting transfers between devices: 7.96 us -> 13.1 us  [outward(): came = lax.ppermute(block, 'tensor', [(b, a) for a, b in line_pairs(step)])]
    ppermute x27, waiting for transfers between devices: 29.1 us -> 24.3 us  [exchange(): return lax.ppermute(block, axis, [(i, i ^ apart) for i in range(count)])]
    dot_general x65 -> x71, matrix products: 36.6 us -> 32.6 us  [dot(): lax.dot_general(left, right, (((left_dim,), (right_dim,)), ((), ())), pre...]
  transfers between devices with their start and end apart: 53 -> 57, of which waited for: 20 -> 19; matrix products, arithmetic and copies ran while one was open for 20% -> 16% of each run, Pallas kernels for 0% -> 0%
where the time goes in v5:
time: 229 us; the launch traced here: 228 us
  starting transfers between devices  91.4 us (40%)
  waiting for transfers between devices  79.9 us (35%)
  matrix products  32.6 us (14%)
  other arithmetic  18.6 us (8%)
  between operations  3.55 us (2%)
    ppermute x10, waiting for transfers between devices, outward(): came = lax.ppermute(block, 'tensor', [(b, a) for a, b in line_pairs(step)])  42.8 us
    ppermute x10, starting transfers between devices, inward(): came = lax.ppermute(total.astype(BF16), 'tensor', line_pairs(step))  40.2 us
    dot_general x71, matrix products, dot(): lax.dot_general(left, right, (((left_dim,), (right_dim,)), ((), ())), pre...  32.6 us
    ppermute x27, starting transfers between devices, exchange(): return lax.ppermute(block, axis, [(i, i ^ apart) for i in range(count)])  31.2 us
    ppermute x27, waiting for transfers between devices, exchange(): return lax.ppermute(block, axis, [(i, i ^ apart) for i in range(count)])  24.3 us
    ppermute x10, starting transfers between devices, outward(): came = lax.ppermute(block, 'tensor', [(b, a) for a, b in line_pairs(step)])  13.1 us
    ppermute x10, waiting for transfers between devices, inward(): came = lax.ppermute(total.astype(BF16), 'tensor', line_pairs(step))  12.8 us
    mul x4, other arithmetic, turn(): rows = block.reshape(-1, width) * (1.0 / math.sqrt(D))  8.59 us
  transfers between devices with their start and end apart: 57, of which 19 were waited for; matrix products, arithmetic and copies ran while one was open for 16% of the time, Pallas kernels for 0%

profile of v5, /device:TPU:0, one launch (start us, length us, event | category | flops | bytes accessed | tf_op | source)
XLA Modules:
  0.0 227.7 jit_solution(11350436826715182670)
XLA Ops:
  1.6 3.0 %collective-permute-start = (bf16[2,32,512]{2,1,0:T(8,128)(2,1)S(1)}, bf16[2,32,512]{2,1,0:T(8,128)(2,1)S(1)}, u32[]{:S(2)}, u32[]{:S(2)}) collective-permute-start(bf16[2,32,512]{2,1,0:T(8,128)(2,1)S(1)} %pad_maximum_fusion.24), channel_id=1, source_target_pairs={{0,1},{1,0},{2,3},{3,2},{4,5},{5,4},{6,7},{7,6},{8,9},{9,8},{10,11... | collective-permute-start | bytes 196616 | tf_op jit(solution)/shard_map/ppermute | solution.py:55
  4.6 2.6 %collective-permute-start.1 = (bf16[2,32,512]{2,1,0:T(8,128)(2,1)S(1)}, bf16[2,32,512]{2,1,0:T(8,128)(2,1)S(1)}, u32[]{:S(2)}, u32[]{:S(2)}) collective-permute-start(bf16[2,32,512]{2,1,0:T(8,128)(2,1)S(1)} %pad_maximum_fusion.24), channel_id=1, source_target_pairs={{0,2},{1,3},{2,0},{3,1},{4,6},{5,7},{6,4},{7,5},{8,10},{9,11},{10,... | collective-permute-start | bytes 196616 | tf_op jit(solution)/shard_map/ppermute | solution.py:55
  8.6 3.3 %collective-permute-done.1 = bf16[2,32,512]{2,1,0:T(8,128)(2,1)S(1)} collective-permute-done((bf16[2,32,512]{2,1,0:T(8,128)(2,1)S(1)}, bf16[2,32,512]{2,1,0:T(8,128)(2,1)S(1)}, u32[]{:S(2)}, u32[]{:S(2)}) %collective-permute-start.1) | collective-permute-done | bytes 65568 | tf_op jit(solution)/shard_map/ppermute | solution.py:55
  13.3 3.3 %add_multiply_fusion.2 = f32[2,32,512]{2,1,0:T(8,128)S(1)} fusion(bf16[2,32,512]{2,1,0:T(8,128)(2,1)S(1)} %collective-permute-done.2, bf16[2,32,512]{2,1,0:T(8,128)(2,1)S(1)} %collective-permute-done.1, bf16[2,32,512]{2,1,0:T(8,128)(2,1)S(1)} %collective-permute-done, f32[]{:T(128)} %bitcast.7, f32[]{:T(128)} %bitcast.6, f32[]{:T(128)} %bitcast.5, ...), kind=kLoop, calls=%fused_computation.297 | loop fusion | flops 491520 | bytes 491536 | tf_op jit(solution)/shard_map/mul | solution.py:65
  25.1 2.3 %collective-permute-done.5 = bf16[2,2,1,16,512]{4,3,2,1,0:T(8,128)(2,1)S(1)} collective-permute-done((bf16[2,2,1,16,512]{4,3,2,1,0:T(8,128)(2,1)S(1)}, bf16[2,2,1,16,512]{4,3,2,1,0:T(8,128)(2,1)S(1)}, u32[]{:S(2)}, u32[]{:S(2)}) %collective-permute-start.5) | collective-permute-done | bytes 65568 | tf_op jit(solution)/shard_map/ppermute | solution.py:55
  28.5 2.3 %collective-permute-start.20 = (bf16[2,48,512]{2,1,0:T(8,128)(2,1)S(1)}, bf16[2,48,512]{2,1,0:T(8,128)(2,1)S(1)}, u32[]{:S(2)}, u32[]{:S(2)}) collective-permute-start(bf16[2,48,512]{2,1,0:T(8,128)(2,1)S(1)} %fusion.77), channel_id=1, source_target_pairs={{0,2},{1,3},{2,0},{3,1},{4,6},{5,7},{6,4},{7,5},{8,10},{9,11},{10,... | collective-permute-start | bytes 294920 | tf_op jit(solution)/shard_map/ppermute | solution.py:55
  30.8 2.0 collective-permute-start.21
  36.6 7.6 %collective-permute-done.7 = bf16[3,64,1024]{2,1,0:T(8,128)(2,1)S(1)} collective-permute-done((bf16[3,64,1024]{2,1,0:T(8,128)(2,1)S(1)}, bf16[3,64,1024]{2,1,0:T(8,128)(2,1)S(1)}, u32[]{:S(2)}, u32[]{:S(2)}) %collective-permute-start.7) | collective-permute-done | bytes 393248 | tf_op jit(solution)/shard_map/ppermute | solution.py:129
  45.6 2.6 %add_multiply_fusion = f32[2,48,512]{2,1,0:T(8,128)S(1)} fusion(bf16[2,48,512]{2,1,0:T(8,128)(2,1)S(1)} %collective-permute-done.21, bf16[2,48,512]{2,1,0:T(8,128)(2,1)S(1)} %collective-permute-done.20, bf16[2,48,512]{2,1,0:T(8,128)(2,1)S(1)} %collective-permute-done.19, f32[]{:T(128)} %bitcast.7, f32[]{:T(128)} %bitcast.6, f32[]{:T(128)} %bitcast.5, ...), kind=kLoop, calls=%fused_computation.230 | loop fusion | flops 884736 | bytes 730640 | tf_op jit(solution)/shard_map/mul | solution.py:65
  49.9 2.5 %collective-permute-start.24 = (bf16[2,3,1,16,512]{4,3,2,1,0:T(8,128)(2,1)S(1)}, bf16[2,3,1,16,512]{4,3,2,1,0:T(8,128)(2,1)S(1)}, u32[]{:S(2)}, u32[]{:S(2)}) collective-permute-start(bf16[2,3,1,16,512]{4,3,2,1,0:T(8,128)(2,1)S(1)} %bitcast.578), channel_id=1, source_target_pairs={{0,24},{4,28},{8,16},{12,20},{16,8},{20,12},{24,0},{28,4},{1,25},{... | collective-permute-start | bytes 294920 | tf_op jit(solution)/shard_map/ppermute | solution.py:55
  52.5 4.4 %collective-permute-start.8 = (bf16[3,64,1024]{2,1,0:T(8,128)(2,1)S(1)}, bf16[3,64,1024]{2,1,0:T(8,128)(2,1)S(1)}, u32[]{:S(2)}, u32[]{:S(2)}) collective-permute-start(bf16[3,64,1024]{2,1,0:T(8,128)(2,1)S(1)} %get-tuple-element.59), channel_id=1, source_target_pairs={{0,1},{3,2},{4,5},{7,6},{8,9},{11,10},{12,13},{15,14},{16,17},{19,... | collective-permute-start | bytes 1179656 | tf_op jit(solution)/shard_map/ppermute | solution.py:129
  58.5 4.4 %collective-permute-start.14 = (bf16[3,64,1024]{2,1,0:T(8,128)(2,1)S(1)}, bf16[3,64,1024]{2,1,0:T(8,128)(2,1)S(1)}, u32[]{:S(2)}, u32[]{:S(2)}) collective-permute-start(bf16[3,64,1024]{2,1,0:T(8,128)(2,1)S(1)} %get-tuple-element.58), channel_id=1, source_target_pairs={{0,1},{3,2},{4,5},{7,6},{8,9},{11,10},{12,13},{15,14},{16,17},{19,... | collective-permute-start | bytes 1179656 | tf_op jit(solution)/shard_map/ppermute | solution.py:129
  63.0 3.4 %collective-permute-done.8 = bf16[3,64,1024]{2,1,0:T(8,128)(2,1)S(1)} collective-permute-done((bf16[3,64,1024]{2,1,0:T(8,128)(2,1)S(1)}, bf16[3,64,1024]{2,1,0:T(8,128)(2,1)S(1)}, u32[]{:S(2)}, u32[]{:S(2)}) %collective-permute-start.8) | collective-permute-done | bytes 393248 | tf_op jit(solution)/shard_map/ppermute | solution.py:129
  69.0 7.5 %collective-permute-start.13 = (bf16[3,64,1024]{2,1,0:T(8,128)(2,1)S(1)}, bf16[3,64,1024]{2,1,0:T(8,128)(2,1)S(1)}, u32[]{:S(2)}, u32[]{:S(2)}) collective-permute-start(bf16[3,64,1024]{2,1,0:T(8,128)(2,1)S(1)} %maximum_select_fusion.2), channel_id=1, source_target_pairs={{0,1},{3,2},{4,5},{7,6},{8,9},{11,10},{12,13},{15,14},{16,17},{19,... | collective-permute-start | bytes 1179656 | tf_op jit(solution)/shard_map/ppermute | solution.py:129
  80.0 4.3 %collective-permute-start.27 = (bf16[3,64,1024]{2,1,0:T(8,128)(2,1)S(1)}, bf16[3,64,1024]{2,1,0:T(8,128)(2,1)S(1)}, u32[]{:S(2)}, u32[]{:S(2)}) collective-permute-start(bf16[3,64,1024]{2,1,0:T(8,128)(2,1)S(1)} %maximum_select_fusion.5), channel_id=1, source_target_pairs={{0,1},{3,2},{4,5},{7,6},{8,9},{11,10},{12,13},{15,14},{16,17},{19,... | collective-permute-start | bytes 1179656 | tf_op jit(solution)/shard_map/ppermute | solution.py:129
  88.7 7.3 %collective-permute-start.26 = (bf16[3,64,1024]{2,1,0:T(8,128)(2,1)S(1)}, bf16[3,64,1024]{2,1,0:T(8,128)(2,1)S(1)}, u32[]{:S(2)}, u32[]{:S(2)}) collective-permute-start(bf16[3,64,1024]{2,1,0:T(8,128)(2,1)S(1)} %maximum_select_fusion.4), channel_id=1, source_target_pairs={{0,1},{3,2},{4,5},{7,6},{8,9},{11,10},{12,13},{15,14},{16,17},{19,... | collective-permute-start | bytes 1179656 | tf_op jit(solution)/shard_map/ppermute | solution.py:129
  98.8 9.2 %collective-permute-done.11 = bf16[3,64,1024]{2,1,0:T(8,128)(2,1)S(1)} collective-permute-done((bf16[3,64,1024]{2,1,0:T(8,128)(2,1)S(1)}, bf16[3,64,1024]{2,1,0:T(8,128)(2,1)S(1)}, u32[]{:S(2)}, u32[]{:S(2)}) %collective-permute-start.11) | collective-permute-done | bytes 393248 | tf_op jit(solution)/shard_map/ppermute | solution.py:136
  108.8 3.2 %collective-permute-start.39 = (bf16[3,64,1024]{2,1,0:T(8,128)(2,1)S(1)}, bf16[3,64,1024]{2,1,0:T(8,128)(2,1)S(1)}, u32[]{:S(2)}, u32[]{:S(2)}) collective-permute-start(bf16[3,64,1024]{2,1,0:T(8,128)(2,1)S(1)} %maximum_select_fusion.7), channel_id=1, source_target_pairs={{0,1},{3,2},{4,5},{7,6},{8,9},{11,10},{12,13},{15,14},{16,17},{19,... | collective-permute-start | bytes 1179656 | tf_op jit(solution)/shard_map/ppermute | solution.py:129
  123.0 6.6 %collective-permute-done.17 = bf16[3,64,1024]{2,1,0:T(8,128)(2,1)S(1)} collective-permute-done((bf16[3,64,1024]{2,1,0:T(8,128)(2,1)S(1)}, bf16[3,64,1024]{2,1,0:T(8,128)(2,1)S(1)}, u32[]{:S(2)}, u32[]{:S(2)}) %collective-permute-start.17) | collective-permute-done | bytes 393248 | tf_op jit(solution)/shard_map/ppermute | solution.py:136
  130.4 5.2 %collective-permute-start.45 = (bf16[3,64,1024]{2,1,0:T(8,128)(2,1)S(1)}, bf16[3,64,1024]{2,1,0:T(8,128)(2,1)S(1)}, u32[]{:S(2)}, u32[]{:S(2)}) collective-permute-start(bf16[3,64,1024]{2,1,0:T(8,128)(2,1)S(1)} %maximum_select_fusion.9), channel_id=1, source_target_pairs={{0,1},{3,2},{4,5},{7,6},{8,9},{11,10},{12,13},{15,14},{16,17},{19,... | collective-permute-start | bytes 1179656 | tf_op jit(solution)/shard_map/ppermute | solution.py:129
  143.7 7.2 %collective-permute-done.30 = bf16[3,64,1024]{2,1,0:T(8,128)(2,1)S(1)} collective-permute-done((bf16[3,64,1024]{2,1,0:T(8,128)(2,1)S(1)}, bf16[3,64,1024]{2,1,0:T(8,128)(2,1)S(1)}, u32[]{:S(2)}, u32[]{:S(2)}) %collective-permute-start.30) | collective-permute-done | bytes 393248 | tf_op jit(solution)/shard_map/ppermute | solution.py:136
  159.0 19.7 %collective-permute-done.42 = bf16[3,64,1024]{2,1,0:T(8,128)(2,1)S(1)} collective-permute-done((bf16[3,64,1024]{2,1,0:T(8,128)(2,1)S(1)}, bf16[3,64,1024]{2,1,0:T(8,128)(2,1)S(1)}, u32[]{:S(2)}, u32[]{:S(2)}) %collective-permute-start.42) | collective-permute-done | bytes 393248 | tf_op jit(solution)/shard_map/ppermute | solution.py:136
  184.1 3.5 %collective-permute-done.33 = bf16[2,3,16,512]{3,2,1,0:T(8,128)(2,1)S(1)} collective-permute-done((bf16[2,3,16,512]{3,2,1,0:T(8,128)(2,1)S(1)}, bf16[2,3,16,512]{3,2,1,0:T(8,128)(2,1)S(1)}, u32[]{:S(2)}, u32[]{:S(2)}) %collective-permute-start.33) | collective-permute-done | bytes 98336 | tf_op jit(solution)/shard_map/ppermute | solution.py:55
  189.3 2.7 %collective-permute-start.36 = (bf16[2,48,512]{2,1,0:T(8,128)(2,1)S(1)}, bf16[2,48,512]{2,1,0:T(8,128)(2,1)S(1)}, u32[]{:S(2)}, u32[]{:S(2)}) collective-permute-start(bf16[2,48,512]{2,1,0:T(8,128)(2,1)S(1)} %bitcast.592), channel_id=1, source_target_pairs={{0,1},{1,0},{2,3},{3,2},{4,5},{5,4},{6,7},{7,6},{8,9},{9,8},{10,11... | collective-permute-start | bytes 294920 | tf_op jit(solution)/shard_map/ppermute | solution.py:55
  192.1 3.4 %collective-permute-done.36 = bf16[2,48,512]{2,1,0:T(8,128)(2,1)S(1)} collective-permute-done((bf16[2,48,512]{2,1,0:T(8,128)(2,1)S(1)}, bf16[2,48,512]{2,1,0:T(8,128)(2,1)S(1)}, u32[]{:S(2)}, u32[]{:S(2)}) %collective-permute-start.36) | collective-permute-done | bytes 98336 | tf_op jit(solution)/shard_map/ppermute | solution.py:55
  197.0 5.2 %collective-permute-done.37 = bf16[2,48,512]{2,1,0:T(8,128)(2,1)S(1)} collective-permute-done((bf16[2,48,512]{2,1,0:T(8,128)(2,1)S(1)}, bf16[2,48,512]{2,1,0:T(8,128)(2,1)S(1)}, u32[]{:S(2)}, u32[]{:S(2)}) %collective-permute-start.37) | collective-permute-done | bytes 98336 | tf_op jit(solution)/shard_map/ppermute | solution.py:55
  206.1 2.0 multiply_convert_fusion
  211.8 2.0 multiply_convert_fusion.1
  215.9 1.8 collective-permute-start.55
  217.7 2.3 %collective-permute-start.56 = (bf16[2,32,512]{2,1,0:T(8,128)(2,1)S(1)}, bf16[2,32,512]{2,1,0:T(8,128)(2,1)S(1)}, u32[]{:S(2)}, u32[]{:S(2)}) collective-permute-start(bf16[2,32,512]{2,1,0:T(8,128)(2,1)S(1)} %bitcast.590), channel_id=1, source_target_pairs={{0,3},{1,2},{2,1},{3,0},{4,7},{5,6},{6,5},{7,4},{8,11},{9,10},{10,... | collective-permute-start | bytes 196616 | tf_op jit(solution)/shard_map/ppermute | solution.py:55
  220.1 2.0 multiply_convert_fusion.2
  223.9 2.6 %add_multiply_fusion.1 = f32[2,32,512]{2,1,0:T(8,128)S(1)} fusion(bf16[2,32,512]{2,1,0:T(8,128)(2,1)S(1)} %collective-permute-done.56, bf16[2,32,512]{2,1,0:T(8,128)(2,1)S(1)} %collective-permute-done.55, bf16[2,32,512]{2,1,0:T(8,128)(2,1)S(1)} %collective-permute-done.54, f32[]{:T(128)} %bitcast.7, f32[]{:T(128)} %bitcast.6, f32[]{:T(128)} %bitcast.5, ...), kind=kLoop, calls=%fused_computation.296 | loop fusion | flops 393216 | bytes 393232 | tf_op jit(solution)/shard_map/mul | solution.py:65
  (275 shorter events, 82.5 us)
Async XLA Ops:
  28.4 17.2 %collective-permute-start.19 = (bf16[2,48,512]{2,1,0:T(8,128)(2,1)S(1)}, bf16[2,48,512]{2,1,0:T(8,128)(2,1)S(1)}, u32[]{:S(2)}, u32[]{:S(2)}) collective-permute-start(bf16[2,48,512]{2,1,0:T(8,128)(2,1)S(1)} %fusion.77), channel_id=1, source_target_pairs={{0,1},{1,0},{2,3},{3,2},{4,5},{5,4},{6,7},{7,6},{8,9},{9,8},{10,11... | collective-permute-start | bytes 294920 | tf_op jit(solution)/shard_map/ppermute | solution.py:55
  28.5 17.1 %collective-permute-start.20 = (bf16[2,48,512]{2,1,0:T(8,128)(2,1)S(1)}, bf16[2,48,512]{2,1,0:T(8,128)(2,1)S(1)}, u32[]{:S(2)}, u32[]{:S(2)}) collective-permute-start(bf16[2,48,512]{2,1,0:T(8,128)(2,1)S(1)} %fusion.77), channel_id=1, source_target_pairs={{0,2},{1,3},{2,0},{3,1},{4,6},{5,7},{6,4},{7,5},{8,10},{9,11},{10,... | collective-permute-start | bytes 294920 | tf_op jit(solution)/shard_map/ppermute | solution.py:55
  30.8 14.8 %collective-permute-start.21 = (bf16[2,48,512]{2,1,0:T(8,128)(2,1)S(1)}, bf16[2,48,512]{2,1,0:T(8,128)(2,1)S(1)}, u32[]{:S(2)}, u32[]{:S(2)}) collective-permute-start(bf16[2,48,512]{2,1,0:T(8,128)(2,1)S(1)} %fusion.77), channel_id=1, source_target_pairs={{0,3},{1,2},{2,1},{3,0},{4,7},{5,6},{6,5},{7,4},{8,11},{9,10},{10,... | collective-permute-start | bytes 294920 | tf_op jit(solution)/shard_map/ppermute | solution.py:55
  49.4 13.5 %collective-permute-start.23 = (bf16[2,3,1,16,512]{4,3,2,1,0:T(8,128)(2,1)S(1)}, bf16[2,3,1,16,512]{4,3,2,1,0:T(8,128)(2,1)S(1)}, u32[]{:S(2)}, u32[]{:S(2)}) collective-permute-start(bf16[2,3,1,16,512]{4,3,2,1,0:T(8,128)(2,1)S(1)} %bitcast.577), channel_id=1, source_target_pairs={{0,16},{4,20},{8,24},{12,28},{16,0},{20,4},{24,8},{28,12},{1,17},{... | collective-permute-start | bytes 294920 | tf_op jit(solution)/shard_map/ppermute | solution.py:55
  49.9 13.0 %collective-permute-start.24 = (bf16[2,3,1,16,512]{4,3,2,1,0:T(8,128)(2,1)S(1)}, bf16[2,3,1,16,512]{4,3,2,1,0:T(8,128)(2,1)S(1)}, u32[]{:S(2)}, u32[]{:S(2)}) collective-permute-start(bf16[2,3,1,16,512]{4,3,2,1,0:T(8,128)(2,1)S(1)} %bitcast.578), channel_id=1, source_target_pairs={{0,24},{4,28},{8,16},{12,20},{16,8},{20,12},{24,0},{28,4},{1,25},{... | collective-permute-start | bytes 294920 | tf_op jit(solution)/shard_map/ppermute | solution.py:55
  52.5 13.9 %collective-permute-start.8 = (bf16[3,64,1024]{2,1,0:T(8,128)(2,1)S(1)}, bf16[3,64,1024]{2,1,0:T(8,128)(2,1)S(1)}, u32[]{:S(2)}, u32[]{:S(2)}) collective-permute-start(bf16[3,64,1024]{2,1,0:T(8,128)(2,1)S(1)} %get-tuple-element.59), channel_id=1, source_target_pairs={{0,1},{3,2},{4,5},{7,6},{8,9},{11,10},{12,13},{15,14},{16,17},{19,... | collective-permute-start | bytes 1179656 | tf_op jit(solution)/shard_map/ppermute | solution.py:129
  58.5 18.0 %collective-permute-start.14 = (bf16[3,64,1024]{2,1,0:T(8,128)(2,1)S(1)}, bf16[3,64,1024]{2,1,0:T(8,128)(2,1)S(1)}, u32[]{:S(2)}, u32[]{:S(2)}) collective-permute-start(bf16[3,64,1024]{2,1,0:T(8,128)(2,1)S(1)} %get-tuple-element.58), channel_id=1, source_target_pairs={{0,1},{3,2},{4,5},{7,6},{8,9},{11,10},{12,13},{15,14},{16,17},{19,... | collective-permute-start | bytes 1179656 | tf_op jit(solution)/shard_map/ppermute | solution.py:129
  62.9 14.4 %collective-permute-start.25 = (bf16[2,3,4,16,512]{4,3,2,1,0:T(8,128)(2,1)S(1)}, bf16[2,3,4,16,512]{4,3,2,1,0:T(8,128)(2,1)S(1)}, u32[]{:S(2)}, u32[]{:S(2)}) collective-permute-start(bf16[2,3,4,16,512]{4,3,2,1,0:T(8,128)(2,1)S(1)} %pad_maximum_fusion.5), channel_id=1, source_target_pairs={{0,4},{4,0},{8,12},{12,8},{16,20},{20,16},{24,28},{28,24},{1,5},{5... | collective-permute-start | bytes 1179656 | tf_op jit(solution)/shard_map/ppermute | solution.py:55
  66.8 21.9 %collective-permute-start.10 = (bf16[3,64,1024]{2,1,0:T(8,128)(2,1)S(1)}, bf16[3,64,1024]{2,1,0:T(8,128)(2,1)S(1)}, u32[]{:S(2)}, u32[]{:S(2)}) collective-permute-start(bf16[3,64,1024]{2,1,0:T(8,128)(2,1)S(1)} %pad_maximum_fusion.3), channel_id=1, source_target_pairs={{1,2},{2,1},{5,6},{6,5},{9,10},{10,9},{13,14},{14,13},{17,18},{18,... | collective-permute-start | bytes 1179656 | tf_op jit(solution)/shard_map/ppermute | solution.py:143
  67.5 41.3 %collective-permute-start.12 = (bf16[3,64,1024]{2,1,0:T(8,128)(2,1)S(1)}, bf16[3,64,1024]{2,1,0:T(8,128)(2,1)S(1)}, u32[]{:S(2)}, u32[]{:S(2)}) collective-permute-start(bf16[3,64,1024]{2,1,0:T(8,128)(2,1)S(1)} %pad_maximum_fusion.3), channel_id=1, source_target_pairs={{1,0},{2,3},{5,4},{6,7},{9,8},{10,11},{13,12},{14,15},{17,16},{18,... | collective-permute-start | bytes 1179656 | tf_op jit(solution)/shard_map/ppermute | solution.py:136
  69.0 16.1 %collective-permute-start.13 = (bf16[3,64,1024]{2,1,0:T(8,128)(2,1)S(1)}, bf16[3,64,1024]{2,1,0:T(8,128)(2,1)S(1)}, u32[]{:S(2)}, u32[]{:S(2)}) collective-permute-start(bf16[3,64,1024]{2,1,0:T(8,128)(2,1)S(1)} %maximum_select_fusion.2), channel_id=1, source_target_pairs={{0,1},{3,2},{4,5},{7,6},{8,9},{11,10},{12,13},{15,14},{16,17},{19,... | collective-permute-start | bytes 1179656 | tf_op jit(solution)/shard_map/ppermute | solution.py:129
  80.0 16.1 %collective-permute-start.27 = (bf16[3,64,1024]{2,1,0:T(8,128)(2,1)S(1)}, bf16[3,64,1024]{2,1,0:T(8,128)(2,1)S(1)}, u32[]{:S(2)}, u32[]{:S(2)}) collective-permute-start(bf16[3,64,1024]{2,1,0:T(8,128)(2,1)S(1)} %maximum_select_fusion.5), channel_id=1, source_target_pairs={{0,1},{3,2},{4,5},{7,6},{8,9},{11,10},{12,13},{15,14},{16,17},{19,... | collective-permute-start | bytes 1179656 | tf_op jit(solution)/shard_map/ppermute | solution.py:129
  85.5 30.9 %collective-permute-start.16 = (bf16[3,64,1024]{2,1,0:T(8,128)(2,1)S(1)}, bf16[3,64,1024]{2,1,0:T(8,128)(2,1)S(1)}, u32[]{:S(2)}, u32[]{:S(2)}) collective-permute-start(bf16[3,64,1024]{2,1,0:T(8,128)(2,1)S(1)} %pad_maximum_fusion.4), channel_id=1, source_target_pairs={{1,2},{2,1},{5,6},{6,5},{9,10},{10,9},{13,14},{14,13},{17,18},{18,... | collective-permute-start | bytes 1179656 | tf_op jit(solution)/shard_map/ppermute | solution.py:143
  86.2 44.1 %collective-permute-start.18 = (bf16[3,64,1024]{2,1,0:T(8,128)(2,1)S(1)}, bf16[3,64,1024]{2,1,0:T(8,128)(2,1)S(1)}, u32[]{:S(2)}, u32[]{:S(2)}) collective-permute-start(bf16[3,64,1024]{2,1,0:T(8,128)(2,1)S(1)} %pad_maximum_fusion.4), channel_id=1, source_target_pairs={{1,0},{2,3},{5,4},{6,7},{9,8},{10,11},{13,12},{14,15},{17,16},{18,... | collective-permute-start | bytes 1179656 | tf_op jit(solution)/shard_map/ppermute | solution.py:136
  88.7 25.8 %collective-permute-start.26 = (bf16[3,64,1024]{2,1,0:T(8,128)(2,1)S(1)}, bf16[3,64,1024]{2,1,0:T(8,128)(2,1)S(1)}, u32[]{:S(2)}, u32[]{:S(2)}) collective-permute-start(bf16[3,64,1024]{2,1,0:T(8,128)(2,1)S(1)} %maximum_select_fusion.4), channel_id=1, source_target_pairs={{0,1},{3,2},{4,5},{7,6},{8,9},{11,10},{12,13},{15,14},{16,17},{19,... | collective-permute-start | bytes 1179656 | tf_op jit(solution)/shard_map/ppermute | solution.py:129
  96.1 11.9 %collective-permute-start.11 = (bf16[3,64,1024]{2,1,0:T(8,128)(2,1)S(1)}, bf16[3,64,1024]{2,1,0:T(8,128)(2,1)S(1)}, u32[]{:S(2)}, u32[]{:S(2)}) collective-permute-start(bf16[3,64,1024]{2,1,0:T(8,128)(2,1)S(1)} %collective-permute-done.10), channel_id=1, source_target_pairs={{1,0},{2,3},{5,4},{6,7},{9,8},{10,11},{13,12},{14,15},{17,16},{18,... | collective-permute-start | bytes 1179656 | tf_op jit(solution)/shard_map/ppermute | solution.py:136
  108.8 12.5 %collective-permute-start.39 = (bf16[3,64,1024]{2,1,0:T(8,128)(2,1)S(1)}, bf16[3,64,1024]{2,1,0:T(8,128)(2,1)S(1)}, u32[]{:S(2)}, u32[]{:S(2)}) collective-permute-start(bf16[3,64,1024]{2,1,0:T(8,128)(2,1)S(1)} %maximum_select_fusion.7), channel_id=1, source_target_pairs={{0,1},{3,2},{4,5},{7,6},{8,9},{11,10},{12,13},{15,14},{16,17},{19,... | collective-permute-start | bytes 1179656 | tf_op jit(solution)/shard_map/ppermute | solution.py:129
  115.1 22.8 %collective-permute-start.38 = (bf16[3,64,1024]{2,1,0:T(8,128)(2,1)S(1)}, bf16[3,64,1024]{2,1,0:T(8,128)(2,1)S(1)}, u32[]{:S(2)}, u32[]{:S(2)}) collective-permute-start(bf16[3,64,1024]{2,1,0:T(8,128)(2,1)S(1)} %maximum_select_fusion.6), channel_id=1, source_target_pairs={{0,1},{3,2},{4,5},{7,6},{8,9},{11,10},{12,13},{15,14},{16,17},{19,... | collective-permute-start | bytes 1179656 | tf_op jit(solution)/shard_map/ppermute | solution.py:129
  116.4 13.1 %collective-permute-start.17 = (bf16[3,64,1024]{2,1,0:T(8,128)(2,1)S(1)}, bf16[3,64,1024]{2,1,0:T(8,128)(2,1)S(1)}, u32[]{:S(2)}, u32[]{:S(2)}) collective-permute-start(bf16[3,64,1024]{2,1,0:T(8,128)(2,1)S(1)} %collective-permute-done.16), channel_id=1, source_target_pairs={{1,0},{2,3},{5,4},{6,7},{9,8},{10,11},{13,12},{14,15},{17,16},{18,... | collective-permute-start | bytes 1179656 | tf_op jit(solution)/shard_map/ppermute | solution.py:136
  118.9 20.8 %collective-permute-start.29 = (bf16[3,64,1024]{2,1,0:T(8,128)(2,1)S(1)}, bf16[3,64,1024]{2,1,0:T(8,128)(2,1)S(1)}, u32[]{:S(2)}, u32[]{:S(2)}) collective-permute-start(bf16[3,64,1024]{2,1,0:T(8,128)(2,1)S(1)} %pad_maximum_fusion.6), channel_id=1, source_target_pairs={{1,2},{2,1},{5,6},{6,5},{9,10},{10,9},{13,14},{14,13},{17,18},{18,... | collective-permute-start | bytes 1179656 | tf_op jit(solution)/shard_map/ppermute | solution.py:143
  121.4 30.3 %collective-permute-start.31 = (bf16[3,64,1024]{2,1,0:T(8,128)(2,1)S(1)}, bf16[3,64,1024]{2,1,0:T(8,128)(2,1)S(1)}, u32[]{:S(2)}, u32[]{:S(2)}) collective-permute-start(bf16[3,64,1024]{2,1,0:T(8,128)(2,1)S(1)} %pad_maximum_fusion.6), channel_id=1, source_target_pairs={{1,0},{2,3},{5,4},{6,7},{9,8},{10,11},{13,12},{14,15},{17,16},{18,... | collective-permute-start | bytes 1179656 | tf_op jit(solution)/shard_map/ppermute | solution.py:136
  129.5 11.5 %collective-permute-start.40 = (bf16[3,64,1024]{2,1,0:T(8,128)(2,1)S(1)}, bf16[3,64,1024]{2,1,0:T(8,128)(2,1)S(1)}, u32[]{:S(2)}, u32[]{:S(2)}) collective-permute-start(bf16[3,64,1024]{2,1,0:T(8,128)(2,1)S(1)} %add_convert_fusion.1), channel_id=1, source_target_pairs={{1,2},{2,1},{5,6},{6,5},{9,10},{10,9},{13,14},{14,13},{17,18},{18,... | collective-permute-start | bytes 1179656 | tf_op jit(solution)/shard_map/ppermute | solution.py:143
  130.4 11.8 %collective-permute-start.45 = (bf16[3,64,1024]{2,1,0:T(8,128)(2,1)S(1)}, bf16[3,64,1024]{2,1,0:T(8,128)(2,1)S(1)}, u32[]{:S(2)}, u32[]{:S(2)}) collective-permute-start(bf16[3,64,1024]{2,1,0:T(8,128)(2,1)S(1)} %maximum_select_fusion.9), channel_id=1, source_target_pairs={{0,1},{3,2},{4,5},{7,6},{8,9},{11,10},{12,13},{15,14},{16,17},{19,... | collective-permute-start | bytes 1179656 | tf_op jit(solution)/shard_map/ppermute | solution.py:129
  138.0 16.4 %collective-permute-start.44 = (bf16[3,64,1024]{2,1,0:T(8,128)(2,1)S(1)}, bf16[3,64,1024]{2,1,0:T(8,128)(2,1)S(1)}, u32[]{:S(2)}, u32[]{:S(2)}) collective-permute-start(bf16[3,64,1024]{2,1,0:T(8,128)(2,1)S(1)} %maximum_select_fusion.8), channel_id=1, source_target_pairs={{0,1},{3,2},{4,5},{7,6},{8,9},{11,10},{12,13},{15,14},{16,17},{19,... | collective-permute-start | bytes 1179656 | tf_op jit(solution)/shard_map/ppermute | solution.py:129
  139.7 11.1 %collective-permute-start.30 = (bf16[3,64,1024]{2,1,0:T(8,128)(2,1)S(1)}, bf16[3,64,1024]{2,1,0:T(8,128)(2,1)S(1)}, u32[]{:S(2)}, u32[]{:S(2)}) collective-permute-start(bf16[3,64,1024]{2,1,0:T(8,128)(2,1)S(1)} %collective-permute-done.29), channel_id=1, source_target_pairs={{1,0},{2,3},{5,4},{6,7},{9,8},{10,11},{13,12},{14,15},{17,16},{18,... | collective-permute-start | bytes 1179656 | tf_op jit(solution)/shard_map/ppermute | solution.py:136
  141.5 15.4 %collective-permute-start.41 = (bf16[3,64,1024]{2,1,0:T(8,128)(2,1)S(1)}, bf16[3,64,1024]{2,1,0:T(8,128)(2,1)S(1)}, u32[]{:S(2)}, u32[]{:S(2)}) collective-permute-start(bf16[3,64,1024]{2,1,0:T(8,128)(2,1)S(1)} %pad_maximum_fusion.8), channel_id=1, source_target_pairs={{1,2},{2,1},{5,6},{6,5},{9,10},{10,9},{13,14},{14,13},{17,18},{18,... | collective-permute-start | bytes 1179656 | tf_op jit(solution)/shard_map/ppermute | solution.py:143
  142.2 37.9 %collective-permute-start.43 = (bf16[3,64,1024]{2,1,0:T(8,128)(2,1)S(1)}, bf16[3,64,1024]{2,1,0:T(8,128)(2,1)S(1)}, u32[]{:S(2)}, u32[]{:S(2)}) collective-permute-start(bf16[3,64,1024]{2,1,0:T(8,128)(2,1)S(1)} %pad_maximum_fusion.8), channel_id=1, source_target_pairs={{1,0},{2,3},{5,4},{6,7},{9,8},{10,11},{13,12},{14,15},{17,16},{18,... | collective-permute-start | bytes 1179656 | tf_op jit(solution)/shard_map/ppermute | solution.py:136
  154.9 26.6 %collective-permute-start.47 = (bf16[3,64,1024]{2,1,0:T(8,128)(2,1)S(1)}, bf16[3,64,1024]{2,1,0:T(8,128)(2,1)S(1)}, u32[]{:S(2)}, u32[]{:S(2)}) collective-permute-start(bf16[3,64,1024]{2,1,0:T(8,128)(2,1)S(1)} %pad_maximum_fusion.9), channel_id=1, source_target_pairs={{1,2},{2,1},{5,6},{6,5},{9,10},{10,9},{13,14},{14,13},{17,18},{18,... | collective-permute-start | bytes 1179656 | tf_op jit(solution)/shard_map/ppermute | solution.py:143
  155.5 47.5 %collective-permute-start.49 = (bf16[3,64,1024]{2,1,0:T(8,128)(2,1)S(1)}, bf16[3,64,1024]{2,1,0:T(8,128)(2,1)S(1)}, u32[]{:S(2)}, u32[]{:S(2)}) collective-permute-start(bf16[3,64,1024]{2,1,0:T(8,128)(2,1)S(1)} %pad_maximum_fusion.9), channel_id=1, source_target_pairs={{1,0},{2,3},{5,4},{6,7},{9,8},{10,11},{13,12},{14,15},{17,16},{18,... | collective-permute-start | bytes 1179656 | tf_op jit(solution)/shard_map/ppermute | solution.py:136
  156.9 21.9 %collective-permute-start.42 = (bf16[3,64,1024]{2,1,0:T(8,128)(2,1)S(1)}, bf16[3,64,1024]{2,1,0:T(8,128)(2,1)S(1)}, u32[]{:S(2)}, u32[]{:S(2)}) collective-permute-start(bf16[3,64,1024]{2,1,0:T(8,128)(2,1)S(1)} %collective-permute-done.41), channel_id=1, source_target_pairs={{1,0},{2,3},{5,4},{6,7},{9,8},{10,11},{13,12},{14,15},{17,16},{18,... | collective-permute-start | bytes 1179656 | tf_op jit(solution)/shard_map/ppermute | solution.py:136
  158.4 25.7 %collective-permute-start.35 = (bf16[2,3,16,512]{3,2,1,0:T(8,128)(2,1)S(1)}, bf16[2,3,16,512]{3,2,1,0:T(8,128)(2,1)S(1)}, u32[]{:S(2)}, u32[]{:S(2)}) collective-permute-start(bf16[2,3,16,512]{3,2,1,0:T(8,128)(2,1)S(1)} %get-tuple-element.45), channel_id=1, source_target_pairs={{0,24},{4,28},{8,16},{12,20},{16,8},{20,12},{24,0},{28,4},{1,25},{... | collective-permute-start | bytes 294920 | tf_op jit(solution)/shard_map/ppermute | solution.py:55
  181.5 21.4 %collective-permute-start.48 = (bf16[3,64,1024]{2,1,0:T(8,128)(2,1)S(1)}, bf16[3,64,1024]{2,1,0:T(8,128)(2,1)S(1)}, u32[]{:S(2)}, u32[]{:S(2)}) collective-permute-start(bf16[3,64,1024]{2,1,0:T(8,128)(2,1)S(1)} %broadcast_select_fusion.12), channel_id=1, source_target_pairs={{1,0},{2,3},{5,4},{6,7},{9,8},{10,11},{13,12},{14,15},{17,16},{18,... | collective-permute-start | bytes 1179656 | tf_op jit(solution)/shard_map/ppermute | solution.py:136
  (31 other events, 285.5 us)

commit v6 on v5

--- a/solution.py
+++ b/solution.py
@@ -45,7 +45,7 @@
     columns += [signs[me, me ^ apart] for apart in range(groups)]
     columns += [1 - 2 * (me >> bit & 1) for bit in range(groups.bit_length() - 1)]
     table = np.stack(columns, axis=1).astype(np.float32)[:, :, None, None]
-    table = jnp.asarray(np.broadcast_to(table, table.shape[:3] + (length,)))
+    table = jnp.asarray(np.tile(table, (1, 1, 1, length)))
     row = lax.dynamic_index_in_dim(table, lax.axis_index("tensor"), keepdims=False)
     return row[0], row[1], row[2 : 2 + groups], row[2 + groups :]
 
@@ -131,9 +131,12 @@
     return total, came
 
 
-def outward(block, depth):
+def outward(parts, depth, ahead=None):
+    block = jnp.concatenate(parts, axis=1)
     for step in reversed(fold_steps()):
         came = lax.ppermute(block, "tensor", [(b, a) for a, b in line_pairs(step)])
+        if ahead is not None and step == 0:
+            block = jnp.concatenate([after(parts[0], ahead)] + parts[1:], axis=1)
         block = jnp.where(depth[:, : block.shape[-1]] == step, came, block)
     return block
 
@@ -176,49 +179,54 @@
     late = spread(after(both[:, first * step :], early[1])) if chunks > first else None
     groups = [arrive(rotate(early, signs).astype(BF16))]
 
-    done, arrived, crossed = [], [], []
+    done, mids, acts = [], [], []
     for i in range(chunks):
         group, place = (groups[0], i) if i < first else (groups[1], i - first)
         sums = []
         for which, (x, g) in enumerate([(part[0, place], part[1, place]) for part in group]):
-            ahead = arrived[max(2 * i - 4 + which, 0)] if i > 0 else message if arrived else None
-            if ahead is not None:
-                x, g = after(x, ahead), after(g, ahead)
+            if i > 0:
+                ahead = [acts[i - 1]] if which else [mids[i - 1]]
+                ahead += [crossed[i - 2]] if i > 1 and not which else []
+            else:
+                ahead, crossed = [message[2:]] if which else [], []
+            for other in ahead:
+                x, g = after(x, other), after(g, other)
             parts = [dot(x, gate_weight, 1, 0), dot(x, up_weight, 1, 0), dot(g, down_weight, 1, 1)]
-            block = jnp.stack(parts).astype(BF16)
-            block = after(block, arrived[max(len(arrived) - 2, 0)]) if arrived else block
-            message = message if arrived else block[2:]
-            total, came = inward(block)
-            arrived.append(came)
+            message = jnp.stack(parts).astype(BF16)
+            if i == 0 and which:
+                message = after(message, came)
+            total, came = inward(message)
             sums.append(total)
             if len(groups) == 1 and chunks > first:
-                late[0] = after(late[0], came)
+                tick = exchange(message[2, :step, :width], "dp", 1)
+                late[0] = after(late[0], tick)
                 groups.append(arrive(rotate(late, signs).astype(BF16)))
-        other, own = sums
-        sums = own + across(other.astype(BF16)).astype(F32)
-        own = activations(sums[0], sums[1], sums[2])
-        crossed.append(across(own))
-        if i < chunks - 1:
-            done.append([outward(crossed[i], depth), outward(own, depth)])
+        mids.append(sums[0].astype(BF16))
+        sums = sums[1] + across(mids[i]).astype(F32)
+        acts.append(activations(sums[0], sums[1], sums[2]))
+        crossed.append(across(acts[i]))
+        if i > 0:
+            done.append([outward([crossed[i - 1], acts[i - 1]], depth, crossed[i])])
 
     def leave(blocks):
         lows, highs = [], []
-        for halves in blocks:
+        for parts in blocks:
             sums = []
-            for acts in halves:
-                mixed = dot(acts[0], down_weight, 1, 0)
-                grads = dot(acts[1], gate_weight, 1, 1) + dot(acts[2], up_weight, 1, 1)
+            for block in parts:
+                mixed = dot(block[0], down_weight, 1, 0)
+                grads = dot(block[1], gate_weight, 1, 1) + dot(block[2], up_weight, 1, 1)
                 sums.append(jnp.stack([mixed, grads]))
-            lows.append(jnp.where(far, sums[0], sums[1]))
-            highs.append(jnp.where(far, sums[1], sums[0]).astype(BF16))
+            sums = jnp.concatenate(sums, axis=1)
+            lows.append(jnp.where(far, sums[:, :half], sums[:, half:]))
+            highs.append(jnp.where(far, sums[:, half:], sums[:, :half]).astype(BF16))
         return jnp.stack(lows, axis=1), jnp.stack(highs, axis=1)
 
     split, ends = max(chunks - 2, 0), []
     if split > 0:
-        sums, came, last = scatter_dp(*leave(done[:split]))
+        low, high = leave(done[:split])
+        sums, _, last = scatter_dp(low, after(high, crossed[-1]))
         ends.append(rotate_by_halves(sums.reshape(2, -1, width), bits))
-        crossed[-1] = after(crossed[-1], came)
-    done.append([outward(crossed[-1], depth), outward(own, depth)])
+    done.append([outward([crossed[-1]], depth), outward([acts[-1]], depth)])
     low, high = leave(done[split:])
     if split > 0:
         high = after(high, last)
@@ -226,7 +234,7 @@
     ends.append(rotate(spread(sums.reshape(2, -1, width).astype(BF16)), signs))
     ends = jnp.concatenate(ends, axis=1)
 
-    acts = jnp.concatenate([half for halves in done for half in halves], axis=1)
+    acts = jnp.concatenate([block for parts in done for block in parts], axis=1)
     rows = [jnp.stack(group, axis=2).reshape(2, -1, width) for group in groups]
     rows = after(jnp.concatenate(rows, axis=1), high[0, 0, :1])
     factor = 1.0 / math.sqrt(rows.shape[1])

time: 229 us -> 215 us (0.939)
  other arithmetic: 18.6 us -> 10.9 us
  matrix products: 32.6 us -> 26.6 us
    ppermute x10, waiting for transfers between devices: 12.8 us -> 35.8 us  [inward(): came = lax.ppermute(total.astype(BF16), 'tensor', line_pairs(step))]
    ppermute x10 -> x6, waiting for transfers between devices: 42.8 us -> 23.3 us  [outward(): came = lax.ppermute(block, 'tensor', [(b, a) for a, b in line_pairs(step)])]
    mul x4, other arithmetic: 8.59 us -> 1.05 us  [turn(): rows = block.reshape(-1, width) * (1.0 / math.sqrt(D))]
    dot_general x71 -> x59, matrix products: 32.6 us -> 26.6 us  [dot(): lax.dot_general(left, right, (((left_dim,), (right_dim,)), ((), ())), pre...]
    ppermute x10 -> x6, starting transfers between devices: 13.1 us -> 7.97 us  [outward(): came = lax.ppermute(block, 'tensor', [(b, a) for a, b in line_pairs(step)])]
    ppermute x10, starting transfers between devices: 40.2 us -> 45 us  [inward(): came = lax.ppermute(total.astype(BF16), 'tensor', line_pairs(step))]
    ppermute x27 -> x28, waiting for transfers between devices: 24.3 us -> 21.2 us  [exchange(): return lax.ppermute(block, axis, [(i, i ^ apart) for i in range(count)])]
    ppermute x27 -> x28, starting transfers between devices: 31.2 us -> 32.3 us  [exchange(): return lax.ppermute(block, axis, [(i, i ^ apart) for i in range(count)])]
  transfers between devices with their start and end apart: 57 -> 54, of which waited for: 19 -> 26; matrix products, arithmetic and copies ran while one was open for 16% -> 15% of each run, Pallas kernels for 0% -> 0%
where the time goes in v6:
time: 215 us; the launch traced here: 214 us
  starting transfers between devices  92.2 us (43%)
  waiting for transfers between devices  80.4 us (37%)
  matrix products  26.6 us (12%)
  other arithmetic  10.9 us (5%)
  between operations  2.18 us (1%)
    ppermute x10, starting transfers between devices, inward(): came = lax.ppermute(total.astype(BF16), 'tensor', line_pairs(step))  45 us
    ppermute x10, waiting for transfers between devices, inward(): came = lax.ppermute(total.astype(BF16), 'tensor', line_pairs(step))  35.8 us
    ppermute x28, starting transfers between devices, exchange(): return lax.ppermute(block, axis, [(i, i ^ apart) for i in range(count)])  32.3 us
    dot_general x59, matrix products, dot(): lax.dot_general(left, right, (((left_dim,), (right_dim,)), ((), ())), pre...  26.6 us
    ppermute x6, waiting for transfers between devices, outward(): came = lax.ppermute(block, 'tensor', [(b, a) for a, b in line_pairs(step)])  23.3 us
    ppermute x28, waiting for transfers between devices, exchange(): return lax.ppermute(block, axis, [(i, i ^ apart) for i in range(count)])  21.2 us
    ppermute x6, starting transfers between devices, outward(): came = lax.ppermute(block, 'tensor', [(b, a) for a, b in line_pairs(step)])  7.97 us
    ppermute x10, starting transfers between devices, across(): return lax.ppermute(block, 'tensor', [(half - 1, half), (half, half - 1)])  6.86 us
  transfers between devices with their start and end apart: 54, of which 26 were waited for; matrix products, arithmetic and copies ran while one was open for 15% of the time, Pallas kernels for 0%

profile of v6, /device:TPU:0, one launch (start us, length us, event | category | flops | bytes accessed | tf_op | source)
XLA Modules:
  0.0 213.9 jit_solution(11654797331908582642)
XLA Ops:
  1.6 5.0 %collective-permute-start.2 = (bf16[2,32,512]{2,1,0:T(8,128)(2,1)S(1)}, bf16[2,32,512]{2,1,0:T(8,128)(2,1)S(1)}, u32[]{:S(2)}, u32[]{:S(2)}) collective-permute-start(bf16[2,32,512]{2,1,0:T(8,128)(2,1)S(1)} %pad_maximum_fusion.34), channel_id=1, source_target_pairs={{0,3},{1,2},{2,1},{3,0},{4,7},{5,6},{6,5},{7,4},{8,11},{9,10},{10,... | collective-permute-start | bytes 196616 | tf_op jit(solution)/shard_map/ppermute | solution.py:55
  9.2 3.0 %collective-permute-done.1 = bf16[2,32,512]{2,1,0:T(8,128)(2,1)S(1)} collective-permute-done((bf16[2,32,512]{2,1,0:T(8,128)(2,1)S(1)}, bf16[2,32,512]{2,1,0:T(8,128)(2,1)S(1)}, u32[]{:S(2)}, u32[]{:S(2)}) %collective-permute-start.1) | collective-permute-done | bytes 65568 | tf_op jit(solution)/shard_map/ppermute | solution.py:55
  14.6 2.5 %collective-permute-start.5 = (bf16[2,2,1,16,512]{4,3,2,1,0:T(8,128)(2,1)S(1)}, bf16[2,2,1,16,512]{4,3,2,1,0:T(8,128)(2,1)S(1)}, u32[]{:S(2)}, u32[]{:S(2)}) collective-permute-start(bf16[2,2,1,16,512]{4,3,2,1,0:T(8,128)(2,1)S(1)} %bitcast.551), channel_id=1, source_target_pairs={{0,24},{4,28},{8,16},{12,20},{16,8},{20,12},{24,0},{28,4},{1,25},{... | collective-permute-start | bytes 196616 | tf_op jit(solution)/shard_map/ppermute | solution.py:55
  22.1 2.8 %collective-permute-start.20 = (bf16[2,48,512]{2,1,0:T(8,128)(2,1)S(1)}, bf16[2,48,512]{2,1,0:T(8,128)(2,1)S(1)}, u32[]{:S(2)}, u32[]{:S(2)}) collective-permute-start(bf16[2,48,512]{2,1,0:T(8,128)(2,1)S(1)} %fusion.73), channel_id=1, source_target_pairs={{0,3},{1,2},{2,1},{3,0},{4,7},{5,6},{6,5},{7,4},{8,11},{9,10},{10,... | collective-permute-start | bytes 294920 | tf_op jit(solution)/shard_map/ppermute | solution.py:55
  29.0 2.3 %collective-permute-start.7 = (bf16[3,64,1024]{2,1,0:T(8,128)(2,1)S(1)}, bf16[3,64,1024]{2,1,0:T(8,128)(2,1)S(1)}, u32[]{:S(2)}, u32[]{:S(2)}) collective-permute-start(bf16[3,64,1024]{2,1,0:T(8,128)(2,1)S(1)} %pad_maximum_fusion.10), channel_id=1, source_target_pairs={{0,1},{3,2},{4,5},{7,6},{8,9},{11,10},{12,13},{15,14},{16,17},{19,... | collective-permute-start | bytes 1179656 | tf_op jit(solution)/shard_map/ppermute | solution.py:129
  38.6 2.5 %collective-permute-done.23 = bf16[2,3,1,16,512]{4,3,2,1,0:T(8,128)(2,1)S(1)} collective-permute-done((bf16[2,3,1,16,512]{4,3,2,1,0:T(8,128)(2,1)S(1)}, bf16[2,3,1,16,512]{4,3,2,1,0:T(8,128)(2,1)S(1)}, u32[]{:S(2)}, u32[]{:S(2)}) %collective-permute-start.23) | collective-permute-done | bytes 98336 | tf_op jit(solution)/shard_map/ppermute | solution.py:55
  43.5 4.3 %collective-permute-start.8 = (bf16[3,64,1024]{2,1,0:T(8,128)(2,1)S(1)}, bf16[3,64,1024]{2,1,0:T(8,128)(2,1)S(1)}, u32[]{:S(2)}, u32[]{:S(2)}) collective-permute-start(bf16[3,64,1024]{2,1,0:T(8,128)(2,1)S(1)} %maximum_select_fusion.5), channel_id=1, source_target_pairs={{0,1},{3,2},{4,5},{7,6},{8,9},{11,10},{12,13},{15,14},{16,17},{19,... | collective-permute-start | bytes 1179656 | tf_op jit(solution)/shard_map/ppermute | solution.py:129
  50.4 6.9 %collective-permute-done.8 = bf16[3,64,1024]{2,1,0:T(8,128)(2,1)S(1)} collective-permute-done((bf16[3,64,1024]{2,1,0:T(8,128)(2,1)S(1)}, bf16[3,64,1024]{2,1,0:T(8,128)(2,1)S(1)}, u32[]{:S(2)}, u32[]{:S(2)}) %collective-permute-start.8) | collective-permute-done | bytes 393248 | tf_op jit(solution)/shard_map/ppermute | solution.py:129
  59.2 5.0 %collective-permute-done.13 = bf16[3,64,1024]{2,1,0:T(8,128)(2,1)S(1)} collective-permute-done((bf16[3,64,1024]{2,1,0:T(8,128)(2,1)S(1)}, bf16[3,64,1024]{2,1,0:T(8,128)(2,1)S(1)}, u32[]{:S(2)}, u32[]{:S(2)}) %collective-permute-start.13) | collective-permute-done | bytes 393248 | tf_op jit(solution)/shard_map/ppermute | solution.py:129
  65.4 7.4 %collective-permute-start.12 = (bf16[3,64,1024]{2,1,0:T(8,128)(2,1)S(1)}, bf16[3,64,1024]{2,1,0:T(8,128)(2,1)S(1)}, u32[]{:S(2)}, u32[]{:S(2)}) collective-permute-start(bf16[3,64,1024]{2,1,0:T(8,128)(2,1)S(1)} %pad_maximum_fusion.12), channel_id=1, source_target_pairs={{0,1},{3,2},{4,5},{7,6},{8,9},{11,10},{12,13},{15,14},{16,17},{19,... | collective-permute-start | bytes 1179656 | tf_op jit(solution)/shard_map/ppermute | solution.py:129
  75.2 5.0 %collective-permute-done.12 = bf16[3,64,1024]{2,1,0:T(8,128)(2,1)S(1)} collective-permute-done((bf16[3,64,1024]{2,1,0:T(8,128)(2,1)S(1)}, bf16[3,64,1024]{2,1,0:T(8,128)(2,1)S(1)}, u32[]{:S(2)}, u32[]{:S(2)}) %collective-permute-start.12) | collective-permute-done | bytes 393248 | tf_op jit(solution)/shard_map/ppermute | solution.py:129
  81.4 5.9 %collective-permute-start.26 = (bf16[3,64,1024]{2,1,0:T(8,128)(2,1)S(1)}, bf16[3,64,1024]{2,1,0:T(8,128)(2,1)S(1)}, u32[]{:S(2)}, u32[]{:S(2)}) collective-permute-start(bf16[3,64,1024]{2,1,0:T(8,128)(2,1)S(1)} %pad_maximum_fusion.17), channel_id=1, source_target_pairs={{0,1},{3,2},{4,5},{7,6},{8,9},{11,10},{12,13},{15,14},{16,17},{19,... | collective-permute-start | bytes 1179656 | tf_op jit(solution)/shard_map/ppermute | solution.py:129
  89.8 7.1 %collective-permute-done.26 = bf16[3,64,1024]{2,1,0:T(8,128)(2,1)S(1)} collective-permute-done((bf16[3,64,1024]{2,1,0:T(8,128)(2,1)S(1)}, bf16[3,64,1024]{2,1,0:T(8,128)(2,1)S(1)}, u32[]{:S(2)}, u32[]{:S(2)}) %collective-permute-start.26) | collective-permute-done | bytes 393248 | tf_op jit(solution)/shard_map/ppermute | solution.py:129
  100.2 7.4 %collective-permute-start.31 = (bf16[3,64,1024]{2,1,0:T(8,128)(2,1)S(1)}, bf16[3,64,1024]{2,1,0:T(8,128)(2,1)S(1)}, u32[]{:S(2)}, u32[]{:S(2)}) collective-permute-start(bf16[3,64,1024]{2,1,0:T(8,128)(2,1)S(1)} %pad_maximum_fusion.20), channel_id=1, source_target_pairs={{0,1},{3,2},{4,5},{7,6},{8,9},{11,10},{12,13},{15,14},{16,17},{19,... | collective-permute-start | bytes 1179656 | tf_op jit(solution)/shard_map/ppermute | solution.py:129
  108.9 4.0 %collective-permute-done.31 = bf16[3,64,1024]{2,1,0:T(8,128)(2,1)S(1)} collective-permute-done((bf16[3,64,1024]{2,1,0:T(8,128)(2,1)S(1)}, bf16[3,64,1024]{2,1,0:T(8,128)(2,1)S(1)}, u32[]{:S(2)}, u32[]{:S(2)}) %collective-permute-start.31) | collective-permute-done | bytes 393248 | tf_op jit(solution)/shard_map/ppermute | solution.py:129
  114.8 6.3 %collective-permute-start.30 = (bf16[3,64,1024]{2,1,0:T(8,128)(2,1)S(1)}, bf16[3,64,1024]{2,1,0:T(8,128)(2,1)S(1)}, u32[]{:S(2)}, u32[]{:S(2)}) collective-permute-start(bf16[3,64,1024]{2,1,0:T(8,128)(2,1)S(1)} %pad_maximum_fusion.19), channel_id=1, source_target_pairs={{0,1},{3,2},{4,5},{7,6},{8,9},{11,10},{12,13},{15,14},{16,17},{19,... | collective-permute-start | bytes 1179656 | tf_op jit(solution)/shard_map/ppermute | solution.py:129
  123.6 2.5 %collective-permute-done.30 = bf16[3,64,1024]{2,1,0:T(8,128)(2,1)S(1)} collective-permute-done((bf16[3,64,1024]{2,1,0:T(8,128)(2,1)S(1)}, bf16[3,64,1024]{2,1,0:T(8,128)(2,1)S(1)}, u32[]{:S(2)}, u32[]{:S(2)}) %collective-permute-start.30) | collective-permute-done | bytes 393248 | tf_op jit(solution)/shard_map/ppermute | solution.py:129
  131.4 7.6 %collective-permute-start.35 = (bf16[3,64,1024]{2,1,0:T(8,128)(2,1)S(1)}, bf16[3,64,1024]{2,1,0:T(8,128)(2,1)S(1)}, u32[]{:S(2)}, u32[]{:S(2)}) collective-permute-start(bf16[3,64,1024]{2,1,0:T(8,128)(2,1)S(1)} %pad_maximum_fusion.23), channel_id=1, source_target_pairs={{0,1},{3,2},{4,5},{7,6},{8,9},{11,10},{12,13},{15,14},{16,17},{19,... | collective-permute-start | bytes 1179656 | tf_op jit(solution)/shard_map/ppermute | solution.py:129
  142.2 2.0 collective-permute-done.35
  145.2 3.3 %collective-permute-done.34 = bf16[3,64,1024]{2,1,0:T(8,128)(2,1)S(1)} collective-permute-done((bf16[3,64,1024]{2,1,0:T(8,128)(2,1)S(1)}, bf16[3,64,1024]{2,1,0:T(8,128)(2,1)S(1)}, u32[]{:S(2)}, u32[]{:S(2)}) %collective-permute-start.34) | collective-permute-done | bytes 393248 | tf_op jit(solution)/shard_map/ppermute | solution.py:129
  153.0 12.7 %collective-permute-done.44 = bf16[3,128,1024]{2,1,0:T(8,128)(2,1)S(1)} collective-permute-done((bf16[3,128,1024]{2,1,0:T(8,128)(2,1)S(1)}, bf16[3,128,1024]{2,1,0:T(8,128)(2,1)S(1)}, u32[]{:S(2)}, u32[]{:S(2)}) %collective-permute-start.44) | collective-permute-done | bytes 786464 | tf_op jit(solution)/shard_map/ppermute | solution.py:137
  169.7 10.3 %collective-permute-done.45 = bf16[3,64,1024]{2,1,0:T(8,128)(2,1)S(1)} collective-permute-done((bf16[3,64,1024]{2,1,0:T(8,128)(2,1)S(1)}, bf16[3,64,1024]{2,1,0:T(8,128)(2,1)S(1)}, u32[]{:S(2)}, u32[]{:S(2)}) %collective-permute-start.45) | collective-permute-done | bytes 393248 | tf_op jit(solution)/shard_map/ppermute | solution.py:137
  182.9 2.0 collective-permute-start.41
  186.6 1.9 collective-permute-done.41
  189.0 2.0 multiply_convert_fusion
  190.9 2.0 multiply_convert_fusion.2
  193.6 2.0 multiply_convert_fusion.1
  195.7 2.1 collective-permute-start.50
  199.3 3.0 %collective-permute-start.43 = (bf16[2,48,512]{2,1,0:T(8,128)(2,1)S(1)}, bf16[2,48,512]{2,1,0:T(8,128)(2,1)S(1)}, u32[]{:S(2)}, u32[]{:S(2)}) collective-permute-start(bf16[2,48,512]{2,1,0:T(8,128)(2,1)S(1)} %fusion.72), channel_id=1, source_target_pairs={{0,2},{1,3},{2,0},{3,1},{4,6},{5,7},{6,4},{7,5},{8,10},{9,11},{10,... | collective-permute-start | bytes 294920 | tf_op jit(solution)/shard_map/ppermute | solution.py:55
  203.0 2.7 %collective-permute-start.53 = (bf16[2,32,512]{2,1,0:T(8,128)(2,1)S(1)}, bf16[2,32,512]{2,1,0:T(8,128)(2,1)S(1)}, u32[]{:S(2)}, u32[]{:S(2)}) collective-permute-start(bf16[2,32,512]{2,1,0:T(8,128)(2,1)S(1)} %bitcast.557), channel_id=1, source_target_pairs={{0,3},{1,2},{2,1},{3,0},{4,7},{5,6},{6,5},{7,4},{8,11},{9,10},{10,... | collective-permute-start | bytes 196616 | tf_op jit(solution)/shard_map/ppermute | solution.py:55
  207.4 2.4 %collective-permute-done.43 = bf16[2,48,512]{2,1,0:T(8,128)(2,1)S(1)} collective-permute-done((bf16[2,48,512]{2,1,0:T(8,128)(2,1)S(1)}, bf16[2,48,512]{2,1,0:T(8,128)(2,1)S(1)}, u32[]{:S(2)}, u32[]{:S(2)}) %collective-permute-start.43) | collective-permute-done | bytes 98336 | tf_op jit(solution)/shard_map/ppermute | solution.py:55
  209.9 2.7 %collective-permute-done.52 = bf16[2,32,512]{2,1,0:T(8,128)(2,1)S(1)} collective-permute-done((bf16[2,32,512]{2,1,0:T(8,128)(2,1)S(1)}, bf16[2,32,512]{2,1,0:T(8,128)(2,1)S(1)}, u32[]{:S(2)}, u32[]{:S(2)}) %collective-permute-start.52) | collective-permute-done | bytes 65568 | tf_op jit(solution)/shard_map/ppermute | solution.py:55
  (264 shorter events, 73.2 us)
Async XLA Ops:
  1.6 7.6 %collective-permute-start.2 = (bf16[2,32,512]{2,1,0:T(8,128)(2,1)S(1)}, bf16[2,32,512]{2,1,0:T(8,128)(2,1)S(1)}, u32[]{:S(2)}, u32[]{:S(2)}) collective-permute-start(bf16[2,32,512]{2,1,0:T(8,128)(2,1)S(1)} %pad_maximum_fusion.34), channel_id=1, source_target_pairs={{0,3},{1,2},{2,1},{3,0},{4,7},{5,6},{6,5},{7,4},{8,11},{9,10},{10,... | collective-permute-start | bytes 196616 | tf_op jit(solution)/shard_map/ppermute | solution.py:55
  22.1 10.5 %collective-permute-start.20 = (bf16[2,48,512]{2,1,0:T(8,128)(2,1)S(1)}, bf16[2,48,512]{2,1,0:T(8,128)(2,1)S(1)}, u32[]{:S(2)}, u32[]{:S(2)}) collective-permute-start(bf16[2,48,512]{2,1,0:T(8,128)(2,1)S(1)} %fusion.73), channel_id=1, source_target_pairs={{0,3},{1,2},{2,1},{3,0},{4,7},{5,6},{6,5},{7,4},{8,11},{9,10},{10,... | collective-permute-start | bytes 294920 | tf_op jit(solution)/shard_map/ppermute | solution.py:55
  24.8 9.3 %collective-permute-start.19 = (bf16[2,48,512]{2,1,0:T(8,128)(2,1)S(1)}, bf16[2,48,512]{2,1,0:T(8,128)(2,1)S(1)}, u32[]{:S(2)}, u32[]{:S(2)}) collective-permute-start(bf16[2,48,512]{2,1,0:T(8,128)(2,1)S(1)} %fusion.73), channel_id=1, source_target_pairs={{0,2},{1,3},{2,0},{3,1},{4,6},{5,7},{6,4},{7,5},{8,10},{9,11},{10,... | collective-permute-start | bytes 294920 | tf_op jit(solution)/shard_map/ppermute | solution.py:55
  24.8 9.3 %collective-permute-start.18 = (bf16[2,48,512]{2,1,0:T(8,128)(2,1)S(1)}, bf16[2,48,512]{2,1,0:T(8,128)(2,1)S(1)}, u32[]{:S(2)}, u32[]{:S(2)}) collective-permute-start(bf16[2,48,512]{2,1,0:T(8,128)(2,1)S(1)} %fusion.73), channel_id=1, source_target_pairs={{0,1},{1,0},{2,3},{3,2},{4,5},{5,4},{6,7},{7,6},{8,9},{9,8},{10,11... | collective-permute-start | bytes 294920 | tf_op jit(solution)/shard_map/ppermute | solution.py:55
  29.0 13.5 %collective-permute-start.7 = (bf16[3,64,1024]{2,1,0:T(8,128)(2,1)S(1)}, bf16[3,64,1024]{2,1,0:T(8,128)(2,1)S(1)}, u32[]{:S(2)}, u32[]{:S(2)}) collective-permute-start(bf16[3,64,1024]{2,1,0:T(8,128)(2,1)S(1)} %pad_maximum_fusion.10), channel_id=1, source_target_pairs={{0,1},{3,2},{4,5},{7,6},{8,9},{11,10},{12,13},{15,14},{16,17},{19,... | collective-permute-start | bytes 1179656 | tf_op jit(solution)/shard_map/ppermute | solution.py:129
  42.4 7.8 %collective-permute-start.24 = (bf16[2,3,4,16,512]{4,3,2,1,0:T(8,128)(2,1)S(1)}, bf16[2,3,4,16,512]{4,3,2,1,0:T(8,128)(2,1)S(1)}, u32[]{:S(2)}, u32[]{:S(2)}) collective-permute-start(bf16[2,3,4,16,512]{4,3,2,1,0:T(8,128)(2,1)S(1)} %pad_maximum_fusion.15), channel_id=1, source_target_pairs={{0,4},{4,0},{8,12},{12,8},{16,20},{20,16},{24,28},{28,24},{1,5},{5... | collective-permute-start | bytes 1179656 | tf_op jit(solution)/shard_map/ppermute | solution.py:55
  42.6 7.8 %collective-permute-start.9 = (bf16[3,64,1024]{2,1,0:T(8,128)(2,1)S(1)}, bf16[3,64,1024]{2,1,0:T(8,128)(2,1)S(1)}, u32[]{:S(2)}, u32[]{:S(2)}) collective-permute-start(bf16[3,64,1024]{2,1,0:T(8,128)(2,1)S(1)} %add_convert_fusion.4), channel_id=1, source_target_pairs={{1,2},{2,1},{5,6},{6,5},{9,10},{10,9},{13,14},{14,13},{17,18},{18,... | collective-permute-start | bytes 1179656 | tf_op jit(solution)/shard_map/ppermute | solution.py:146
  43.5 13.8 %collective-permute-start.8 = (bf16[3,64,1024]{2,1,0:T(8,128)(2,1)S(1)}, bf16[3,64,1024]{2,1,0:T(8,128)(2,1)S(1)}, u32[]{:S(2)}, u32[]{:S(2)}) collective-permute-start(bf16[3,64,1024]{2,1,0:T(8,128)(2,1)S(1)} %maximum_select_fusion.5), channel_id=1, source_target_pairs={{0,1},{3,2},{4,5},{7,6},{8,9},{11,10},{12,13},{15,14},{16,17},{19,... | collective-permute-start | bytes 1179656 | tf_op jit(solution)/shard_map/ppermute | solution.py:129
  48.9 15.3 %collective-permute-start.13 = (bf16[3,64,1024]{2,1,0:T(8,128)(2,1)S(1)}, bf16[3,64,1024]{2,1,0:T(8,128)(2,1)S(1)}, u32[]{:S(2)}, u32[]{:S(2)}) collective-permute-start(bf16[3,64,1024]{2,1,0:T(8,128)(2,1)S(1)} %pad_maximum_fusion.13), channel_id=1, source_target_pairs={{0,1},{3,2},{4,5},{7,6},{8,9},{11,10},{12,13},{15,14},{16,17},{19,... | collective-permute-start | bytes 1179656 | tf_op jit(solution)/shard_map/ppermute | solution.py:129
  57.7 15.0 %collective-permute-start.10 = (bf16[3,64,1024]{2,1,0:T(8,128)(2,1)S(1)}, bf16[3,64,1024]{2,1,0:T(8,128)(2,1)S(1)}, u32[]{:S(2)}, u32[]{:S(2)}) collective-permute-start(bf16[3,64,1024]{2,1,0:T(8,128)(2,1)S(1)} %pad_maximum_fusion.11), channel_id=1, source_target_pairs={{1,2},{2,1},{5,6},{6,5},{9,10},{10,9},{13,14},{14,13},{17,18},{18,... | collective-permute-start | bytes 1179656 | tf_op jit(solution)/shard_map/ppermute | solution.py:146
  64.6 10.6 %collective-permute-start.14 = (bf16[3,64,1024]{2,1,0:T(8,128)(2,1)S(1)}, bf16[3,64,1024]{2,1,0:T(8,128)(2,1)S(1)}, u32[]{:S(2)}, u32[]{:S(2)}) collective-permute-start(bf16[3,64,1024]{2,1,0:T(8,128)(2,1)S(1)} %add_convert_fusion.3), channel_id=1, source_target_pairs={{1,2},{2,1},{5,6},{6,5},{9,10},{10,9},{13,14},{14,13},{17,18},{18,... | collective-permute-start | bytes 1179656 | tf_op jit(solution)/shard_map/ppermute | solution.py:146
  65.4 14.8 %collective-permute-start.12 = (bf16[3,64,1024]{2,1,0:T(8,128)(2,1)S(1)}, bf16[3,64,1024]{2,1,0:T(8,128)(2,1)S(1)}, u32[]{:S(2)}, u32[]{:S(2)}) collective-permute-start(bf16[3,64,1024]{2,1,0:T(8,128)(2,1)S(1)} %pad_maximum_fusion.12), channel_id=1, source_target_pairs={{0,1},{3,2},{4,5},{7,6},{8,9},{11,10},{12,13},{15,14},{16,17},{19,... | collective-permute-start | bytes 1179656 | tf_op jit(solution)/shard_map/ppermute | solution.py:129
  72.9 48.3 %collective-permute-start.11 = (bf16[3,128,1024]{2,1,0:T(8,128)(2,1)S(1)}, bf16[3,128,1024]{2,1,0:T(8,128)(2,1)S(1)}, u32[]{:S(2)}, u32[]{:S(2)}) collective-permute-start(bf16[3,128,1024]{2,1,0:T(8,128)(2,1)S(1)} %pad_maximum_fusion.1), channel_id=1, source_target_pairs={{1,0},{2,3},{5,4},{6,7},{9,8},{10,11},{13,12},{14,15},{17,16},{18,... | collective-permute-start | bytes 2359304 | tf_op jit(solution)/shard_map/ppermute | solution.py:137
  80.6 17.1 %collective-permute-start.15 = (bf16[3,64,1024]{2,1,0:T(8,128)(2,1)S(1)}, bf16[3,64,1024]{2,1,0:T(8,128)(2,1)S(1)}, u32[]{:S(2)}, u32[]{:S(2)}) collective-permute-start(bf16[3,64,1024]{2,1,0:T(8,128)(2,1)S(1)} %pad_maximum_fusion.14), channel_id=1, source_target_pairs={{1,2},{2,1},{5,6},{6,5},{9,10},{10,9},{13,14},{14,13},{17,18},{18,... | collective-permute-start | bytes 1179656 | tf_op jit(solution)/shard_map/ppermute | solution.py:146
  81.4 15.5 %collective-permute-start.26 = (bf16[3,64,1024]{2,1,0:T(8,128)(2,1)S(1)}, bf16[3,64,1024]{2,1,0:T(8,128)(2,1)S(1)}, u32[]{:S(2)}, u32[]{:S(2)}) collective-permute-start(bf16[3,64,1024]{2,1,0:T(8,128)(2,1)S(1)} %pad_maximum_fusion.17), channel_id=1, source_target_pairs={{0,1},{3,2},{4,5},{7,6},{8,9},{11,10},{12,13},{15,14},{16,17},{19,... | collective-permute-start | bytes 1179656 | tf_op jit(solution)/shard_map/ppermute | solution.py:129
  88.4 19.3 %collective-permute-start.25 = (bf16[3,64,1024]{2,1,0:T(8,128)(2,1)S(1)}, bf16[3,64,1024]{2,1,0:T(8,128)(2,1)S(1)}, u32[]{:S(2)}, u32[]{:S(2)}) collective-permute-start(bf16[3,64,1024]{2,1,0:T(8,128)(2,1)S(1)} %pad_maximum_fusion.16), channel_id=1, source_target_pairs={{0,1},{3,2},{4,5},{7,6},{8,9},{11,10},{12,13},{15,14},{16,17},{19,... | collective-permute-start | bytes 1179656 | tf_op jit(solution)/shard_map/ppermute | solution.py:129
  97.0 10.8 %collective-permute-start.27 = (bf16[3,64,1024]{2,1,0:T(8,128)(2,1)S(1)}, bf16[3,64,1024]{2,1,0:T(8,128)(2,1)S(1)}, u32[]{:S(2)}, u32[]{:S(2)}) collective-permute-start(bf16[3,64,1024]{2,1,0:T(8,128)(2,1)S(1)} %add_convert_fusion.2), channel_id=1, source_target_pairs={{1,2},{2,1},{5,6},{6,5},{9,10},{10,9},{13,14},{14,13},{17,18},{18,... | collective-permute-start | bytes 1179656 | tf_op jit(solution)/shard_map/ppermute | solution.py:146
  98.9 29.2 %collective-permute-start.16 = (bf16[3,128,1024]{2,1,0:T(8,128)(2,1)S(1)}, bf16[3,128,1024]{2,1,0:T(8,128)(2,1)S(1)}, u32[]{:S(2)}, u32[]{:S(2)}) collective-permute-start(bf16[3,128,1024]{2,1,0:T(8,128)(2,1)S(1)} %pad_maximum_fusion.3), channel_id=1, source_target_pairs={{1,0},{2,3},{5,4},{6,7},{9,8},{10,11},{13,12},{14,15},{17,16},{18,... | collective-permute-start | bytes 2359304 | tf_op jit(solution)/shard_map/ppermute | solution.py:137
  100.2 12.7 %collective-permute-start.31 = (bf16[3,64,1024]{2,1,0:T(8,128)(2,1)S(1)}, bf16[3,64,1024]{2,1,0:T(8,128)(2,1)S(1)}, u32[]{:S(2)}, u32[]{:S(2)}) collective-permute-start(bf16[3,64,1024]{2,1,0:T(8,128)(2,1)S(1)} %pad_maximum_fusion.20), channel_id=1, source_target_pairs={{0,1},{3,2},{4,5},{7,6},{8,9},{11,10},{12,13},{15,14},{16,17},{19,... | collective-permute-start | bytes 1179656 | tf_op jit(solution)/shard_map/ppermute | solution.py:129
  108.2 14.7 %collective-permute-start.28 = (bf16[3,64,1024]{2,1,0:T(8,128)(2,1)S(1)}, bf16[3,64,1024]{2,1,0:T(8,128)(2,1)S(1)}, u32[]{:S(2)}, u32[]{:S(2)}) collective-permute-start(bf16[3,64,1024]{2,1,0:T(8,128)(2,1)S(1)} %pad_maximum_fusion.18), channel_id=1, source_target_pairs={{1,2},{2,1},{5,6},{6,5},{9,10},{10,9},{13,14},{14,13},{17,18},{18,... | collective-permute-start | bytes 1179656 | tf_op jit(solution)/shard_map/ppermute | solution.py:146
  113.0 10.6 %collective-permute-start.32 = (bf16[3,64,1024]{2,1,0:T(8,128)(2,1)S(1)}, bf16[3,64,1024]{2,1,0:T(8,128)(2,1)S(1)}, u32[]{:S(2)}, u32[]{:S(2)}) collective-permute-start(bf16[3,64,1024]{2,1,0:T(8,128)(2,1)S(1)} %add_convert_fusion.1), channel_id=1, source_target_pairs={{1,2},{2,1},{5,6},{6,5},{9,10},{10,9},{13,14},{14,13},{17,18},{18,... | collective-permute-start | bytes 1179656 | tf_op jit(solution)/shard_map/ppermute | solution.py:146
  114.8 11.3 %collective-permute-start.30 = (bf16[3,64,1024]{2,1,0:T(8,128)(2,1)S(1)}, bf16[3,64,1024]{2,1,0:T(8,128)(2,1)S(1)}, u32[]{:S(2)}, u32[]{:S(2)}) collective-permute-start(bf16[3,64,1024]{2,1,0:T(8,128)(2,1)S(1)} %pad_maximum_fusion.19), channel_id=1, source_target_pairs={{0,1},{3,2},{4,5},{7,6},{8,9},{11,10},{12,13},{15,14},{16,17},{19,... | collective-permute-start | bytes 1179656 | tf_op jit(solution)/shard_map/ppermute | solution.py:129
  129.3 21.9 %collective-permute-start.29 = (bf16[3,128,1024]{2,1,0:T(8,128)(2,1)S(1)}, bf16[3,128,1024]{2,1,0:T(8,128)(2,1)S(1)}, u32[]{:S(2)}, u32[]{:S(2)}) collective-permute-start(bf16[3,128,1024]{2,1,0:T(8,128)(2,1)S(1)} %pad_maximum_fusion.5), channel_id=1, source_target_pairs={{1,0},{2,3},{5,4},{6,7},{9,8},{10,11},{13,12},{14,15},{17,16},{18,... | collective-permute-start | bytes 2359304 | tf_op jit(solution)/shard_map/ppermute | solution.py:137
  130.6 10.2 %collective-permute-start.33 = (bf16[3,64,1024]{2,1,0:T(8,128)(2,1)S(1)}, bf16[3,64,1024]{2,1,0:T(8,128)(2,1)S(1)}, u32[]{:S(2)}, u32[]{:S(2)}) collective-permute-start(bf16[3,64,1024]{2,1,0:T(8,128)(2,1)S(1)} %pad_maximum_fusion.21), channel_id=1, source_target_pairs={{1,2},{2,1},{5,6},{6,5},{9,10},{10,9},{13,14},{14,13},{17,18},{18,... | collective-permute-start | bytes 1179656 | tf_op jit(solution)/shard_map/ppermute | solution.py:146
  131.4 12.8 %collective-permute-start.35 = (bf16[3,64,1024]{2,1,0:T(8,128)(2,1)S(1)}, bf16[3,64,1024]{2,1,0:T(8,128)(2,1)S(1)}, u32[]{:S(2)}, u32[]{:S(2)}) collective-permute-start(bf16[3,64,1024]{2,1,0:T(8,128)(2,1)S(1)} %pad_maximum_fusion.23), channel_id=1, source_target_pairs={{0,1},{3,2},{4,5},{7,6},{8,9},{11,10},{12,13},{15,14},{16,17},{19,... | collective-permute-start | bytes 1179656 | tf_op jit(solution)/shard_map/ppermute | solution.py:129
  139.0 9.4 %collective-permute-start.34 = (bf16[3,64,1024]{2,1,0:T(8,128)(2,1)S(1)}, bf16[3,64,1024]{2,1,0:T(8,128)(2,1)S(1)}, u32[]{:S(2)}, u32[]{:S(2)}) collective-permute-start(bf16[3,64,1024]{2,1,0:T(8,128)(2,1)S(1)} %pad_maximum_fusion.22), channel_id=1, source_target_pairs={{0,1},{3,2},{4,5},{7,6},{8,9},{11,10},{12,13},{15,14},{16,17},{19,... | collective-permute-start | bytes 1179656 | tf_op jit(solution)/shard_map/ppermute | solution.py:129
  140.9 24.8 %collective-permute-start.44 = (bf16[3,128,1024]{2,1,0:T(8,128)(2,1)S(1)}, bf16[3,128,1024]{2,1,0:T(8,128)(2,1)S(1)}, u32[]{:S(2)}, u32[]{:S(2)}) collective-permute-start(bf16[3,128,1024]{2,1,0:T(8,128)(2,1)S(1)} %pad_maximum_fusion.7), channel_id=1, source_target_pairs={{1,0},{2,3},{5,4},{6,7},{9,8},{10,11},{13,12},{14,15},{17,16},{18,... | collective-permute-start | bytes 2359304 | tf_op jit(solution)/shard_map/ppermute | solution.py:137
  149.6 30.6 %collective-permute-start.46 = (bf16[3,64,1024]{2,1,0:T(8,128)(2,1)S(1)}, bf16[3,64,1024]{2,1,0:T(8,128)(2,1)S(1)}, u32[]{:S(2)}, u32[]{:S(2)}) collective-permute-start(bf16[3,64,1024]{2,1,0:T(8,128)(2,1)S(1)} %pad_maximum_fusion.24), channel_id=1, source_target_pairs={{1,0},{2,3},{5,4},{6,7},{9,8},{10,11},{13,12},{14,15},{17,16},{18,... | collective-permute-start | bytes 1179656 | tf_op jit(solution)/shard_map/ppermute | solution.py:137
  167.8 12.2 %collective-permute-start.45 = (bf16[3,64,1024]{2,1,0:T(8,128)(2,1)S(1)}, bf16[3,64,1024]{2,1,0:T(8,128)(2,1)S(1)}, u32[]{:S(2)}, u32[]{:S(2)}) collective-permute-start(bf16[3,64,1024]{2,1,0:T(8,128)(2,1)S(1)} %collective-permute-done.37), channel_id=1, source_target_pairs={{1,0},{2,3},{5,4},{6,7},{9,8},{10,11},{13,12},{14,15},{17,16},{18,... | collective-permute-start | bytes 1179656 | tf_op jit(solution)/shard_map/ppermute | solution.py:137
  169.4 13.3 %collective-permute-start.38 = (bf16[2,3,64,512]{3,2,0,1:T(8,128)(2,1)S(1)}, bf16[2,3,64,512]{3,2,0,1:T(8,128)(2,1)S(1)}, u32[]{:S(2)}, u32[]{:S(2)}) collective-permute-start(bf16[2,3,64,512]{3,2,0,1:T(8,128)(2,1)S(1)} %maximum_select_fusion.6), channel_id=1, source_target_pairs={{0,4},{4,0},{8,12},{12,8},{16,20},{20,16},{24,28},{28,24},{1,5},{5... | collective-permute-start | bytes 1179656 | tf_op jit(solution)/shard_map/ppermute | solution.py:55
  185.0 7.9 %collective-permute-start.40 = (bf16[2,3,16,512]{3,2,1,0:T(8,128)(2,1)S(1)}, bf16[2,3,16,512]{3,2,1,0:T(8,128)(2,1)S(1)}, u32[]{:S(2)}, u32[]{:S(2)}) collective-permute-start(bf16[2,3,16,512]{3,2,1,0:T(8,128)(2,1)S(1)} %get-tuple-element.38), channel_id=1, source_target_pairs={{0,16},{4,20},{8,24},{12,28},{16,0},{20,4},{24,8},{28,12},{1,17},{... | collective-permute-start | bytes 294920 | tf_op jit(solution)/shard_map/ppermute | solution.py:55
  199.3 10.6 %collective-permute-start.43 = (bf16[2,48,512]{2,1,0:T(8,128)(2,1)S(1)}, bf16[2,48,512]{2,1,0:T(8,128)(2,1)S(1)}, u32[]{:S(2)}, u32[]{:S(2)}) collective-permute-start(bf16[2,48,512]{2,1,0:T(8,128)(2,1)S(1)} %fusion.72), channel_id=1, source_target_pairs={{0,2},{1,3},{2,0},{3,1},{4,6},{5,7},{6,4},{7,5},{8,10},{9,11},{10,... | collective-permute-start | bytes 294920 | tf_op jit(solution)/shard_map/ppermute | solution.py:55
  (30 other events, 230.9 us)

commit v7 on v5

--- a/solution.py
+++ b/solution.py
@@ -10,6 +10,7 @@
 BF16 = jnp.bfloat16
 F32 = jnp.float32
 STEP = 16
+LAG = 3
 
 
 def sylvester(order):
@@ -41,13 +42,15 @@
     groups = lax.axis_size("tensor")
     signs = sylvester(groups)
     me = np.arange(groups)
-    columns = [me >= groups // 2, np.minimum(me, groups - 1 - me)]
+    away = np.minimum(me, groups - 1 - me)
+    columns = [me >= groups // 2, away]
     columns += [signs[me, me ^ apart] for apart in range(groups)]
     columns += [1 - 2 * (me >> bit & 1) for bit in range(groups.bit_length() - 1)]
+    columns += [away, away]
     table = np.stack(columns, axis=1).astype(np.float32)[:, :, None, None]
-    table = jnp.asarray(np.broadcast_to(table, table.shape[:3] + (length,)))
+    table = jnp.asarray(np.tile(table, (1, 1, 1, length)))
     row = lax.dynamic_index_in_dim(table, lax.axis_index("tensor"), keepdims=False)
-    return row[0], row[1], row[2 : 2 + groups], row[2 + groups :]
+    return row[0], row[1], row[2 : 2 + groups], row[2 + groups : -2], row[-2:]
 
 
 def exchange(block, axis, apart):
@@ -124,18 +127,32 @@
 
 
 def inward(own):
-    came, total = own, own.astype(F32)
-    for step in fold_steps():
-        came = lax.ppermute(total.astype(BF16), "tensor", line_pairs(step))
-        total = total + came.astype(F32)
-    return total, came
+    total = own
+    for step in fold_steps()[:-1]:
+        came = lax.ppermute(total, "tensor", line_pairs(step))
+        total = (total.astype(F32) + came.astype(F32)).astype(BF16)
+    return total
 
 
 def outward(block, depth):
-    for step in reversed(fold_steps()):
+    for step in reversed(fold_steps()[:-1]):
         came = lax.ppermute(block, "tensor", [(b, a) for a, b in line_pairs(step)])
         block = jnp.where(depth[:, : block.shape[-1]] == step, came, block)
     return block
+
+
+def swap(into, out, depth):
+    if not fold_steps():
+        return jnp.zeros_like(into if out is None else out)
+    inner = len(fold_steps()) - 1
+    pairs = line_pairs(inner)
+    back = [(b, a) for a, b in pairs]
+    if out is None:
+        return lax.ppermute(into, "tensor", pairs)
+    if into is None:
+        return lax.ppermute(out, "tensor", back)
+    block = jnp.where(depth[:, : out.shape[-1]] > inner, out, into)
+    return lax.ppermute(block, "tensor", pairs + back)
 
 
 def across(block):
@@ -161,7 +178,7 @@
     step = STEP if mine % STEP == 0 else mine
     chunks = mine // step
     half = peers * step // 2
-    far, depth, signs, bits = my_row(max(width, gate_weight.shape[1]))
+    far, depth, signs, bits, depths = my_row(max(width, gate_weight.shape[1]))
     far = far[:, :width] > 0.5
 
     both = jnp.stack([tokens, out_grad])
@@ -176,57 +193,68 @@
     late = spread(after(both[:, first * step :], early[1])) if chunks > first else None
     groups = [arrive(rotate(early, signs).astype(BF16))]
 
-    done, arrived, crossed = [], [], []
-    for i in range(chunks):
-        group, place = (groups[0], i) if i < first else (groups[1], i - first)
+    def leave(blocks):
         sums = []
-        for which, (x, g) in enumerate([(part[0, place], part[1, place]) for part in group]):
-            ahead = arrived[max(2 * i - 4 + which, 0)] if i > 0 else message if arrived else None
-            if ahead is not None:
-                x, g = after(x, ahead), after(g, ahead)
+        for block in blocks:
+            mixed = dot(block[0], down_weight, 1, 0)
+            grads = dot(block[1], gate_weight, 1, 1) + dot(block[2], up_weight, 1, 1)
+            sums.append(jnp.stack([mixed, grads]))
+        sums = jnp.concatenate(sums, axis=1).reshape(2, -1, 2, half, width)
+        low = jnp.where(far, sums[:, :, 0], sums[:, :, 1])
+        return low, jnp.where(far, sums[:, :, 1], sums[:, :, 0]).astype(BF16)
+
+    def done(i):
+        parts = []
+        for k in (2 * i + 1, 2 * i):
+            inner = depth[:, : outs[k].shape[-1]] > len(fold_steps()) - 1
+            parts.append(outward(jnp.where(inner, outs[k], came[k + LAG]), depth))
+        return jnp.concatenate(parts, axis=1)
+
+    steps = 2 * chunks
+    split, ends = max(chunks - 2, 0), []
+    messages, came, crossed, acts, outs = [], [], [], [], []
+    for s in range(steps + LAG):
+        if s < steps:
+            i, which = divmod(s, 2)
+            group, place = (groups[0], i) if i < first else (groups[1], i - first)
+            x, g = group[which][0, place], group[which][1, place]
+            if s > 0:
+                other = came[s - 2] if s > 1 else messages[0][2:]
+                x, g = after(x, other), after(g, other)
             parts = [dot(x, gate_weight, 1, 0), dot(x, up_weight, 1, 0), dot(g, down_weight, 1, 1)]
-            block = jnp.stack(parts).astype(BF16)
-            block = after(block, arrived[max(len(arrived) - 2, 0)]) if arrived else block
-            message = message if arrived else block[2:]
-            total, came = inward(block)
-            arrived.append(came)
-            sums.append(total)
-            if len(groups) == 1 and chunks > first:
-                late[0] = after(late[0], came)
-                groups.append(arrive(rotate(late, signs).astype(BF16)))
-        other, own = sums
-        sums = own + across(other.astype(BF16)).astype(F32)
-        own = activations(sums[0], sums[1], sums[2])
-        crossed.append(across(own))
-        if i < chunks - 1:
-            done.append([outward(crossed[i], depth), outward(own, depth)])
-
-    def leave(blocks):
-        lows, highs = [], []
-        for halves in blocks:
-            sums = []
-            for acts in halves:
-                mixed = dot(acts[0], down_weight, 1, 0)
-                grads = dot(acts[1], gate_weight, 1, 1) + dot(acts[2], up_weight, 1, 1)
-                sums.append(jnp.stack([mixed, grads]))
-            lows.append(jnp.where(far, sums[0], sums[1]))
-            highs.append(jnp.where(far, sums[1], sums[0]).astype(BF16))
-        return jnp.stack(lows, axis=1), jnp.stack(highs, axis=1)
-
-    split, ends = max(chunks - 2, 0), []
-    if split > 0:
-        sums, came, last = scatter_dp(*leave(done[:split]))
-        ends.append(rotate_by_halves(sums.reshape(2, -1, width), bits))
-        crossed[-1] = after(crossed[-1], came)
-    done.append([outward(crossed[-1], depth), outward(own, depth)])
-    low, high = leave(done[split:])
-    if split > 0:
-        high = after(high, last)
+            message = jnp.stack(parts).astype(BF16)
+            messages.append(inward(after(message, came[0]) if s == 1 else message))
+        if s == steps + LAG - 1 and split > 0:
+            low, high = leave([done(i) for i in range(split)])
+            sums, _, last = scatter_dp(low, high)
+            ends.append(rotate_by_halves(sums.reshape(2, -1, width), bits))
+            outs[-1] = after(outs[-1], last)
+        came.append(
+            swap(
+                messages[s] if s < steps else None,
+                outs[s - LAG] if s >= LAG else None,
+                depths[s % 2],
+            )
+        )
+        if s == 0 and chunks > first:
+            tick = exchange(message[2, :step, :width], "dp", 1)
+            late[0] = after(late[0], tick)
+            groups.append(arrive(rotate(late, signs).astype(BF16)))
+        if s < steps:
+            total = messages[s].astype(F32) + came[s].astype(F32)
+            if which == 0:
+                other_sums = across(total.astype(BF16))
+            else:
+                gate, up, grad_hidden = total + other_sums.astype(F32)
+                acts.append(activations(gate, up, grad_hidden))
+                crossed.append(across(acts[i]))
+                outs += [acts[i], crossed[i]]
+    low, high = leave([done(i) for i in range(split, chunks)])
     sums, _, _ = scatter_dp(low, high)
     ends.append(rotate(spread(sums.reshape(2, -1, width).astype(BF16)), signs))
     ends = jnp.concatenate(ends, axis=1)
 
-    acts = jnp.concatenate([half for halves in done for half in halves], axis=1)
+    acts = jnp.concatenate([done(i) for i in range(chunks)], axis=1)
     rows = [jnp.stack(group, axis=2).reshape(2, -1, width) for group in groups]
     rows = after(jnp.concatenate(rows, axis=1), high[0, 0, :1])
     factor = 1.0 / math.sqrt(rows.shape[1])

time: 229 us -> 193 us (0.84)
  waiting for transfers between devices: 79.9 us -> 59.9 us
  other arithmetic: 18.6 us -> 10.1 us
  matrix products: 32.6 us -> 26.7 us
    ppermute x20 -> x13, waiting for transfers between devices: 55.5 us -> 32.9 us  [the longest x3 13.3 us: swap(): return lax.ppermute(out, 'tensor', back)]
    mul x4, other arithmetic: 8.59 us -> 1.05 us  [turn(): rows = block.reshape(-1, width) * (1.0 / math.sqrt(D))]
    dot_general x71 -> x56, matrix products: 32.6 us -> 26.7 us  [dot(): lax.dot_general(left, right, (((left_dim,), (right_dim,)), ((), ())), pre...]
    ppermute x27 -> x28, waiting for transfers between devices: 24.3 us -> 26.9 us  [exchange(): return lax.ppermute(block, axis, [(i, i ^ apart) for i in range(count)])]
    ppermute x27 -> x28, starting transfers between devices: 31.2 us -> 32 us  [exchange(): return lax.ppermute(block, axis, [(i, i ^ apart) for i in range(count)])]
    ppermute x20 -> x13, starting transfers between devices: 53.4 us -> 53.8 us  [the longest x7 42.1 us: swap(): return lax.ppermute(block, 'tensor', pairs + back)]
  transfers between devices with their start and end apart: 57 -> 51, of which waited for: 19 -> 24; matrix products, arithmetic and copies ran while one was open for 16% -> 16% of each run, Pallas kernels for 0% -> 0%
where the time goes in v7:
time: 193 us
  starting transfers between devices  92.9 us (48%)
  waiting for transfers between devices  59.9 us (31%)
  matrix products  26.7 us (14%)
  other arithmetic  10.1 us (5%)
    ppermute x7, starting transfers between devices, swap(): return lax.ppermute(block, 'tensor', pairs + back)  42.1 us
    ppermute x28, starting transfers between devices, exchange(): return lax.ppermute(block, axis, [(i, i ^ apart) for i in range(count)])  32 us
    ppermute x28, waiting for transfers between devices, exchange(): return lax.ppermute(block, axis, [(i, i ^ apart) for i in range(count)])  26.9 us
    dot_general x56, matrix products, dot(): lax.dot_general(left, right, (((left_dim,), (right_dim,)), ((), ())), pre...  26.7 us
    ppermute x3, waiting for transfers between devices, swap(): return lax.ppermute(out, 'tensor', back)  13.3 us
    ppermute x7, waiting for transfers between devices, swap(): return lax.ppermute(block, 'tensor', pairs + back)  13.2 us
    ppermute x3, starting transfers between devices, swap(): return lax.ppermute(into, 'tensor', pairs)  7.65 us
    ppermute x10, starting transfers between devices, across(): return lax.ppermute(block, 'tensor', [(half - 1, half), (half, half - 1)])  7.04 us
  transfers between devices with their start and end apart: 51, of which 24 were waited for; matrix products, arithmetic and copies ran while one was open for 16% of the time, Pallas kernels for 0%

profile of v7, /device:TPU:0, one launch (start us, length us, event | category | flops | bytes accessed | tf_op | source)
XLA Modules:
  0.0 192.6 jit_solution(756902263226962782)
XLA Ops:
  1.5 5.0 %collective-permute-start.2 = (bf16[2,32,512]{2,1,0:T(8,128)(2,1)S(1)}, bf16[2,32,512]{2,1,0:T(8,128)(2,1)S(1)}, u32[]{:S(2)}, u32[]{:S(2)}) collective-permute-start(bf16[2,32,512]{2,1,0:T(8,128)(2,1)S(1)} %pad_maximum_fusion.25), channel_id=1, source_target_pairs={{0,3},{1,2},{2,1},{3,0},{4,7},{5,6},{6,5},{7,4},{8,11},{9,10},{10,... | collective-permute-start | bytes 196616 | tf_op jit(solution)/shard_map/ppermute | solution.py:58
  9.2 3.0 %collective-permute-done.1 = bf16[2,32,512]{2,1,0:T(8,128)(2,1)S(1)} collective-permute-done((bf16[2,32,512]{2,1,0:T(8,128)(2,1)S(1)}, bf16[2,32,512]{2,1,0:T(8,128)(2,1)S(1)}, u32[]{:S(2)}, u32[]{:S(2)}) %collective-permute-start.1) | collective-permute-done | bytes 65568 | tf_op jit(solution)/shard_map/ppermute | solution.py:58
  15.6 2.5 %collective-permute-start.5 = (bf16[2,2,1,16,512]{4,3,2,1,0:T(8,128)(2,1)S(1)}, bf16[2,2,1,16,512]{4,3,2,1,0:T(8,128)(2,1)S(1)}, u32[]{:S(2)}, u32[]{:S(2)}) collective-permute-start(bf16[2,2,1,16,512]{4,3,2,1,0:T(8,128)(2,1)S(1)} %bitcast.527), channel_id=1, source_target_pairs={{0,24},{4,28},{8,16},{12,20},{16,8},{20,12},{24,0},{28,4},{1,25},{... | collective-permute-start | bytes 196616 | tf_op jit(solution)/shard_map/ppermute | solution.py:58
  23.1 2.8 %collective-permute-start.15 = (bf16[2,48,512]{2,1,0:T(8,128)(2,1)S(1)}, bf16[2,48,512]{2,1,0:T(8,128)(2,1)S(1)}, u32[]{:S(2)}, u32[]{:S(2)}) collective-permute-start(bf16[2,48,512]{2,1,0:T(8,128)(2,1)S(1)} %fusion.107), channel_id=1, source_target_pairs={{0,3},{1,2},{2,1},{3,0},{4,7},{5,6},{6,5},{7,4},{8,11},{9,10},{10,... | collective-permute-start | bytes 294920 | tf_op jit(solution)/shard_map/ppermute | solution.py:58
  29.5 2.4 %collective-permute-start.7 = (bf16[3,64,1024]{2,1,0:T(8,128)(2,1)S(1)}, bf16[3,64,1024]{2,1,0:T(8,128)(2,1)S(1)}, u32[]{:S(2)}, u32[]{:S(2)}) collective-permute-start(bf16[3,64,1024]{2,1,0:T(8,128)(2,1)S(1)} %pad_maximum_fusion.2), channel_id=1, source_target_pairs={{0,1},{3,2},{4,5},{7,6},{8,9},{11,10},{12,13},{15,14},{16,17},{19,... | collective-permute-start | bytes 1179656 | tf_op jit(solution)/shard_map/ppermute | solution.py:151
  33.2 1.9 %collective-permute-done.14 = bf16[2,48,512]{2,1,0:T(8,128)(2,1)S(1)} collective-permute-done((bf16[2,48,512]{2,1,0:T(8,128)(2,1)S(1)}, bf16[2,48,512]{2,1,0:T(8,128)(2,1)S(1)}, u32[]{:S(2)}, u32[]{:S(2)}) %collective-permute-start.14) | collective-permute-done | bytes 98336 | tf_op jit(solution)/shard_map/ppermute | solution.py:58
  39.6 2.5 %collective-permute-done.18 = bf16[2,3,1,16,512]{4,3,2,1,0:T(8,128)(2,1)S(1)} collective-permute-done((bf16[2,3,1,16,512]{4,3,2,1,0:T(8,128)(2,1)S(1)}, bf16[2,3,1,16,512]{4,3,2,1,0:T(8,128)(2,1)S(1)}, u32[]{:S(2)}, u32[]{:S(2)}) %collective-permute-start.18) | collective-permute-done | bytes 98336 | tf_op jit(solution)/shard_map/ppermute | solution.py:58
  44.1 2.2 %collective-permute-start.8 = (bf16[3,64,1024]{2,1,0:T(8,128)(2,1)S(1)}, bf16[3,64,1024]{2,1,0:T(8,128)(2,1)S(1)}, u32[]{:S(2)}, u32[]{:S(2)}) collective-permute-start(bf16[3,64,1024]{2,1,0:T(8,128)(2,1)S(1)} %maximum_select_fusion.1), channel_id=1, source_target_pairs={{0,1},{3,2},{4,5},{7,6},{8,9},{11,10},{12,13},{15,14},{16,17},{19,... | collective-permute-start | bytes 1179656 | tf_op jit(solution)/shard_map/ppermute | solution.py:151
  47.7 3.1 %collective-permute-start.11 = (bf16[3,64,1024]{2,1,0:T(8,128)(2,1)S(1)}, bf16[3,64,1024]{2,1,0:T(8,128)(2,1)S(1)}, u32[]{:S(2)}, u32[]{:S(2)}) collective-permute-start(bf16[3,64,1024]{2,1,0:T(8,128)(2,1)S(1)} %pad_maximum_fusion.4), channel_id=1, source_target_pairs={{0,1},{3,2},{4,5},{7,6},{8,9},{11,10},{12,13},{15,14},{16,17},{19,... | collective-permute-start | bytes 1179656 | tf_op jit(solution)/shard_map/ppermute | solution.py:151
  51.0 4.6 %collective-permute-done.8 = bf16[3,64,1024]{2,1,0:T(8,128)(2,1)S(1)} collective-permute-done((bf16[3,64,1024]{2,1,0:T(8,128)(2,1)S(1)}, bf16[3,64,1024]{2,1,0:T(8,128)(2,1)S(1)}, u32[]{:S(2)}, u32[]{:S(2)}) %collective-permute-start.8) | collective-permute-done | bytes 393248 | tf_op jit(solution)/shard_map/ppermute | solution.py:151
  57.9 4.4 %collective-permute-start.21 = (bf16[3,64,1024]{2,1,0:T(8,128)(2,1)S(1)}, bf16[3,64,1024]{2,1,0:T(8,128)(2,1)S(1)}, u32[]{:S(2)}, u32[]{:S(2)}) collective-permute-start(bf16[3,64,1024]{2,1,0:T(8,128)(2,1)S(1)} %get-tuple-element.56), channel_id=1, source_target_pairs={{0,1},{3,2},{1,0},{2,3},{4,5},{7,6},{5,4},{6,7},{8,9},{11,10},{9,8... | collective-permute-start | bytes 1179656 | tf_op jit(solution)/shard_map/ppermute | solution.py:155
  62.3 1.8 collective-permute-done.11
  66.1 7.8 %collective-permute-start.20 = (bf16[3,64,1024]{2,1,0:T(8,128)(2,1)S(1)}, bf16[3,64,1024]{2,1,0:T(8,128)(2,1)S(1)}, u32[]{:S(2)}, u32[]{:S(2)}) collective-permute-start(bf16[3,64,1024]{2,1,0:T(8,128)(2,1)S(1)} %broadcast_select_fusion.9), channel_id=1, source_target_pairs={{0,1},{3,2},{1,0},{2,3},{4,5},{7,6},{5,4},{6,7},{8,9},{11,10},{9,8... | collective-permute-start | bytes 1179656 | tf_op jit(solution)/shard_map/ppermute | solution.py:155
  76.1 7.9 %collective-permute-start.25 = (bf16[3,64,1024]{2,1,0:T(8,128)(2,1)S(1)}, bf16[3,64,1024]{2,1,0:T(8,128)(2,1)S(1)}, u32[]{:S(2)}, u32[]{:S(2)}) collective-permute-start(bf16[3,64,1024]{2,1,0:T(8,128)(2,1)S(1)} %get-tuple-element.54), channel_id=1, source_target_pairs={{0,1},{3,2},{1,0},{2,3},{4,5},{7,6},{5,4},{6,7},{8,9},{11,10},{9,8... | collective-permute-start | bytes 1179656 | tf_op jit(solution)/shard_map/ppermute | solution.py:155
  84.8 7.0 %collective-permute-done.25 = bf16[3,64,1024]{2,1,0:T(8,128)(2,1)S(1)} collective-permute-done((bf16[3,64,1024]{2,1,0:T(8,128)(2,1)S(1)}, bf16[3,64,1024]{2,1,0:T(8,128)(2,1)S(1)}, u32[]{:S(2)}, u32[]{:S(2)}) %collective-permute-start.25) | collective-permute-done | bytes 393248 | tf_op jit(solution)/shard_map/ppermute | solution.py:155
  92.9 1.8 collective-permute-start.24
  97.8 4.1 %collective-permute-done.24 = bf16[3,64,1024]{2,1,0:T(8,128)(2,1)S(1)} collective-permute-done((bf16[3,64,1024]{2,1,0:T(8,128)(2,1)S(1)}, bf16[3,64,1024]{2,1,0:T(8,128)(2,1)S(1)}, u32[]{:S(2)}, u32[]{:S(2)}) %collective-permute-start.24) | collective-permute-done | bytes 393248 | tf_op jit(solution)/shard_map/ppermute | solution.py:155
  105.0 5.5 %collective-permute-start.29 = (bf16[3,64,1024]{2,1,0:T(8,128)(2,1)S(1)}, bf16[3,64,1024]{2,1,0:T(8,128)(2,1)S(1)}, u32[]{:S(2)}, u32[]{:S(2)}) collective-permute-start(bf16[3,64,1024]{2,1,0:T(8,128)(2,1)S(1)} %get-tuple-element.52), channel_id=1, source_target_pairs={{0,1},{3,2},{1,0},{2,3},{4,5},{7,6},{5,4},{6,7},{8,9},{11,10},{9,8... | collective-permute-start | bytes 1179656 | tf_op jit(solution)/shard_map/ppermute | solution.py:155
  112.2 8.9 %collective-permute-start.28 = (bf16[3,64,1024]{2,1,0:T(8,128)(2,1)S(1)}, bf16[3,64,1024]{2,1,0:T(8,128)(2,1)S(1)}, u32[]{:S(2)}, u32[]{:S(2)}) collective-permute-start(bf16[3,64,1024]{2,1,0:T(8,128)(2,1)S(1)} %broadcast_select_fusion.7), channel_id=1, source_target_pairs={{0,1},{3,2},{1,0},{2,3},{4,5},{7,6},{5,4},{6,7},{8,9},{11,10},{9,8... | collective-permute-start | bytes 1179656 | tf_op jit(solution)/shard_map/ppermute | solution.py:155
  123.4 5.7 %collective-permute-start.39 = (bf16[3,64,1024]{2,1,0:T(8,128)(2,1)S(1)}, bf16[3,64,1024]{2,1,0:T(8,128)(2,1)S(1)}, u32[]{:S(2)}, u32[]{:S(2)}) collective-permute-start(bf16[3,64,1024]{2,1,0:T(8,128)(2,1)S(1)} %get-tuple-element.47), channel_id=1, source_target_pairs={{0,1},{3,2},{1,0},{2,3},{4,5},{7,6},{5,4},{6,7},{8,9},{11,10},{9,8... | collective-permute-start | bytes 1179656 | tf_op jit(solution)/shard_map/ppermute | solution.py:155
  133.2 2.1 %collective-permute-done.39 = bf16[3,64,1024]{2,1,0:T(8,128)(2,1)S(1)} collective-permute-done((bf16[3,64,1024]{2,1,0:T(8,128)(2,1)S(1)}, bf16[3,64,1024]{2,1,0:T(8,128)(2,1)S(1)}, u32[]{:S(2)}, u32[]{:S(2)}) %collective-permute-start.39) | collective-permute-done | bytes 393248 | tf_op jit(solution)/shard_map/ppermute | solution.py:155
  138.0 2.4 %collective-permute-start.33 = (bf16[2,3,16,512]{3,2,1,0:T(8,128)(2,1)S(1)}, bf16[2,3,16,512]{3,2,1,0:T(8,128)(2,1)S(1)}, u32[]{:S(2)}, u32[]{:S(2)}) collective-permute-start(bf16[2,3,16,512]{3,2,1,0:T(8,128)(2,1)S(1)} %get-tuple-element.50), channel_id=1, source_target_pairs={{0,24},{4,28},{8,16},{12,20},{16,8},{20,12},{24,0},{28,4},{1,25},{... | collective-permute-start | bytes 294920 | tf_op jit(solution)/shard_map/ppermute | solution.py:58
  141.0 9.2 %collective-permute-done.38 = bf16[3,64,1024]{2,1,0:T(8,128)(2,1)S(1)} collective-permute-done((bf16[3,64,1024]{2,1,0:T(8,128)(2,1)S(1)}, bf16[3,64,1024]{2,1,0:T(8,128)(2,1)S(1)}, u32[]{:S(2)}, u32[]{:S(2)}) %collective-permute-start.38) | collective-permute-done | bytes 393248 | tf_op jit(solution)/shard_map/ppermute | solution.py:153
  156.8 4.6 %collective-permute-done.34 = bf16[2,48,512]{2,1,0:T(8,128)(2,1)S(1)} collective-permute-done((bf16[2,48,512]{2,1,0:T(8,128)(2,1)S(1)}, bf16[2,48,512]{2,1,0:T(8,128)(2,1)S(1)}, u32[]{:S(2)}, u32[]{:S(2)}) %collective-permute-start.34) | collective-permute-done | bytes 98336 | tf_op jit(solution)/shard_map/ppermute | solution.py:58
  163.7 3.8 %collective-permute-done.35 = bf16[2,48,512]{2,1,0:T(8,128)(2,1)S(1)} collective-permute-done((bf16[2,48,512]{2,1,0:T(8,128)(2,1)S(1)}, bf16[2,48,512]{2,1,0:T(8,128)(2,1)S(1)}, u32[]{:S(2)}, u32[]{:S(2)}) %collective-permute-start.35) | collective-permute-done | bytes 98336 | tf_op jit(solution)/shard_map/ppermute | solution.py:58
  167.6 4.1 %collective-permute-done.42 = bf16[3,64,1024]{2,1,0:T(8,128)(2,1)S(1)} collective-permute-done((bf16[3,64,1024]{2,1,0:T(8,128)(2,1)S(1)}, bf16[3,64,1024]{2,1,0:T(8,128)(2,1)S(1)}, u32[]{:S(2)}, u32[]{:S(2)}) %collective-permute-start.42) | collective-permute-done | bytes 393248 | tf_op jit(solution)/shard_map/ppermute | solution.py:153
  174.0 2.0 %multiply_convert_fusion = bf16[1024,512]{1,0:T(8,128)(2,1)} fusion(bf16[3,640,1024]{2,1,0:T(8,128)(2,1)S(1)} %get-tuple-element.8, bf16[2,640,512]{2,1,0:T(8,128)(2,1)S(1)} %maximum_select_fusion), kind=kOutput, calls=%fused_computation | convolution fusion | flops 672137216 | bytes 3014656 | tf_op jit(solution)/shard_map/dot_general | solution.py:24
  176.1 2.4 %collective-permute-start.47 = (bf16[2,2,16,512]{3,2,1,0:T(8,128)(2,1)S(1)}, bf16[2,2,16,512]{3,2,1,0:T(8,128)(2,1)S(1)}, u32[]{:S(2)}, u32[]{:S(2)}) collective-permute-start(bf16[2,2,16,512]{3,2,1,0:T(8,128)(2,1)S(1)} %get-tuple-element.61), channel_id=1, source_target_pairs={{0,24},{4,28},{8,16},{12,20},{16,8},{20,12},{24,0},{28,4},{1,25},{... | collective-permute-start | bytes 196616 | tf_op jit(solution)/shard_map/ppermute | solution.py:58
  179.7 2.0 %multiply_convert_fusion.2 = bf16[512,1024]{1,0:T(8,128)(2,1)} fusion(bf16[3,640,1024]{2,1,0:T(8,128)(2,1)S(1)} %get-tuple-element.8, bf16[2,640,512]{2,1,0:T(8,128)(2,1)S(1)} %maximum_select_fusion), kind=kOutput, calls=%fused_computation.2 | convolution fusion | flops 672137216 | bytes 3014656 | tf_op jit(solution)/shard_map/dot_general | solution.py:24
  183.3 1.9 collective-permute-start.50
  185.2 2.5 %collective-permute-start.48 = (bf16[2,32,512]{2,1,0:T(8,128)(2,1)S(1)}, bf16[2,32,512]{2,1,0:T(8,128)(2,1)S(1)}, u32[]{:S(2)}, u32[]{:S(2)}) collective-permute-start(bf16[2,32,512]{2,1,0:T(8,128)(2,1)S(1)} %bitcast.535), channel_id=1, source_target_pairs={{0,1},{1,0},{2,3},{3,2},{4,5},{5,4},{6,7},{7,6},{8,9},{9,8},{10,11... | collective-permute-start | bytes 196616 | tf_op jit(solution)/shard_map/ppermute | solution.py:58
  187.8 2.0 %multiply_convert_fusion.1 = bf16[512,1024]{1,0:T(8,128)(2,1)} fusion(bf16[3,640,1024]{2,1,0:T(8,128)(2,1)S(1)} %get-tuple-element.8, bf16[2,640,512]{2,1,0:T(8,128)(2,1)S(1)} %maximum_select_fusion), kind=kOutput, calls=%fused_computation.1 | convolution fusion | flops 672137216 | bytes 3014656 | tf_op jit(solution)/shard_map/dot_general | solution.py:24
  (235 shorter events, 66.6 us)
Async XLA Ops:
  1.5 7.6 %collective-permute-start.2 = (bf16[2,32,512]{2,1,0:T(8,128)(2,1)S(1)}, bf16[2,32,512]{2,1,0:T(8,128)(2,1)S(1)}, u32[]{:S(2)}, u32[]{:S(2)}) collective-permute-start(bf16[2,32,512]{2,1,0:T(8,128)(2,1)S(1)} %pad_maximum_fusion.25), channel_id=1, source_target_pairs={{0,3},{1,2},{2,1},{3,0},{4,7},{5,6},{6,5},{7,4},{8,11},{9,10},{10,... | collective-permute-start | bytes 196616 | tf_op jit(solution)/shard_map/ppermute | solution.py:58
  23.1 10.1 %collective-permute-start.15 = (bf16[2,48,512]{2,1,0:T(8,128)(2,1)S(1)}, bf16[2,48,512]{2,1,0:T(8,128)(2,1)S(1)}, u32[]{:S(2)}, u32[]{:S(2)}) collective-permute-start(bf16[2,48,512]{2,1,0:T(8,128)(2,1)S(1)} %fusion.107), channel_id=1, source_target_pairs={{0,3},{1,2},{2,1},{3,0},{4,7},{5,6},{6,5},{7,4},{8,11},{9,10},{10,... | collective-permute-start | bytes 294920 | tf_op jit(solution)/shard_map/ppermute | solution.py:58
  25.8 9.3 %collective-permute-start.14 = (bf16[2,48,512]{2,1,0:T(8,128)(2,1)S(1)}, bf16[2,48,512]{2,1,0:T(8,128)(2,1)S(1)}, u32[]{:S(2)}, u32[]{:S(2)}) collective-permute-start(bf16[2,48,512]{2,1,0:T(8,128)(2,1)S(1)} %fusion.107), channel_id=1, source_target_pairs={{0,2},{1,3},{2,0},{3,1},{4,6},{5,7},{6,4},{7,5},{8,10},{9,11},{10,... | collective-permute-start | bytes 294920 | tf_op jit(solution)/shard_map/ppermute | solution.py:58
  25.8 9.3 %collective-permute-start.13 = (bf16[2,48,512]{2,1,0:T(8,128)(2,1)S(1)}, bf16[2,48,512]{2,1,0:T(8,128)(2,1)S(1)}, u32[]{:S(2)}, u32[]{:S(2)}) collective-permute-start(bf16[2,48,512]{2,1,0:T(8,128)(2,1)S(1)} %fusion.107), channel_id=1, source_target_pairs={{0,1},{1,0},{2,3},{3,2},{4,5},{5,4},{6,7},{7,6},{8,9},{9,8},{10,11... | collective-permute-start | bytes 294920 | tf_op jit(solution)/shard_map/ppermute | solution.py:58
  29.5 14.0 %collective-permute-start.7 = (bf16[3,64,1024]{2,1,0:T(8,128)(2,1)S(1)}, bf16[3,64,1024]{2,1,0:T(8,128)(2,1)S(1)}, u32[]{:S(2)}, u32[]{:S(2)}) collective-permute-start(bf16[3,64,1024]{2,1,0:T(8,128)(2,1)S(1)} %pad_maximum_fusion.2), channel_id=1, source_target_pairs={{0,1},{3,2},{4,5},{7,6},{8,9},{11,10},{12,13},{15,14},{16,17},{19,... | collective-permute-start | bytes 1179656 | tf_op jit(solution)/shard_map/ppermute | solution.py:151
  35.7 6.4 %collective-permute-start.18 = (bf16[2,3,1,16,512]{4,3,2,1,0:T(8,128)(2,1)S(1)}, bf16[2,3,1,16,512]{4,3,2,1,0:T(8,128)(2,1)S(1)}, u32[]{:S(2)}, u32[]{:S(2)}) collective-permute-start(bf16[2,3,1,16,512]{4,3,2,1,0:T(8,128)(2,1)S(1)} %bitcast.522), channel_id=1, source_target_pairs={{0,24},{4,28},{8,16},{12,20},{16,8},{20,12},{24,0},{28,4},{1,25},{... | collective-permute-start | bytes 294920 | tf_op jit(solution)/shard_map/ppermute | solution.py:58
  43.4 7.4 %collective-permute-start.19 = (bf16[2,3,4,16,512]{4,3,2,1,0:T(8,128)(2,1)S(1)}, bf16[2,3,4,16,512]{4,3,2,1,0:T(8,128)(2,1)S(1)}, u32[]{:S(2)}, u32[]{:S(2)}) collective-permute-start(bf16[2,3,4,16,512]{4,3,2,1,0:T(8,128)(2,1)S(1)} %pad_maximum_fusion.5), channel_id=1, source_target_pairs={{0,4},{4,0},{8,12},{12,8},{16,20},{20,16},{24,28},{28,24},{1,5},{5... | collective-permute-start | bytes 1179656 | tf_op jit(solution)/shard_map/ppermute | solution.py:58
  44.1 11.6 %collective-permute-start.8 = (bf16[3,64,1024]{2,1,0:T(8,128)(2,1)S(1)}, bf16[3,64,1024]{2,1,0:T(8,128)(2,1)S(1)}, u32[]{:S(2)}, u32[]{:S(2)}) collective-permute-start(bf16[3,64,1024]{2,1,0:T(8,128)(2,1)S(1)} %maximum_select_fusion.1), channel_id=1, source_target_pairs={{0,1},{3,2},{4,5},{7,6},{8,9},{11,10},{12,13},{15,14},{16,17},{19,... | collective-permute-start | bytes 1179656 | tf_op jit(solution)/shard_map/ppermute | solution.py:151
  46.4 10.0 %collective-permute-start.9 = (bf16[3,64,1024]{2,1,0:T(8,128)(2,1)S(1)}, bf16[3,64,1024]{2,1,0:T(8,128)(2,1)S(1)}, u32[]{:S(2)}, u32[]{:S(2)}) collective-permute-start(bf16[3,64,1024]{2,1,0:T(8,128)(2,1)S(1)} %add_convert_fusion.4), channel_id=1, source_target_pairs={{1,2},{2,1},{5,6},{6,5},{9,10},{10,9},{13,14},{14,13},{17,18},{18,... | collective-permute-start | bytes 1179656 | tf_op jit(solution)/shard_map/ppermute | solution.py:160
  47.7 16.3 %collective-permute-start.11 = (bf16[3,64,1024]{2,1,0:T(8,128)(2,1)S(1)}, bf16[3,64,1024]{2,1,0:T(8,128)(2,1)S(1)}, u32[]{:S(2)}, u32[]{:S(2)}) collective-permute-start(bf16[3,64,1024]{2,1,0:T(8,128)(2,1)S(1)} %pad_maximum_fusion.4), channel_id=1, source_target_pairs={{0,1},{3,2},{4,5},{7,6},{8,9},{11,10},{12,13},{15,14},{16,17},{19,... | collective-permute-start | bytes 1179656 | tf_op jit(solution)/shard_map/ppermute | solution.py:151
  57.2 8.8 %collective-permute-start.10 = (bf16[3,64,1024]{2,1,0:T(8,128)(2,1)S(1)}, bf16[3,64,1024]{2,1,0:T(8,128)(2,1)S(1)}, u32[]{:S(2)}, u32[]{:S(2)}) collective-permute-start(bf16[3,64,1024]{2,1,0:T(8,128)(2,1)S(1)} %get-tuple-element.57), channel_id=1, source_target_pairs={{1,2},{2,1},{5,6},{6,5},{9,10},{10,9},{13,14},{14,13},{17,18},{18,... | collective-permute-start | bytes 1179656 | tf_op jit(solution)/shard_map/ppermute | solution.py:160
  57.9 16.0 %collective-permute-start.21 = (bf16[3,64,1024]{2,1,0:T(8,128)(2,1)S(1)}, bf16[3,64,1024]{2,1,0:T(8,128)(2,1)S(1)}, u32[]{:S(2)}, u32[]{:S(2)}) collective-permute-start(bf16[3,64,1024]{2,1,0:T(8,128)(2,1)S(1)} %get-tuple-element.56), channel_id=1, source_target_pairs={{0,1},{3,2},{1,0},{2,3},{4,5},{7,6},{5,4},{6,7},{8,9},{11,10},{9,8... | collective-permute-start | bytes 1179656 | tf_op jit(solution)/shard_map/ppermute | solution.py:155
  64.2 10.4 %collective-permute-start.22 = (bf16[3,64,1024]{2,1,0:T(8,128)(2,1)S(1)}, bf16[3,64,1024]{2,1,0:T(8,128)(2,1)S(1)}, u32[]{:S(2)}, u32[]{:S(2)}) collective-permute-start(bf16[3,64,1024]{2,1,0:T(8,128)(2,1)S(1)} %add_convert_fusion.3), channel_id=1, source_target_pairs={{1,2},{2,1},{5,6},{6,5},{9,10},{10,9},{13,14},{14,13},{17,18},{18,... | collective-permute-start | bytes 1179656 | tf_op jit(solution)/shard_map/ppermute | solution.py:160
  66.1 18.0 %collective-permute-start.20 = (bf16[3,64,1024]{2,1,0:T(8,128)(2,1)S(1)}, bf16[3,64,1024]{2,1,0:T(8,128)(2,1)S(1)}, u32[]{:S(2)}, u32[]{:S(2)}) collective-permute-start(bf16[3,64,1024]{2,1,0:T(8,128)(2,1)S(1)} %broadcast_select_fusion.9), channel_id=1, source_target_pairs={{0,1},{3,2},{1,0},{2,3},{4,5},{7,6},{5,4},{6,7},{8,9},{11,10},{9,8... | collective-permute-start | bytes 1179656 | tf_op jit(solution)/shard_map/ppermute | solution.py:155
  75.4 17.4 %collective-permute-start.23 = (bf16[3,64,1024]{2,1,0:T(8,128)(2,1)S(1)}, bf16[3,64,1024]{2,1,0:T(8,128)(2,1)S(1)}, u32[]{:S(2)}, u32[]{:S(2)}) collective-permute-start(bf16[3,64,1024]{2,1,0:T(8,128)(2,1)S(1)} %get-tuple-element.55), channel_id=1, source_target_pairs={{1,2},{2,1},{5,6},{6,5},{9,10},{10,9},{13,14},{14,13},{17,18},{18,... | collective-permute-start | bytes 1179656 | tf_op jit(solution)/shard_map/ppermute | solution.py:160
  76.1 15.7 %collective-permute-start.25 = (bf16[3,64,1024]{2,1,0:T(8,128)(2,1)S(1)}, bf16[3,64,1024]{2,1,0:T(8,128)(2,1)S(1)}, u32[]{:S(2)}, u32[]{:S(2)}) collective-permute-start(bf16[3,64,1024]{2,1,0:T(8,128)(2,1)S(1)} %get-tuple-element.54), channel_id=1, source_target_pairs={{0,1},{3,2},{1,0},{2,3},{4,5},{7,6},{5,4},{6,7},{8,9},{11,10},{9,8... | collective-permute-start | bytes 1179656 | tf_op jit(solution)/shard_map/ppermute | solution.py:155
  92.9 8.9 %collective-permute-start.24 = (bf16[3,64,1024]{2,1,0:T(8,128)(2,1)S(1)}, bf16[3,64,1024]{2,1,0:T(8,128)(2,1)S(1)}, u32[]{:S(2)}, u32[]{:S(2)}) collective-permute-start(bf16[3,64,1024]{2,1,0:T(8,128)(2,1)S(1)} %broadcast_select_fusion.8), channel_id=1, source_target_pairs={{0,1},{3,2},{1,0},{2,3},{4,5},{7,6},{5,4},{6,7},{8,9},{11,10},{9,8... | collective-permute-start | bytes 1179656 | tf_op jit(solution)/shard_map/ppermute | solution.py:155
  96.1 7.7 %collective-permute-start.26 = (bf16[3,64,1024]{2,1,0:T(8,128)(2,1)S(1)}, bf16[3,64,1024]{2,1,0:T(8,128)(2,1)S(1)}, u32[]{:S(2)}, u32[]{:S(2)}) collective-permute-start(bf16[3,64,1024]{2,1,0:T(8,128)(2,1)S(1)} %add_convert_fusion.2), channel_id=1, source_target_pairs={{1,2},{2,1},{5,6},{6,5},{9,10},{10,9},{13,14},{14,13},{17,18},{18,... | collective-permute-start | bytes 1179656 | tf_op jit(solution)/shard_map/ppermute | solution.py:160
  104.3 7.9 %collective-permute-start.27 = (bf16[3,64,1024]{2,1,0:T(8,128)(2,1)S(1)}, bf16[3,64,1024]{2,1,0:T(8,128)(2,1)S(1)}, u32[]{:S(2)}, u32[]{:S(2)}) collective-permute-start(bf16[3,64,1024]{2,1,0:T(8,128)(2,1)S(1)} %get-tuple-element.53), channel_id=1, source_target_pairs={{1,2},{2,1},{5,6},{6,5},{9,10},{10,9},{13,14},{14,13},{17,18},{18,... | collective-permute-start | bytes 1179656 | tf_op jit(solution)/shard_map/ppermute | solution.py:160
  105.0 16.2 %collective-permute-start.29 = (bf16[3,64,1024]{2,1,0:T(8,128)(2,1)S(1)}, bf16[3,64,1024]{2,1,0:T(8,128)(2,1)S(1)}, u32[]{:S(2)}, u32[]{:S(2)}) collective-permute-start(bf16[3,64,1024]{2,1,0:T(8,128)(2,1)S(1)} %get-tuple-element.52), channel_id=1, source_target_pairs={{0,1},{3,2},{1,0},{2,3},{4,5},{7,6},{5,4},{6,7},{8,9},{11,10},{9,8... | collective-permute-start | bytes 1179656 | tf_op jit(solution)/shard_map/ppermute | solution.py:155
  110.6 11.3 %collective-permute-start.36 = (bf16[3,64,1024]{2,1,0:T(8,128)(2,1)S(1)}, bf16[3,64,1024]{2,1,0:T(8,128)(2,1)S(1)}, u32[]{:S(2)}, u32[]{:S(2)}) collective-permute-start(bf16[3,64,1024]{2,1,0:T(8,128)(2,1)S(1)} %add_convert_fusion.1), channel_id=1, source_target_pairs={{1,2},{2,1},{5,6},{6,5},{9,10},{10,9},{13,14},{14,13},{17,18},{18,... | collective-permute-start | bytes 1179656 | tf_op jit(solution)/shard_map/ppermute | solution.py:160
  112.2 16.9 %collective-permute-start.28 = (bf16[3,64,1024]{2,1,0:T(8,128)(2,1)S(1)}, bf16[3,64,1024]{2,1,0:T(8,128)(2,1)S(1)}, u32[]{:S(2)}, u32[]{:S(2)}) collective-permute-start(bf16[3,64,1024]{2,1,0:T(8,128)(2,1)S(1)} %broadcast_select_fusion.7), channel_id=1, source_target_pairs={{0,1},{3,2},{1,0},{2,3},{4,5},{7,6},{5,4},{6,7},{8,9},{11,10},{9,8... | collective-permute-start | bytes 1179656 | tf_op jit(solution)/shard_map/ppermute | solution.py:155
  122.7 9.2 %collective-permute-start.37 = (bf16[3,64,1024]{2,1,0:T(8,128)(2,1)S(1)}, bf16[3,64,1024]{2,1,0:T(8,128)(2,1)S(1)}, u32[]{:S(2)}, u32[]{:S(2)}) collective-permute-start(bf16[3,64,1024]{2,1,0:T(8,128)(2,1)S(1)} %get-tuple-element.48), channel_id=1, source_target_pairs={{1,2},{2,1},{5,6},{6,5},{9,10},{10,9},{13,14},{14,13},{17,18},{18,... | collective-permute-start | bytes 1179656 | tf_op jit(solution)/shard_map/ppermute | solution.py:160
  123.4 11.9 %collective-permute-start.39 = (bf16[3,64,1024]{2,1,0:T(8,128)(2,1)S(1)}, bf16[3,64,1024]{2,1,0:T(8,128)(2,1)S(1)}, u32[]{:S(2)}, u32[]{:S(2)}) collective-permute-start(bf16[3,64,1024]{2,1,0:T(8,128)(2,1)S(1)} %get-tuple-element.47), channel_id=1, source_target_pairs={{0,1},{3,2},{1,0},{2,3},{4,5},{7,6},{5,4},{6,7},{8,9},{11,10},{9,8... | collective-permute-start | bytes 1179656 | tf_op jit(solution)/shard_map/ppermute | solution.py:155
  131.9 18.2 %collective-permute-start.38 = (bf16[3,64,1024]{2,1,0:T(8,128)(2,1)S(1)}, bf16[3,64,1024]{2,1,0:T(8,128)(2,1)S(1)}, u32[]{:S(2)}, u32[]{:S(2)}) collective-permute-start(bf16[3,64,1024]{2,1,0:T(8,128)(2,1)S(1)} %collective-permute-done.37), channel_id=1, source_target_pairs={{1,0},{2,3},{5,4},{6,7},{9,8},{10,11},{13,12},{14,15},{17,16},{18,... | collective-permute-start | bytes 1179656 | tf_op jit(solution)/shard_map/ppermute | solution.py:153
  135.7 26.1 %collective-permute-start.41 = (bf16[3,64,1024]{2,1,0:T(8,128)(2,1)S(1)}, bf16[3,64,1024]{2,1,0:T(8,128)(2,1)S(1)}, u32[]{:S(2)}, u32[]{:S(2)}) collective-permute-start(bf16[3,64,1024]{2,1,0:T(8,128)(2,1)S(1)} %pad_maximum_fusion.16), channel_id=1, source_target_pairs={{1,2},{2,1},{5,6},{6,5},{9,10},{10,9},{13,14},{14,13},{17,18},{18,... | collective-permute-start | bytes 1179656 | tf_op jit(solution)/shard_map/ppermute | solution.py:160
  136.4 35.5 %collective-permute-start.43 = (bf16[3,64,1024]{2,1,0:T(8,128)(2,1)S(1)}, bf16[3,64,1024]{2,1,0:T(8,128)(2,1)S(1)}, u32[]{:S(2)}, u32[]{:S(2)}) collective-permute-start(bf16[3,64,1024]{2,1,0:T(8,128)(2,1)S(1)} %pad_maximum_fusion.16), channel_id=1, source_target_pairs={{1,0},{2,3},{5,4},{6,7},{9,8},{10,11},{13,12},{14,15},{17,16},{18,... | collective-permute-start | bytes 1179656 | tf_op jit(solution)/shard_map/ppermute | solution.py:153
  138.0 15.1 %collective-permute-start.33 = (bf16[2,3,16,512]{3,2,1,0:T(8,128)(2,1)S(1)}, bf16[2,3,16,512]{3,2,1,0:T(8,128)(2,1)S(1)}, u32[]{:S(2)}, u32[]{:S(2)}) collective-permute-start(bf16[2,3,16,512]{3,2,1,0:T(8,128)(2,1)S(1)} %get-tuple-element.50), channel_id=1, source_target_pairs={{0,24},{4,28},{8,16},{12,20},{16,8},{20,12},{24,0},{28,4},{1,25},{... | collective-permute-start | bytes 294920 | tf_op jit(solution)/shard_map/ppermute | solution.py:58
  140.4 12.7 %collective-permute-start.32 = (bf16[2,3,16,512]{3,2,1,0:T(8,128)(2,1)S(1)}, bf16[2,3,16,512]{3,2,1,0:T(8,128)(2,1)S(1)}, u32[]{:S(2)}, u32[]{:S(2)}) collective-permute-start(bf16[2,3,16,512]{3,2,1,0:T(8,128)(2,1)S(1)} %get-tuple-element.51), channel_id=1, source_target_pairs={{0,16},{4,20},{8,24},{12,28},{16,0},{20,4},{24,8},{28,12},{1,17},{... | collective-permute-start | bytes 294920 | tf_op jit(solution)/shard_map/ppermute | solution.py:58
  161.9 9.9 %collective-permute-start.42 = (bf16[3,64,1024]{2,1,0:T(8,128)(2,1)S(1)}, bf16[3,64,1024]{2,1,0:T(8,128)(2,1)S(1)}, u32[]{:S(2)}, u32[]{:S(2)}) collective-permute-start(bf16[3,64,1024]{2,1,0:T(8,128)(2,1)S(1)} %broadcast_select_fusion), channel_id=1, source_target_pairs={{1,0},{2,3},{5,4},{6,7},{9,8},{10,11},{13,12},{14,15},{17,16},{18,... | collective-permute-start | bytes 1179656 | tf_op jit(solution)/shard_map/ppermute | solution.py:153
  183.3 6.6 %collective-permute-start.50 = (bf16[2,32,512]{2,1,0:T(8,128)(2,1)S(1)}, bf16[2,32,512]{2,1,0:T(8,128)(2,1)S(1)}, u32[]{:S(2)}, u32[]{:S(2)}) collective-permute-start(bf16[2,32,512]{2,1,0:T(8,128)(2,1)S(1)} %bitcast.533), channel_id=1, source_target_pairs={{0,3},{1,2},{2,1},{3,0},{4,7},{5,6},{6,5},{7,4},{8,11},{9,10},{10,... | collective-permute-start | bytes 196616 | tf_op jit(solution)/shard_map/ppermute | solution.py:58
  185.2 6.1 %collective-permute-start.48 = (bf16[2,32,512]{2,1,0:T(8,128)(2,1)S(1)}, bf16[2,32,512]{2,1,0:T(8,128)(2,1)S(1)}, u32[]{:S(2)}, u32[]{:S(2)}) collective-permute-start(bf16[2,32,512]{2,1,0:T(8,128)(2,1)S(1)} %bitcast.535), channel_id=1, source_target_pairs={{0,1},{1,0},{2,3},{3,2},{4,5},{5,4},{6,7},{7,6},{8,9},{9,8},{10,11... | collective-permute-start | bytes 196616 | tf_op jit(solution)/shard_map/ppermute | solution.py:58
  (25 other events, 200.7 us)

commit v8 on v7

--- a/solution.py
+++ b/solution.py
@@ -11,6 +11,7 @@
 F32 = jnp.float32
 STEP = 16
 LAG = 3
+KINDS = 4
 
 
 def sylvester(order):
@@ -46,11 +47,11 @@
     columns = [me >= groups // 2, away]
     columns += [signs[me, me ^ apart] for apart in range(groups)]
     columns += [1 - 2 * (me >> bit & 1) for bit in range(groups.bit_length() - 1)]
-    columns += [away, away]
+    columns += [away] * KINDS
     table = np.stack(columns, axis=1).astype(np.float32)[:, :, None, None]
     table = jnp.asarray(np.tile(table, (1, 1, 1, length)))
     row = lax.dynamic_index_in_dim(table, lax.axis_index("tensor"), keepdims=False)
-    return row[0], row[1], row[2 : 2 + groups], row[2 + groups : -2], row[-2:]
+    return row[0], row[1], row[2 : 2 + groups], row[2 + groups : -KINDS], row[-KINDS:]
 
 
 def exchange(block, axis, apart):
@@ -95,10 +96,12 @@
     return stages
 
 
-def gather_dp(block, axis):
+def gather_dp(block, axis, ahead):
     stages = dp_stages()
     for stage in stages[:-1]:
         came = [exchange(block, "dp", apart) for apart in stage[1:]]
+        for other in ahead:
+            block = after(block, other)
         block = jnp.concatenate([block] + came, axis=axis)
     return block, exchange(block, "dp", stages[-1][1])
 
@@ -183,8 +186,8 @@
 
     both = jnp.stack([tokens, out_grad])
 
-    def arrive(turned):
-        low, high = gather_dp(turned.reshape(2, -1, 1, step, width), 2)
+    def arrive(turned, ahead=()):
+        low, high = gather_dp(turned.reshape(2, -1, 1, step, width), 2, ahead)
         other, own = jnp.where(far, low, high), jnp.where(far, high, low)
         return [part.reshape(2, -1, half, width) for part in (other, own)]
 
@@ -219,37 +222,40 @@
             group, place = (groups[0], i) if i < first else (groups[1], i - first)
             x, g = group[which][0, place], group[which][1, place]
             if s > 0:
-                other = came[s - 2] if s > 1 else messages[0][2:]
+                other = came[max(s - LAG, 0)] if s > 1 else messages[0][2:]
                 x, g = after(x, other), after(g, other)
             parts = [dot(x, gate_weight, 1, 0), dot(x, up_weight, 1, 0), dot(g, down_weight, 1, 1)]
             message = jnp.stack(parts).astype(BF16)
             messages.append(inward(after(message, came[0]) if s == 1 else message))
         if s == steps + LAG - 1 and split > 0:
             low, high = leave([done(i) for i in range(split)])
-            sums, _, last = scatter_dp(low, high)
+            sums, early, ahead = scatter_dp(low, high)
             ends.append(rotate_by_halves(sums.reshape(2, -1, width), bits))
-            outs[-1] = after(outs[-1], last)
+            outs[-1] = after(outs[-1], early)
         came.append(
             swap(
                 messages[s] if s < steps else None,
                 outs[s - LAG] if s >= LAG else None,
-                depths[s % 2],
+                depths[s % KINDS],
             )
         )
         if s == 0 and chunks > first:
             tick = exchange(message[2, :step, :width], "dp", 1)
             late[0] = after(late[0], tick)
-            groups.append(arrive(rotate(late, signs).astype(BF16)))
+        if s == 1 and chunks > first:
+            groups.append(arrive(rotate(late, signs).astype(BF16), [messages[1], middle]))
         if s < steps:
             total = messages[s].astype(F32) + came[s].astype(F32)
             if which == 0:
-                other_sums = across(total.astype(BF16))
+                middle = total.astype(BF16)
+                other_sums = across(middle)
             else:
                 gate, up, grad_hidden = total + other_sums.astype(F32)
                 acts.append(activations(gate, up, grad_hidden))
                 crossed.append(across(acts[i]))
                 outs += [acts[i], crossed[i]]
     low, high = leave([done(i) for i in range(split, chunks)])
+    high = after(high, ahead) if split > 0 else high
     sums, _, _ = scatter_dp(low, high)
     ends.append(rotate(spread(sums.reshape(2, -1, width).astype(BF16)), signs))
     ends = jnp.concatenate(ends, axis=1)

time: 193 us -> 193 us (level)
  waiting for transfers between devices: 59.9 us -> 57.4 us
    ppermute x28, starting transfers between devices: 32 us -> 29.3 us  [exchange(): return lax.ppermute(block, axis, [(i, i ^ apart) for i in range(count)])]
    ppermute x3, starting transfers between devices: 7.65 us -> 9.82 us  [swap(): return lax.ppermute(into, 'tensor', pairs)]
    ppermute x7, waiting for transfers between devices: 13.2 us -> 11.1 us  [swap(): return lax.ppermute(block, 'tensor', pairs + back)]
  transfers between devices with their start and end apart: 51 -> 51, of which waited for: 24 -> 20; matrix products, arithmetic and copies ran while one was open for 16% -> 16% of each run, Pallas kernels for 0% -> 0%
where the time goes in v8:
time: 193 us; the launch traced here: 192 us
  starting transfers between devices  94.1 us (49%)
  waiting for transfers between devices  57.4 us (30%)
  matrix products  26.8 us (14%)
  other arithmetic  10.2 us (5%)
  between operations  2.03 us (1%)
    ppermute x7, starting transfers between devices, swap(): return lax.ppermute(block, 'tensor', pairs + back)  43.9 us
    ppermute x28, starting transfers between devices, exchange(): return lax.ppermute(block, axis, [(i, i ^ apart) for i in range(count)])  29.3 us
    ppermute x28, waiting for transfers between devices, exchange(): return lax.ppermute(block, axis, [(i, i ^ apart) for i in range(count)])  27.9 us
    dot_general x56, matrix products, dot(): lax.dot_general(left, right, (((left_dim,), (right_dim,)), ((), ())), pre...  26.8 us
    ppermute x3, waiting for transfers between devices, swap(): return lax.ppermute(out, 'tensor', back)  12.9 us
    ppermute x7, waiting for transfers between devices, swap(): return lax.ppermute(block, 'tensor', pairs + back)  11.1 us
    ppermute x3, starting transfers between devices, swap(): return lax.ppermute(into, 'tensor', pairs)  9.82 us
    ppermute x10, starting transfers between devices, across(): return lax.ppermute(block, 'tensor', [(half - 1, half), (half, half - 1)])  7.04 us
  transfers between devices with their start and end apart: 51, of which 20 were waited for; matrix products, arithmetic and copies ran while one was open for 16% of the time, Pallas kernels for 0%

profile of v8, /device:TPU:0, one launch (start us, length us, event | category | flops | bytes accessed | tf_op | source)
XLA Modules:
  0.0 191.8 jit_solution(8338001039352399948)
XLA Ops:
  1.5 3.0 %collective-permute-start = (bf16[2,32,512]{2,1,0:T(8,128)(2,1)S(1)}, bf16[2,32,512]{2,1,0:T(8,128)(2,1)S(1)}, u32[]{:S(2)}, u32[]{:S(2)}) collective-permute-start(bf16[2,32,512]{2,1,0:T(8,128)(2,1)S(1)} %pad_maximum_fusion.26), channel_id=1, source_target_pairs={{0,1},{1,0},{2,3},{3,2},{4,5},{5,4},{6,7},{7,6},{8,9},{9,8},{10,11... | collective-permute-start | bytes 196616 | tf_op jit(solution)/shard_map/ppermute | solution.py:59
  4.6 2.6 %collective-permute-start.1 = (bf16[2,32,512]{2,1,0:T(8,128)(2,1)S(1)}, bf16[2,32,512]{2,1,0:T(8,128)(2,1)S(1)}, u32[]{:S(2)}, u32[]{:S(2)}) collective-permute-start(bf16[2,32,512]{2,1,0:T(8,128)(2,1)S(1)} %pad_maximum_fusion.26), channel_id=1, source_target_pairs={{0,2},{1,3},{2,0},{3,1},{4,6},{5,7},{6,4},{7,5},{8,10},{9,11},{10,... | collective-permute-start | bytes 196616 | tf_op jit(solution)/shard_map/ppermute | solution.py:59
  8.8 3.0 %collective-permute-done.1 = bf16[2,32,512]{2,1,0:T(8,128)(2,1)S(1)} collective-permute-done((bf16[2,32,512]{2,1,0:T(8,128)(2,1)S(1)}, bf16[2,32,512]{2,1,0:T(8,128)(2,1)S(1)}, u32[]{:S(2)}, u32[]{:S(2)}) %collective-permute-start.1) | collective-permute-done | bytes 65568 | tf_op jit(solution)/shard_map/ppermute | solution.py:59
  22.5 2.3 %collective-permute-done.5 = bf16[2,2,1,16,512]{4,3,2,1,0:T(8,128)(2,1)S(1)} collective-permute-done((bf16[2,2,1,16,512]{4,3,2,1,0:T(8,128)(2,1)S(1)}, bf16[2,2,1,16,512]{4,3,2,1,0:T(8,128)(2,1)S(1)}, u32[]{:S(2)}, u32[]{:S(2)}) %collective-permute-start.5) | collective-permute-done | bytes 65568 | tf_op jit(solution)/shard_map/ppermute | solution.py:59
  25.1 2.3 %collective-permute-start.13 = (bf16[2,48,512]{2,1,0:T(8,128)(2,1)S(1)}, bf16[2,48,512]{2,1,0:T(8,128)(2,1)S(1)}, u32[]{:S(2)}, u32[]{:S(2)}) collective-permute-start(bf16[2,48,512]{2,1,0:T(8,128)(2,1)S(1)} %fusion.108), channel_id=1, source_target_pairs={{0,2},{1,3},{2,0},{3,1},{4,6},{5,7},{6,4},{7,5},{8,10},{9,11},{10,... | collective-permute-start | bytes 294920 | tf_op jit(solution)/shard_map/ppermute | solution.py:59
  27.4 2.0 %collective-permute-start.14 = (bf16[2,48,512]{2,1,0:T(8,128)(2,1)S(1)}, bf16[2,48,512]{2,1,0:T(8,128)(2,1)S(1)}, u32[]{:S(2)}, u32[]{:S(2)}) collective-permute-start(bf16[2,48,512]{2,1,0:T(8,128)(2,1)S(1)} %fusion.108), channel_id=1, source_target_pairs={{0,3},{1,2},{2,1},{3,0},{4,7},{5,6},{6,5},{7,4},{8,11},{9,10},{10,... | collective-permute-start | bytes 294920 | tf_op jit(solution)/shard_map/ppermute | solution.py:59
  33.5 2.4 %collective-permute-done.13 = bf16[2,48,512]{2,1,0:T(8,128)(2,1)S(1)} collective-permute-done((bf16[2,48,512]{2,1,0:T(8,128)(2,1)S(1)}, bf16[2,48,512]{2,1,0:T(8,128)(2,1)S(1)}, u32[]{:S(2)}, u32[]{:S(2)}) %collective-permute-start.13) | collective-permute-done | bytes 98336 | tf_op jit(solution)/shard_map/ppermute | solution.py:59
  37.6 2.5 %collective-permute-start.17 = (bf16[2,3,1,16,512]{4,3,2,1,0:T(8,128)(2,1)S(1)}, bf16[2,3,1,16,512]{4,3,2,1,0:T(8,128)(2,1)S(1)}, u32[]{:S(2)}, u32[]{:S(2)}) collective-permute-start(bf16[2,3,1,16,512]{4,3,2,1,0:T(8,128)(2,1)S(1)} %bitcast.538), channel_id=1, source_target_pairs={{0,24},{4,28},{8,16},{12,20},{16,8},{20,12},{24,0},{28,4},{1,25},{... | collective-permute-start | bytes 294920 | tf_op jit(solution)/shard_map/ppermute | solution.py:59
  40.1 2.5 %collective-permute-done.7 = bf16[3,64,1024]{2,1,0:T(8,128)(2,1)S(1)} collective-permute-done((bf16[3,64,1024]{2,1,0:T(8,128)(2,1)S(1)}, bf16[3,64,1024]{2,1,0:T(8,128)(2,1)S(1)}, u32[]{:S(2)}, u32[]{:S(2)}) %collective-permute-start.7) | collective-permute-done | bytes 393248 | tf_op jit(solution)/shard_map/ppermute | solution.py:154
  43.0 4.4 %collective-permute-start.8 = (bf16[3,64,1024]{2,1,0:T(8,128)(2,1)S(1)}, bf16[3,64,1024]{2,1,0:T(8,128)(2,1)S(1)}, u32[]{:S(2)}, u32[]{:S(2)}) collective-permute-start(bf16[3,64,1024]{2,1,0:T(8,128)(2,1)S(1)} %maximum_select_fusion.1), channel_id=1, source_target_pairs={{0,1},{3,2},{4,5},{7,6},{8,9},{11,10},{12,13},{15,14},{16,17},{19,... | collective-permute-start | bytes 1179656 | tf_op jit(solution)/shard_map/ppermute | solution.py:154
  49.7 4.1 %collective-permute-start.21 = (bf16[3,64,1024]{2,1,0:T(8,128)(2,1)S(1)}, bf16[3,64,1024]{2,1,0:T(8,128)(2,1)S(1)}, u32[]{:S(2)}, u32[]{:S(2)}) collective-permute-start(bf16[3,64,1024]{2,1,0:T(8,128)(2,1)S(1)} %pad_maximum_fusion.7), channel_id=1, source_target_pairs={{0,1},{3,2},{4,5},{7,6},{8,9},{11,10},{12,13},{15,14},{16,17},{19,... | collective-permute-start | bytes 1179656 | tf_op jit(solution)/shard_map/ppermute | solution.py:154
  54.5 2.3 %collective-permute-done.8 = bf16[3,64,1024]{2,1,0:T(8,128)(2,1)S(1)} collective-permute-done((bf16[3,64,1024]{2,1,0:T(8,128)(2,1)S(1)}, bf16[3,64,1024]{2,1,0:T(8,128)(2,1)S(1)}, u32[]{:S(2)}, u32[]{:S(2)}) %collective-permute-start.8) | collective-permute-done | bytes 393248 | tf_op jit(solution)/shard_map/ppermute | solution.py:154
  58.0 5.4 %collective-permute-start.20 = (bf16[3,64,1024]{2,1,0:T(8,128)(2,1)S(1)}, bf16[3,64,1024]{2,1,0:T(8,128)(2,1)S(1)}, u32[]{:S(2)}, u32[]{:S(2)}) collective-permute-start(bf16[3,64,1024]{2,1,0:T(8,128)(2,1)S(1)} %get-tuple-element.58), channel_id=1, source_target_pairs={{0,1},{3,2},{1,0},{2,3},{4,5},{7,6},{5,4},{6,7},{8,9},{11,10},{9,8... | collective-permute-start | bytes 1179656 | tf_op jit(solution)/shard_map/ppermute | solution.py:158
  67.4 6.4 %collective-permute-start.19 = (bf16[3,64,1024]{2,1,0:T(8,128)(2,1)S(1)}, bf16[3,64,1024]{2,1,0:T(8,128)(2,1)S(1)}, u32[]{:S(2)}, u32[]{:S(2)}) collective-permute-start(bf16[3,64,1024]{2,1,0:T(8,128)(2,1)S(1)} %broadcast_select_fusion.9), channel_id=1, source_target_pairs={{0,1},{3,2},{1,0},{2,3},{4,5},{7,6},{5,4},{6,7},{8,9},{11,10},{9,8... | collective-permute-start | bytes 1179656 | tf_op jit(solution)/shard_map/ppermute | solution.py:158
  75.2 9.1 %collective-permute-start.25 = (bf16[3,64,1024]{2,1,0:T(8,128)(2,1)S(1)}, bf16[3,64,1024]{2,1,0:T(8,128)(2,1)S(1)}, u32[]{:S(2)}, u32[]{:S(2)}) collective-permute-start(bf16[3,64,1024]{2,1,0:T(8,128)(2,1)S(1)} %get-tuple-element.56), channel_id=1, source_target_pairs={{0,1},{3,2},{1,0},{2,3},{4,5},{7,6},{5,4},{6,7},{8,9},{11,10},{9,8... | collective-permute-start | bytes 1179656 | tf_op jit(solution)/shard_map/ppermute | solution.py:158
  85.8 5.8 %collective-permute-done.25 = bf16[3,64,1024]{2,1,0:T(8,128)(2,1)S(1)} collective-permute-done((bf16[3,64,1024]{2,1,0:T(8,128)(2,1)S(1)}, bf16[3,64,1024]{2,1,0:T(8,128)(2,1)S(1)}, u32[]{:S(2)}, u32[]{:S(2)}) %collective-permute-start.25) | collective-permute-done | bytes 393248 | tf_op jit(solution)/shard_map/ppermute | solution.py:158
  92.8 1.8 collective-permute-start.24
  97.7 3.5 %collective-permute-done.24 = bf16[3,64,1024]{2,1,0:T(8,128)(2,1)S(1)} collective-permute-done((bf16[3,64,1024]{2,1,0:T(8,128)(2,1)S(1)}, bf16[3,64,1024]{2,1,0:T(8,128)(2,1)S(1)}, u32[]{:S(2)}, u32[]{:S(2)}) %collective-permute-start.24) | collective-permute-done | bytes 393248 | tf_op jit(solution)/shard_map/ppermute | solution.py:158
  104.2 6.0 %collective-permute-start.29 = (bf16[3,64,1024]{2,1,0:T(8,128)(2,1)S(1)}, bf16[3,64,1024]{2,1,0:T(8,128)(2,1)S(1)}, u32[]{:S(2)}, u32[]{:S(2)}) collective-permute-start(bf16[3,64,1024]{2,1,0:T(8,128)(2,1)S(1)} %get-tuple-element.54), channel_id=1, source_target_pairs={{0,1},{3,2},{1,0},{2,3},{4,5},{7,6},{5,4},{6,7},{8,9},{11,10},{9,8... | collective-permute-start | bytes 1179656 | tf_op jit(solution)/shard_map/ppermute | solution.py:158
  112.0 8.1 %collective-permute-start.28 = (bf16[3,64,1024]{2,1,0:T(8,128)(2,1)S(1)}, bf16[3,64,1024]{2,1,0:T(8,128)(2,1)S(1)}, u32[]{:S(2)}, u32[]{:S(2)}) collective-permute-start(bf16[3,64,1024]{2,1,0:T(8,128)(2,1)S(1)} %broadcast_select_fusion.8), channel_id=1, source_target_pairs={{0,1},{3,2},{1,0},{2,3},{4,5},{7,6},{5,4},{6,7},{8,9},{11,10},{9,8... | collective-permute-start | bytes 1179656 | tf_op jit(solution)/shard_map/ppermute | solution.py:158
  121.3 7.1 %collective-permute-start.39 = (bf16[3,64,1024]{2,1,0:T(8,128)(2,1)S(1)}, bf16[3,64,1024]{2,1,0:T(8,128)(2,1)S(1)}, u32[]{:S(2)}, u32[]{:S(2)}) collective-permute-start(bf16[3,64,1024]{2,1,0:T(8,128)(2,1)S(1)} %get-tuple-element.49), channel_id=1, source_target_pairs={{0,1},{3,2},{1,0},{2,3},{4,5},{7,6},{5,4},{6,7},{8,9},{11,10},{9,8... | collective-permute-start | bytes 1179656 | tf_op jit(solution)/shard_map/ppermute | solution.py:158
  132.5 1.8 collective-permute-done.39
  136.7 12.9 %collective-permute-done.38 = bf16[3,64,1024]{2,1,0:T(8,128)(2,1)S(1)} collective-permute-done((bf16[3,64,1024]{2,1,0:T(8,128)(2,1)S(1)}, bf16[3,64,1024]{2,1,0:T(8,128)(2,1)S(1)}, u32[]{:S(2)}, u32[]{:S(2)}) %collective-permute-start.38) | collective-permute-done | bytes 393248 | tf_op jit(solution)/shard_map/ppermute | solution.py:156
  160.6 4.4 %collective-permute-done.34 = bf16[2,48,512]{2,1,0:T(8,128)(2,1)S(1)} collective-permute-done((bf16[2,48,512]{2,1,0:T(8,128)(2,1)S(1)}, bf16[2,48,512]{2,1,0:T(8,128)(2,1)S(1)}, u32[]{:S(2)}, u32[]{:S(2)}) %collective-permute-start.34) | collective-permute-done | bytes 98336 | tf_op jit(solution)/shard_map/ppermute | solution.py:59
  165.1 5.5 %collective-permute-done.35 = bf16[2,48,512]{2,1,0:T(8,128)(2,1)S(1)} collective-permute-done((bf16[2,48,512]{2,1,0:T(8,128)(2,1)S(1)}, bf16[2,48,512]{2,1,0:T(8,128)(2,1)S(1)}, u32[]{:S(2)}, u32[]{:S(2)}) %collective-permute-start.35) | collective-permute-done | bytes 98336 | tf_op jit(solution)/shard_map/ppermute | solution.py:59
  173.0 2.0 %multiply_convert_fusion = bf16[1024,512]{1,0:T(8,128)(2,1)} fusion(bf16[3,640,1024]{2,1,0:T(8,128)(2,1)S(1)} %get-tuple-element.10, bf16[2,640,512]{2,1,0:T(8,128)(2,1)S(1)} %maximum_select_fusion), kind=kOutput, calls=%fused_computation | convolution fusion | flops 672137216 | bytes 3014656 | tf_op jit(solution)/shard_map/dot_general | solution.py:25
  178.7 2.0 %multiply_convert_fusion.1 = bf16[512,1024]{1,0:T(8,128)(2,1)} fusion(bf16[3,640,1024]{2,1,0:T(8,128)(2,1)S(1)} %get-tuple-element.10, bf16[2,640,512]{2,1,0:T(8,128)(2,1)S(1)} %maximum_select_fusion), kind=kOutput, calls=%fused_computation.1 | convolution fusion | flops 672137216 | bytes 3014656 | tf_op jit(solution)/shard_map/dot_general | solution.py:25
  180.7 1.8 collective-permute-done.47
  182.6 1.8 collective-permute-start.49
  184.4 2.5 %collective-permute-start.50 = (bf16[2,32,512]{2,1,0:T(8,128)(2,1)S(1)}, bf16[2,32,512]{2,1,0:T(8,128)(2,1)S(1)}, u32[]{:S(2)}, u32[]{:S(2)}) collective-permute-start(bf16[2,32,512]{2,1,0:T(8,128)(2,1)S(1)} %bitcast.542), channel_id=1, source_target_pairs={{0,3},{1,2},{2,1},{3,0},{4,7},{5,6},{6,5},{7,4},{8,11},{9,10},{10,... | collective-permute-start | bytes 196616 | tf_op jit(solution)/shard_map/ppermute | solution.py:59
  187.0 2.0 %multiply_convert_fusion.2 = bf16[512,1024]{1,0:T(8,128)(2,1)} fusion(bf16[3,640,1024]{2,1,0:T(8,128)(2,1)S(1)} %get-tuple-element.10, bf16[2,640,512]{2,1,0:T(8,128)(2,1)S(1)} %maximum_select_fusion), kind=kOutput, calls=%fused_computation.2 | convolution fusion | flops 672137216 | bytes 3014656 | tf_op jit(solution)/shard_map/dot_general | solution.py:25
  189.0 1.6 collective-permute-done.50
  (243 shorter events, 64.8 us)
Async XLA Ops:
  1.5 7.3 %collective-permute-start = (bf16[2,32,512]{2,1,0:T(8,128)(2,1)S(1)}, bf16[2,32,512]{2,1,0:T(8,128)(2,1)S(1)}, u32[]{:S(2)}, u32[]{:S(2)}) collective-permute-start(bf16[2,32,512]{2,1,0:T(8,128)(2,1)S(1)} %pad_maximum_fusion.26), channel_id=1, source_target_pairs={{0,1},{1,0},{2,3},{3,2},{4,5},{5,4},{6,7},{7,6},{8,9},{9,8},{10,11... | collective-permute-start | bytes 196616 | tf_op jit(solution)/shard_map/ppermute | solution.py:59
  4.6 7.3 %collective-permute-start.1 = (bf16[2,32,512]{2,1,0:T(8,128)(2,1)S(1)}, bf16[2,32,512]{2,1,0:T(8,128)(2,1)S(1)}, u32[]{:S(2)}, u32[]{:S(2)}) collective-permute-start(bf16[2,32,512]{2,1,0:T(8,128)(2,1)S(1)} %pad_maximum_fusion.26), channel_id=1, source_target_pairs={{0,2},{1,3},{2,0},{3,1},{4,6},{5,7},{6,4},{7,5},{8,10},{9,11},{10,... | collective-permute-start | bytes 196616 | tf_op jit(solution)/shard_map/ppermute | solution.py:59
  25.0 8.5 %collective-permute-start.12 = (bf16[2,48,512]{2,1,0:T(8,128)(2,1)S(1)}, bf16[2,48,512]{2,1,0:T(8,128)(2,1)S(1)}, u32[]{:S(2)}, u32[]{:S(2)}) collective-permute-start(bf16[2,48,512]{2,1,0:T(8,128)(2,1)S(1)} %fusion.108), channel_id=1, source_target_pairs={{0,1},{1,0},{2,3},{3,2},{4,5},{5,4},{6,7},{7,6},{8,9},{9,8},{10,11... | collective-permute-start | bytes 294920 | tf_op jit(solution)/shard_map/ppermute | solution.py:59
  25.1 10.8 %collective-permute-start.13 = (bf16[2,48,512]{2,1,0:T(8,128)(2,1)S(1)}, bf16[2,48,512]{2,1,0:T(8,128)(2,1)S(1)}, u32[]{:S(2)}, u32[]{:S(2)}) collective-permute-start(bf16[2,48,512]{2,1,0:T(8,128)(2,1)S(1)} %fusion.108), channel_id=1, source_target_pairs={{0,2},{1,3},{2,0},{3,1},{4,6},{5,7},{6,4},{7,5},{8,10},{9,11},{10,... | collective-permute-start | bytes 294920 | tf_op jit(solution)/shard_map/ppermute | solution.py:59
  27.4 8.5 %collective-permute-start.14 = (bf16[2,48,512]{2,1,0:T(8,128)(2,1)S(1)}, bf16[2,48,512]{2,1,0:T(8,128)(2,1)S(1)}, u32[]{:S(2)}, u32[]{:S(2)}) collective-permute-start(bf16[2,48,512]{2,1,0:T(8,128)(2,1)S(1)} %fusion.108), channel_id=1, source_target_pairs={{0,3},{1,2},{2,1},{3,0},{4,7},{5,6},{6,5},{7,4},{8,11},{9,10},{10,... | collective-permute-start | bytes 294920 | tf_op jit(solution)/shard_map/ppermute | solution.py:59
  32.0 10.6 %collective-permute-start.7 = (bf16[3,64,1024]{2,1,0:T(8,128)(2,1)S(1)}, bf16[3,64,1024]{2,1,0:T(8,128)(2,1)S(1)}, u32[]{:S(2)}, u32[]{:S(2)}) collective-permute-start(bf16[3,64,1024]{2,1,0:T(8,128)(2,1)S(1)} %pad_maximum_fusion.2), channel_id=1, source_target_pairs={{0,1},{3,2},{4,5},{7,6},{8,9},{11,10},{12,13},{15,14},{16,17},{19,... | collective-permute-start | bytes 1179656 | tf_op jit(solution)/shard_map/ppermute | solution.py:154
  36.5 12.9 %collective-permute-start.15 = (bf16[2,3,1,16,512]{4,3,2,1,0:T(8,128)(2,1)S(1)}, bf16[2,3,1,16,512]{4,3,2,1,0:T(8,128)(2,1)S(1)}, u32[]{:S(2)}, u32[]{:S(2)}) collective-permute-start(bf16[2,3,1,16,512]{4,3,2,1,0:T(8,128)(2,1)S(1)} %bitcast.536), channel_id=1, source_target_pairs={{0,8},{4,12},{8,0},{12,4},{16,24},{20,28},{24,16},{28,20},{1,9},{5... | collective-permute-start | bytes 294920 | tf_op jit(solution)/shard_map/ppermute | solution.py:59
  37.1 12.4 %collective-permute-start.16 = (bf16[2,3,1,16,512]{4,3,2,1,0:T(8,128)(2,1)S(1)}, bf16[2,3,1,16,512]{4,3,2,1,0:T(8,128)(2,1)S(1)}, u32[]{:S(2)}, u32[]{:S(2)}) collective-permute-start(bf16[2,3,1,16,512]{4,3,2,1,0:T(8,128)(2,1)S(1)} %bitcast.537), channel_id=1, source_target_pairs={{0,16},{4,20},{8,24},{12,28},{16,0},{20,4},{24,8},{28,12},{1,17},{... | collective-permute-start | bytes 294920 | tf_op jit(solution)/shard_map/ppermute | solution.py:59
  37.6 11.9 %collective-permute-start.17 = (bf16[2,3,1,16,512]{4,3,2,1,0:T(8,128)(2,1)S(1)}, bf16[2,3,1,16,512]{4,3,2,1,0:T(8,128)(2,1)S(1)}, u32[]{:S(2)}, u32[]{:S(2)}) collective-permute-start(bf16[2,3,1,16,512]{4,3,2,1,0:T(8,128)(2,1)S(1)} %bitcast.538), channel_id=1, source_target_pairs={{0,24},{4,28},{8,16},{12,20},{16,8},{20,12},{24,0},{28,4},{1,25},{... | collective-permute-start | bytes 294920 | tf_op jit(solution)/shard_map/ppermute | solution.py:59
  43.0 13.9 %collective-permute-start.8 = (bf16[3,64,1024]{2,1,0:T(8,128)(2,1)S(1)}, bf16[3,64,1024]{2,1,0:T(8,128)(2,1)S(1)}, u32[]{:S(2)}, u32[]{:S(2)}) collective-permute-start(bf16[3,64,1024]{2,1,0:T(8,128)(2,1)S(1)} %maximum_select_fusion.1), channel_id=1, source_target_pairs={{0,1},{3,2},{4,5},{7,6},{8,9},{11,10},{12,13},{15,14},{16,17},{19,... | collective-permute-start | bytes 1179656 | tf_op jit(solution)/shard_map/ppermute | solution.py:154
  47.4 9.5 %collective-permute-start.9 = (bf16[3,64,1024]{2,1,0:T(8,128)(2,1)S(1)}, bf16[3,64,1024]{2,1,0:T(8,128)(2,1)S(1)}, u32[]{:S(2)}, u32[]{:S(2)}) collective-permute-start(bf16[3,64,1024]{2,1,0:T(8,128)(2,1)S(1)} %add_convert_fusion.4), channel_id=1, source_target_pairs={{1,2},{2,1},{5,6},{6,5},{9,10},{10,9},{13,14},{14,13},{17,18},{18,... | collective-permute-start | bytes 1179656 | tf_op jit(solution)/shard_map/ppermute | solution.py:163
  49.6 13.9 %collective-permute-start.18 = (bf16[2,3,4,16,512]{4,3,2,1,0:T(8,128)(2,1)S(1)}, bf16[2,3,4,16,512]{4,3,2,1,0:T(8,128)(2,1)S(1)}, u32[]{:S(2)}, u32[]{:S(2)}) collective-permute-start(bf16[2,3,4,16,512]{4,3,2,1,0:T(8,128)(2,1)S(1)} %pad_maximum_fusion.4), channel_id=1, source_target_pairs={{0,4},{4,0},{8,12},{12,8},{16,20},{20,16},{24,28},{28,24},{1,5},{5... | collective-permute-start | bytes 1179656 | tf_op jit(solution)/shard_map/ppermute | solution.py:59
  49.7 15.6 %collective-permute-start.21 = (bf16[3,64,1024]{2,1,0:T(8,128)(2,1)S(1)}, bf16[3,64,1024]{2,1,0:T(8,128)(2,1)S(1)}, u32[]{:S(2)}, u32[]{:S(2)}) collective-permute-start(bf16[3,64,1024]{2,1,0:T(8,128)(2,1)S(1)} %pad_maximum_fusion.7), channel_id=1, source_target_pairs={{0,1},{3,2},{4,5},{7,6},{8,9},{11,10},{12,13},{15,14},{16,17},{19,... | collective-permute-start | bytes 1179656 | tf_op jit(solution)/shard_map/ppermute | solution.py:154
  57.3 9.9 %collective-permute-start.10 = (bf16[3,64,1024]{2,1,0:T(8,128)(2,1)S(1)}, bf16[3,64,1024]{2,1,0:T(8,128)(2,1)S(1)}, u32[]{:S(2)}, u32[]{:S(2)}) collective-permute-start(bf16[3,64,1024]{2,1,0:T(8,128)(2,1)S(1)} %get-tuple-element.59), channel_id=1, source_target_pairs={{1,2},{2,1},{5,6},{6,5},{9,10},{10,9},{13,14},{14,13},{17,18},{18,... | collective-permute-start | bytes 1179656 | tf_op jit(solution)/shard_map/ppermute | solution.py:163
  58.0 15.7 %collective-permute-start.20 = (bf16[3,64,1024]{2,1,0:T(8,128)(2,1)S(1)}, bf16[3,64,1024]{2,1,0:T(8,128)(2,1)S(1)}, u32[]{:S(2)}, u32[]{:S(2)}) collective-permute-start(bf16[3,64,1024]{2,1,0:T(8,128)(2,1)S(1)} %get-tuple-element.58), channel_id=1, source_target_pairs={{0,1},{3,2},{1,0},{2,3},{4,5},{7,6},{5,4},{6,7},{8,9},{11,10},{9,8... | collective-permute-start | bytes 1179656 | tf_op jit(solution)/shard_map/ppermute | solution.py:158
  65.4 8.3 %collective-permute-start.22 = (bf16[3,64,1024]{2,1,0:T(8,128)(2,1)S(1)}, bf16[3,64,1024]{2,1,0:T(8,128)(2,1)S(1)}, u32[]{:S(2)}, u32[]{:S(2)}) collective-permute-start(bf16[3,64,1024]{2,1,0:T(8,128)(2,1)S(1)} %add_convert_fusion.3), channel_id=1, source_target_pairs={{1,2},{2,1},{5,6},{6,5},{9,10},{10,9},{13,14},{14,13},{17,18},{18,... | collective-permute-start | bytes 1179656 | tf_op jit(solution)/shard_map/ppermute | solution.py:163
  67.4 17.8 %collective-permute-start.19 = (bf16[3,64,1024]{2,1,0:T(8,128)(2,1)S(1)}, bf16[3,64,1024]{2,1,0:T(8,128)(2,1)S(1)}, u32[]{:S(2)}, u32[]{:S(2)}) collective-permute-start(bf16[3,64,1024]{2,1,0:T(8,128)(2,1)S(1)} %broadcast_select_fusion.9), channel_id=1, source_target_pairs={{0,1},{3,2},{1,0},{2,3},{4,5},{7,6},{5,4},{6,7},{8,9},{11,10},{9,8... | collective-permute-start | bytes 1179656 | tf_op jit(solution)/shard_map/ppermute | solution.py:158
  74.2 18.5 %collective-permute-start.23 = (bf16[3,64,1024]{2,1,0:T(8,128)(2,1)S(1)}, bf16[3,64,1024]{2,1,0:T(8,128)(2,1)S(1)}, u32[]{:S(2)}, u32[]{:S(2)}) collective-permute-start(bf16[3,64,1024]{2,1,0:T(8,128)(2,1)S(1)} %get-tuple-element.57), channel_id=1, source_target_pairs={{1,2},{2,1},{5,6},{6,5},{9,10},{10,9},{13,14},{14,13},{17,18},{18,... | collective-permute-start | bytes 1179656 | tf_op jit(solution)/shard_map/ppermute | solution.py:163
  75.2 16.4 %collective-permute-start.25 = (bf16[3,64,1024]{2,1,0:T(8,128)(2,1)S(1)}, bf16[3,64,1024]{2,1,0:T(8,128)(2,1)S(1)}, u32[]{:S(2)}, u32[]{:S(2)}) collective-permute-start(bf16[3,64,1024]{2,1,0:T(8,128)(2,1)S(1)} %get-tuple-element.56), channel_id=1, source_target_pairs={{0,1},{3,2},{1,0},{2,3},{4,5},{7,6},{5,4},{6,7},{8,9},{11,10},{9,8... | collective-permute-start | bytes 1179656 | tf_op jit(solution)/shard_map/ppermute | solution.py:158
  92.8 8.4 %collective-permute-start.24 = (bf16[3,64,1024]{2,1,0:T(8,128)(2,1)S(1)}, bf16[3,64,1024]{2,1,0:T(8,128)(2,1)S(1)}, u32[]{:S(2)}, u32[]{:S(2)}) collective-permute-start(bf16[3,64,1024]{2,1,0:T(8,128)(2,1)S(1)} %broadcast_select_fusion.3), channel_id=1, source_target_pairs={{0,1},{3,2},{1,0},{2,3},{4,5},{7,6},{5,4},{6,7},{8,9},{11,10},{9,8... | collective-permute-start | bytes 1179656 | tf_op jit(solution)/shard_map/ppermute | solution.py:158
  96.0 7.0 %collective-permute-start.26 = (bf16[3,64,1024]{2,1,0:T(8,128)(2,1)S(1)}, bf16[3,64,1024]{2,1,0:T(8,128)(2,1)S(1)}, u32[]{:S(2)}, u32[]{:S(2)}) collective-permute-start(bf16[3,64,1024]{2,1,0:T(8,128)(2,1)S(1)} %add_convert_fusion.2), channel_id=1, source_target_pairs={{1,2},{2,1},{5,6},{6,5},{9,10},{10,9},{13,14},{14,13},{17,18},{18,... | collective-permute-start | bytes 1179656 | tf_op jit(solution)/shard_map/ppermute | solution.py:163
  103.5 8.5 %collective-permute-start.27 = (bf16[3,64,1024]{2,1,0:T(8,128)(2,1)S(1)}, bf16[3,64,1024]{2,1,0:T(8,128)(2,1)S(1)}, u32[]{:S(2)}, u32[]{:S(2)}) collective-permute-start(bf16[3,64,1024]{2,1,0:T(8,128)(2,1)S(1)} %get-tuple-element.55), channel_id=1, source_target_pairs={{1,2},{2,1},{5,6},{6,5},{9,10},{10,9},{13,14},{14,13},{17,18},{18,... | collective-permute-start | bytes 1179656 | tf_op jit(solution)/shard_map/ppermute | solution.py:163
  104.2 16.0 %collective-permute-start.29 = (bf16[3,64,1024]{2,1,0:T(8,128)(2,1)S(1)}, bf16[3,64,1024]{2,1,0:T(8,128)(2,1)S(1)}, u32[]{:S(2)}, u32[]{:S(2)}) collective-permute-start(bf16[3,64,1024]{2,1,0:T(8,128)(2,1)S(1)} %get-tuple-element.54), channel_id=1, source_target_pairs={{0,1},{3,2},{1,0},{2,3},{4,5},{7,6},{5,4},{6,7},{8,9},{11,10},{9,8... | collective-permute-start | bytes 1179656 | tf_op jit(solution)/shard_map/ppermute | solution.py:158
  110.3 9.8 %collective-permute-start.36 = (bf16[3,64,1024]{2,1,0:T(8,128)(2,1)S(1)}, bf16[3,64,1024]{2,1,0:T(8,128)(2,1)S(1)}, u32[]{:S(2)}, u32[]{:S(2)}) collective-permute-start(bf16[3,64,1024]{2,1,0:T(8,128)(2,1)S(1)} %add_convert_fusion.1), channel_id=1, source_target_pairs={{1,2},{2,1},{5,6},{6,5},{9,10},{10,9},{13,14},{14,13},{17,18},{18,... | collective-permute-start | bytes 1179656 | tf_op jit(solution)/shard_map/ppermute | solution.py:163
  112.0 16.4 %collective-permute-start.28 = (bf16[3,64,1024]{2,1,0:T(8,128)(2,1)S(1)}, bf16[3,64,1024]{2,1,0:T(8,128)(2,1)S(1)}, u32[]{:S(2)}, u32[]{:S(2)}) collective-permute-start(bf16[3,64,1024]{2,1,0:T(8,128)(2,1)S(1)} %broadcast_select_fusion.8), channel_id=1, source_target_pairs={{0,1},{3,2},{1,0},{2,3},{4,5},{7,6},{5,4},{6,7},{8,9},{11,10},{9,8... | collective-permute-start | bytes 1179656 | tf_op jit(solution)/shard_map/ppermute | solution.py:158
  120.6 10.6 %collective-permute-start.37 = (bf16[3,64,1024]{2,1,0:T(8,128)(2,1)S(1)}, bf16[3,64,1024]{2,1,0:T(8,128)(2,1)S(1)}, u32[]{:S(2)}, u32[]{:S(2)}) collective-permute-start(bf16[3,64,1024]{2,1,0:T(8,128)(2,1)S(1)} %get-tuple-element.50), channel_id=1, source_target_pairs={{1,2},{2,1},{5,6},{6,5},{9,10},{10,9},{13,14},{14,13},{17,18},{18,... | collective-permute-start | bytes 1179656 | tf_op jit(solution)/shard_map/ppermute | solution.py:163
  121.3 13.0 %collective-permute-start.39 = (bf16[3,64,1024]{2,1,0:T(8,128)(2,1)S(1)}, bf16[3,64,1024]{2,1,0:T(8,128)(2,1)S(1)}, u32[]{:S(2)}, u32[]{:S(2)}) collective-permute-start(bf16[3,64,1024]{2,1,0:T(8,128)(2,1)S(1)} %get-tuple-element.49), channel_id=1, source_target_pairs={{0,1},{3,2},{1,0},{2,3},{4,5},{7,6},{5,4},{6,7},{8,9},{11,10},{9,8... | collective-permute-start | bytes 1179656 | tf_op jit(solution)/shard_map/ppermute | solution.py:158
  131.1 19.7 %collective-permute-start.30 = (bf16[2,3,64,512]{3,2,1,0:T(8,128)(2,1)S(1)}, bf16[2,3,64,512]{3,2,1,0:T(8,128)(2,1)S(1)}, u32[]{:S(2)}, u32[]{:S(2)}) collective-permute-start(bf16[2,3,64,512]{3,2,1,0:T(8,128)(2,1)S(1)} %select_convert_fusion), channel_id=1, source_target_pairs={{0,4},{4,0},{8,12},{12,8},{16,20},{20,16},{24,28},{28,24},{1,5},{5... | collective-permute-start | bytes 1179656 | tf_op jit(solution)/shard_map/ppermute | solution.py:59
  131.2 18.4 %collective-permute-start.38 = (bf16[3,64,1024]{2,1,0:T(8,128)(2,1)S(1)}, bf16[3,64,1024]{2,1,0:T(8,128)(2,1)S(1)}, u32[]{:S(2)}, u32[]{:S(2)}) collective-permute-start(bf16[3,64,1024]{2,1,0:T(8,128)(2,1)S(1)} %collective-permute-done.37), channel_id=1, source_target_pairs={{1,0},{2,3},{5,4},{6,7},{9,8},{10,11},{13,12},{14,15},{17,16},{18,... | collective-permute-start | bytes 1179656 | tf_op jit(solution)/shard_map/ppermute | solution.py:156
  134.7 24.3 %collective-permute-start.41 = (bf16[3,64,1024]{2,1,0:T(8,128)(2,1)S(1)}, bf16[3,64,1024]{2,1,0:T(8,128)(2,1)S(1)}, u32[]{:S(2)}, u32[]{:S(2)}) collective-permute-start(bf16[3,64,1024]{2,1,0:T(8,128)(2,1)S(1)} %pad_maximum_fusion.16), channel_id=1, source_target_pairs={{1,2},{2,1},{5,6},{6,5},{9,10},{10,9},{13,14},{14,13},{17,18},{18,... | collective-permute-start | bytes 1179656 | tf_op jit(solution)/shard_map/ppermute | solution.py:163
  135.4 35.5 %collective-permute-start.43 = (bf16[3,64,1024]{2,1,0:T(8,128)(2,1)S(1)}, bf16[3,64,1024]{2,1,0:T(8,128)(2,1)S(1)}, u32[]{:S(2)}, u32[]{:S(2)}) collective-permute-start(bf16[3,64,1024]{2,1,0:T(8,128)(2,1)S(1)} %pad_maximum_fusion.16), channel_id=1, source_target_pairs={{1,0},{2,3},{5,4},{6,7},{9,8},{10,11},{13,12},{14,15},{17,16},{18,... | collective-permute-start | bytes 1179656 | tf_op jit(solution)/shard_map/ppermute | solution.py:156
  159.1 11.7 %collective-permute-start.42 = (bf16[3,64,1024]{2,1,0:T(8,128)(2,1)S(1)}, bf16[3,64,1024]{2,1,0:T(8,128)(2,1)S(1)}, u32[]{:S(2)}, u32[]{:S(2)}) collective-permute-start(bf16[3,64,1024]{2,1,0:T(8,128)(2,1)S(1)} %broadcast_select_fusion), channel_id=1, source_target_pairs={{1,0},{2,3},{5,4},{6,7},{9,8},{10,11},{13,12},{14,15},{17,16},{18,... | collective-permute-start | bytes 1179656 | tf_op jit(solution)/shard_map/ppermute | solution.py:156
  (25 other events, 187.5 us)

commit v9 on v8

--- a/solution.py
+++ b/solution.py
@@ -222,16 +222,15 @@
             group, place = (groups[0], i) if i < first else (groups[1], i - first)
             x, g = group[which][0, place], group[which][1, place]
             if s > 0:
-                other = came[max(s - LAG, 0)] if s > 1 else messages[0][2:]
+                other = acts[i - 2] if i > 1 else middle if i == 1 else messages[0][2:]
                 x, g = after(x, other), after(g, other)
             parts = [dot(x, gate_weight, 1, 0), dot(x, up_weight, 1, 0), dot(g, down_weight, 1, 1)]
             message = jnp.stack(parts).astype(BF16)
             messages.append(inward(after(message, came[0]) if s == 1 else message))
         if s == steps + LAG - 1 and split > 0:
             low, high = leave([done(i) for i in range(split)])
-            sums, early, ahead = scatter_dp(low, high)
-            ends.append(rotate_by_halves(sums.reshape(2, -1, width), bits))
-            outs[-1] = after(outs[-1], early)
+            first_sums, ahead, _ = scatter_dp(low, high)
+            outs[-1] = after(outs[-1], ahead)
         came.append(
             swap(
                 messages[s] if s < steps else None,
@@ -255,7 +254,9 @@
                 crossed.append(across(acts[i]))
                 outs += [acts[i], crossed[i]]
     low, high = leave([done(i) for i in range(split, chunks)])
-    high = after(high, ahead) if split > 0 else high
+    if split > 0:
+        first_sums = after(first_sums.reshape(2, -1, width), came[-1])
+        ends.append(rotate_by_halves(first_sums, bits))
     sums, _, _ = scatter_dp(low, high)
     ends.append(rotate(spread(sums.reshape(2, -1, width).astype(BF16)), signs))
     ends = jnp.concatenate(ends, axis=1)

time: 193 us -> 201 us (1.041)
  waiting for transfers between devices: 57.4 us -> 68.7 us
  starting transfers between devices: 94.1 us -> 91 us
    ppermute x28, waiting for transfers between devices: 27.9 us -> 16.6 us  [exchange(): return lax.ppermute(block, axis, [(i, i ^ apart) for i in range(count)])]
    ppermute x3, waiting for transfers between devices: 5.49 us -> 15 us  [swap(): return lax.ppermute(into, 'tensor', pairs)]
    ppermute x7, waiting for transfers between devices: 11.1 us -> 19.3 us  [swap(): return lax.ppermute(block, 'tensor', pairs + back)]
    ppermute x7, starting transfers between devices: 43.9 us -> 38.9 us  [swap(): return lax.ppermute(block, 'tensor', pairs + back)]
    ppermute x3, waiting for transfers between devices: 12.9 us -> 17.8 us  [swap(): return lax.ppermute(out, 'tensor', back)]
  transfers between devices with their start and end apart: 51 -> 51, of which waited for: 20 -> 23; matrix products, arithmetic and copies ran while one was open for 16% -> 14% of each run, Pallas kernels for 0% -> 0%
where the time goes in v9:
time: 201 us; the launch traced here: 200 us
  starting transfers between devices  91 us (45%)
  waiting for transfers between devices  68.7 us (34%)
  matrix products  26.8 us (13%)
  other arithmetic  10.3 us (5%)
    ppermute x7, starting transfers between devices, swap(): return lax.ppermute(block, 'tensor', pairs + back)  38.9 us
    ppermute x28, starting transfers between devices, exchange(): return lax.ppermute(block, axis, [(i, i ^ apart) for i in range(count)])  30.7 us
    dot_general x56, matrix products, dot(): lax.dot_general(left, right, (((left_dim,), (right_dim,)), ((), ())), pre...  26.8 us
    ppermute x7, waiting for transfers between devices, swap(): return lax.ppermute(block, 'tensor', pairs + back)  19.3 us
    ppermute x3, waiting for transfers between devices, swap(): return lax.ppermute(out, 'tensor', back)  17.8 us
    ppermute x28, waiting for transfers between devices, exchange(): return lax.ppermute(block, axis, [(i, i ^ apart) for i in range(count)])  16.6 us
    ppermute x3, waiting for transfers between devices, swap(): return lax.ppermute(into, 'tensor', pairs)  15 us
    ppermute x3, starting transfers between devices, swap(): return lax.ppermute(into, 'tensor', pairs)  10.2 us
  transfers between devices with their start and end apart: 51, of which 23 were waited for; matrix products, arithmetic and copies ran while one was open for 14% of the time, Pallas kernels for 0%

profile of v9, /device:TPU:0, one launch (start us, length us, event | category | flops | bytes accessed | tf_op | source)
XLA Modules:
  0.0 199.9 jit_solution(14802730606555371589)
XLA Ops:
  1.5 5.0 %collective-permute-start.2 = (bf16[2,32,512]{2,1,0:T(8,128)(2,1)S(1)}, bf16[2,32,512]{2,1,0:T(8,128)(2,1)S(1)}, u32[]{:S(2)}, u32[]{:S(2)}) collective-permute-start(bf16[2,32,512]{2,1,0:T(8,128)(2,1)S(1)} %pad_maximum_fusion.26), channel_id=1, source_target_pairs={{0,3},{1,2},{2,1},{3,0},{4,7},{5,6},{6,5},{7,4},{8,11},{9,10},{10,... | collective-permute-start | bytes 196616 | tf_op jit(solution)/shard_map/ppermute | solution.py:59
  9.2 3.0 %collective-permute-done.1 = bf16[2,32,512]{2,1,0:T(8,128)(2,1)S(1)} collective-permute-done((bf16[2,32,512]{2,1,0:T(8,128)(2,1)S(1)}, bf16[2,32,512]{2,1,0:T(8,128)(2,1)S(1)}, u32[]{:S(2)}, u32[]{:S(2)}) %collective-permute-start.1) | collective-permute-done | bytes 65568 | tf_op jit(solution)/shard_map/ppermute | solution.py:59
  15.7 2.5 %collective-permute-start.5 = (bf16[2,2,1,16,512]{4,3,2,1,0:T(8,128)(2,1)S(1)}, bf16[2,2,1,16,512]{4,3,2,1,0:T(8,128)(2,1)S(1)}, u32[]{:S(2)}, u32[]{:S(2)}) collective-permute-start(bf16[2,2,1,16,512]{4,3,2,1,0:T(8,128)(2,1)S(1)} %bitcast.554), channel_id=1, source_target_pairs={{0,24},{4,28},{8,16},{12,20},{16,8},{20,12},{24,0},{28,4},{1,25},{... | collective-permute-start | bytes 196616 | tf_op jit(solution)/shard_map/ppermute | solution.py:59
  19.2 1.7 collective-permute-done.5
  23.1 2.8 %collective-permute-start.14 = (bf16[2,48,512]{2,1,0:T(8,128)(2,1)S(1)}, bf16[2,48,512]{2,1,0:T(8,128)(2,1)S(1)}, u32[]{:S(2)}, u32[]{:S(2)}) collective-permute-start(bf16[2,48,512]{2,1,0:T(8,128)(2,1)S(1)} %fusion.107), channel_id=1, source_target_pairs={{0,3},{1,2},{2,1},{3,0},{4,7},{5,6},{6,5},{7,4},{8,11},{9,10},{10,... | collective-permute-start | bytes 294920 | tf_op jit(solution)/shard_map/ppermute | solution.py:59
  25.9 1.7 collective-permute-start.12
  29.9 2.4 %collective-permute-start.7 = (bf16[3,64,1024]{2,1,0:T(8,128)(2,1)S(1)}, bf16[3,64,1024]{2,1,0:T(8,128)(2,1)S(1)}, u32[]{:S(2)}, u32[]{:S(2)}) collective-permute-start(bf16[3,64,1024]{2,1,0:T(8,128)(2,1)S(1)} %pad_maximum_fusion.2), channel_id=1, source_target_pairs={{0,1},{3,2},{4,5},{7,6},{8,9},{11,10},{12,13},{15,14},{16,17},{19,... | collective-permute-start | bytes 1179656 | tf_op jit(solution)/shard_map/ppermute | solution.py:154
  33.6 1.6 collective-permute-done.13
  39.4 1.9 collective-permute-done.7
  43.3 6.5 %collective-permute-start.20 = (bf16[3,64,1024]{2,1,0:T(8,128)(2,1)S(1)}, bf16[3,64,1024]{2,1,0:T(8,128)(2,1)S(1)}, u32[]{:S(2)}, u32[]{:S(2)}) collective-permute-start(bf16[3,64,1024]{2,1,0:T(8,128)(2,1)S(1)} %pad_maximum_fusion.6), channel_id=1, source_target_pairs={{0,1},{3,2},{4,5},{7,6},{8,9},{11,10},{12,13},{15,14},{16,17},{19,... | collective-permute-start | bytes 1179656 | tf_op jit(solution)/shard_map/ppermute | solution.py:154
  51.5 7.8 %collective-permute-done.20 = bf16[3,64,1024]{2,1,0:T(8,128)(2,1)S(1)} collective-permute-done((bf16[3,64,1024]{2,1,0:T(8,128)(2,1)S(1)}, bf16[3,64,1024]{2,1,0:T(8,128)(2,1)S(1)}, u32[]{:S(2)}, u32[]{:S(2)}) %collective-permute-start.20) | collective-permute-done | bytes 393248 | tf_op jit(solution)/shard_map/ppermute | solution.py:154
  60.3 5.3 %collective-permute-done.8 = bf16[3,64,1024]{2,1,0:T(8,128)(2,1)S(1)} collective-permute-done((bf16[3,64,1024]{2,1,0:T(8,128)(2,1)S(1)}, bf16[3,64,1024]{2,1,0:T(8,128)(2,1)S(1)}, u32[]{:S(2)}, u32[]{:S(2)}) %collective-permute-start.8) | collective-permute-done | bytes 393248 | tf_op jit(solution)/shard_map/ppermute | solution.py:154
  68.9 7.0 %collective-permute-start.21 = (bf16[3,64,1024]{2,1,0:T(8,128)(2,1)S(1)}, bf16[3,64,1024]{2,1,0:T(8,128)(2,1)S(1)}, u32[]{:S(2)}, u32[]{:S(2)}) collective-permute-start(bf16[3,64,1024]{2,1,0:T(8,128)(2,1)S(1)} %get-tuple-element.58), channel_id=1, source_target_pairs={{0,1},{3,2},{1,0},{2,3},{4,5},{7,6},{5,4},{6,7},{8,9},{11,10},{9,8... | collective-permute-start | bytes 1179656 | tf_op jit(solution)/shard_map/ppermute | solution.py:158
  77.0 5.9 %collective-permute-done.21 = bf16[3,64,1024]{2,1,0:T(8,128)(2,1)S(1)} collective-permute-done((bf16[3,64,1024]{2,1,0:T(8,128)(2,1)S(1)}, bf16[3,64,1024]{2,1,0:T(8,128)(2,1)S(1)}, u32[]{:S(2)}, u32[]{:S(2)}) %collective-permute-start.21) | collective-permute-done | bytes 393248 | tf_op jit(solution)/shard_map/ppermute | solution.py:158
  85.7 7.1 %collective-permute-start.19 = (bf16[3,64,1024]{2,1,0:T(8,128)(2,1)S(1)}, bf16[3,64,1024]{2,1,0:T(8,128)(2,1)S(1)}, u32[]{:S(2)}, u32[]{:S(2)}) collective-permute-start(bf16[3,64,1024]{2,1,0:T(8,128)(2,1)S(1)} %broadcast_select_fusion.9), channel_id=1, source_target_pairs={{0,1},{3,2},{1,0},{2,3},{4,5},{7,6},{5,4},{6,7},{8,9},{11,10},{9,8... | collective-permute-start | bytes 1179656 | tf_op jit(solution)/shard_map/ppermute | solution.py:158
  93.6 4.5 %collective-permute-start.24 = (bf16[3,64,1024]{2,1,0:T(8,128)(2,1)S(1)}, bf16[3,64,1024]{2,1,0:T(8,128)(2,1)S(1)}, u32[]{:S(2)}, u32[]{:S(2)}) collective-permute-start(bf16[3,64,1024]{2,1,0:T(8,128)(2,1)S(1)} %broadcast_select_fusion.3), channel_id=1, source_target_pairs={{0,1},{3,2},{1,0},{2,3},{4,5},{7,6},{5,4},{6,7},{8,9},{11,10},{9,8... | collective-permute-start | bytes 1179656 | tf_op jit(solution)/shard_map/ppermute | solution.py:158
  98.1 4.7 %collective-permute-done.19 = bf16[3,64,1024]{2,1,0:T(8,128)(2,1)S(1)} collective-permute-done((bf16[3,64,1024]{2,1,0:T(8,128)(2,1)S(1)}, bf16[3,64,1024]{2,1,0:T(8,128)(2,1)S(1)}, u32[]{:S(2)}, u32[]{:S(2)}) %collective-permute-start.19) | collective-permute-done | bytes 393248 | tf_op jit(solution)/shard_map/ppermute | solution.py:158
  105.5 3.9 %collective-permute-done.25 = bf16[3,64,1024]{2,1,0:T(8,128)(2,1)S(1)} collective-permute-done((bf16[3,64,1024]{2,1,0:T(8,128)(2,1)S(1)}, bf16[3,64,1024]{2,1,0:T(8,128)(2,1)S(1)}, u32[]{:S(2)}, u32[]{:S(2)}) %collective-permute-start.25) | collective-permute-done | bytes 393248 | tf_op jit(solution)/shard_map/ppermute | solution.py:158
  111.6 2.0 %collective-permute-done.24 = bf16[3,64,1024]{2,1,0:T(8,128)(2,1)S(1)} collective-permute-done((bf16[3,64,1024]{2,1,0:T(8,128)(2,1)S(1)}, bf16[3,64,1024]{2,1,0:T(8,128)(2,1)S(1)}, u32[]{:S(2)}, u32[]{:S(2)}) %collective-permute-start.24) | collective-permute-done | bytes 393248 | tf_op jit(solution)/shard_map/ppermute | solution.py:158
  115.6 6.2 %collective-permute-start.29 = (bf16[3,64,1024]{2,1,0:T(8,128)(2,1)S(1)}, bf16[3,64,1024]{2,1,0:T(8,128)(2,1)S(1)}, u32[]{:S(2)}, u32[]{:S(2)}) collective-permute-start(bf16[3,64,1024]{2,1,0:T(8,128)(2,1)S(1)} %get-tuple-element.54), channel_id=1, source_target_pairs={{0,1},{3,2},{1,0},{2,3},{4,5},{7,6},{5,4},{6,7},{8,9},{11,10},{9,8... | collective-permute-start | bytes 1179656 | tf_op jit(solution)/shard_map/ppermute | solution.py:158
  123.5 4.4 %collective-permute-start.28 = (bf16[3,64,1024]{2,1,0:T(8,128)(2,1)S(1)}, bf16[3,64,1024]{2,1,0:T(8,128)(2,1)S(1)}, u32[]{:S(2)}, u32[]{:S(2)}) collective-permute-start(bf16[3,64,1024]{2,1,0:T(8,128)(2,1)S(1)} %broadcast_select_fusion.8), channel_id=1, source_target_pairs={{0,1},{3,2},{1,0},{2,3},{4,5},{7,6},{5,4},{6,7},{8,9},{11,10},{9,8... | collective-permute-start | bytes 1179656 | tf_op jit(solution)/shard_map/ppermute | solution.py:158
  130.1 9.6 %collective-permute-start.32 = (bf16[3,64,1024]{2,1,0:T(8,128)(2,1)S(1)}, bf16[3,64,1024]{2,1,0:T(8,128)(2,1)S(1)}, u32[]{:S(2)}, u32[]{:S(2)}) collective-permute-start(bf16[3,64,1024]{2,1,0:T(8,128)(2,1)S(1)} %get-tuple-element.50), channel_id=1, source_target_pairs={{0,1},{3,2},{1,0},{2,3},{4,5},{7,6},{5,4},{6,7},{8,9},{11,10},{9,8... | collective-permute-start | bytes 1179656 | tf_op jit(solution)/shard_map/ppermute | solution.py:158
  143.9 1.6 collective-permute-done.32
  150.3 6.7 %collective-permute-done.42 = bf16[3,64,1024]{2,1,0:T(8,128)(2,1)S(1)} collective-permute-done((bf16[3,64,1024]{2,1,0:T(8,128)(2,1)S(1)}, bf16[3,64,1024]{2,1,0:T(8,128)(2,1)S(1)}, u32[]{:S(2)}, u32[]{:S(2)}) %collective-permute-start.42) | collective-permute-done | bytes 393248 | tf_op jit(solution)/shard_map/ppermute | solution.py:156
  161.7 11.1 %collective-permute-done.35 = bf16[3,64,1024]{2,1,0:T(8,128)(2,1)S(1)} collective-permute-done((bf16[3,64,1024]{2,1,0:T(8,128)(2,1)S(1)}, bf16[3,64,1024]{2,1,0:T(8,128)(2,1)S(1)}, u32[]{:S(2)}, u32[]{:S(2)}) %collective-permute-start.35) | collective-permute-done | bytes 393248 | tf_op jit(solution)/shard_map/ppermute | solution.py:156
  175.1 2.0 multiply_convert_fusion.2
  177.1 2.0 %multiply_convert_fusion = bf16[1024,512]{1,0:T(8,128)(2,1)} fusion(bf16[3,640,1024]{2,1,0:T(8,128)(2,1)S(1)} %get-tuple-element.10, bf16[2,640,512]{2,1,0:T(8,128)(2,1)S(1)} %maximum_select_fusion), kind=kOutput, calls=%fused_computation | convolution fusion | flops 672137216 | bytes 3014656 | tf_op jit(solution)/shard_map/dot_general | solution.py:25
  179.7 2.0 multiply_convert_fusion.1
  185.5 2.4 %collective-permute-start.40 = (bf16[2,48,512]{2,1,0:T(8,128)(2,1)S(1)}, bf16[2,48,512]{2,1,0:T(8,128)(2,1)S(1)}, u32[]{:S(2)}, u32[]{:S(2)}) collective-permute-start(bf16[2,48,512]{2,1,0:T(8,128)(2,1)S(1)} %fusion.106), channel_id=1, source_target_pairs={{0,2},{1,3},{2,0},{3,1},{4,6},{5,7},{6,4},{7,5},{8,10},{9,11},{10,... | collective-permute-start | bytes 294920 | tf_op jit(solution)/shard_map/ppermute | solution.py:59
  188.8 1.9 collective-permute-start.50
  193.4 2.3 %collective-permute-done.50 = bf16[2,32,512]{2,1,0:T(8,128)(2,1)S(1)} collective-permute-done((bf16[2,32,512]{2,1,0:T(8,128)(2,1)S(1)}, bf16[2,32,512]{2,1,0:T(8,128)(2,1)S(1)}, u32[]{:S(2)}, u32[]{:S(2)}) %collective-permute-start.50) | collective-permute-done | bytes 65568 | tf_op jit(solution)/shard_map/ppermute | solution.py:59
  195.7 2.9 %collective-permute-done.49 = bf16[2,32,512]{2,1,0:T(8,128)(2,1)S(1)} collective-permute-done((bf16[2,32,512]{2,1,0:T(8,128)(2,1)S(1)}, bf16[2,32,512]{2,1,0:T(8,128)(2,1)S(1)}, u32[]{:S(2)}, u32[]{:S(2)}) %collective-permute-start.49) | collective-permute-done | bytes 65568 | tf_op jit(solution)/shard_map/ppermute | solution.py:59
  (240 shorter events, 65.2 us)
Async XLA Ops:
  1.5 7.6 %collective-permute-start.2 = (bf16[2,32,512]{2,1,0:T(8,128)(2,1)S(1)}, bf16[2,32,512]{2,1,0:T(8,128)(2,1)S(1)}, u32[]{:S(2)}, u32[]{:S(2)}) collective-permute-start(bf16[2,32,512]{2,1,0:T(8,128)(2,1)S(1)} %pad_maximum_fusion.26), channel_id=1, source_target_pairs={{0,3},{1,2},{2,1},{3,0},{4,7},{5,6},{6,5},{7,4},{8,11},{9,10},{10,... | collective-permute-start | bytes 196616 | tf_op jit(solution)/shard_map/ppermute | solution.py:59
  23.1 10.5 %collective-permute-start.14 = (bf16[2,48,512]{2,1,0:T(8,128)(2,1)S(1)}, bf16[2,48,512]{2,1,0:T(8,128)(2,1)S(1)}, u32[]{:S(2)}, u32[]{:S(2)}) collective-permute-start(bf16[2,48,512]{2,1,0:T(8,128)(2,1)S(1)} %fusion.107), channel_id=1, source_target_pairs={{0,3},{1,2},{2,1},{3,0},{4,7},{5,6},{6,5},{7,4},{8,11},{9,10},{10,... | collective-permute-start | bytes 294920 | tf_op jit(solution)/shard_map/ppermute | solution.py:59
  25.9 9.3 %collective-permute-start.13 = (bf16[2,48,512]{2,1,0:T(8,128)(2,1)S(1)}, bf16[2,48,512]{2,1,0:T(8,128)(2,1)S(1)}, u32[]{:S(2)}, u32[]{:S(2)}) collective-permute-start(bf16[2,48,512]{2,1,0:T(8,128)(2,1)S(1)} %fusion.107), channel_id=1, source_target_pairs={{0,2},{1,3},{2,0},{3,1},{4,6},{5,7},{6,4},{7,5},{8,10},{9,11},{10,... | collective-permute-start | bytes 294920 | tf_op jit(solution)/shard_map/ppermute | solution.py:59
  25.9 9.3 %collective-permute-start.12 = (bf16[2,48,512]{2,1,0:T(8,128)(2,1)S(1)}, bf16[2,48,512]{2,1,0:T(8,128)(2,1)S(1)}, u32[]{:S(2)}, u32[]{:S(2)}) collective-permute-start(bf16[2,48,512]{2,1,0:T(8,128)(2,1)S(1)} %fusion.107), channel_id=1, source_target_pairs={{0,1},{1,0},{2,3},{3,2},{4,5},{5,4},{6,7},{7,6},{8,9},{9,8},{10,11... | collective-permute-start | bytes 294920 | tf_op jit(solution)/shard_map/ppermute | solution.py:59
  29.9 11.4 %collective-permute-start.7 = (bf16[3,64,1024]{2,1,0:T(8,128)(2,1)S(1)}, bf16[3,64,1024]{2,1,0:T(8,128)(2,1)S(1)}, u32[]{:S(2)}, u32[]{:S(2)}) collective-permute-start(bf16[3,64,1024]{2,1,0:T(8,128)(2,1)S(1)} %pad_maximum_fusion.2), channel_id=1, source_target_pairs={{0,1},{3,2},{4,5},{7,6},{8,9},{11,10},{12,13},{15,14},{16,17},{19,... | collective-permute-start | bytes 1179656 | tf_op jit(solution)/shard_map/ppermute | solution.py:154
  35.9 14.2 %collective-permute-start.17 = (bf16[2,3,1,16,512]{4,3,2,1,0:T(8,128)(2,1)S(1)}, bf16[2,3,1,16,512]{4,3,2,1,0:T(8,128)(2,1)S(1)}, u32[]{:S(2)}, u32[]{:S(2)}) collective-permute-start(bf16[2,3,1,16,512]{4,3,2,1,0:T(8,128)(2,1)S(1)} %bitcast.561), channel_id=1, source_target_pairs={{0,24},{4,28},{8,16},{12,20},{16,8},{20,12},{24,0},{28,4},{1,25},{... | collective-permute-start | bytes 294920 | tf_op jit(solution)/shard_map/ppermute | solution.py:59
  37.4 14.0 %collective-permute-start.16 = (bf16[2,3,1,16,512]{4,3,2,1,0:T(8,128)(2,1)S(1)}, bf16[2,3,1,16,512]{4,3,2,1,0:T(8,128)(2,1)S(1)}, u32[]{:S(2)}, u32[]{:S(2)}) collective-permute-start(bf16[2,3,1,16,512]{4,3,2,1,0:T(8,128)(2,1)S(1)} %bitcast.562), channel_id=1, source_target_pairs={{0,16},{4,20},{8,24},{12,28},{16,0},{20,4},{24,8},{28,12},{1,17},{... | collective-permute-start | bytes 294920 | tf_op jit(solution)/shard_map/ppermute | solution.py:59
  37.9 13.5 %collective-permute-start.15 = (bf16[2,3,1,16,512]{4,3,2,1,0:T(8,128)(2,1)S(1)}, bf16[2,3,1,16,512]{4,3,2,1,0:T(8,128)(2,1)S(1)}, u32[]{:S(2)}, u32[]{:S(2)}) collective-permute-start(bf16[2,3,1,16,512]{4,3,2,1,0:T(8,128)(2,1)S(1)} %bitcast.563), channel_id=1, source_target_pairs={{0,8},{4,12},{8,0},{12,4},{16,24},{20,28},{24,16},{28,20},{1,9},{5... | collective-permute-start | bytes 294920 | tf_op jit(solution)/shard_map/ppermute | solution.py:59
  42.5 17.7 %collective-permute-start.9 = (bf16[3,64,1024]{2,1,0:T(8,128)(2,1)S(1)}, bf16[3,64,1024]{2,1,0:T(8,128)(2,1)S(1)}, u32[]{:S(2)}, u32[]{:S(2)}) collective-permute-start(bf16[3,64,1024]{2,1,0:T(8,128)(2,1)S(1)} %add_convert_fusion.4), channel_id=1, source_target_pairs={{1,2},{2,1},{5,6},{6,5},{9,10},{10,9},{13,14},{14,13},{17,18},{18,... | collective-permute-start | bytes 1179656 | tf_op jit(solution)/shard_map/ppermute | solution.py:163
  43.3 16.0 %collective-permute-start.20 = (bf16[3,64,1024]{2,1,0:T(8,128)(2,1)S(1)}, bf16[3,64,1024]{2,1,0:T(8,128)(2,1)S(1)}, u32[]{:S(2)}, u32[]{:S(2)}) collective-permute-start(bf16[3,64,1024]{2,1,0:T(8,128)(2,1)S(1)} %pad_maximum_fusion.6), channel_id=1, source_target_pairs={{0,1},{3,2},{4,5},{7,6},{8,9},{11,10},{12,13},{15,14},{16,17},{19,... | collective-permute-start | bytes 1179656 | tf_op jit(solution)/shard_map/ppermute | solution.py:154
  50.1 15.5 %collective-permute-start.8 = (bf16[3,64,1024]{2,1,0:T(8,128)(2,1)S(1)}, bf16[3,64,1024]{2,1,0:T(8,128)(2,1)S(1)}, u32[]{:S(2)}, u32[]{:S(2)}) collective-permute-start(bf16[3,64,1024]{2,1,0:T(8,128)(2,1)S(1)} %maximum_select_fusion.1), channel_id=1, source_target_pairs={{0,1},{3,2},{4,5},{7,6},{8,9},{11,10},{12,13},{15,14},{16,17},{19,... | collective-permute-start | bytes 1179656 | tf_op jit(solution)/shard_map/ppermute | solution.py:154
  51.5 14.8 %collective-permute-start.18 = (bf16[2,3,4,16,512]{4,3,2,1,0:T(8,128)(2,1)S(1)}, bf16[2,3,4,16,512]{4,3,2,1,0:T(8,128)(2,1)S(1)}, u32[]{:S(2)}, u32[]{:S(2)}) collective-permute-start(bf16[2,3,4,16,512]{4,3,2,1,0:T(8,128)(2,1)S(1)} %pad_maximum_fusion.4), channel_id=1, source_target_pairs={{0,4},{4,0},{8,12},{12,8},{16,20},{20,16},{24,28},{28,24},{1,5},{5... | collective-permute-start | bytes 1179656 | tf_op jit(solution)/shard_map/ppermute | solution.py:59
  67.4 15.6 %collective-permute-start.22 = (bf16[3,64,1024]{2,1,0:T(8,128)(2,1)S(1)}, bf16[3,64,1024]{2,1,0:T(8,128)(2,1)S(1)}, u32[]{:S(2)}, u32[]{:S(2)}) collective-permute-start(bf16[3,64,1024]{2,1,0:T(8,128)(2,1)S(1)} %add_convert_fusion.3), channel_id=1, source_target_pairs={{1,2},{2,1},{5,6},{6,5},{9,10},{10,9},{13,14},{14,13},{17,18},{18,... | collective-permute-start | bytes 1179656 | tf_op jit(solution)/shard_map/ppermute | solution.py:163
  68.2 17.0 %collective-permute-start.10 = (bf16[3,64,1024]{2,1,0:T(8,128)(2,1)S(1)}, bf16[3,64,1024]{2,1,0:T(8,128)(2,1)S(1)}, u32[]{:S(2)}, u32[]{:S(2)}) collective-permute-start(bf16[3,64,1024]{2,1,0:T(8,128)(2,1)S(1)} %get-tuple-element.59), channel_id=1, source_target_pairs={{1,2},{2,1},{5,6},{6,5},{9,10},{10,9},{13,14},{14,13},{17,18},{18,... | collective-permute-start | bytes 1179656 | tf_op jit(solution)/shard_map/ppermute | solution.py:163
  68.9 14.1 %collective-permute-start.21 = (bf16[3,64,1024]{2,1,0:T(8,128)(2,1)S(1)}, bf16[3,64,1024]{2,1,0:T(8,128)(2,1)S(1)}, u32[]{:S(2)}, u32[]{:S(2)}) collective-permute-start(bf16[3,64,1024]{2,1,0:T(8,128)(2,1)S(1)} %get-tuple-element.58), channel_id=1, source_target_pairs={{0,1},{3,2},{1,0},{2,3},{4,5},{7,6},{5,4},{6,7},{8,9},{11,10},{9,8... | collective-permute-start | bytes 1179656 | tf_op jit(solution)/shard_map/ppermute | solution.py:158
  83.4 10.1 %collective-permute-start.23 = (bf16[3,64,1024]{2,1,0:T(8,128)(2,1)S(1)}, bf16[3,64,1024]{2,1,0:T(8,128)(2,1)S(1)}, u32[]{:S(2)}, u32[]{:S(2)}) collective-permute-start(bf16[3,64,1024]{2,1,0:T(8,128)(2,1)S(1)} %get-tuple-element.57), channel_id=1, source_target_pairs={{1,2},{2,1},{5,6},{6,5},{9,10},{10,9},{13,14},{14,13},{17,18},{18,... | collective-permute-start | bytes 1179656 | tf_op jit(solution)/shard_map/ppermute | solution.py:163
  85.7 17.1 %collective-permute-start.19 = (bf16[3,64,1024]{2,1,0:T(8,128)(2,1)S(1)}, bf16[3,64,1024]{2,1,0:T(8,128)(2,1)S(1)}, u32[]{:S(2)}, u32[]{:S(2)}) collective-permute-start(bf16[3,64,1024]{2,1,0:T(8,128)(2,1)S(1)} %broadcast_select_fusion.9), channel_id=1, source_target_pairs={{0,1},{3,2},{1,0},{2,3},{4,5},{7,6},{5,4},{6,7},{8,9},{11,10},{9,8... | collective-permute-start | bytes 1179656 | tf_op jit(solution)/shard_map/ppermute | solution.py:158
  92.8 16.6 %collective-permute-start.25 = (bf16[3,64,1024]{2,1,0:T(8,128)(2,1)S(1)}, bf16[3,64,1024]{2,1,0:T(8,128)(2,1)S(1)}, u32[]{:S(2)}, u32[]{:S(2)}) collective-permute-start(bf16[3,64,1024]{2,1,0:T(8,128)(2,1)S(1)} %get-tuple-element.56), channel_id=1, source_target_pairs={{0,1},{3,2},{1,0},{2,3},{4,5},{7,6},{5,4},{6,7},{8,9},{11,10},{9,8... | collective-permute-start | bytes 1179656 | tf_op jit(solution)/shard_map/ppermute | solution.py:158
  93.6 20.1 %collective-permute-start.24 = (bf16[3,64,1024]{2,1,0:T(8,128)(2,1)S(1)}, bf16[3,64,1024]{2,1,0:T(8,128)(2,1)S(1)}, u32[]{:S(2)}, u32[]{:S(2)}) collective-permute-start(bf16[3,64,1024]{2,1,0:T(8,128)(2,1)S(1)} %broadcast_select_fusion.3), channel_id=1, source_target_pairs={{0,1},{3,2},{1,0},{2,3},{4,5},{7,6},{5,4},{6,7},{8,9},{11,10},{9,8... | collective-permute-start | bytes 1179656 | tf_op jit(solution)/shard_map/ppermute | solution.py:158
  114.9 8.5 %collective-permute-start.27 = (bf16[3,64,1024]{2,1,0:T(8,128)(2,1)S(1)}, bf16[3,64,1024]{2,1,0:T(8,128)(2,1)S(1)}, u32[]{:S(2)}, u32[]{:S(2)}) collective-permute-start(bf16[3,64,1024]{2,1,0:T(8,128)(2,1)S(1)} %get-tuple-element.55), channel_id=1, source_target_pairs={{1,2},{2,1},{5,6},{6,5},{9,10},{10,9},{13,14},{14,13},{17,18},{18,... | collective-permute-start | bytes 1179656 | tf_op jit(solution)/shard_map/ppermute | solution.py:163
  115.6 13.3 %collective-permute-start.29 = (bf16[3,64,1024]{2,1,0:T(8,128)(2,1)S(1)}, bf16[3,64,1024]{2,1,0:T(8,128)(2,1)S(1)}, u32[]{:S(2)}, u32[]{:S(2)}) collective-permute-start(bf16[3,64,1024]{2,1,0:T(8,128)(2,1)S(1)} %get-tuple-element.54), channel_id=1, source_target_pairs={{0,1},{3,2},{1,0},{2,3},{4,5},{7,6},{5,4},{6,7},{8,9},{11,10},{9,8... | collective-permute-start | bytes 1179656 | tf_op jit(solution)/shard_map/ppermute | solution.py:158
  123.5 16.2 %collective-permute-start.28 = (bf16[3,64,1024]{2,1,0:T(8,128)(2,1)S(1)}, bf16[3,64,1024]{2,1,0:T(8,128)(2,1)S(1)}, u32[]{:S(2)}, u32[]{:S(2)}) collective-permute-start(bf16[3,64,1024]{2,1,0:T(8,128)(2,1)S(1)} %broadcast_select_fusion.8), channel_id=1, source_target_pairs={{0,1},{3,2},{1,0},{2,3},{4,5},{7,6},{5,4},{6,7},{8,9},{11,10},{9,8... | collective-permute-start | bytes 1179656 | tf_op jit(solution)/shard_map/ppermute | solution.py:158
  129.4 13.1 %collective-permute-start.41 = (bf16[3,64,1024]{2,1,0:T(8,128)(2,1)S(1)}, bf16[3,64,1024]{2,1,0:T(8,128)(2,1)S(1)}, u32[]{:S(2)}, u32[]{:S(2)}) collective-permute-start(bf16[3,64,1024]{2,1,0:T(8,128)(2,1)S(1)} %get-tuple-element.49), channel_id=1, source_target_pairs={{1,2},{2,1},{5,6},{6,5},{9,10},{10,9},{13,14},{14,13},{17,18},{18,... | collective-permute-start | bytes 1179656 | tf_op jit(solution)/shard_map/ppermute | solution.py:163
  130.1 15.4 %collective-permute-start.32 = (bf16[3,64,1024]{2,1,0:T(8,128)(2,1)S(1)}, bf16[3,64,1024]{2,1,0:T(8,128)(2,1)S(1)}, u32[]{:S(2)}, u32[]{:S(2)}) collective-permute-start(bf16[3,64,1024]{2,1,0:T(8,128)(2,1)S(1)} %get-tuple-element.50), channel_id=1, source_target_pairs={{0,1},{3,2},{1,0},{2,3},{4,5},{7,6},{5,4},{6,7},{8,9},{11,10},{9,8... | collective-permute-start | bytes 1179656 | tf_op jit(solution)/shard_map/ppermute | solution.py:158
  142.6 14.5 %collective-permute-start.42 = (bf16[3,64,1024]{2,1,0:T(8,128)(2,1)S(1)}, bf16[3,64,1024]{2,1,0:T(8,128)(2,1)S(1)}, u32[]{:S(2)}, u32[]{:S(2)}) collective-permute-start(bf16[3,64,1024]{2,1,0:T(8,128)(2,1)S(1)} %collective-permute-done.41), channel_id=1, source_target_pairs={{1,0},{2,3},{5,4},{6,7},{9,8},{10,11},{13,12},{14,15},{17,16},{18,... | collective-permute-start | bytes 1179656 | tf_op jit(solution)/shard_map/ppermute | solution.py:156
  145.9 13.0 %collective-permute-start.34 = (bf16[3,64,1024]{2,1,0:T(8,128)(2,1)S(1)}, bf16[3,64,1024]{2,1,0:T(8,128)(2,1)S(1)}, u32[]{:S(2)}, u32[]{:S(2)}) collective-permute-start(bf16[3,64,1024]{2,1,0:T(8,128)(2,1)S(1)} %pad_maximum_fusion.16), channel_id=1, source_target_pairs={{1,2},{2,1},{5,6},{6,5},{9,10},{10,9},{13,14},{14,13},{17,18},{18,... | collective-permute-start | bytes 1179656 | tf_op jit(solution)/shard_map/ppermute | solution.py:163
  146.6 26.4 %collective-permute-start.43 = (bf16[3,64,1024]{2,1,0:T(8,128)(2,1)S(1)}, bf16[3,64,1024]{2,1,0:T(8,128)(2,1)S(1)}, u32[]{:S(2)}, u32[]{:S(2)}) collective-permute-start(bf16[3,64,1024]{2,1,0:T(8,128)(2,1)S(1)} %pad_maximum_fusion.16), channel_id=1, source_target_pairs={{1,0},{2,3},{5,4},{6,7},{9,8},{10,11},{13,12},{14,15},{17,16},{18,... | collective-permute-start | bytes 1179656 | tf_op jit(solution)/shard_map/ppermute | solution.py:156
  148.2 12.6 %collective-permute-start.38 = (bf16[2,3,16,512]{3,2,1,0:T(8,128)(2,1)S(1)}, bf16[2,3,16,512]{3,2,1,0:T(8,128)(2,1)S(1)}, u32[]{:S(2)}, u32[]{:S(2)}) collective-permute-start(bf16[2,3,16,512]{3,2,1,0:T(8,128)(2,1)S(1)} %get-tuple-element.52), channel_id=1, source_target_pairs={{0,24},{4,28},{8,16},{12,20},{16,8},{20,12},{24,0},{28,4},{1,25},{... | collective-permute-start | bytes 294920 | tf_op jit(solution)/shard_map/ppermute | solution.py:59
  149.8 11.1 %collective-permute-start.37 = (bf16[2,3,16,512]{3,2,1,0:T(8,128)(2,1)S(1)}, bf16[2,3,16,512]{3,2,1,0:T(8,128)(2,1)S(1)}, u32[]{:S(2)}, u32[]{:S(2)}) collective-permute-start(bf16[2,3,16,512]{3,2,1,0:T(8,128)(2,1)S(1)} %get-tuple-element.53), channel_id=1, source_target_pairs={{0,16},{4,20},{8,24},{12,28},{16,0},{20,4},{24,8},{28,12},{1,17},{... | collective-permute-start | bytes 294920 | tf_op jit(solution)/shard_map/ppermute | solution.py:59
  159.0 13.8 %collective-permute-start.35 = (bf16[3,64,1024]{2,1,0:T(8,128)(2,1)S(1)}, bf16[3,64,1024]{2,1,0:T(8,128)(2,1)S(1)}, u32[]{:S(2)}, u32[]{:S(2)}) collective-permute-start(bf16[3,64,1024]{2,1,0:T(8,128)(2,1)S(1)} %broadcast_select_fusion), channel_id=1, source_target_pairs={{1,0},{2,3},{5,4},{6,7},{9,8},{10,11},{13,12},{14,15},{17,16},{18,... | collective-permute-start | bytes 1179656 | tf_op jit(solution)/shard_map/ppermute | solution.py:156
  185.5 7.9 %collective-permute-start.40 = (bf16[2,48,512]{2,1,0:T(8,128)(2,1)S(1)}, bf16[2,48,512]{2,1,0:T(8,128)(2,1)S(1)}, u32[]{:S(2)}, u32[]{:S(2)}) collective-permute-start(bf16[2,48,512]{2,1,0:T(8,128)(2,1)S(1)} %fusion.106), channel_id=1, source_target_pairs={{0,2},{1,3},{2,0},{3,1},{4,6},{5,7},{6,4},{7,5},{8,10},{9,11},{10,... | collective-permute-start | bytes 294920 | tf_op jit(solution)/shard_map/ppermute | solution.py:59
  190.7 7.9 %collective-permute-start.49 = (bf16[2,32,512]{2,1,0:T(8,128)(2,1)S(1)}, bf16[2,32,512]{2,1,0:T(8,128)(2,1)S(1)}, u32[]{:S(2)}, u32[]{:S(2)}) collective-permute-start(bf16[2,32,512]{2,1,0:T(8,128)(2,1)S(1)} %bitcast.566), channel_id=1, source_target_pairs={{0,2},{1,3},{2,0},{3,1},{4,6},{5,7},{6,4},{7,5},{8,10},{9,11},{10,... | collective-permute-start | bytes 196616 | tf_op jit(solution)/shard_map/ppermute | solution.py:59
  (25 other events, 213.7 us)

commit v10 on v9

--- a/solution.py
+++ b/solution.py
@@ -222,7 +222,7 @@
             group, place = (groups[0], i) if i < first else (groups[1], i - first)
             x, g = group[which][0, place], group[which][1, place]
             if s > 0:
-                other = acts[i - 2] if i > 1 else middle if i == 1 else messages[0][2:]
+                other = acts[i - 2] if i > 3 else came[max(s - LAG, 0)] if s > 1 else messages[0][2:]
                 x, g = after(x, other), after(g, other)
             parts = [dot(x, gate_weight, 1, 0), dot(x, up_weight, 1, 0), dot(g, down_weight, 1, 1)]
             message = jnp.stack(parts).astype(BF16)

time: 201 us -> 189 us (0.940)
  waiting for transfers between devices: 68.7 us -> 48.8 us
  starting transfers between devices: 91 us -> 99.2 us
    ppermute x7, waiting for transfers between devices: 19.3 us -> 4.87 us  [swap(): return lax.ppermute(block, 'tensor', pairs + back)]
    ppermute x7, starting transfers between devices: 38.9 us -> 47.6 us  [swap(): return lax.ppermute(block, 'tensor', pairs + back)]
    ppermute x3, waiting for transfers between devices: 15 us -> 7.08 us  [swap(): return lax.ppermute(into, 'tensor', pairs)]
  transfers between devices with their start and end apart: 51 -> 51, of which waited for: 23 -> 21; matrix products, arithmetic and copies ran while one was open for 14% -> 16% of each run, Pallas kernels for 0% -> 0%
where the time goes in v10:
time: 189 us; the launch traced here: 188 us
  starting transfers between devices  99.2 us (52%)
  waiting for transfers between devices  48.8 us (26%)
  matrix products  26.8 us (14%)
  other arithmetic  10.4 us (6%)
  between operations  2 us (1%)
    ppermute x7, starting transfers between devices, swap(): return lax.ppermute(block, 'tensor', pairs + back)  47.6 us
    ppermute x28, starting transfers between devices, exchange(): return lax.ppermute(block, axis, [(i, i ^ apart) for i in range(count)])  30.2 us
    dot_general x56, matrix products, dot(): lax.dot_general(left, right, (((left_dim,), (right_dim,)), ((), ())), pre...  26.8 us
    ppermute x3, waiting for transfers between devices, swap(): return lax.ppermute(out, 'tensor', back)  19.7 us
    ppermute x28, waiting for transfers between devices, exchange(): return lax.ppermute(block, axis, [(i, i ^ apart) for i in range(count)])  17.1 us
    ppermute x3, starting transfers between devices, swap(): return lax.ppermute(into, 'tensor', pairs)  10.2 us
    ppermute x3, waiting for transfers between devices, swap(): return lax.ppermute(into, 'tensor', pairs)  7.08 us
    ppermute x10, starting transfers between devices, across(): return lax.ppermute(block, 'tensor', [(half - 1, half), (half, half - 1)])  7.04 us
  transfers between devices with their start and end apart: 51, of which 21 were waited for; matrix products, arithmetic and copies ran while one was open for 16% of the time, Pallas kernels for 0%

profile of v10, /device:TPU:0, one launch (start us, length us, event | category | flops | bytes accessed | tf_op | source)
XLA Modules:
  0.0 188.3 jit_solution(10623026590513859151)
XLA Ops:
  1.5 5.0 %collective-permute-start.2 = (bf16[2,32,512]{2,1,0:T(8,128)(2,1)S(1)}, bf16[2,32,512]{2,1,0:T(8,128)(2,1)S(1)}, u32[]{:S(2)}, u32[]{:S(2)}) collective-permute-start(bf16[2,32,512]{2,1,0:T(8,128)(2,1)S(1)} %pad_maximum_fusion.26), channel_id=1, source_target_pairs={{0,3},{1,2},{2,1},{3,0},{4,7},{5,6},{6,5},{7,4},{8,11},{9,10},{10,... | collective-permute-start | bytes 196616 | tf_op jit(solution)/shard_map/ppermute | solution.py:59
  9.2 3.0 %collective-permute-done.1 = bf16[2,32,512]{2,1,0:T(8,128)(2,1)S(1)} collective-permute-done((bf16[2,32,512]{2,1,0:T(8,128)(2,1)S(1)}, bf16[2,32,512]{2,1,0:T(8,128)(2,1)S(1)}, u32[]{:S(2)}, u32[]{:S(2)}) %collective-permute-start.1) | collective-permute-done | bytes 65568 | tf_op jit(solution)/shard_map/ppermute | solution.py:59
  15.7 2.5 %collective-permute-start.5 = (bf16[2,2,1,16,512]{4,3,2,1,0:T(8,128)(2,1)S(1)}, bf16[2,2,1,16,512]{4,3,2,1,0:T(8,128)(2,1)S(1)}, u32[]{:S(2)}, u32[]{:S(2)}) collective-permute-start(bf16[2,2,1,16,512]{4,3,2,1,0:T(8,128)(2,1)S(1)} %bitcast.544), channel_id=1, source_target_pairs={{0,24},{4,28},{8,16},{12,20},{16,8},{20,12},{24,0},{28,4},{1,25},{... | collective-permute-start | bytes 196616 | tf_op jit(solution)/shard_map/ppermute | solution.py:59
  19.2 1.7 collective-permute-done.5
  23.1 2.8 %collective-permute-start.14 = (bf16[2,48,512]{2,1,0:T(8,128)(2,1)S(1)}, bf16[2,48,512]{2,1,0:T(8,128)(2,1)S(1)}, u32[]{:S(2)}, u32[]{:S(2)}) collective-permute-start(bf16[2,48,512]{2,1,0:T(8,128)(2,1)S(1)} %fusion.107), channel_id=1, source_target_pairs={{0,3},{1,2},{2,1},{3,0},{4,7},{5,6},{6,5},{7,4},{8,11},{9,10},{10,... | collective-permute-start | bytes 294920 | tf_op jit(solution)/shard_map/ppermute | solution.py:59
  25.9 1.7 collective-permute-start.12
  29.9 2.4 %collective-permute-start.7 = (bf16[3,64,1024]{2,1,0:T(8,128)(2,1)S(1)}, bf16[3,64,1024]{2,1,0:T(8,128)(2,1)S(1)}, u32[]{:S(2)}, u32[]{:S(2)}) collective-permute-start(bf16[3,64,1024]{2,1,0:T(8,128)(2,1)S(1)} %pad_maximum_fusion.2), channel_id=1, source_target_pairs={{0,1},{3,2},{4,5},{7,6},{8,9},{11,10},{12,13},{15,14},{16,17},{19,... | collective-permute-start | bytes 1179656 | tf_op jit(solution)/shard_map/ppermute | solution.py:154
  33.6 1.6 collective-permute-done.13
  39.4 1.9 %collective-permute-done.7 = bf16[3,64,1024]{2,1,0:T(8,128)(2,1)S(1)} collective-permute-done((bf16[3,64,1024]{2,1,0:T(8,128)(2,1)S(1)}, bf16[3,64,1024]{2,1,0:T(8,128)(2,1)S(1)}, u32[]{:S(2)}, u32[]{:S(2)}) %collective-permute-start.7) | collective-permute-done | bytes 393248 | tf_op jit(solution)/shard_map/ppermute | solution.py:154
  41.9 4.4 %collective-permute-start.8 = (bf16[3,64,1024]{2,1,0:T(8,128)(2,1)S(1)}, bf16[3,64,1024]{2,1,0:T(8,128)(2,1)S(1)}, u32[]{:S(2)}, u32[]{:S(2)}) collective-permute-start(bf16[3,64,1024]{2,1,0:T(8,128)(2,1)S(1)} %maximum_select_fusion.1), channel_id=1, source_target_pairs={{0,1},{3,2},{4,5},{7,6},{8,9},{11,10},{12,13},{15,14},{16,17},{19,... | collective-permute-start | bytes 1179656 | tf_op jit(solution)/shard_map/ppermute | solution.py:154
  48.5 3.4 %collective-permute-start.21 = (bf16[3,64,1024]{2,1,0:T(8,128)(2,1)S(1)}, bf16[3,64,1024]{2,1,0:T(8,128)(2,1)S(1)}, u32[]{:S(2)}, u32[]{:S(2)}) collective-permute-start(bf16[3,64,1024]{2,1,0:T(8,128)(2,1)S(1)} %pad_maximum_fusion.7), channel_id=1, source_target_pairs={{0,1},{3,2},{4,5},{7,6},{8,9},{11,10},{12,13},{15,14},{16,17},{19,... | collective-permute-start | bytes 1179656 | tf_op jit(solution)/shard_map/ppermute | solution.py:154
  52.6 3.3 %collective-permute-done.8 = bf16[3,64,1024]{2,1,0:T(8,128)(2,1)S(1)} collective-permute-done((bf16[3,64,1024]{2,1,0:T(8,128)(2,1)S(1)}, bf16[3,64,1024]{2,1,0:T(8,128)(2,1)S(1)}, u32[]{:S(2)}, u32[]{:S(2)}) %collective-permute-start.8) | collective-permute-done | bytes 393248 | tf_op jit(solution)/shard_map/ppermute | solution.py:154
  57.0 4.2 %collective-permute-start.20 = (bf16[3,64,1024]{2,1,0:T(8,128)(2,1)S(1)}, bf16[3,64,1024]{2,1,0:T(8,128)(2,1)S(1)}, u32[]{:S(2)}, u32[]{:S(2)}) collective-permute-start(bf16[3,64,1024]{2,1,0:T(8,128)(2,1)S(1)} %get-tuple-element.58), channel_id=1, source_target_pairs={{0,1},{3,2},{1,0},{2,3},{4,5},{7,6},{5,4},{6,7},{8,9},{11,10},{9,8... | collective-permute-start | bytes 1179656 | tf_op jit(solution)/shard_map/ppermute | solution.py:158
  62.3 1.9 %collective-permute-done.21 = bf16[3,64,1024]{2,1,0:T(8,128)(2,1)S(1)} collective-permute-done((bf16[3,64,1024]{2,1,0:T(8,128)(2,1)S(1)}, bf16[3,64,1024]{2,1,0:T(8,128)(2,1)S(1)}, u32[]{:S(2)}, u32[]{:S(2)}) %collective-permute-start.21) | collective-permute-done | bytes 393248 | tf_op jit(solution)/shard_map/ppermute | solution.py:154
  66.3 6.0 %collective-permute-start.19 = (bf16[3,64,1024]{2,1,0:T(8,128)(2,1)S(1)}, bf16[3,64,1024]{2,1,0:T(8,128)(2,1)S(1)}, u32[]{:S(2)}, u32[]{:S(2)}) collective-permute-start(bf16[3,64,1024]{2,1,0:T(8,128)(2,1)S(1)} %broadcast_select_fusion.9), channel_id=1, source_target_pairs={{0,1},{3,2},{1,0},{2,3},{4,5},{7,6},{5,4},{6,7},{8,9},{11,10},{9,8... | collective-permute-start | bytes 1179656 | tf_op jit(solution)/shard_map/ppermute | solution.py:158
  74.3 7.8 %collective-permute-start.25 = (bf16[3,64,1024]{2,1,0:T(8,128)(2,1)S(1)}, bf16[3,64,1024]{2,1,0:T(8,128)(2,1)S(1)}, u32[]{:S(2)}, u32[]{:S(2)}) collective-permute-start(bf16[3,64,1024]{2,1,0:T(8,128)(2,1)S(1)} %get-tuple-element.56), channel_id=1, source_target_pairs={{0,1},{3,2},{1,0},{2,3},{4,5},{7,6},{5,4},{6,7},{8,9},{11,10},{9,8... | collective-permute-start | bytes 1179656 | tf_op jit(solution)/shard_map/ppermute | solution.py:158
  83.4 7.1 %collective-permute-start.24 = (bf16[3,64,1024]{2,1,0:T(8,128)(2,1)S(1)}, bf16[3,64,1024]{2,1,0:T(8,128)(2,1)S(1)}, u32[]{:S(2)}, u32[]{:S(2)}) collective-permute-start(bf16[3,64,1024]{2,1,0:T(8,128)(2,1)S(1)} %broadcast_select_fusion.3), channel_id=1, source_target_pairs={{0,1},{3,2},{1,0},{2,3},{4,5},{7,6},{5,4},{6,7},{8,9},{11,10},{9,8... | collective-permute-start | bytes 1179656 | tf_op jit(solution)/shard_map/ppermute | solution.py:158
  95.8 2.0 %collective-permute-done.24 = bf16[3,64,1024]{2,1,0:T(8,128)(2,1)S(1)} collective-permute-done((bf16[3,64,1024]{2,1,0:T(8,128)(2,1)S(1)}, bf16[3,64,1024]{2,1,0:T(8,128)(2,1)S(1)}, u32[]{:S(2)}, u32[]{:S(2)}) %collective-permute-start.24) | collective-permute-done | bytes 393248 | tf_op jit(solution)/shard_map/ppermute | solution.py:158
  99.8 7.2 %collective-permute-start.29 = (bf16[3,64,1024]{2,1,0:T(8,128)(2,1)S(1)}, bf16[3,64,1024]{2,1,0:T(8,128)(2,1)S(1)}, u32[]{:S(2)}, u32[]{:S(2)}) collective-permute-start(bf16[3,64,1024]{2,1,0:T(8,128)(2,1)S(1)} %get-tuple-element.54), channel_id=1, source_target_pairs={{0,1},{3,2},{1,0},{2,3},{4,5},{7,6},{5,4},{6,7},{8,9},{11,10},{9,8... | collective-permute-start | bytes 1179656 | tf_op jit(solution)/shard_map/ppermute | solution.py:158
  108.8 9.0 %collective-permute-start.28 = (bf16[3,64,1024]{2,1,0:T(8,128)(2,1)S(1)}, bf16[3,64,1024]{2,1,0:T(8,128)(2,1)S(1)}, u32[]{:S(2)}, u32[]{:S(2)}) collective-permute-start(bf16[3,64,1024]{2,1,0:T(8,128)(2,1)S(1)} %broadcast_select_fusion.8), channel_id=1, source_target_pairs={{0,1},{3,2},{1,0},{2,3},{4,5},{7,6},{5,4},{6,7},{8,9},{11,10},{9,8... | collective-permute-start | bytes 1179656 | tf_op jit(solution)/shard_map/ppermute | solution.py:158
  118.9 6.5 %collective-permute-start.32 = (bf16[3,64,1024]{2,1,0:T(8,128)(2,1)S(1)}, bf16[3,64,1024]{2,1,0:T(8,128)(2,1)S(1)}, u32[]{:S(2)}, u32[]{:S(2)}) collective-permute-start(bf16[3,64,1024]{2,1,0:T(8,128)(2,1)S(1)} %get-tuple-element.50), channel_id=1, source_target_pairs={{0,1},{3,2},{1,0},{2,3},{4,5},{7,6},{5,4},{6,7},{8,9},{11,10},{9,8... | collective-permute-start | bytes 1179656 | tf_op jit(solution)/shard_map/ppermute | solution.py:158
  129.5 2.4 %collective-permute-done.32 = bf16[3,64,1024]{2,1,0:T(8,128)(2,1)S(1)} collective-permute-done((bf16[3,64,1024]{2,1,0:T(8,128)(2,1)S(1)}, bf16[3,64,1024]{2,1,0:T(8,128)(2,1)S(1)}, u32[]{:S(2)}, u32[]{:S(2)}) %collective-permute-start.32) | collective-permute-done | bytes 393248 | tf_op jit(solution)/shard_map/ppermute | solution.py:158
  134.7 1.6 collective-permute-start.38
  136.9 9.5 %collective-permute-done.42 = bf16[3,64,1024]{2,1,0:T(8,128)(2,1)S(1)} collective-permute-done((bf16[3,64,1024]{2,1,0:T(8,128)(2,1)S(1)}, bf16[3,64,1024]{2,1,0:T(8,128)(2,1)S(1)}, u32[]{:S(2)}, u32[]{:S(2)}) %collective-permute-start.42) | collective-permute-done | bytes 393248 | tf_op jit(solution)/shard_map/ppermute | solution.py:156
  151.0 10.2 %collective-permute-done.35 = bf16[3,64,1024]{2,1,0:T(8,128)(2,1)S(1)} collective-permute-done((bf16[3,64,1024]{2,1,0:T(8,128)(2,1)S(1)}, bf16[3,64,1024]{2,1,0:T(8,128)(2,1)S(1)}, u32[]{:S(2)}, u32[]{:S(2)}) %collective-permute-start.35) | collective-permute-done | bytes 393248 | tf_op jit(solution)/shard_map/ppermute | solution.py:156
  163.5 2.0 %multiply_convert_fusion.2 = bf16[512,1024]{1,0:T(8,128)(2,1)} fusion(bf16[3,640,1024]{2,1,0:T(8,128)(2,1)S(1)} %get-tuple-element.10, bf16[2,640,512]{2,1,0:T(8,128)(2,1)S(1)} %maximum_select_fusion), kind=kOutput, calls=%fused_computation.2 | convolution fusion | flops 672137216 | bytes 3014656 | tf_op jit(solution)/shard_map/dot_general | solution.py:25
  165.5 2.0 %multiply_convert_fusion = bf16[1024,512]{1,0:T(8,128)(2,1)} fusion(bf16[3,640,1024]{2,1,0:T(8,128)(2,1)S(1)} %get-tuple-element.10, bf16[2,640,512]{2,1,0:T(8,128)(2,1)S(1)} %maximum_select_fusion), kind=kOutput, calls=%fused_computation | convolution fusion | flops 672137216 | bytes 3014656 | tf_op jit(solution)/shard_map/dot_general | solution.py:25
  168.1 2.0 %multiply_convert_fusion.1 = bf16[512,1024]{1,0:T(8,128)(2,1)} fusion(bf16[3,640,1024]{2,1,0:T(8,128)(2,1)S(1)} %get-tuple-element.10, bf16[2,640,512]{2,1,0:T(8,128)(2,1)S(1)} %maximum_select_fusion), kind=kOutput, calls=%fused_computation.1 | convolution fusion | flops 672137216 | bytes 3014656 | tf_op jit(solution)/shard_map/dot_general | solution.py:25
  173.9 1.9 collective-permute-start.40
  178.6 1.9 %collective-permute-start.49 = (bf16[2,32,512]{2,1,0:T(8,128)(2,1)S(1)}, bf16[2,32,512]{2,1,0:T(8,128)(2,1)S(1)}, u32[]{:S(2)}, u32[]{:S(2)}) collective-permute-start(bf16[2,32,512]{2,1,0:T(8,128)(2,1)S(1)} %bitcast.556), channel_id=1, source_target_pairs={{0,2},{1,3},{2,0},{3,1},{4,6},{5,7},{6,4},{7,5},{8,10},{9,11},{10,... | collective-permute-start | bytes 196616 | tf_op jit(solution)/shard_map/ppermute | solution.py:59
  181.8 2.3 %collective-permute-done.50 = bf16[2,32,512]{2,1,0:T(8,128)(2,1)S(1)} collective-permute-done((bf16[2,32,512]{2,1,0:T(8,128)(2,1)S(1)}, bf16[2,32,512]{2,1,0:T(8,128)(2,1)S(1)}, u32[]{:S(2)}, u32[]{:S(2)}) %collective-permute-start.50) | collective-permute-done | bytes 65568 | tf_op jit(solution)/shard_map/ppermute | solution.py:59
  184.1 2.9 %collective-permute-done.49 = bf16[2,32,512]{2,1,0:T(8,128)(2,1)S(1)} collective-permute-done((bf16[2,32,512]{2,1,0:T(8,128)(2,1)S(1)}, bf16[2,32,512]{2,1,0:T(8,128)(2,1)S(1)}, u32[]{:S(2)}, u32[]{:S(2)}) %collective-permute-start.49) | collective-permute-done | bytes 65568 | tf_op jit(solution)/shard_map/ppermute | solution.py:59
  (242 shorter events, 62.2 us)
Async XLA Ops:
  1.5 7.6 %collective-permute-start.2 = (bf16[2,32,512]{2,1,0:T(8,128)(2,1)S(1)}, bf16[2,32,512]{2,1,0:T(8,128)(2,1)S(1)}, u32[]{:S(2)}, u32[]{:S(2)}) collective-permute-start(bf16[2,32,512]{2,1,0:T(8,128)(2,1)S(1)} %pad_maximum_fusion.26), channel_id=1, source_target_pairs={{0,3},{1,2},{2,1},{3,0},{4,7},{5,6},{6,5},{7,4},{8,11},{9,10},{10,... | collective-permute-start | bytes 196616 | tf_op jit(solution)/shard_map/ppermute | solution.py:59
  23.1 10.5 %collective-permute-start.14 = (bf16[2,48,512]{2,1,0:T(8,128)(2,1)S(1)}, bf16[2,48,512]{2,1,0:T(8,128)(2,1)S(1)}, u32[]{:S(2)}, u32[]{:S(2)}) collective-permute-start(bf16[2,48,512]{2,1,0:T(8,128)(2,1)S(1)} %fusion.107), channel_id=1, source_target_pairs={{0,3},{1,2},{2,1},{3,0},{4,7},{5,6},{6,5},{7,4},{8,11},{9,10},{10,... | collective-permute-start | bytes 294920 | tf_op jit(solution)/shard_map/ppermute | solution.py:59
  25.9 9.3 %collective-permute-start.13 = (bf16[2,48,512]{2,1,0:T(8,128)(2,1)S(1)}, bf16[2,48,512]{2,1,0:T(8,128)(2,1)S(1)}, u32[]{:S(2)}, u32[]{:S(2)}) collective-permute-start(bf16[2,48,512]{2,1,0:T(8,128)(2,1)S(1)} %fusion.107), channel_id=1, source_target_pairs={{0,2},{1,3},{2,0},{3,1},{4,6},{5,7},{6,4},{7,5},{8,10},{9,11},{10,... | collective-permute-start | bytes 294920 | tf_op jit(solution)/shard_map/ppermute | solution.py:59
  25.9 9.3 %collective-permute-start.12 = (bf16[2,48,512]{2,1,0:T(8,128)(2,1)S(1)}, bf16[2,48,512]{2,1,0:T(8,128)(2,1)S(1)}, u32[]{:S(2)}, u32[]{:S(2)}) collective-permute-start(bf16[2,48,512]{2,1,0:T(8,128)(2,1)S(1)} %fusion.107), channel_id=1, source_target_pairs={{0,1},{1,0},{2,3},{3,2},{4,5},{5,4},{6,7},{7,6},{8,9},{9,8},{10,11... | collective-permute-start | bytes 294920 | tf_op jit(solution)/shard_map/ppermute | solution.py:59
  29.9 11.4 %collective-permute-start.7 = (bf16[3,64,1024]{2,1,0:T(8,128)(2,1)S(1)}, bf16[3,64,1024]{2,1,0:T(8,128)(2,1)S(1)}, u32[]{:S(2)}, u32[]{:S(2)}) collective-permute-start(bf16[3,64,1024]{2,1,0:T(8,128)(2,1)S(1)} %pad_maximum_fusion.2), channel_id=1, source_target_pairs={{0,1},{3,2},{4,5},{7,6},{8,9},{11,10},{12,13},{15,14},{16,17},{19,... | collective-permute-start | bytes 1179656 | tf_op jit(solution)/shard_map/ppermute | solution.py:154
  35.9 12.5 %collective-permute-start.17 = (bf16[2,3,1,16,512]{4,3,2,1,0:T(8,128)(2,1)S(1)}, bf16[2,3,1,16,512]{4,3,2,1,0:T(8,128)(2,1)S(1)}, u32[]{:S(2)}, u32[]{:S(2)}) collective-permute-start(bf16[2,3,1,16,512]{4,3,2,1,0:T(8,128)(2,1)S(1)} %bitcast.551), channel_id=1, source_target_pairs={{0,24},{4,28},{8,16},{12,20},{16,8},{20,12},{24,0},{28,4},{1,25},{... | collective-permute-start | bytes 294920 | tf_op jit(solution)/shard_map/ppermute | solution.py:59
  37.4 10.9 %collective-permute-start.16 = (bf16[2,3,1,16,512]{4,3,2,1,0:T(8,128)(2,1)S(1)}, bf16[2,3,1,16,512]{4,3,2,1,0:T(8,128)(2,1)S(1)}, u32[]{:S(2)}, u32[]{:S(2)}) collective-permute-start(bf16[2,3,1,16,512]{4,3,2,1,0:T(8,128)(2,1)S(1)} %bitcast.552), channel_id=1, source_target_pairs={{0,16},{4,20},{8,24},{12,28},{16,0},{20,4},{24,8},{28,12},{1,17},{... | collective-permute-start | bytes 294920 | tf_op jit(solution)/shard_map/ppermute | solution.py:59
  37.9 10.4 %collective-permute-start.15 = (bf16[2,3,1,16,512]{4,3,2,1,0:T(8,128)(2,1)S(1)}, bf16[2,3,1,16,512]{4,3,2,1,0:T(8,128)(2,1)S(1)}, u32[]{:S(2)}, u32[]{:S(2)}) collective-permute-start(bf16[2,3,1,16,512]{4,3,2,1,0:T(8,128)(2,1)S(1)} %bitcast.553), channel_id=1, source_target_pairs={{0,8},{4,12},{8,0},{12,4},{16,24},{20,28},{24,16},{28,20},{1,9},{5... | collective-permute-start | bytes 294920 | tf_op jit(solution)/shard_map/ppermute | solution.py:59
  41.9 13.9 %collective-permute-start.8 = (bf16[3,64,1024]{2,1,0:T(8,128)(2,1)S(1)}, bf16[3,64,1024]{2,1,0:T(8,128)(2,1)S(1)}, u32[]{:S(2)}, u32[]{:S(2)}) collective-permute-start(bf16[3,64,1024]{2,1,0:T(8,128)(2,1)S(1)} %maximum_select_fusion.1), channel_id=1, source_target_pairs={{0,1},{3,2},{4,5},{7,6},{8,9},{11,10},{12,13},{15,14},{16,17},{19,... | collective-permute-start | bytes 1179656 | tf_op jit(solution)/shard_map/ppermute | solution.py:154
  48.4 12.8 %collective-permute-start.18 = (bf16[2,3,4,16,512]{4,3,2,1,0:T(8,128)(2,1)S(1)}, bf16[2,3,4,16,512]{4,3,2,1,0:T(8,128)(2,1)S(1)}, u32[]{:S(2)}, u32[]{:S(2)}) collective-permute-start(bf16[2,3,4,16,512]{4,3,2,1,0:T(8,128)(2,1)S(1)} %pad_maximum_fusion.4), channel_id=1, source_target_pairs={{0,4},{4,0},{8,12},{12,8},{16,20},{20,16},{24,28},{28,24},{1,5},{5... | collective-permute-start | bytes 1179656 | tf_op jit(solution)/shard_map/ppermute | solution.py:59
  48.5 15.7 %collective-permute-start.21 = (bf16[3,64,1024]{2,1,0:T(8,128)(2,1)S(1)}, bf16[3,64,1024]{2,1,0:T(8,128)(2,1)S(1)}, u32[]{:S(2)}, u32[]{:S(2)}) collective-permute-start(bf16[3,64,1024]{2,1,0:T(8,128)(2,1)S(1)} %pad_maximum_fusion.7), channel_id=1, source_target_pairs={{0,1},{3,2},{4,5},{7,6},{8,9},{11,10},{12,13},{15,14},{16,17},{19,... | collective-permute-start | bytes 1179656 | tf_op jit(solution)/shard_map/ppermute | solution.py:154
  56.3 9.9 %collective-permute-start.10 = (bf16[3,64,1024]{2,1,0:T(8,128)(2,1)S(1)}, bf16[3,64,1024]{2,1,0:T(8,128)(2,1)S(1)}, u32[]{:S(2)}, u32[]{:S(2)}) collective-permute-start(bf16[3,64,1024]{2,1,0:T(8,128)(2,1)S(1)} %get-tuple-element.59), channel_id=1, source_target_pairs={{1,2},{2,1},{5,6},{6,5},{9,10},{10,9},{13,14},{14,13},{17,18},{18,... | collective-permute-start | bytes 1179656 | tf_op jit(solution)/shard_map/ppermute | solution.py:163
  57.0 15.7 %collective-permute-start.20 = (bf16[3,64,1024]{2,1,0:T(8,128)(2,1)S(1)}, bf16[3,64,1024]{2,1,0:T(8,128)(2,1)S(1)}, u32[]{:S(2)}, u32[]{:S(2)}) collective-permute-start(bf16[3,64,1024]{2,1,0:T(8,128)(2,1)S(1)} %get-tuple-element.58), channel_id=1, source_target_pairs={{0,1},{3,2},{1,0},{2,3},{4,5},{7,6},{5,4},{6,7},{8,9},{11,10},{9,8... | collective-permute-start | bytes 1179656 | tf_op jit(solution)/shard_map/ppermute | solution.py:158
  64.4 8.3 %collective-permute-start.22 = (bf16[3,64,1024]{2,1,0:T(8,128)(2,1)S(1)}, bf16[3,64,1024]{2,1,0:T(8,128)(2,1)S(1)}, u32[]{:S(2)}, u32[]{:S(2)}) collective-permute-start(bf16[3,64,1024]{2,1,0:T(8,128)(2,1)S(1)} %add_convert_fusion.3), channel_id=1, source_target_pairs={{1,2},{2,1},{5,6},{6,5},{9,10},{10,9},{13,14},{14,13},{17,18},{18,... | collective-permute-start | bytes 1179656 | tf_op jit(solution)/shard_map/ppermute | solution.py:163
  66.3 16.3 %collective-permute-start.19 = (bf16[3,64,1024]{2,1,0:T(8,128)(2,1)S(1)}, bf16[3,64,1024]{2,1,0:T(8,128)(2,1)S(1)}, u32[]{:S(2)}, u32[]{:S(2)}) collective-permute-start(bf16[3,64,1024]{2,1,0:T(8,128)(2,1)S(1)} %broadcast_select_fusion.9), channel_id=1, source_target_pairs={{0,1},{3,2},{1,0},{2,3},{4,5},{7,6},{5,4},{6,7},{8,9},{11,10},{9,8... | collective-permute-start | bytes 1179656 | tf_op jit(solution)/shard_map/ppermute | solution.py:158
  73.1 10.2 %collective-permute-start.23 = (bf16[3,64,1024]{2,1,0:T(8,128)(2,1)S(1)}, bf16[3,64,1024]{2,1,0:T(8,128)(2,1)S(1)}, u32[]{:S(2)}, u32[]{:S(2)}) collective-permute-start(bf16[3,64,1024]{2,1,0:T(8,128)(2,1)S(1)} %get-tuple-element.57), channel_id=1, source_target_pairs={{1,2},{2,1},{5,6},{6,5},{9,10},{10,9},{13,14},{14,13},{17,18},{18,... | collective-permute-start | bytes 1179656 | tf_op jit(solution)/shard_map/ppermute | solution.py:163
  74.3 19.4 %collective-permute-start.25 = (bf16[3,64,1024]{2,1,0:T(8,128)(2,1)S(1)}, bf16[3,64,1024]{2,1,0:T(8,128)(2,1)S(1)}, u32[]{:S(2)}, u32[]{:S(2)}) collective-permute-start(bf16[3,64,1024]{2,1,0:T(8,128)(2,1)S(1)} %get-tuple-element.56), channel_id=1, source_target_pairs={{0,1},{3,2},{1,0},{2,3},{4,5},{7,6},{5,4},{6,7},{8,9},{11,10},{9,8... | collective-permute-start | bytes 1179656 | tf_op jit(solution)/shard_map/ppermute | solution.py:158
  83.4 14.5 %collective-permute-start.24 = (bf16[3,64,1024]{2,1,0:T(8,128)(2,1)S(1)}, bf16[3,64,1024]{2,1,0:T(8,128)(2,1)S(1)}, u32[]{:S(2)}, u32[]{:S(2)}) collective-permute-start(bf16[3,64,1024]{2,1,0:T(8,128)(2,1)S(1)} %broadcast_select_fusion.3), channel_id=1, source_target_pairs={{0,1},{3,2},{1,0},{2,3},{4,5},{7,6},{5,4},{6,7},{8,9},{11,10},{9,8... | collective-permute-start | bytes 1179656 | tf_op jit(solution)/shard_map/ppermute | solution.py:158
  99.1 9.6 %collective-permute-start.27 = (bf16[3,64,1024]{2,1,0:T(8,128)(2,1)S(1)}, bf16[3,64,1024]{2,1,0:T(8,128)(2,1)S(1)}, u32[]{:S(2)}, u32[]{:S(2)}) collective-permute-start(bf16[3,64,1024]{2,1,0:T(8,128)(2,1)S(1)} %get-tuple-element.55), channel_id=1, source_target_pairs={{1,2},{2,1},{5,6},{6,5},{9,10},{10,9},{13,14},{14,13},{17,18},{18,... | collective-permute-start | bytes 1179656 | tf_op jit(solution)/shard_map/ppermute | solution.py:163
  99.8 17.9 %collective-permute-start.29 = (bf16[3,64,1024]{2,1,0:T(8,128)(2,1)S(1)}, bf16[3,64,1024]{2,1,0:T(8,128)(2,1)S(1)}, u32[]{:S(2)}, u32[]{:S(2)}) collective-permute-start(bf16[3,64,1024]{2,1,0:T(8,128)(2,1)S(1)} %get-tuple-element.54), channel_id=1, source_target_pairs={{0,1},{3,2},{1,0},{2,3},{4,5},{7,6},{5,4},{6,7},{8,9},{11,10},{9,8... | collective-permute-start | bytes 1179656 | tf_op jit(solution)/shard_map/ppermute | solution.py:158
  107.2 10.6 %collective-permute-start.31 = (bf16[3,64,1024]{2,1,0:T(8,128)(2,1)S(1)}, bf16[3,64,1024]{2,1,0:T(8,128)(2,1)S(1)}, u32[]{:S(2)}, u32[]{:S(2)}) collective-permute-start(bf16[3,64,1024]{2,1,0:T(8,128)(2,1)S(1)} %add_convert_fusion.1), channel_id=1, source_target_pairs={{1,2},{2,1},{5,6},{6,5},{9,10},{10,9},{13,14},{14,13},{17,18},{18,... | collective-permute-start | bytes 1179656 | tf_op jit(solution)/shard_map/ppermute | solution.py:163
  108.8 16.6 %collective-permute-start.28 = (bf16[3,64,1024]{2,1,0:T(8,128)(2,1)S(1)}, bf16[3,64,1024]{2,1,0:T(8,128)(2,1)S(1)}, u32[]{:S(2)}, u32[]{:S(2)}) collective-permute-start(bf16[3,64,1024]{2,1,0:T(8,128)(2,1)S(1)} %broadcast_select_fusion.8), channel_id=1, source_target_pairs={{0,1},{3,2},{1,0},{2,3},{4,5},{7,6},{5,4},{6,7},{8,9},{11,10},{9,8... | collective-permute-start | bytes 1179656 | tf_op jit(solution)/shard_map/ppermute | solution.py:158
  118.2 10.0 %collective-permute-start.41 = (bf16[3,64,1024]{2,1,0:T(8,128)(2,1)S(1)}, bf16[3,64,1024]{2,1,0:T(8,128)(2,1)S(1)}, u32[]{:S(2)}, u32[]{:S(2)}) collective-permute-start(bf16[3,64,1024]{2,1,0:T(8,128)(2,1)S(1)} %get-tuple-element.49), channel_id=1, source_target_pairs={{1,2},{2,1},{5,6},{6,5},{9,10},{10,9},{13,14},{14,13},{17,18},{18,... | collective-permute-start | bytes 1179656 | tf_op jit(solution)/shard_map/ppermute | solution.py:163
  118.9 13.0 %collective-permute-start.32 = (bf16[3,64,1024]{2,1,0:T(8,128)(2,1)S(1)}, bf16[3,64,1024]{2,1,0:T(8,128)(2,1)S(1)}, u32[]{:S(2)}, u32[]{:S(2)}) collective-permute-start(bf16[3,64,1024]{2,1,0:T(8,128)(2,1)S(1)} %get-tuple-element.50), channel_id=1, source_target_pairs={{0,1},{3,2},{1,0},{2,3},{4,5},{7,6},{5,4},{6,7},{8,9},{11,10},{9,8... | collective-permute-start | bytes 1179656 | tf_op jit(solution)/shard_map/ppermute | solution.py:158
  128.2 18.1 %collective-permute-start.42 = (bf16[3,64,1024]{2,1,0:T(8,128)(2,1)S(1)}, bf16[3,64,1024]{2,1,0:T(8,128)(2,1)S(1)}, u32[]{:S(2)}, u32[]{:S(2)}) collective-permute-start(bf16[3,64,1024]{2,1,0:T(8,128)(2,1)S(1)} %collective-permute-done.41), channel_id=1, source_target_pairs={{1,0},{2,3},{5,4},{6,7},{9,8},{10,11},{13,12},{14,15},{17,16},{18,... | collective-permute-start | bytes 1179656 | tf_op jit(solution)/shard_map/ppermute | solution.py:156
  132.4 15.9 %collective-permute-start.34 = (bf16[3,64,1024]{2,1,0:T(8,128)(2,1)S(1)}, bf16[3,64,1024]{2,1,0:T(8,128)(2,1)S(1)}, u32[]{:S(2)}, u32[]{:S(2)}) collective-permute-start(bf16[3,64,1024]{2,1,0:T(8,128)(2,1)S(1)} %pad_maximum_fusion.16), channel_id=1, source_target_pairs={{1,2},{2,1},{5,6},{6,5},{9,10},{10,9},{13,14},{14,13},{17,18},{18,... | collective-permute-start | bytes 1179656 | tf_op jit(solution)/shard_map/ppermute | solution.py:163
  133.1 28.4 %collective-permute-start.43 = (bf16[3,64,1024]{2,1,0:T(8,128)(2,1)S(1)}, bf16[3,64,1024]{2,1,0:T(8,128)(2,1)S(1)}, u32[]{:S(2)}, u32[]{:S(2)}) collective-permute-start(bf16[3,64,1024]{2,1,0:T(8,128)(2,1)S(1)} %pad_maximum_fusion.16), channel_id=1, source_target_pairs={{1,0},{2,3},{5,4},{6,7},{9,8},{10,11},{13,12},{14,15},{17,16},{18,... | collective-permute-start | bytes 1179656 | tf_op jit(solution)/shard_map/ppermute | solution.py:156
  134.7 15.5 %collective-permute-start.38 = (bf16[2,3,16,512]{3,2,1,0:T(8,128)(2,1)S(1)}, bf16[2,3,16,512]{3,2,1,0:T(8,128)(2,1)S(1)}, u32[]{:S(2)}, u32[]{:S(2)}) collective-permute-start(bf16[2,3,16,512]{3,2,1,0:T(8,128)(2,1)S(1)} %get-tuple-element.52), channel_id=1, source_target_pairs={{0,24},{4,28},{8,16},{12,20},{16,8},{20,12},{24,0},{28,4},{1,25},{... | collective-permute-start | bytes 294920 | tf_op jit(solution)/shard_map/ppermute | solution.py:59
  136.3 13.9 %collective-permute-start.37 = (bf16[2,3,16,512]{3,2,1,0:T(8,128)(2,1)S(1)}, bf16[2,3,16,512]{3,2,1,0:T(8,128)(2,1)S(1)}, u32[]{:S(2)}, u32[]{:S(2)}) collective-permute-start(bf16[2,3,16,512]{3,2,1,0:T(8,128)(2,1)S(1)} %get-tuple-element.53), channel_id=1, source_target_pairs={{0,16},{4,20},{8,24},{12,28},{16,0},{20,4},{24,8},{28,12},{1,17},{... | collective-permute-start | bytes 294920 | tf_op jit(solution)/shard_map/ppermute | solution.py:59
  148.4 12.9 %collective-permute-start.35 = (bf16[3,64,1024]{2,1,0:T(8,128)(2,1)S(1)}, bf16[3,64,1024]{2,1,0:T(8,128)(2,1)S(1)}, u32[]{:S(2)}, u32[]{:S(2)}) collective-permute-start(bf16[3,64,1024]{2,1,0:T(8,128)(2,1)S(1)} %broadcast_select_fusion), channel_id=1, source_target_pairs={{1,0},{2,3},{5,4},{6,7},{9,8},{10,11},{13,12},{14,15},{17,16},{18,... | collective-permute-start | bytes 1179656 | tf_op jit(solution)/shard_map/ppermute | solution.py:156
  173.9 7.9 %collective-permute-start.40 = (bf16[2,48,512]{2,1,0:T(8,128)(2,1)S(1)}, bf16[2,48,512]{2,1,0:T(8,128)(2,1)S(1)}, u32[]{:S(2)}, u32[]{:S(2)}) collective-permute-start(bf16[2,48,512]{2,1,0:T(8,128)(2,1)S(1)} %fusion.106), channel_id=1, source_target_pairs={{0,2},{1,3},{2,0},{3,1},{4,6},{5,7},{6,4},{7,5},{8,10},{9,11},{10,... | collective-permute-start | bytes 294920 | tf_op jit(solution)/shard_map/ppermute | solution.py:59
  178.6 8.4 %collective-permute-start.49 = (bf16[2,32,512]{2,1,0:T(8,128)(2,1)S(1)}, bf16[2,32,512]{2,1,0:T(8,128)(2,1)S(1)}, u32[]{:S(2)}, u32[]{:S(2)}) collective-permute-start(bf16[2,32,512]{2,1,0:T(8,128)(2,1)S(1)} %bitcast.556), channel_id=1, source_target_pairs={{0,2},{1,3},{2,0},{3,1},{4,6},{5,7},{6,4},{7,5},{8,10},{9,11},{10,... | collective-permute-start | bytes 196616 | tf_op jit(solution)/shard_map/ppermute | solution.py:59
  (25 other events, 210.4 us)

commit v11 on v10

--- a/solution.py
+++ b/solution.py
@@ -77,10 +77,11 @@
     return turn(sum(piece.astype(F32) * sign[:, :width] for piece, sign in zip(pieces, signs)))
 
 
-def rotate_by_halves(block, bits):
+def rotate_by_halves(block, bits, ahead):
     block = turn(block)
     for level, bit in enumerate(bits):
-        came = exchange(block.astype(BF16), "tensor", 1 << level)
+        message = block.astype(BF16)
+        came = exchange(message if level else after(message, ahead), "tensor", 1 << level)
         block = block * bit[:, : block.shape[-1]] + came.astype(F32)
     return block
 
@@ -255,21 +256,21 @@
                 outs += [acts[i], crossed[i]]
     low, high = leave([done(i) for i in range(split, chunks)])
     if split > 0:
-        first_sums = after(first_sums.reshape(2, -1, width), came[-1])
-        ends.append(rotate_by_halves(first_sums, bits))
-    sums, _, _ = scatter_dp(low, high)
+        ends.append(rotate_by_halves(first_sums.reshape(2, -1, width), bits, crossed[-1]))
+    sums, _, ahead = scatter_dp(low, high)
     ends.append(rotate(spread(sums.reshape(2, -1, width).astype(BF16)), signs))
     ends = jnp.concatenate(ends, axis=1)
 
     acts = jnp.concatenate([done(i) for i in range(chunks)], axis=1)
     rows = [jnp.stack(group, axis=2).reshape(2, -1, width) for group in groups]
     rows = after(jnp.concatenate(rows, axis=1), high[0, 0, :1])
+    late_rows = after(rows[0], ahead[0, 0, :1])
     factor = 1.0 / math.sqrt(rows.shape[1])
     return (
         ends[0],
         ends[1],
-        (dot(rows[0], acts[1], 0, 0) * factor).astype(BF16),
-        (dot(rows[0], acts[2], 0, 0) * factor).astype(BF16),
+        (dot(late_rows, acts[1], 0, 0) * factor).astype(BF16),
+        (dot(late_rows, acts[2], 0, 0) * factor).astype(BF16),
         (dot(acts[0], rows[1], 0, 0) * factor).astype(BF16),
     )
 

time: 189 us -> 188 us (level)
    ppermute x28, waiting for transfers between devices: 17.1 us -> 25 us  [exchange(): return lax.ppermute(block, axis, [(i, i ^ apart) for i in range(count)])]
    ppermute x3, waiting for transfers between devices: 19.7 us -> 11.9 us  [swap(): return lax.ppermute(out, 'tensor', back)]
  transfers between devices with their start and end apart: 51 -> 51, of which waited for: 21 -> 22; matrix products, arithmetic and copies ran while one was open for 16% -> 16% of each run, Pallas kernels for 0% -> 0%
where the time goes in v11:
time: 188 us; the launch traced here: 187 us
  starting transfers between devices  98.3 us (52%)
  waiting for transfers between devices  48.9 us (26%)
  matrix products  26.8 us (14%)
  other arithmetic  10.3 us (5%)
  between operations  2.01 us (1%)
    ppermute x7, starting transfers between devices, swap(): return lax.ppermute(block, 'tensor', pairs + back)  47.6 us
    ppermute x28, starting transfers between devices, exchange(): return lax.ppermute(block, axis, [(i, i ^ apart) for i in range(count)])  29.3 us
    dot_general x56, matrix products, dot(): lax.dot_general(left, right, (((left_dim,), (right_dim,)), ((), ())), pre...  26.8 us
    ppermute x28, waiting for transfers between devices, exchange(): return lax.ppermute(block, axis, [(i, i ^ apart) for i in range(count)])  25 us
    ppermute x3, waiting for transfers between devices, swap(): return lax.ppermute(out, 'tensor', back)  11.9 us
    ppermute x3, starting transfers between devices, swap(): return lax.ppermute(into, 'tensor', pairs)  10.2 us
    ppermute x3, waiting for transfers between devices, swap(): return lax.ppermute(into, 'tensor', pairs)  7.08 us
    ppermute x10, starting transfers between devices, across(): return lax.ppermute(block, 'tensor', [(half - 1, half), (half, half - 1)])  7.04 us
  transfers between devices with their start and end apart: 51, of which 22 were waited for; matrix products, arithmetic and copies ran while one was open for 16% of the time, Pallas kernels for 0%

profile of v11, /device:TPU:0, one launch (start us, length us, event | category | flops | bytes accessed | tf_op | source)
XLA Modules:
  0.0 187.4 jit_solution(18138648251773649526)
XLA Ops:
  1.5 5.0 %collective-permute-start.2 = (bf16[2,32,512]{2,1,0:T(8,128)(2,1)S(1)}, bf16[2,32,512]{2,1,0:T(8,128)(2,1)S(1)}, u32[]{:S(2)}, u32[]{:S(2)}) collective-permute-start(bf16[2,32,512]{2,1,0:T(8,128)(2,1)S(1)} %pad_maximum_fusion.26), channel_id=1, source_target_pairs={{0,3},{1,2},{2,1},{3,0},{4,7},{5,6},{6,5},{7,4},{8,11},{9,10},{10,... | collective-permute-start | bytes 196616 | tf_op jit(solution)/shard_map/ppermute | solution.py:59
  9.2 3.0 %collective-permute-done.1 = bf16[2,32,512]{2,1,0:T(8,128)(2,1)S(1)} collective-permute-done((bf16[2,32,512]{2,1,0:T(8,128)(2,1)S(1)}, bf16[2,32,512]{2,1,0:T(8,128)(2,1)S(1)}, u32[]{:S(2)}, u32[]{:S(2)}) %collective-permute-start.1) | collective-permute-done | bytes 65568 | tf_op jit(solution)/shard_map/ppermute | solution.py:59
  15.7 2.5 %collective-permute-start.5 = (bf16[2,2,1,16,512]{4,3,2,1,0:T(8,128)(2,1)S(1)}, bf16[2,2,1,16,512]{4,3,2,1,0:T(8,128)(2,1)S(1)}, u32[]{:S(2)}, u32[]{:S(2)}) collective-permute-start(bf16[2,2,1,16,512]{4,3,2,1,0:T(8,128)(2,1)S(1)} %bitcast.529), channel_id=1, source_target_pairs={{0,24},{4,28},{8,16},{12,20},{16,8},{20,12},{24,0},{28,4},{1,25},{... | collective-permute-start | bytes 196616 | tf_op jit(solution)/shard_map/ppermute | solution.py:59
  19.2 1.7 collective-permute-done.5
  23.1 2.8 %collective-permute-start.14 = (bf16[2,48,512]{2,1,0:T(8,128)(2,1)S(1)}, bf16[2,48,512]{2,1,0:T(8,128)(2,1)S(1)}, u32[]{:S(2)}, u32[]{:S(2)}) collective-permute-start(bf16[2,48,512]{2,1,0:T(8,128)(2,1)S(1)} %fusion.112), channel_id=1, source_target_pairs={{0,3},{1,2},{2,1},{3,0},{4,7},{5,6},{6,5},{7,4},{8,11},{9,10},{10,... | collective-permute-start | bytes 294920 | tf_op jit(solution)/shard_map/ppermute | solution.py:59
  25.9 1.7 collective-permute-start.12
  29.9 2.4 %collective-permute-start.7 = (bf16[3,64,1024]{2,1,0:T(8,128)(2,1)S(1)}, bf16[3,64,1024]{2,1,0:T(8,128)(2,1)S(1)}, u32[]{:S(2)}, u32[]{:S(2)}) collective-permute-start(bf16[3,64,1024]{2,1,0:T(8,128)(2,1)S(1)} %pad_maximum_fusion.2), channel_id=1, source_target_pairs={{0,1},{3,2},{4,5},{7,6},{8,9},{11,10},{12,13},{15,14},{16,17},{19,... | collective-permute-start | bytes 1179656 | tf_op jit(solution)/shard_map/ppermute | solution.py:155
  33.6 1.6 collective-permute-done.13
  39.4 1.9 %collective-permute-done.7 = bf16[3,64,1024]{2,1,0:T(8,128)(2,1)S(1)} collective-permute-done((bf16[3,64,1024]{2,1,0:T(8,128)(2,1)S(1)}, bf16[3,64,1024]{2,1,0:T(8,128)(2,1)S(1)}, u32[]{:S(2)}, u32[]{:S(2)}) %collective-permute-start.7) | collective-permute-done | bytes 393248 | tf_op jit(solution)/shard_map/ppermute | solution.py:155
  41.9 4.4 %collective-permute-start.8 = (bf16[3,64,1024]{2,1,0:T(8,128)(2,1)S(1)}, bf16[3,64,1024]{2,1,0:T(8,128)(2,1)S(1)}, u32[]{:S(2)}, u32[]{:S(2)}) collective-permute-start(bf16[3,64,1024]{2,1,0:T(8,128)(2,1)S(1)} %maximum_select_fusion.1), channel_id=1, source_target_pairs={{0,1},{3,2},{4,5},{7,6},{8,9},{11,10},{12,13},{15,14},{16,17},{19,... | collective-permute-start | bytes 1179656 | tf_op jit(solution)/shard_map/ppermute | solution.py:155
  48.5 3.4 %collective-permute-start.21 = (bf16[3,64,1024]{2,1,0:T(8,128)(2,1)S(1)}, bf16[3,64,1024]{2,1,0:T(8,128)(2,1)S(1)}, u32[]{:S(2)}, u32[]{:S(2)}) collective-permute-start(bf16[3,64,1024]{2,1,0:T(8,128)(2,1)S(1)} %pad_maximum_fusion.7), channel_id=1, source_target_pairs={{0,1},{3,2},{4,5},{7,6},{8,9},{11,10},{12,13},{15,14},{16,17},{19,... | collective-permute-start | bytes 1179656 | tf_op jit(solution)/shard_map/ppermute | solution.py:155
  52.6 3.3 %collective-permute-done.8 = bf16[3,64,1024]{2,1,0:T(8,128)(2,1)S(1)} collective-permute-done((bf16[3,64,1024]{2,1,0:T(8,128)(2,1)S(1)}, bf16[3,64,1024]{2,1,0:T(8,128)(2,1)S(1)}, u32[]{:S(2)}, u32[]{:S(2)}) %collective-permute-start.8) | collective-permute-done | bytes 393248 | tf_op jit(solution)/shard_map/ppermute | solution.py:155
  57.0 4.2 %collective-permute-start.20 = (bf16[3,64,1024]{2,1,0:T(8,128)(2,1)S(1)}, bf16[3,64,1024]{2,1,0:T(8,128)(2,1)S(1)}, u32[]{:S(2)}, u32[]{:S(2)}) collective-permute-start(bf16[3,64,1024]{2,1,0:T(8,128)(2,1)S(1)} %get-tuple-element.58), channel_id=1, source_target_pairs={{0,1},{3,2},{1,0},{2,3},{4,5},{7,6},{5,4},{6,7},{8,9},{11,10},{9,8... | collective-permute-start | bytes 1179656 | tf_op jit(solution)/shard_map/ppermute | solution.py:159
  62.3 1.9 %collective-permute-done.21 = bf16[3,64,1024]{2,1,0:T(8,128)(2,1)S(1)} collective-permute-done((bf16[3,64,1024]{2,1,0:T(8,128)(2,1)S(1)}, bf16[3,64,1024]{2,1,0:T(8,128)(2,1)S(1)}, u32[]{:S(2)}, u32[]{:S(2)}) %collective-permute-start.21) | collective-permute-done | bytes 393248 | tf_op jit(solution)/shard_map/ppermute | solution.py:155
  66.3 6.0 %collective-permute-start.19 = (bf16[3,64,1024]{2,1,0:T(8,128)(2,1)S(1)}, bf16[3,64,1024]{2,1,0:T(8,128)(2,1)S(1)}, u32[]{:S(2)}, u32[]{:S(2)}) collective-permute-start(bf16[3,64,1024]{2,1,0:T(8,128)(2,1)S(1)} %broadcast_select_fusion.9), channel_id=1, source_target_pairs={{0,1},{3,2},{1,0},{2,3},{4,5},{7,6},{5,4},{6,7},{8,9},{11,10},{9,8... | collective-permute-start | bytes 1179656 | tf_op jit(solution)/shard_map/ppermute | solution.py:159
  74.3 7.8 %collective-permute-start.25 = (bf16[3,64,1024]{2,1,0:T(8,128)(2,1)S(1)}, bf16[3,64,1024]{2,1,0:T(8,128)(2,1)S(1)}, u32[]{:S(2)}, u32[]{:S(2)}) collective-permute-start(bf16[3,64,1024]{2,1,0:T(8,128)(2,1)S(1)} %get-tuple-element.56), channel_id=1, source_target_pairs={{0,1},{3,2},{1,0},{2,3},{4,5},{7,6},{5,4},{6,7},{8,9},{11,10},{9,8... | collective-permute-start | bytes 1179656 | tf_op jit(solution)/shard_map/ppermute | solution.py:159
  83.4 7.1 %collective-permute-start.24 = (bf16[3,64,1024]{2,1,0:T(8,128)(2,1)S(1)}, bf16[3,64,1024]{2,1,0:T(8,128)(2,1)S(1)}, u32[]{:S(2)}, u32[]{:S(2)}) collective-permute-start(bf16[3,64,1024]{2,1,0:T(8,128)(2,1)S(1)} %broadcast_select_fusion.3), channel_id=1, source_target_pairs={{0,1},{3,2},{1,0},{2,3},{4,5},{7,6},{5,4},{6,7},{8,9},{11,10},{9,8... | collective-permute-start | bytes 1179656 | tf_op jit(solution)/shard_map/ppermute | solution.py:159
  95.8 2.0 %collective-permute-done.24 = bf16[3,64,1024]{2,1,0:T(8,128)(2,1)S(1)} collective-permute-done((bf16[3,64,1024]{2,1,0:T(8,128)(2,1)S(1)}, bf16[3,64,1024]{2,1,0:T(8,128)(2,1)S(1)}, u32[]{:S(2)}, u32[]{:S(2)}) %collective-permute-start.24) | collective-permute-done | bytes 393248 | tf_op jit(solution)/shard_map/ppermute | solution.py:159
  99.8 7.2 %collective-permute-start.29 = (bf16[3,64,1024]{2,1,0:T(8,128)(2,1)S(1)}, bf16[3,64,1024]{2,1,0:T(8,128)(2,1)S(1)}, u32[]{:S(2)}, u32[]{:S(2)}) collective-permute-start(bf16[3,64,1024]{2,1,0:T(8,128)(2,1)S(1)} %get-tuple-element.54), channel_id=1, source_target_pairs={{0,1},{3,2},{1,0},{2,3},{4,5},{7,6},{5,4},{6,7},{8,9},{11,10},{9,8... | collective-permute-start | bytes 1179656 | tf_op jit(solution)/shard_map/ppermute | solution.py:159
  108.8 9.0 %collective-permute-start.28 = (bf16[3,64,1024]{2,1,0:T(8,128)(2,1)S(1)}, bf16[3,64,1024]{2,1,0:T(8,128)(2,1)S(1)}, u32[]{:S(2)}, u32[]{:S(2)}) collective-permute-start(bf16[3,64,1024]{2,1,0:T(8,128)(2,1)S(1)} %broadcast_select_fusion.8), channel_id=1, source_target_pairs={{0,1},{3,2},{1,0},{2,3},{4,5},{7,6},{5,4},{6,7},{8,9},{11,10},{9,8... | collective-permute-start | bytes 1179656 | tf_op jit(solution)/shard_map/ppermute | solution.py:159
  118.9 6.5 %collective-permute-start.35 = (bf16[3,64,1024]{2,1,0:T(8,128)(2,1)S(1)}, bf16[3,64,1024]{2,1,0:T(8,128)(2,1)S(1)}, u32[]{:S(2)}, u32[]{:S(2)}) collective-permute-start(bf16[3,64,1024]{2,1,0:T(8,128)(2,1)S(1)} %get-tuple-element.50), channel_id=1, source_target_pairs={{0,1},{3,2},{1,0},{2,3},{4,5},{7,6},{5,4},{6,7},{8,9},{11,10},{9,8... | collective-permute-start | bytes 1179656 | tf_op jit(solution)/shard_map/ppermute | solution.py:159
  129.5 2.4 %collective-permute-done.35 = bf16[3,64,1024]{2,1,0:T(8,128)(2,1)S(1)} collective-permute-done((bf16[3,64,1024]{2,1,0:T(8,128)(2,1)S(1)}, bf16[3,64,1024]{2,1,0:T(8,128)(2,1)S(1)}, u32[]{:S(2)}, u32[]{:S(2)}) %collective-permute-start.35) | collective-permute-done | bytes 393248 | tf_op jit(solution)/shard_map/ppermute | solution.py:159
  134.4 11.9 %collective-permute-done.41 = bf16[3,64,1024]{2,1,0:T(8,128)(2,1)S(1)} collective-permute-done((bf16[3,64,1024]{2,1,0:T(8,128)(2,1)S(1)}, bf16[3,64,1024]{2,1,0:T(8,128)(2,1)S(1)}, u32[]{:S(2)}, u32[]{:S(2)}) %collective-permute-start.41) | collective-permute-done | bytes 393248 | tf_op jit(solution)/shard_map/ppermute | solution.py:157
  151.6 2.0 %collective-permute-done.33 = bf16[2,3,16,512]{3,2,1,0:T(8,128)(2,1)S(1)} collective-permute-done((bf16[2,3,16,512]{3,2,1,0:T(8,128)(2,1)S(1)}, bf16[2,3,16,512]{3,2,1,0:T(8,128)(2,1)S(1)}, u32[]{:S(2)}, u32[]{:S(2)}) %collective-permute-start.33) | collective-permute-done | bytes 98336 | tf_op jit(solution)/shard_map/ppermute | solution.py:59
  157.1 4.6 %collective-permute-done.38 = bf16[2,48,512]{2,1,0:T(8,128)(2,1)S(1)} collective-permute-done((bf16[2,48,512]{2,1,0:T(8,128)(2,1)S(1)}, bf16[2,48,512]{2,1,0:T(8,128)(2,1)S(1)}, u32[]{:S(2)}, u32[]{:S(2)}) %collective-permute-start.38) | collective-permute-done | bytes 98336 | tf_op jit(solution)/shard_map/ppermute | solution.py:59
  162.1 5.2 %collective-permute-done.39 = bf16[2,48,512]{2,1,0:T(8,128)(2,1)S(1)} collective-permute-done((bf16[2,48,512]{2,1,0:T(8,128)(2,1)S(1)}, bf16[2,48,512]{2,1,0:T(8,128)(2,1)S(1)}, u32[]{:S(2)}, u32[]{:S(2)}) %collective-permute-start.39) | collective-permute-done | bytes 98336 | tf_op jit(solution)/shard_map/ppermute | solution.py:59
  171.0 1.9 %collective-permute-start.47 = (bf16[2,2,16,512]{3,2,1,0:T(8,128)(2,1)S(1)}, bf16[2,2,16,512]{3,2,1,0:T(8,128)(2,1)S(1)}, u32[]{:S(2)}, u32[]{:S(2)}) collective-permute-start(bf16[2,2,16,512]{3,2,1,0:T(8,128)(2,1)S(1)} %get-tuple-element.63), channel_id=1, source_target_pairs={{0,24},{4,28},{8,16},{12,20},{16,8},{20,12},{24,0},{28,4},{1,25},{... | collective-permute-start | bytes 196616 | tf_op jit(solution)/shard_map/ppermute | solution.py:59
  174.5 2.0 %multiply_convert_fusion = bf16[1024,512]{1,0:T(8,128)(2,1)} fusion(bf16[3,640,1024]{2,1,0:T(8,128)(2,1)S(1)} %get-tuple-element.10, bf16[2,640,512]{2,1,0:T(8,128)(2,1)S(1)} %maximum_select_fusion), kind=kOutput, calls=%fused_computation | convolution fusion | flops 672137216 | bytes 3014656 | tf_op jit(solution)/shard_map/dot_general | solution.py:25
  177.7 2.0 %collective-permute-start.50 = (bf16[2,32,512]{2,1,0:T(8,128)(2,1)S(1)}, bf16[2,32,512]{2,1,0:T(8,128)(2,1)S(1)}, u32[]{:S(2)}, u32[]{:S(2)}) collective-permute-start(bf16[2,32,512]{2,1,0:T(8,128)(2,1)S(1)} %bitcast.540), channel_id=1, source_target_pairs={{0,3},{1,2},{2,1},{3,0},{4,7},{5,6},{6,5},{7,4},{8,11},{9,10},{10,... | collective-permute-start | bytes 196616 | tf_op jit(solution)/shard_map/ppermute | solution.py:59
  179.7 2.5 %collective-permute-start.48 = (bf16[2,32,512]{2,1,0:T(8,128)(2,1)S(1)}, bf16[2,32,512]{2,1,0:T(8,128)(2,1)S(1)}, u32[]{:S(2)}, u32[]{:S(2)}) collective-permute-start(bf16[2,32,512]{2,1,0:T(8,128)(2,1)S(1)} %bitcast.542), channel_id=1, source_target_pairs={{0,1},{1,0},{2,3},{3,2},{4,5},{5,4},{6,7},{7,6},{8,9},{9,8},{10,11... | collective-permute-start | bytes 196616 | tf_op jit(solution)/shard_map/ppermute | solution.py:59
  182.2 2.0 %multiply_convert_fusion.2 = bf16[512,1024]{1,0:T(8,128)(2,1)} fusion(bf16[3,640,1024]{2,1,0:T(8,128)(2,1)S(1)} %get-tuple-element.10, bf16[2,640,512]{2,1,0:T(8,128)(2,1)S(1)} %maximum_select_fusion, pred[512]{0:T(512)(128)(4,1)S(1)} %ne.87, bf16[512]{0:T(512)(128)(2,1)S(1)} %slice_reduce_fusion.1), kind=kOutput, calls=%fused_computation.2 | convolution fusion | flops 672464896 | bytes 3016192 | tf_op jit(solution)/shard_map/dot_general | solution.py:25
  184.2 2.0 %multiply_convert_fusion.1 = bf16[512,1024]{1,0:T(8,128)(2,1)} fusion(bf16[3,640,1024]{2,1,0:T(8,128)(2,1)S(1)} %get-tuple-element.10, bf16[2,640,512]{2,1,0:T(8,128)(2,1)S(1)} %maximum_select_fusion, pred[512]{0:T(512)(128)(4,1)S(1)} %ne.87, bf16[512]{0:T(512)(128)(2,1)S(1)} %slice_reduce_fusion.1), kind=kOutput, calls=%fused_computation.1 | convolution fusion | flops 672464896 | bytes 3016192 | tf_op jit(solution)/shard_map/dot_general | solution.py:25
  (244 shorter events, 61.5 us)
Async XLA Ops:
  1.5 7.6 %collective-permute-start.2 = (bf16[2,32,512]{2,1,0:T(8,128)(2,1)S(1)}, bf16[2,32,512]{2,1,0:T(8,128)(2,1)S(1)}, u32[]{:S(2)}, u32[]{:S(2)}) collective-permute-start(bf16[2,32,512]{2,1,0:T(8,128)(2,1)S(1)} %pad_maximum_fusion.26), channel_id=1, source_target_pairs={{0,3},{1,2},{2,1},{3,0},{4,7},{5,6},{6,5},{7,4},{8,11},{9,10},{10,... | collective-permute-start | bytes 196616 | tf_op jit(solution)/shard_map/ppermute | solution.py:59
  23.1 10.5 %collective-permute-start.14 = (bf16[2,48,512]{2,1,0:T(8,128)(2,1)S(1)}, bf16[2,48,512]{2,1,0:T(8,128)(2,1)S(1)}, u32[]{:S(2)}, u32[]{:S(2)}) collective-permute-start(bf16[2,48,512]{2,1,0:T(8,128)(2,1)S(1)} %fusion.112), channel_id=1, source_target_pairs={{0,3},{1,2},{2,1},{3,0},{4,7},{5,6},{6,5},{7,4},{8,11},{9,10},{10,... | collective-permute-start | bytes 294920 | tf_op jit(solution)/shard_map/ppermute | solution.py:59
  25.9 9.3 %collective-permute-start.13 = (bf16[2,48,512]{2,1,0:T(8,128)(2,1)S(1)}, bf16[2,48,512]{2,1,0:T(8,128)(2,1)S(1)}, u32[]{:S(2)}, u32[]{:S(2)}) collective-permute-start(bf16[2,48,512]{2,1,0:T(8,128)(2,1)S(1)} %fusion.112), channel_id=1, source_target_pairs={{0,2},{1,3},{2,0},{3,1},{4,6},{5,7},{6,4},{7,5},{8,10},{9,11},{10,... | collective-permute-start | bytes 294920 | tf_op jit(solution)/shard_map/ppermute | solution.py:59
  25.9 9.3 %collective-permute-start.12 = (bf16[2,48,512]{2,1,0:T(8,128)(2,1)S(1)}, bf16[2,48,512]{2,1,0:T(8,128)(2,1)S(1)}, u32[]{:S(2)}, u32[]{:S(2)}) collective-permute-start(bf16[2,48,512]{2,1,0:T(8,128)(2,1)S(1)} %fusion.112), channel_id=1, source_target_pairs={{0,1},{1,0},{2,3},{3,2},{4,5},{5,4},{6,7},{7,6},{8,9},{9,8},{10,11... | collective-permute-start | bytes 294920 | tf_op jit(solution)/shard_map/ppermute | solution.py:59
  29.9 11.4 %collective-permute-start.7 = (bf16[3,64,1024]{2,1,0:T(8,128)(2,1)S(1)}, bf16[3,64,1024]{2,1,0:T(8,128)(2,1)S(1)}, u32[]{:S(2)}, u32[]{:S(2)}) collective-permute-start(bf16[3,64,1024]{2,1,0:T(8,128)(2,1)S(1)} %pad_maximum_fusion.2), channel_id=1, source_target_pairs={{0,1},{3,2},{4,5},{7,6},{8,9},{11,10},{12,13},{15,14},{16,17},{19,... | collective-permute-start | bytes 1179656 | tf_op jit(solution)/shard_map/ppermute | solution.py:155
  35.9 12.5 %collective-permute-start.17 = (bf16[2,3,1,16,512]{4,3,2,1,0:T(8,128)(2,1)S(1)}, bf16[2,3,1,16,512]{4,3,2,1,0:T(8,128)(2,1)S(1)}, u32[]{:S(2)}, u32[]{:S(2)}) collective-permute-start(bf16[2,3,1,16,512]{4,3,2,1,0:T(8,128)(2,1)S(1)} %bitcast.536), channel_id=1, source_target_pairs={{0,24},{4,28},{8,16},{12,20},{16,8},{20,12},{24,0},{28,4},{1,25},{... | collective-permute-start | bytes 294920 | tf_op jit(solution)/shard_map/ppermute | solution.py:59
  37.4 10.9 %collective-permute-start.16 = (bf16[2,3,1,16,512]{4,3,2,1,0:T(8,128)(2,1)S(1)}, bf16[2,3,1,16,512]{4,3,2,1,0:T(8,128)(2,1)S(1)}, u32[]{:S(2)}, u32[]{:S(2)}) collective-permute-start(bf16[2,3,1,16,512]{4,3,2,1,0:T(8,128)(2,1)S(1)} %bitcast.537), channel_id=1, source_target_pairs={{0,16},{4,20},{8,24},{12,28},{16,0},{20,4},{24,8},{28,12},{1,17},{... | collective-permute-start | bytes 294920 | tf_op jit(solution)/shard_map/ppermute | solution.py:59
  37.9 10.4 %collective-permute-start.15 = (bf16[2,3,1,16,512]{4,3,2,1,0:T(8,128)(2,1)S(1)}, bf16[2,3,1,16,512]{4,3,2,1,0:T(8,128)(2,1)S(1)}, u32[]{:S(2)}, u32[]{:S(2)}) collective-permute-start(bf16[2,3,1,16,512]{4,3,2,1,0:T(8,128)(2,1)S(1)} %bitcast.538), channel_id=1, source_target_pairs={{0,8},{4,12},{8,0},{12,4},{16,24},{20,28},{24,16},{28,20},{1,9},{5... | collective-permute-start | bytes 294920 | tf_op jit(solution)/shard_map/ppermute | solution.py:59
  41.9 13.9 %collective-permute-start.8 = (bf16[3,64,1024]{2,1,0:T(8,128)(2,1)S(1)}, bf16[3,64,1024]{2,1,0:T(8,128)(2,1)S(1)}, u32[]{:S(2)}, u32[]{:S(2)}) collective-permute-start(bf16[3,64,1024]{2,1,0:T(8,128)(2,1)S(1)} %maximum_select_fusion.1), channel_id=1, source_target_pairs={{0,1},{3,2},{4,5},{7,6},{8,9},{11,10},{12,13},{15,14},{16,17},{19,... | collective-permute-start | bytes 1179656 | tf_op jit(solution)/shard_map/ppermute | solution.py:155
  48.4 12.8 %collective-permute-start.18 = (bf16[2,3,4,16,512]{4,3,2,1,0:T(8,128)(2,1)S(1)}, bf16[2,3,4,16,512]{4,3,2,1,0:T(8,128)(2,1)S(1)}, u32[]{:S(2)}, u32[]{:S(2)}) collective-permute-start(bf16[2,3,4,16,512]{4,3,2,1,0:T(8,128)(2,1)S(1)} %pad_maximum_fusion.4), channel_id=1, source_target_pairs={{0,4},{4,0},{8,12},{12,8},{16,20},{20,16},{24,28},{28,24},{1,5},{5... | collective-permute-start | bytes 1179656 | tf_op jit(solution)/shard_map/ppermute | solution.py:59
  48.5 15.7 %collective-permute-start.21 = (bf16[3,64,1024]{2,1,0:T(8,128)(2,1)S(1)}, bf16[3,64,1024]{2,1,0:T(8,128)(2,1)S(1)}, u32[]{:S(2)}, u32[]{:S(2)}) collective-permute-start(bf16[3,64,1024]{2,1,0:T(8,128)(2,1)S(1)} %pad_maximum_fusion.7), channel_id=1, source_target_pairs={{0,1},{3,2},{4,5},{7,6},{8,9},{11,10},{12,13},{15,14},{16,17},{19,... | collective-permute-start | bytes 1179656 | tf_op jit(solution)/shard_map/ppermute | solution.py:155
  56.3 9.9 %collective-permute-start.10 = (bf16[3,64,1024]{2,1,0:T(8,128)(2,1)S(1)}, bf16[3,64,1024]{2,1,0:T(8,128)(2,1)S(1)}, u32[]{:S(2)}, u32[]{:S(2)}) collective-permute-start(bf16[3,64,1024]{2,1,0:T(8,128)(2,1)S(1)} %get-tuple-element.59), channel_id=1, source_target_pairs={{1,2},{2,1},{5,6},{6,5},{9,10},{10,9},{13,14},{14,13},{17,18},{18,... | collective-permute-start | bytes 1179656 | tf_op jit(solution)/shard_map/ppermute | solution.py:164
  57.0 15.7 %collective-permute-start.20 = (bf16[3,64,1024]{2,1,0:T(8,128)(2,1)S(1)}, bf16[3,64,1024]{2,1,0:T(8,128)(2,1)S(1)}, u32[]{:S(2)}, u32[]{:S(2)}) collective-permute-start(bf16[3,64,1024]{2,1,0:T(8,128)(2,1)S(1)} %get-tuple-element.58), channel_id=1, source_target_pairs={{0,1},{3,2},{1,0},{2,3},{4,5},{7,6},{5,4},{6,7},{8,9},{11,10},{9,8... | collective-permute-start | bytes 1179656 | tf_op jit(solution)/shard_map/ppermute | solution.py:159
  64.4 8.3 %collective-permute-start.22 = (bf16[3,64,1024]{2,1,0:T(8,128)(2,1)S(1)}, bf16[3,64,1024]{2,1,0:T(8,128)(2,1)S(1)}, u32[]{:S(2)}, u32[]{:S(2)}) collective-permute-start(bf16[3,64,1024]{2,1,0:T(8,128)(2,1)S(1)} %add_convert_fusion.3), channel_id=1, source_target_pairs={{1,2},{2,1},{5,6},{6,5},{9,10},{10,9},{13,14},{14,13},{17,18},{18,... | collective-permute-start | bytes 1179656 | tf_op jit(solution)/shard_map/ppermute | solution.py:164
  66.3 16.3 %collective-permute-start.19 = (bf16[3,64,1024]{2,1,0:T(8,128)(2,1)S(1)}, bf16[3,64,1024]{2,1,0:T(8,128)(2,1)S(1)}, u32[]{:S(2)}, u32[]{:S(2)}) collective-permute-start(bf16[3,64,1024]{2,1,0:T(8,128)(2,1)S(1)} %broadcast_select_fusion.9), channel_id=1, source_target_pairs={{0,1},{3,2},{1,0},{2,3},{4,5},{7,6},{5,4},{6,7},{8,9},{11,10},{9,8... | collective-permute-start | bytes 1179656 | tf_op jit(solution)/shard_map/ppermute | solution.py:159
  73.1 10.2 %collective-permute-start.23 = (bf16[3,64,1024]{2,1,0:T(8,128)(2,1)S(1)}, bf16[3,64,1024]{2,1,0:T(8,128)(2,1)S(1)}, u32[]{:S(2)}, u32[]{:S(2)}) collective-permute-start(bf16[3,64,1024]{2,1,0:T(8,128)(2,1)S(1)} %get-tuple-element.57), channel_id=1, source_target_pairs={{1,2},{2,1},{5,6},{6,5},{9,10},{10,9},{13,14},{14,13},{17,18},{18,... | collective-permute-start | bytes 1179656 | tf_op jit(solution)/shard_map/ppermute | solution.py:164
  74.3 19.4 %collective-permute-start.25 = (bf16[3,64,1024]{2,1,0:T(8,128)(2,1)S(1)}, bf16[3,64,1024]{2,1,0:T(8,128)(2,1)S(1)}, u32[]{:S(2)}, u32[]{:S(2)}) collective-permute-start(bf16[3,64,1024]{2,1,0:T(8,128)(2,1)S(1)} %get-tuple-element.56), channel_id=1, source_target_pairs={{0,1},{3,2},{1,0},{2,3},{4,5},{7,6},{5,4},{6,7},{8,9},{11,10},{9,8... | collective-permute-start | bytes 1179656 | tf_op jit(solution)/shard_map/ppermute | solution.py:159
  83.4 14.5 %collective-permute-start.24 = (bf16[3,64,1024]{2,1,0:T(8,128)(2,1)S(1)}, bf16[3,64,1024]{2,1,0:T(8,128)(2,1)S(1)}, u32[]{:S(2)}, u32[]{:S(2)}) collective-permute-start(bf16[3,64,1024]{2,1,0:T(8,128)(2,1)S(1)} %broadcast_select_fusion.3), channel_id=1, source_target_pairs={{0,1},{3,2},{1,0},{2,3},{4,5},{7,6},{5,4},{6,7},{8,9},{11,10},{9,8... | collective-permute-start | bytes 1179656 | tf_op jit(solution)/shard_map/ppermute | solution.py:159
  99.1 9.6 %collective-permute-start.27 = (bf16[3,64,1024]{2,1,0:T(8,128)(2,1)S(1)}, bf16[3,64,1024]{2,1,0:T(8,128)(2,1)S(1)}, u32[]{:S(2)}, u32[]{:S(2)}) collective-permute-start(bf16[3,64,1024]{2,1,0:T(8,128)(2,1)S(1)} %get-tuple-element.55), channel_id=1, source_target_pairs={{1,2},{2,1},{5,6},{6,5},{9,10},{10,9},{13,14},{14,13},{17,18},{18,... | collective-permute-start | bytes 1179656 | tf_op jit(solution)/shard_map/ppermute | solution.py:164
  99.8 17.9 %collective-permute-start.29 = (bf16[3,64,1024]{2,1,0:T(8,128)(2,1)S(1)}, bf16[3,64,1024]{2,1,0:T(8,128)(2,1)S(1)}, u32[]{:S(2)}, u32[]{:S(2)}) collective-permute-start(bf16[3,64,1024]{2,1,0:T(8,128)(2,1)S(1)} %get-tuple-element.54), channel_id=1, source_target_pairs={{0,1},{3,2},{1,0},{2,3},{4,5},{7,6},{5,4},{6,7},{8,9},{11,10},{9,8... | collective-permute-start | bytes 1179656 | tf_op jit(solution)/shard_map/ppermute | solution.py:159
  107.2 10.6 %collective-permute-start.34 = (bf16[3,64,1024]{2,1,0:T(8,128)(2,1)S(1)}, bf16[3,64,1024]{2,1,0:T(8,128)(2,1)S(1)}, u32[]{:S(2)}, u32[]{:S(2)}) collective-permute-start(bf16[3,64,1024]{2,1,0:T(8,128)(2,1)S(1)} %add_convert_fusion.1), channel_id=1, source_target_pairs={{1,2},{2,1},{5,6},{6,5},{9,10},{10,9},{13,14},{14,13},{17,18},{18,... | collective-permute-start | bytes 1179656 | tf_op jit(solution)/shard_map/ppermute | solution.py:164
  108.8 16.6 %collective-permute-start.28 = (bf16[3,64,1024]{2,1,0:T(8,128)(2,1)S(1)}, bf16[3,64,1024]{2,1,0:T(8,128)(2,1)S(1)}, u32[]{:S(2)}, u32[]{:S(2)}) collective-permute-start(bf16[3,64,1024]{2,1,0:T(8,128)(2,1)S(1)} %broadcast_select_fusion.8), channel_id=1, source_target_pairs={{0,1},{3,2},{1,0},{2,3},{4,5},{7,6},{5,4},{6,7},{8,9},{11,10},{9,8... | collective-permute-start | bytes 1179656 | tf_op jit(solution)/shard_map/ppermute | solution.py:159
  118.2 10.0 %collective-permute-start.40 = (bf16[3,64,1024]{2,1,0:T(8,128)(2,1)S(1)}, bf16[3,64,1024]{2,1,0:T(8,128)(2,1)S(1)}, u32[]{:S(2)}, u32[]{:S(2)}) collective-permute-start(bf16[3,64,1024]{2,1,0:T(8,128)(2,1)S(1)} %get-tuple-element.49), channel_id=1, source_target_pairs={{1,2},{2,1},{5,6},{6,5},{9,10},{10,9},{13,14},{14,13},{17,18},{18,... | collective-permute-start | bytes 1179656 | tf_op jit(solution)/shard_map/ppermute | solution.py:164
  118.9 13.0 %collective-permute-start.35 = (bf16[3,64,1024]{2,1,0:T(8,128)(2,1)S(1)}, bf16[3,64,1024]{2,1,0:T(8,128)(2,1)S(1)}, u32[]{:S(2)}, u32[]{:S(2)}) collective-permute-start(bf16[3,64,1024]{2,1,0:T(8,128)(2,1)S(1)} %get-tuple-element.50), channel_id=1, source_target_pairs={{0,1},{3,2},{1,0},{2,3},{4,5},{7,6},{5,4},{6,7},{8,9},{11,10},{9,8... | collective-permute-start | bytes 1179656 | tf_op jit(solution)/shard_map/ppermute | solution.py:159
  128.1 6.2 %collective-permute-start.30 = (bf16[2,3,64,512]{3,2,1,0:T(8,128)(2,1)S(1)}, bf16[2,3,64,512]{3,2,1,0:T(8,128)(2,1)S(1)}, u32[]{:S(2)}, u32[]{:S(2)}) collective-permute-start(bf16[2,3,64,512]{3,2,1,0:T(8,128)(2,1)S(1)} %select_convert_fusion), channel_id=1, source_target_pairs={{0,4},{4,0},{8,12},{12,8},{16,20},{20,16},{24,28},{28,24},{1,5},{5... | collective-permute-start | bytes 1179656 | tf_op jit(solution)/shard_map/ppermute | solution.py:59
  128.2 18.1 %collective-permute-start.41 = (bf16[3,64,1024]{2,1,0:T(8,128)(2,1)S(1)}, bf16[3,64,1024]{2,1,0:T(8,128)(2,1)S(1)}, u32[]{:S(2)}, u32[]{:S(2)}) collective-permute-start(bf16[3,64,1024]{2,1,0:T(8,128)(2,1)S(1)} %collective-permute-done.40), channel_id=1, source_target_pairs={{1,0},{2,3},{5,4},{6,7},{9,8},{10,11},{13,12},{14,15},{17,16},{18,... | collective-permute-start | bytes 1179656 | tf_op jit(solution)/shard_map/ppermute | solution.py:157
  132.4 22.9 %collective-permute-start.37 = (bf16[3,64,1024]{2,1,0:T(8,128)(2,1)S(1)}, bf16[3,64,1024]{2,1,0:T(8,128)(2,1)S(1)}, u32[]{:S(2)}, u32[]{:S(2)}) collective-permute-start(bf16[3,64,1024]{2,1,0:T(8,128)(2,1)S(1)} %pad_maximum_fusion.16), channel_id=1, source_target_pairs={{1,2},{2,1},{5,6},{6,5},{9,10},{10,9},{13,14},{14,13},{17,18},{18,... | collective-permute-start | bytes 1179656 | tf_op jit(solution)/shard_map/ppermute | solution.py:164
  133.1 34.5 %collective-permute-start.43 = (bf16[3,64,1024]{2,1,0:T(8,128)(2,1)S(1)}, bf16[3,64,1024]{2,1,0:T(8,128)(2,1)S(1)}, u32[]{:S(2)}, u32[]{:S(2)}) collective-permute-start(bf16[3,64,1024]{2,1,0:T(8,128)(2,1)S(1)} %pad_maximum_fusion.16), channel_id=1, source_target_pairs={{1,0},{2,3},{5,4},{6,7},{9,8},{10,11},{13,12},{14,15},{17,16},{18,... | collective-permute-start | bytes 1179656 | tf_op jit(solution)/shard_map/ppermute | solution.py:157
  155.5 11.8 %collective-permute-start.42 = (bf16[3,64,1024]{2,1,0:T(8,128)(2,1)S(1)}, bf16[3,64,1024]{2,1,0:T(8,128)(2,1)S(1)}, u32[]{:S(2)}, u32[]{:S(2)}) collective-permute-start(bf16[3,64,1024]{2,1,0:T(8,128)(2,1)S(1)} %broadcast_select_fusion), channel_id=1, source_target_pairs={{1,0},{2,3},{5,4},{6,7},{9,8},{10,11},{13,12},{14,15},{17,16},{18,... | collective-permute-start | bytes 1179656 | tf_op jit(solution)/shard_map/ppermute | solution.py:157
  177.7 8.5 %collective-permute-start.50 = (bf16[2,32,512]{2,1,0:T(8,128)(2,1)S(1)}, bf16[2,32,512]{2,1,0:T(8,128)(2,1)S(1)}, u32[]{:S(2)}, u32[]{:S(2)}) collective-permute-start(bf16[2,32,512]{2,1,0:T(8,128)(2,1)S(1)} %bitcast.540), channel_id=1, source_target_pairs={{0,3},{1,2},{2,1},{3,0},{4,7},{5,6},{6,5},{7,4},{8,11},{9,10},{10,... | collective-permute-start | bytes 196616 | tf_op jit(solution)/shard_map/ppermute | solution.py:59
  179.7 6.5 %collective-permute-start.49 = (bf16[2,32,512]{2,1,0:T(8,128)(2,1)S(1)}, bf16[2,32,512]{2,1,0:T(8,128)(2,1)S(1)}, u32[]{:S(2)}, u32[]{:S(2)}) collective-permute-start(bf16[2,32,512]{2,1,0:T(8,128)(2,1)S(1)} %bitcast.541), channel_id=1, source_target_pairs={{0,2},{1,3},{2,0},{3,1},{4,6},{5,7},{6,4},{7,5},{8,10},{9,11},{10,... | collective-permute-start | bytes 196616 | tf_op jit(solution)/shard_map/ppermute | solution.py:59
  179.7 6.5 %collective-permute-start.48 = (bf16[2,32,512]{2,1,0:T(8,128)(2,1)S(1)}, bf16[2,32,512]{2,1,0:T(8,128)(2,1)S(1)}, u32[]{:S(2)}, u32[]{:S(2)}) collective-permute-start(bf16[2,32,512]{2,1,0:T(8,128)(2,1)S(1)} %bitcast.542), channel_id=1, source_target_pairs={{0,1},{1,0},{2,3},{3,2},{4,5},{5,4},{6,7},{7,6},{8,9},{9,8},{10,11... | collective-permute-start | bytes 196616 | tf_op jit(solution)/shard_map/ppermute | solution.py:59
  (25 other events, 200.9 us)

commit v12 on v11

--- a/solution.py
+++ b/solution.py
@@ -81,7 +81,7 @@
     block = turn(block)
     for level, bit in enumerate(bits):
         message = block.astype(BF16)
-        came = exchange(message if level else after(message, ahead), "tensor", 1 << level)
+        came = exchange(after(message, ahead[level]) if level < len(ahead) else message, "tensor", 1 << level)
         block = block * bit[:, : block.shape[-1]] + came.astype(F32)
     return block
 
@@ -255,9 +255,10 @@
                 crossed.append(across(acts[i]))
                 outs += [acts[i], crossed[i]]
     low, high = leave([done(i) for i in range(split, chunks)])
+    sums, _, ahead = scatter_dp(low, high)
     if split > 0:
-        ends.append(rotate_by_halves(first_sums.reshape(2, -1, width), bits, crossed[-1]))
-    sums, _, ahead = scatter_dp(low, high)
+        first_sums = first_sums.reshape(2, -1, width)
+        ends.append(rotate_by_halves(first_sums, bits, [came[-1], ahead]))
     ends.append(rotate(spread(sums.reshape(2, -1, width).astype(BF16)), signs))
     ends = jnp.concatenate(ends, axis=1)
 

time: 188 us -> 192 us (1.021)
  waiting for transfers between devices: 48.9 us -> 52.1 us
    ppermute x3, waiting for transfers between devices: 11.9 us -> 19.7 us  [swap(): return lax.ppermute(out, 'tensor', back)]
    ppermute x28, waiting for transfers between devices: 25 us -> 20.4 us  [exchange(): return lax.ppermute(block, axis, [(i, i ^ apart) for i in range(count)])]
where the time goes in v12:
time: 192 us; the launch traced here: 191 us
  starting transfers between devices  98.9 us (52%)
  waiting for transfers between devices  52.1 us (27%)
  matrix products  26.8 us (14%)
  other arithmetic  10.4 us (5%)
  between operations  2.02 us (1%)
    ppermute x7, starting transfers between devices, swap(): return lax.ppermute(block, 'tensor', pairs + back)  47.6 us
    ppermute x28, starting transfers between devices, exchange(): return lax.ppermute(block, axis, [(i, i ^ apart) for i in range(count)])  29.9 us
    dot_general x56, matrix products, dot(): lax.dot_general(left, right, (((left_dim,), (right_dim,)), ((), ())), pre...  26.8 us
    ppermute x28, waiting for transfers between devices, exchange(): return lax.ppermute(block, axis, [(i, i ^ apart) for i in range(count)])  20.4 us
    ppermute x3, waiting for transfers between devices, swap(): return lax.ppermute(out, 'tensor', back)  19.7 us
    ppermute x3, starting transfers between devices, swap(): return lax.ppermute(into, 'tensor', pairs)  10.2 us
    ppermute x3, waiting for transfers between devices, swap(): return lax.ppermute(into, 'tensor', pairs)  7.08 us
    ppermute x10, starting transfers between devices, across(): return lax.ppermute(block, 'tensor', [(half - 1, half), (half, half - 1)])  7.04 us
  transfers between devices with their start and end apart: 51, of which 22 were waited for; matrix products, arithmetic and copies ran while one was open for 16% of the time, Pallas kernels for 0%

profile of v12, /device:TPU:0, one launch (start us, length us, event | category | flops | bytes accessed | tf_op | source)
XLA Modules:
  0.0 191.3 jit_solution(9312194265681117139)
XLA Ops:
  1.5 5.0 %collective-permute-start.2 = (bf16[2,32,512]{2,1,0:T(8,128)(2,1)S(1)}, bf16[2,32,512]{2,1,0:T(8,128)(2,1)S(1)}, u32[]{:S(2)}, u32[]{:S(2)}) collective-permute-start(bf16[2,32,512]{2,1,0:T(8,128)(2,1)S(1)} %pad_maximum_fusion.26), channel_id=1, source_target_pairs={{0,3},{1,2},{2,1},{3,0},{4,7},{5,6},{6,5},{7,4},{8,11},{9,10},{10,... | collective-permute-start | bytes 196616 | tf_op jit(solution)/shard_map/ppermute | solution.py:59
  9.2 3.0 %collective-permute-done.1 = bf16[2,32,512]{2,1,0:T(8,128)(2,1)S(1)} collective-permute-done((bf16[2,32,512]{2,1,0:T(8,128)(2,1)S(1)}, bf16[2,32,512]{2,1,0:T(8,128)(2,1)S(1)}, u32[]{:S(2)}, u32[]{:S(2)}) %collective-permute-start.1) | collective-permute-done | bytes 65568 | tf_op jit(solution)/shard_map/ppermute | solution.py:59
  15.7 2.5 %collective-permute-start.5 = (bf16[2,2,1,16,512]{4,3,2,1,0:T(8,128)(2,1)S(1)}, bf16[2,2,1,16,512]{4,3,2,1,0:T(8,128)(2,1)S(1)}, u32[]{:S(2)}, u32[]{:S(2)}) collective-permute-start(bf16[2,2,1,16,512]{4,3,2,1,0:T(8,128)(2,1)S(1)} %bitcast.530), channel_id=1, source_target_pairs={{0,24},{4,28},{8,16},{12,20},{16,8},{20,12},{24,0},{28,4},{1,25},{... | collective-permute-start | bytes 196616 | tf_op jit(solution)/shard_map/ppermute | solution.py:59
  19.2 1.7 collective-permute-done.5
  23.1 2.8 %collective-permute-start.14 = (bf16[2,48,512]{2,1,0:T(8,128)(2,1)S(1)}, bf16[2,48,512]{2,1,0:T(8,128)(2,1)S(1)}, u32[]{:S(2)}, u32[]{:S(2)}) collective-permute-start(bf16[2,48,512]{2,1,0:T(8,128)(2,1)S(1)} %fusion.113), channel_id=1, source_target_pairs={{0,3},{1,2},{2,1},{3,0},{4,7},{5,6},{6,5},{7,4},{8,11},{9,10},{10,... | collective-permute-start | bytes 294920 | tf_op jit(solution)/shard_map/ppermute | solution.py:59
  25.9 1.7 collective-permute-start.12
  29.9 2.4 %collective-permute-start.7 = (bf16[3,64,1024]{2,1,0:T(8,128)(2,1)S(1)}, bf16[3,64,1024]{2,1,0:T(8,128)(2,1)S(1)}, u32[]{:S(2)}, u32[]{:S(2)}) collective-permute-start(bf16[3,64,1024]{2,1,0:T(8,128)(2,1)S(1)} %pad_maximum_fusion.2), channel_id=1, source_target_pairs={{0,1},{3,2},{4,5},{7,6},{8,9},{11,10},{12,13},{15,14},{16,17},{19,... | collective-permute-start | bytes 1179656 | tf_op jit(solution)/shard_map/ppermute | solution.py:155
  33.6 1.6 collective-permute-done.13
  39.4 1.9 %collective-permute-done.7 = bf16[3,64,1024]{2,1,0:T(8,128)(2,1)S(1)} collective-permute-done((bf16[3,64,1024]{2,1,0:T(8,128)(2,1)S(1)}, bf16[3,64,1024]{2,1,0:T(8,128)(2,1)S(1)}, u32[]{:S(2)}, u32[]{:S(2)}) %collective-permute-start.7) | collective-permute-done | bytes 393248 | tf_op jit(solution)/shard_map/ppermute | solution.py:155
  41.9 4.4 %collective-permute-start.8 = (bf16[3,64,1024]{2,1,0:T(8,128)(2,1)S(1)}, bf16[3,64,1024]{2,1,0:T(8,128)(2,1)S(1)}, u32[]{:S(2)}, u32[]{:S(2)}) collective-permute-start(bf16[3,64,1024]{2,1,0:T(8,128)(2,1)S(1)} %maximum_select_fusion.1), channel_id=1, source_target_pairs={{0,1},{3,2},{4,5},{7,6},{8,9},{11,10},{12,13},{15,14},{16,17},{19,... | collective-permute-start | bytes 1179656 | tf_op jit(solution)/shard_map/ppermute | solution.py:155
  48.5 3.4 %collective-permute-start.21 = (bf16[3,64,1024]{2,1,0:T(8,128)(2,1)S(1)}, bf16[3,64,1024]{2,1,0:T(8,128)(2,1)S(1)}, u32[]{:S(2)}, u32[]{:S(2)}) collective-permute-start(bf16[3,64,1024]{2,1,0:T(8,128)(2,1)S(1)} %pad_maximum_fusion.7), channel_id=1, source_target_pairs={{0,1},{3,2},{4,5},{7,6},{8,9},{11,10},{12,13},{15,14},{16,17},{19,... | collective-permute-start | bytes 1179656 | tf_op jit(solution)/shard_map/ppermute | solution.py:155
  52.6 3.3 %collective-permute-done.8 = bf16[3,64,1024]{2,1,0:T(8,128)(2,1)S(1)} collective-permute-done((bf16[3,64,1024]{2,1,0:T(8,128)(2,1)S(1)}, bf16[3,64,1024]{2,1,0:T(8,128)(2,1)S(1)}, u32[]{:S(2)}, u32[]{:S(2)}) %collective-permute-start.8) | collective-permute-done | bytes 393248 | tf_op jit(solution)/shard_map/ppermute | solution.py:155
  57.0 4.2 %collective-permute-start.20 = (bf16[3,64,1024]{2,1,0:T(8,128)(2,1)S(1)}, bf16[3,64,1024]{2,1,0:T(8,128)(2,1)S(1)}, u32[]{:S(2)}, u32[]{:S(2)}) collective-permute-start(bf16[3,64,1024]{2,1,0:T(8,128)(2,1)S(1)} %get-tuple-element.58), channel_id=1, source_target_pairs={{0,1},{3,2},{1,0},{2,3},{4,5},{7,6},{5,4},{6,7},{8,9},{11,10},{9,8... | collective-permute-start | bytes 1179656 | tf_op jit(solution)/shard_map/ppermute | solution.py:159
  62.3 1.9 %collective-permute-done.21 = bf16[3,64,1024]{2,1,0:T(8,128)(2,1)S(1)} collective-permute-done((bf16[3,64,1024]{2,1,0:T(8,128)(2,1)S(1)}, bf16[3,64,1024]{2,1,0:T(8,128)(2,1)S(1)}, u32[]{:S(2)}, u32[]{:S(2)}) %collective-permute-start.21) | collective-permute-done | bytes 393248 | tf_op jit(solution)/shard_map/ppermute | solution.py:155
  66.3 6.0 %collective-permute-start.19 = (bf16[3,64,1024]{2,1,0:T(8,128)(2,1)S(1)}, bf16[3,64,1024]{2,1,0:T(8,128)(2,1)S(1)}, u32[]{:S(2)}, u32[]{:S(2)}) collective-permute-start(bf16[3,64,1024]{2,1,0:T(8,128)(2,1)S(1)} %broadcast_select_fusion.9), channel_id=1, source_target_pairs={{0,1},{3,2},{1,0},{2,3},{4,5},{7,6},{5,4},{6,7},{8,9},{11,10},{9,8... | collective-permute-start | bytes 1179656 | tf_op jit(solution)/shard_map/ppermute | solution.py:159
  74.3 7.8 %collective-permute-start.25 = (bf16[3,64,1024]{2,1,0:T(8,128)(2,1)S(1)}, bf16[3,64,1024]{2,1,0:T(8,128)(2,1)S(1)}, u32[]{:S(2)}, u32[]{:S(2)}) collective-permute-start(bf16[3,64,1024]{2,1,0:T(8,128)(2,1)S(1)} %get-tuple-element.56), channel_id=1, source_target_pairs={{0,1},{3,2},{1,0},{2,3},{4,5},{7,6},{5,4},{6,7},{8,9},{11,10},{9,8... | collective-permute-start | bytes 1179656 | tf_op jit(solution)/shard_map/ppermute | solution.py:159
  83.4 7.1 %collective-permute-start.24 = (bf16[3,64,1024]{2,1,0:T(8,128)(2,1)S(1)}, bf16[3,64,1024]{2,1,0:T(8,128)(2,1)S(1)}, u32[]{:S(2)}, u32[]{:S(2)}) collective-permute-start(bf16[3,64,1024]{2,1,0:T(8,128)(2,1)S(1)} %broadcast_select_fusion.3), channel_id=1, source_target_pairs={{0,1},{3,2},{1,0},{2,3},{4,5},{7,6},{5,4},{6,7},{8,9},{11,10},{9,8... | collective-permute-start | bytes 1179656 | tf_op jit(solution)/shard_map/ppermute | solution.py:159
  95.8 2.0 %collective-permute-done.24 = bf16[3,64,1024]{2,1,0:T(8,128)(2,1)S(1)} collective-permute-done((bf16[3,64,1024]{2,1,0:T(8,128)(2,1)S(1)}, bf16[3,64,1024]{2,1,0:T(8,128)(2,1)S(1)}, u32[]{:S(2)}, u32[]{:S(2)}) %collective-permute-start.24) | collective-permute-done | bytes 393248 | tf_op jit(solution)/shard_map/ppermute | solution.py:159
  99.8 7.2 %collective-permute-start.29 = (bf16[3,64,1024]{2,1,0:T(8,128)(2,1)S(1)}, bf16[3,64,1024]{2,1,0:T(8,128)(2,1)S(1)}, u32[]{:S(2)}, u32[]{:S(2)}) collective-permute-start(bf16[3,64,1024]{2,1,0:T(8,128)(2,1)S(1)} %get-tuple-element.54), channel_id=1, source_target_pairs={{0,1},{3,2},{1,0},{2,3},{4,5},{7,6},{5,4},{6,7},{8,9},{11,10},{9,8... | collective-permute-start | bytes 1179656 | tf_op jit(solution)/shard_map/ppermute | solution.py:159
  108.8 9.0 %collective-permute-start.28 = (bf16[3,64,1024]{2,1,0:T(8,128)(2,1)S(1)}, bf16[3,64,1024]{2,1,0:T(8,128)(2,1)S(1)}, u32[]{:S(2)}, u32[]{:S(2)}) collective-permute-start(bf16[3,64,1024]{2,1,0:T(8,128)(2,1)S(1)} %broadcast_select_fusion.8), channel_id=1, source_target_pairs={{0,1},{3,2},{1,0},{2,3},{4,5},{7,6},{5,4},{6,7},{8,9},{11,10},{9,8... | collective-permute-start | bytes 1179656 | tf_op jit(solution)/shard_map/ppermute | solution.py:159
  118.9 6.5 %collective-permute-start.35 = (bf16[3,64,1024]{2,1,0:T(8,128)(2,1)S(1)}, bf16[3,64,1024]{2,1,0:T(8,128)(2,1)S(1)}, u32[]{:S(2)}, u32[]{:S(2)}) collective-permute-start(bf16[3,64,1024]{2,1,0:T(8,128)(2,1)S(1)} %get-tuple-element.50), channel_id=1, source_target_pairs={{0,1},{3,2},{1,0},{2,3},{4,5},{7,6},{5,4},{6,7},{8,9},{11,10},{9,8... | collective-permute-start | bytes 1179656 | tf_op jit(solution)/shard_map/ppermute | solution.py:159
  129.5 2.4 %collective-permute-done.35 = bf16[3,64,1024]{2,1,0:T(8,128)(2,1)S(1)} collective-permute-done((bf16[3,64,1024]{2,1,0:T(8,128)(2,1)S(1)}, bf16[3,64,1024]{2,1,0:T(8,128)(2,1)S(1)}, u32[]{:S(2)}, u32[]{:S(2)}) %collective-permute-start.35) | collective-permute-done | bytes 393248 | tf_op jit(solution)/shard_map/ppermute | solution.py:159
  134.4 12.0 %collective-permute-done.41 = bf16[3,64,1024]{2,1,0:T(8,128)(2,1)S(1)} collective-permute-done((bf16[3,64,1024]{2,1,0:T(8,128)(2,1)S(1)}, bf16[3,64,1024]{2,1,0:T(8,128)(2,1)S(1)}, u32[]{:S(2)}, u32[]{:S(2)}) %collective-permute-start.41) | collective-permute-done | bytes 393248 | tf_op jit(solution)/shard_map/ppermute | solution.py:157
  152.0 2.0 %collective-permute-done.33 = bf16[2,3,16,512]{3,2,1,0:T(8,128)(2,1)S(1)} collective-permute-done((bf16[2,3,16,512]{3,2,1,0:T(8,128)(2,1)S(1)}, bf16[2,3,16,512]{3,2,1,0:T(8,128)(2,1)S(1)}, u32[]{:S(2)}, u32[]{:S(2)}) %collective-permute-start.33) | collective-permute-done | bytes 98336 | tf_op jit(solution)/shard_map/ppermute | solution.py:59
  157.3 7.7 %collective-permute-done.38 = bf16[3,64,1024]{2,1,0:T(8,128)(2,1)S(1)} collective-permute-done((bf16[3,64,1024]{2,1,0:T(8,128)(2,1)S(1)}, bf16[3,64,1024]{2,1,0:T(8,128)(2,1)S(1)}, u32[]{:S(2)}, u32[]{:S(2)}) %collective-permute-start.38) | collective-permute-done | bytes 393248 | tf_op jit(solution)/shard_map/ppermute | solution.py:157
  168.7 2.5 %collective-permute-start.44 = (bf16[2,2,16,512]{3,2,1,0:T(8,128)(2,1)S(1)}, bf16[2,2,16,512]{3,2,1,0:T(8,128)(2,1)S(1)}, u32[]{:S(2)}, u32[]{:S(2)}) collective-permute-start(bf16[2,2,16,512]{3,2,1,0:T(8,128)(2,1)S(1)} %get-tuple-element.64), channel_id=1, source_target_pairs={{0,24},{4,28},{8,16},{12,20},{16,8},{20,12},{24,0},{28,4},{1,25},{... | collective-permute-start | bytes 196616 | tf_op jit(solution)/shard_map/ppermute | solution.py:59
  172.2 2.0 %multiply_convert_fusion = bf16[1024,512]{1,0:T(8,128)(2,1)} fusion(bf16[3,640,1024]{2,1,0:T(8,128)(2,1)S(1)} %get-tuple-element.10, bf16[2,640,512]{2,1,0:T(8,128)(2,1)S(1)} %maximum_select_fusion), kind=kOutput, calls=%fused_computation | convolution fusion | flops 672137216 | bytes 3014656 | tf_op jit(solution)/shard_map/dot_general | solution.py:25
  175.9 2.1 %collective-permute-start.50 = (bf16[2,32,512]{2,1,0:T(8,128)(2,1)S(1)}, bf16[2,32,512]{2,1,0:T(8,128)(2,1)S(1)}, u32[]{:S(2)}, u32[]{:S(2)}) collective-permute-start(bf16[2,32,512]{2,1,0:T(8,128)(2,1)S(1)} %bitcast.541), channel_id=1, source_target_pairs={{0,3},{1,2},{2,1},{3,0},{4,7},{5,6},{6,5},{7,4},{8,11},{9,10},{10,... | collective-permute-start | bytes 196616 | tf_op jit(solution)/shard_map/ppermute | solution.py:59
  178.3 2.0 %collective-permute-start.48 = (bf16[2,32,512]{2,1,0:T(8,128)(2,1)S(1)}, bf16[2,32,512]{2,1,0:T(8,128)(2,1)S(1)}, u32[]{:S(2)}, u32[]{:S(2)}) collective-permute-start(bf16[2,32,512]{2,1,0:T(8,128)(2,1)S(1)} %bitcast.543), channel_id=1, source_target_pairs={{0,1},{1,0},{2,3},{3,2},{4,5},{5,4},{6,7},{7,6},{8,9},{9,8},{10,11... | collective-permute-start | bytes 196616 | tf_op jit(solution)/shard_map/ppermute | solution.py:59
  180.4 2.0 %multiply_convert_fusion.2 = bf16[512,1024]{1,0:T(8,128)(2,1)} fusion(bf16[3,640,1024]{2,1,0:T(8,128)(2,1)S(1)} %get-tuple-element.10, bf16[2,640,512]{2,1,0:T(8,128)(2,1)S(1)} %maximum_select_fusion, pred[512]{0:T(512)(128)(4,1)S(1)} %ne.94, bf16[512]{0:T(512)(128)(2,1)S(1)} %slice_reduce_fusion.1), kind=kOutput, calls=%fused_computation.2 | convolution fusion | flops 672464896 | bytes 3016192 | tf_op jit(solution)/shard_map/dot_general | solution.py:25
  182.4 2.0 %multiply_convert_fusion.1 = bf16[512,1024]{1,0:T(8,128)(2,1)} fusion(bf16[3,640,1024]{2,1,0:T(8,128)(2,1)S(1)} %get-tuple-element.10, bf16[2,640,512]{2,1,0:T(8,128)(2,1)S(1)} %maximum_select_fusion, pred[512]{0:T(512)(128)(4,1)S(1)} %ne.94, bf16[512]{0:T(512)(128)(2,1)S(1)} %slice_reduce_fusion.1), kind=kOutput, calls=%fused_computation.1 | convolution fusion | flops 672464896 | bytes 3016192 | tf_op jit(solution)/shard_map/dot_general | solution.py:25
  185.7 4.9 %collective-permute-done.45 = bf16[2,48,512]{2,1,0:T(8,128)(2,1)S(1)} collective-permute-done((bf16[2,48,512]{2,1,0:T(8,128)(2,1)S(1)}, bf16[2,48,512]{2,1,0:T(8,128)(2,1)S(1)}, u32[]{:S(2)}, u32[]{:S(2)}) %collective-permute-start.45) | collective-permute-done | bytes 98336 | tf_op jit(solution)/shard_map/ppermute | solution.py:59
  (246 shorter events, 62.3 us)
Async XLA Ops:
  1.5 7.6 %collective-permute-start.2 = (bf16[2,32,512]{2,1,0:T(8,128)(2,1)S(1)}, bf16[2,32,512]{2,1,0:T(8,128)(2,1)S(1)}, u32[]{:S(2)}, u32[]{:S(2)}) collective-permute-start(bf16[2,32,512]{2,1,0:T(8,128)(2,1)S(1)} %pad_maximum_fusion.26), channel_id=1, source_target_pairs={{0,3},{1,2},{2,1},{3,0},{4,7},{5,6},{6,5},{7,4},{8,11},{9,10},{10,... | collective-permute-start | bytes 196616 | tf_op jit(solution)/shard_map/ppermute | solution.py:59
  23.1 10.5 %collective-permute-start.14 = (bf16[2,48,512]{2,1,0:T(8,128)(2,1)S(1)}, bf16[2,48,512]{2,1,0:T(8,128)(2,1)S(1)}, u32[]{:S(2)}, u32[]{:S(2)}) collective-permute-start(bf16[2,48,512]{2,1,0:T(8,128)(2,1)S(1)} %fusion.113), channel_id=1, source_target_pairs={{0,3},{1,2},{2,1},{3,0},{4,7},{5,6},{6,5},{7,4},{8,11},{9,10},{10,... | collective-permute-start | bytes 294920 | tf_op jit(solution)/shard_map/ppermute | solution.py:59
  25.9 9.3 %collective-permute-start.13 = (bf16[2,48,512]{2,1,0:T(8,128)(2,1)S(1)}, bf16[2,48,512]{2,1,0:T(8,128)(2,1)S(1)}, u32[]{:S(2)}, u32[]{:S(2)}) collective-permute-start(bf16[2,48,512]{2,1,0:T(8,128)(2,1)S(1)} %fusion.113), channel_id=1, source_target_pairs={{0,2},{1,3},{2,0},{3,1},{4,6},{5,7},{6,4},{7,5},{8,10},{9,11},{10,... | collective-permute-start | bytes 294920 | tf_op jit(solution)/shard_map/ppermute | solution.py:59
  25.9 9.3 %collective-permute-start.12 = (bf16[2,48,512]{2,1,0:T(8,128)(2,1)S(1)}, bf16[2,48,512]{2,1,0:T(8,128)(2,1)S(1)}, u32[]{:S(2)}, u32[]{:S(2)}) collective-permute-start(bf16[2,48,512]{2,1,0:T(8,128)(2,1)S(1)} %fusion.113), channel_id=1, source_target_pairs={{0,1},{1,0},{2,3},{3,2},{4,5},{5,4},{6,7},{7,6},{8,9},{9,8},{10,11... | collective-permute-start | bytes 294920 | tf_op jit(solution)/shard_map/ppermute | solution.py:59
  29.9 11.4 %collective-permute-start.7 = (bf16[3,64,1024]{2,1,0:T(8,128)(2,1)S(1)}, bf16[3,64,1024]{2,1,0:T(8,128)(2,1)S(1)}, u32[]{:S(2)}, u32[]{:S(2)}) collective-permute-start(bf16[3,64,1024]{2,1,0:T(8,128)(2,1)S(1)} %pad_maximum_fusion.2), channel_id=1, source_target_pairs={{0,1},{3,2},{4,5},{7,6},{8,9},{11,10},{12,13},{15,14},{16,17},{19,... | collective-permute-start | bytes 1179656 | tf_op jit(solution)/shard_map/ppermute | solution.py:155
  35.9 12.5 %collective-permute-start.17 = (bf16[2,3,1,16,512]{4,3,2,1,0:T(8,128)(2,1)S(1)}, bf16[2,3,1,16,512]{4,3,2,1,0:T(8,128)(2,1)S(1)}, u32[]{:S(2)}, u32[]{:S(2)}) collective-permute-start(bf16[2,3,1,16,512]{4,3,2,1,0:T(8,128)(2,1)S(1)} %bitcast.537), channel_id=1, source_target_pairs={{0,24},{4,28},{8,16},{12,20},{16,8},{20,12},{24,0},{28,4},{1,25},{... | collective-permute-start | bytes 294920 | tf_op jit(solution)/shard_map/ppermute | solution.py:59
  37.4 10.9 %collective-permute-start.16 = (bf16[2,3,1,16,512]{4,3,2,1,0:T(8,128)(2,1)S(1)}, bf16[2,3,1,16,512]{4,3,2,1,0:T(8,128)(2,1)S(1)}, u32[]{:S(2)}, u32[]{:S(2)}) collective-permute-start(bf16[2,3,1,16,512]{4,3,2,1,0:T(8,128)(2,1)S(1)} %bitcast.538), channel_id=1, source_target_pairs={{0,16},{4,20},{8,24},{12,28},{16,0},{20,4},{24,8},{28,12},{1,17},{... | collective-permute-start | bytes 294920 | tf_op jit(solution)/shard_map/ppermute | solution.py:59
  37.9 10.4 %collective-permute-start.15 = (bf16[2,3,1,16,512]{4,3,2,1,0:T(8,128)(2,1)S(1)}, bf16[2,3,1,16,512]{4,3,2,1,0:T(8,128)(2,1)S(1)}, u32[]{:S(2)}, u32[]{:S(2)}) collective-permute-start(bf16[2,3,1,16,512]{4,3,2,1,0:T(8,128)(2,1)S(1)} %bitcast.539), channel_id=1, source_target_pairs={{0,8},{4,12},{8,0},{12,4},{16,24},{20,28},{24,16},{28,20},{1,9},{5... | collective-permute-start | bytes 294920 | tf_op jit(solution)/shard_map/ppermute | solution.py:59
  41.9 13.9 %collective-permute-start.8 = (bf16[3,64,1024]{2,1,0:T(8,128)(2,1)S(1)}, bf16[3,64,1024]{2,1,0:T(8,128)(2,1)S(1)}, u32[]{:S(2)}, u32[]{:S(2)}) collective-permute-start(bf16[3,64,1024]{2,1,0:T(8,128)(2,1)S(1)} %maximum_select_fusion.1), channel_id=1, source_target_pairs={{0,1},{3,2},{4,5},{7,6},{8,9},{11,10},{12,13},{15,14},{16,17},{19,... | collective-permute-start | bytes 1179656 | tf_op jit(solution)/shard_map/ppermute | solution.py:155
  48.4 12.8 %collective-permute-start.18 = (bf16[2,3,4,16,512]{4,3,2,1,0:T(8,128)(2,1)S(1)}, bf16[2,3,4,16,512]{4,3,2,1,0:T(8,128)(2,1)S(1)}, u32[]{:S(2)}, u32[]{:S(2)}) collective-permute-start(bf16[2,3,4,16,512]{4,3,2,1,0:T(8,128)(2,1)S(1)} %pad_maximum_fusion.4), channel_id=1, source_target_pairs={{0,4},{4,0},{8,12},{12,8},{16,20},{20,16},{24,28},{28,24},{1,5},{5... | collective-permute-start | bytes 1179656 | tf_op jit(solution)/shard_map/ppermute | solution.py:59
  48.5 15.7 %collective-permute-start.21 = (bf16[3,64,1024]{2,1,0:T(8,128)(2,1)S(1)}, bf16[3,64,1024]{2,1,0:T(8,128)(2,1)S(1)}, u32[]{:S(2)}, u32[]{:S(2)}) collective-permute-start(bf16[3,64,1024]{2,1,0:T(8,128)(2,1)S(1)} %pad_maximum_fusion.7), channel_id=1, source_target_pairs={{0,1},{3,2},{4,5},{7,6},{8,9},{11,10},{12,13},{15,14},{16,17},{19,... | collective-permute-start | bytes 1179656 | tf_op jit(solution)/shard_map/ppermute | solution.py:155
  56.3 9.9 %collective-permute-start.10 = (bf16[3,64,1024]{2,1,0:T(8,128)(2,1)S(1)}, bf16[3,64,1024]{2,1,0:T(8,128)(2,1)S(1)}, u32[]{:S(2)}, u32[]{:S(2)}) collective-permute-start(bf16[3,64,1024]{2,1,0:T(8,128)(2,1)S(1)} %get-tuple-element.59), channel_id=1, source_target_pairs={{1,2},{2,1},{5,6},{6,5},{9,10},{10,9},{13,14},{14,13},{17,18},{18,... | collective-permute-start | bytes 1179656 | tf_op jit(solution)/shard_map/ppermute | solution.py:164
  57.0 15.7 %collective-permute-start.20 = (bf16[3,64,1024]{2,1,0:T(8,128)(2,1)S(1)}, bf16[3,64,1024]{2,1,0:T(8,128)(2,1)S(1)}, u32[]{:S(2)}, u32[]{:S(2)}) collective-permute-start(bf16[3,64,1024]{2,1,0:T(8,128)(2,1)S(1)} %get-tuple-element.58), channel_id=1, source_target_pairs={{0,1},{3,2},{1,0},{2,3},{4,5},{7,6},{5,4},{6,7},{8,9},{11,10},{9,8... | collective-permute-start | bytes 1179656 | tf_op jit(solution)/shard_map/ppermute | solution.py:159
  64.4 8.3 %collective-permute-start.22 = (bf16[3,64,1024]{2,1,0:T(8,128)(2,1)S(1)}, bf16[3,64,1024]{2,1,0:T(8,128)(2,1)S(1)}, u32[]{:S(2)}, u32[]{:S(2)}) collective-permute-start(bf16[3,64,1024]{2,1,0:T(8,128)(2,1)S(1)} %add_convert_fusion.3), channel_id=1, source_target_pairs={{1,2},{2,1},{5,6},{6,5},{9,10},{10,9},{13,14},{14,13},{17,18},{18,... | collective-permute-start | bytes 1179656 | tf_op jit(solution)/shard_map/ppermute | solution.py:164
  66.3 16.3 %collective-permute-start.19 = (bf16[3,64,1024]{2,1,0:T(8,128)(2,1)S(1)}, bf16[3,64,1024]{2,1,0:T(8,128)(2,1)S(1)}, u32[]{:S(2)}, u32[]{:S(2)}) collective-permute-start(bf16[3,64,1024]{2,1,0:T(8,128)(2,1)S(1)} %broadcast_select_fusion.9), channel_id=1, source_target_pairs={{0,1},{3,2},{1,0},{2,3},{4,5},{7,6},{5,4},{6,7},{8,9},{11,10},{9,8... | collective-permute-start | bytes 1179656 | tf_op jit(solution)/shard_map/ppermute | solution.py:159
  73.1 10.2 %collective-permute-start.23 = (bf16[3,64,1024]{2,1,0:T(8,128)(2,1)S(1)}, bf16[3,64,1024]{2,1,0:T(8,128)(2,1)S(1)}, u32[]{:S(2)}, u32[]{:S(2)}) collective-permute-start(bf16[3,64,1024]{2,1,0:T(8,128)(2,1)S(1)} %get-tuple-element.57), channel_id=1, source_target_pairs={{1,2},{2,1},{5,6},{6,5},{9,10},{10,9},{13,14},{14,13},{17,18},{18,... | collective-permute-start | bytes 1179656 | tf_op jit(solution)/shard_map/ppermute | solution.py:164
  74.3 19.4 %collective-permute-start.25 = (bf16[3,64,1024]{2,1,0:T(8,128)(2,1)S(1)}, bf16[3,64,1024]{2,1,0:T(8,128)(2,1)S(1)}, u32[]{:S(2)}, u32[]{:S(2)}) collective-permute-start(bf16[3,64,1024]{2,1,0:T(8,128)(2,1)S(1)} %get-tuple-element.56), channel_id=1, source_target_pairs={{0,1},{3,2},{1,0},{2,3},{4,5},{7,6},{5,4},{6,7},{8,9},{11,10},{9,8... | collective-permute-start | bytes 1179656 | tf_op jit(solution)/shard_map/ppermute | solution.py:159
  83.4 14.5 %collective-permute-start.24 = (bf16[3,64,1024]{2,1,0:T(8,128)(2,1)S(1)}, bf16[3,64,1024]{2,1,0:T(8,128)(2,1)S(1)}, u32[]{:S(2)}, u32[]{:S(2)}) collective-permute-start(bf16[3,64,1024]{2,1,0:T(8,128)(2,1)S(1)} %broadcast_select_fusion.3), channel_id=1, source_target_pairs={{0,1},{3,2},{1,0},{2,3},{4,5},{7,6},{5,4},{6,7},{8,9},{11,10},{9,8... | collective-permute-start | bytes 1179656 | tf_op jit(solution)/shard_map/ppermute | solution.py:159
  99.1 9.6 %collective-permute-start.27 = (bf16[3,64,1024]{2,1,0:T(8,128)(2,1)S(1)}, bf16[3,64,1024]{2,1,0:T(8,128)(2,1)S(1)}, u32[]{:S(2)}, u32[]{:S(2)}) collective-permute-start(bf16[3,64,1024]{2,1,0:T(8,128)(2,1)S(1)} %get-tuple-element.55), channel_id=1, source_target_pairs={{1,2},{2,1},{5,6},{6,5},{9,10},{10,9},{13,14},{14,13},{17,18},{18,... | collective-permute-start | bytes 1179656 | tf_op jit(solution)/shard_map/ppermute | solution.py:164
  99.8 17.9 %collective-permute-start.29 = (bf16[3,64,1024]{2,1,0:T(8,128)(2,1)S(1)}, bf16[3,64,1024]{2,1,0:T(8,128)(2,1)S(1)}, u32[]{:S(2)}, u32[]{:S(2)}) collective-permute-start(bf16[3,64,1024]{2,1,0:T(8,128)(2,1)S(1)} %get-tuple-element.54), channel_id=1, source_target_pairs={{0,1},{3,2},{1,0},{2,3},{4,5},{7,6},{5,4},{6,7},{8,9},{11,10},{9,8... | collective-permute-start | bytes 1179656 | tf_op jit(solution)/shard_map/ppermute | solution.py:159
  107.2 10.6 %collective-permute-start.34 = (bf16[3,64,1024]{2,1,0:T(8,128)(2,1)S(1)}, bf16[3,64,1024]{2,1,0:T(8,128)(2,1)S(1)}, u32[]{:S(2)}, u32[]{:S(2)}) collective-permute-start(bf16[3,64,1024]{2,1,0:T(8,128)(2,1)S(1)} %add_convert_fusion.1), channel_id=1, source_target_pairs={{1,2},{2,1},{5,6},{6,5},{9,10},{10,9},{13,14},{14,13},{17,18},{18,... | collective-permute-start | bytes 1179656 | tf_op jit(solution)/shard_map/ppermute | solution.py:164
  108.8 16.6 %collective-permute-start.28 = (bf16[3,64,1024]{2,1,0:T(8,128)(2,1)S(1)}, bf16[3,64,1024]{2,1,0:T(8,128)(2,1)S(1)}, u32[]{:S(2)}, u32[]{:S(2)}) collective-permute-start(bf16[3,64,1024]{2,1,0:T(8,128)(2,1)S(1)} %broadcast_select_fusion.8), channel_id=1, source_target_pairs={{0,1},{3,2},{1,0},{2,3},{4,5},{7,6},{5,4},{6,7},{8,9},{11,10},{9,8... | collective-permute-start | bytes 1179656 | tf_op jit(solution)/shard_map/ppermute | solution.py:159
  118.2 10.0 %collective-permute-start.40 = (bf16[3,64,1024]{2,1,0:T(8,128)(2,1)S(1)}, bf16[3,64,1024]{2,1,0:T(8,128)(2,1)S(1)}, u32[]{:S(2)}, u32[]{:S(2)}) collective-permute-start(bf16[3,64,1024]{2,1,0:T(8,128)(2,1)S(1)} %get-tuple-element.49), channel_id=1, source_target_pairs={{1,2},{2,1},{5,6},{6,5},{9,10},{10,9},{13,14},{14,13},{17,18},{18,... | collective-permute-start | bytes 1179656 | tf_op jit(solution)/shard_map/ppermute | solution.py:164
  118.9 13.0 %collective-permute-start.35 = (bf16[3,64,1024]{2,1,0:T(8,128)(2,1)S(1)}, bf16[3,64,1024]{2,1,0:T(8,128)(2,1)S(1)}, u32[]{:S(2)}, u32[]{:S(2)}) collective-permute-start(bf16[3,64,1024]{2,1,0:T(8,128)(2,1)S(1)} %get-tuple-element.50), channel_id=1, source_target_pairs={{0,1},{3,2},{1,0},{2,3},{4,5},{7,6},{5,4},{6,7},{8,9},{11,10},{9,8... | collective-permute-start | bytes 1179656 | tf_op jit(solution)/shard_map/ppermute | solution.py:159
  128.1 19.4 %collective-permute-start.30 = (bf16[2,3,64,512]{3,2,1,0:T(8,128)(2,1)S(1)}, bf16[2,3,64,512]{3,2,1,0:T(8,128)(2,1)S(1)}, u32[]{:S(2)}, u32[]{:S(2)}) collective-permute-start(bf16[2,3,64,512]{3,2,1,0:T(8,128)(2,1)S(1)} %select_convert_fusion), channel_id=1, source_target_pairs={{0,4},{4,0},{8,12},{12,8},{16,20},{20,16},{24,28},{28,24},{1,5},{5... | collective-permute-start | bytes 1179656 | tf_op jit(solution)/shard_map/ppermute | solution.py:59
  128.2 18.1 %collective-permute-start.41 = (bf16[3,64,1024]{2,1,0:T(8,128)(2,1)S(1)}, bf16[3,64,1024]{2,1,0:T(8,128)(2,1)S(1)}, u32[]{:S(2)}, u32[]{:S(2)}) collective-permute-start(bf16[3,64,1024]{2,1,0:T(8,128)(2,1)S(1)} %collective-permute-done.40), channel_id=1, source_target_pairs={{1,0},{2,3},{5,4},{6,7},{9,8},{10,11},{13,12},{14,15},{17,16},{18,... | collective-permute-start | bytes 1179656 | tf_op jit(solution)/shard_map/ppermute | solution.py:157
  132.4 22.9 %collective-permute-start.37 = (bf16[3,64,1024]{2,1,0:T(8,128)(2,1)S(1)}, bf16[3,64,1024]{2,1,0:T(8,128)(2,1)S(1)}, u32[]{:S(2)}, u32[]{:S(2)}) collective-permute-start(bf16[3,64,1024]{2,1,0:T(8,128)(2,1)S(1)} %pad_maximum_fusion.16), channel_id=1, source_target_pairs={{1,2},{2,1},{5,6},{6,5},{9,10},{10,9},{13,14},{14,13},{17,18},{18,... | collective-permute-start | bytes 1179656 | tf_op jit(solution)/shard_map/ppermute | solution.py:164
  133.1 32.1 %collective-permute-start.42 = (bf16[3,64,1024]{2,1,0:T(8,128)(2,1)S(1)}, bf16[3,64,1024]{2,1,0:T(8,128)(2,1)S(1)}, u32[]{:S(2)}, u32[]{:S(2)}) collective-permute-start(bf16[3,64,1024]{2,1,0:T(8,128)(2,1)S(1)} %pad_maximum_fusion.16), channel_id=1, source_target_pairs={{1,0},{2,3},{5,4},{6,7},{9,8},{10,11},{13,12},{14,15},{17,16},{18,... | collective-permute-start | bytes 1179656 | tf_op jit(solution)/shard_map/ppermute | solution.py:157
  155.3 9.7 %collective-permute-start.38 = (bf16[3,64,1024]{2,1,0:T(8,128)(2,1)S(1)}, bf16[3,64,1024]{2,1,0:T(8,128)(2,1)S(1)}, u32[]{:S(2)}, u32[]{:S(2)}) collective-permute-start(bf16[3,64,1024]{2,1,0:T(8,128)(2,1)S(1)} %broadcast_select_fusion), channel_id=1, source_target_pairs={{1,0},{2,3},{5,4},{6,7},{9,8},{10,11},{13,12},{14,15},{17,16},{18,... | collective-permute-start | bytes 1179656 | tf_op jit(solution)/shard_map/ppermute | solution.py:157
  167.0 17.4 %collective-permute-start.39 = (bf16[2,48,512]{2,1,0:T(8,128)(2,1)S(1)}, bf16[2,48,512]{2,1,0:T(8,128)(2,1)S(1)}, u32[]{:S(2)}, u32[]{:S(2)}) collective-permute-start(bf16[2,48,512]{2,1,0:T(8,128)(2,1)S(1)} %convert_select_fusion), channel_id=1, source_target_pairs={{0,1},{1,0},{2,3},{3,2},{4,5},{5,4},{6,7},{7,6},{8,9},{9,8},{10,11... | collective-permute-start | bytes 294920 | tf_op jit(solution)/shard_map/ppermute | solution.py:59
  175.9 9.3 %collective-permute-start.50 = (bf16[2,32,512]{2,1,0:T(8,128)(2,1)S(1)}, bf16[2,32,512]{2,1,0:T(8,128)(2,1)S(1)}, u32[]{:S(2)}, u32[]{:S(2)}) collective-permute-start(bf16[2,32,512]{2,1,0:T(8,128)(2,1)S(1)} %bitcast.541), channel_id=1, source_target_pairs={{0,3},{1,2},{2,1},{3,0},{4,7},{5,6},{6,5},{7,4},{8,11},{9,10},{10,... | collective-permute-start | bytes 196616 | tf_op jit(solution)/shard_map/ppermute | solution.py:59
  178.0 7.1 %collective-permute-start.49 = (bf16[2,32,512]{2,1,0:T(8,128)(2,1)S(1)}, bf16[2,32,512]{2,1,0:T(8,128)(2,1)S(1)}, u32[]{:S(2)}, u32[]{:S(2)}) collective-permute-start(bf16[2,32,512]{2,1,0:T(8,128)(2,1)S(1)} %bitcast.542), channel_id=1, source_target_pairs={{0,2},{1,3},{2,0},{3,1},{4,6},{5,7},{6,4},{7,5},{8,10},{9,11},{10,... | collective-permute-start | bytes 196616 | tf_op jit(solution)/shard_map/ppermute | solution.py:59
  (25 other events, 201.7 us)

commit v13 on v11

--- a/solution.py
+++ b/solution.py
@@ -19,6 +19,18 @@
     while table.shape[0] < order:
         table = np.block([[table, table], [table, -table]])
     return table
+
+
+def signs_of(order, ahead):
+    shape = (order, order)
+    common = lax.broadcasted_iota(jnp.int32, shape, 0) & lax.broadcasted_iota(jnp.int32, shape, 1)
+    shift = 1
+    while shift < order.bit_length():
+        shift *= 2
+    while shift > 1:
+        shift //= 2
+        common = common ^ (common >> shift)
+    return lax.optimization_barrier(after((1 - 2 * (common & 1)).astype(BF16), ahead))
 
 
 def dot(left, right, left_dim, right_dim):
@@ -63,25 +75,23 @@
     return [block] + [exchange(block, "tensor", k) for k in range(1, lax.axis_size("tensor"))]
 
 
-def turn(block):
+def turn(block, square):
     width = block.shape[-1]
-    square = jnp.asarray(sylvester(width), BF16)
     rows = block.reshape(-1, width) * (1.0 / math.sqrt(D))
     high = lax.reduce_precision(rows, 8, 7)
     low = (rows - high).astype(BF16)
     return (dot(high.astype(BF16), square, 1, 0) + dot(low, square, 1, 0)).reshape(block.shape)
 
 
-def rotate(pieces, signs):
+def rotate(pieces, signs, square):
     width = pieces[0].shape[-1]
-    return turn(sum(piece.astype(F32) * sign[:, :width] for piece, sign in zip(pieces, signs)))
-
-
-def rotate_by_halves(block, bits, ahead):
-    block = turn(block)
+    return turn(sum(piece.astype(F32) * sign[:, :width] for piece, sign in zip(pieces, signs)), square)
+
+
+def rotate_by_halves(block, bits, square):
+    block = turn(block, square)
     for level, bit in enumerate(bits):
-        message = block.astype(BF16)
-        came = exchange(message if level else after(message, ahead), "tensor", 1 << level)
+        came = exchange(block.astype(BF16), "tensor", 1 << level)
         block = block * bit[:, : block.shape[-1]] + came.astype(F32)
     return block
 
@@ -185,6 +195,7 @@
     far, depth, signs, bits, depths = my_row(max(width, gate_weight.shape[1]))
     far = far[:, :width] > 0.5
 
+    square = signs_of(width, depth)
     both = jnp.stack([tokens, out_grad])
 
     def arrive(turned, ahead=()):
@@ -195,7 +206,7 @@
     first = min(2, chunks)
     early = spread(both[:, : first * step])
     late = spread(after(both[:, first * step :], early[1])) if chunks > first else None
-    groups = [arrive(rotate(early, signs).astype(BF16))]
+    groups = [arrive(rotate(early, signs, square).astype(BF16))]
 
     def leave(blocks):
         sums = []
@@ -243,7 +254,7 @@
             tick = exchange(message[2, :step, :width], "dp", 1)
             late[0] = after(late[0], tick)
         if s == 1 and chunks > first:
-            groups.append(arrive(rotate(late, signs).astype(BF16), [messages[1], middle]))
+            groups.append(arrive(rotate(late, signs, square).astype(BF16), [messages[1], middle]))
         if s < steps:
             total = messages[s].astype(F32) + came[s].astype(F32)
             if which == 0:
@@ -256,9 +267,10 @@
                 outs += [acts[i], crossed[i]]
     low, high = leave([done(i) for i in range(split, chunks)])
     if split > 0:
-        ends.append(rotate_by_halves(first_sums.reshape(2, -1, width), bits, crossed[-1]))
+        first_sums = after(first_sums.reshape(2, -1, width), came[-1])
+        ends.append(rotate_by_halves(first_sums, bits, square))
     sums, _, ahead = scatter_dp(low, high)
-    ends.append(rotate(spread(sums.reshape(2, -1, width).astype(BF16)), signs))
+    ends.append(rotate(spread(sums.reshape(2, -1, width).astype(BF16)), signs, square))
     ends = jnp.concatenate(ends, axis=1)
 
     acts = jnp.concatenate([done(i) for i in range(chunks)], axis=1)

time: 188 us -> 186 us (0.989)
  waiting for transfers between devices: 48.9 us -> 46.7 us
  matrix products: 26.8 us -> 24.7 us
    ppermute x28, waiting for transfers between devices: 25 us -> 15.8 us  [exchange(): return lax.ppermute(block, axis, [(i, i ^ apart) for i in range(count)])]
    ppermute x3, waiting for transfers between devices: 11.9 us -> 19 us  [swap(): return lax.ppermute(out, 'tensor', back)]
    dot_general x56, matrix products: 26.8 us -> 24.7 us  [dot(): lax.dot_general(left, right, (((left_dim,), (right_dim,)), ((), ())), pre...]
  transfers between devices with their start and end apart: 51 -> 51, of which waited for: 22 -> 19; matrix products, arithmetic and copies ran while one was open for 16% -> 17% of each run, Pallas kernels for 0% -> 0%
where the time goes in v13:
time: 186 us; the launch traced here: 185 us
  starting transfers between devices  99.1 us (53%)
  waiting for transfers between devices  46.7 us (25%)
  matrix products  24.7 us (13%)
  other arithmetic  11 us (6%)
  between operations  2.02 us (1%)
    ppermute x7, starting transfers between devices, swap(): return lax.ppermute(block, 'tensor', pairs + back)  48.8 us
    ppermute x28, starting transfers between devices, exchange(): return lax.ppermute(block, axis, [(i, i ^ apart) for i in range(count)])  29.2 us
    dot_general x56, matrix products, dot(): lax.dot_general(left, right, (((left_dim,), (right_dim,)), ((), ())), pre...  24.7 us
    ppermute x3, waiting for transfers between devices, swap(): return lax.ppermute(out, 'tensor', back)  19 us
    ppermute x28, waiting for transfers between devices, exchange(): return lax.ppermute(block, axis, [(i, i ^ apart) for i in range(count)])  15.8 us
    ppermute x3, starting transfers between devices, swap(): return lax.ppermute(into, 'tensor', pairs)  9.93 us
    ppermute x3, waiting for transfers between devices, swap(): return lax.ppermute(into, 'tensor', pairs)  7.15 us
    ppermute x10, starting transfers between devices, across(): return lax.ppermute(block, 'tensor', [(half - 1, half), (half, half - 1)])  7.04 us
  transfers between devices with their start and end apart: 51, of which 19 were waited for; matrix products, arithmetic and copies ran while one was open for 17% of the time, Pallas kernels for 0%

profile of v13, /device:TPU:0, one launch (start us, length us, event | category | flops | bytes accessed | tf_op | source)
XLA Modules:
  0.0 185.3 jit_solution(7942253372320271411)
XLA Ops:
  1.5 5.0 %collective-permute-start.2 = (bf16[2,32,512]{2,1,0:T(8,128)(2,1)S(1)}, bf16[2,32,512]{2,1,0:T(8,128)(2,1)S(1)}, u32[]{:S(2)}, u32[]{:S(2)}) collective-permute-start(bf16[2,32,512]{2,1,0:T(8,128)(2,1)S(1)} %pad_maximum_fusion.26), channel_id=1, source_target_pairs={{0,3},{1,2},{2,1},{3,0},{4,7},{5,6},{6,5},{7,4},{8,11},{9,10},{10,... | collective-permute-start | bytes 196616 | tf_op jit(solution)/shard_map/ppermute | solution.py:71
  10.3 1.9 %collective-permute-done.1 = bf16[2,32,512]{2,1,0:T(8,128)(2,1)S(1)} collective-permute-done((bf16[2,32,512]{2,1,0:T(8,128)(2,1)S(1)}, bf16[2,32,512]{2,1,0:T(8,128)(2,1)S(1)}, u32[]{:S(2)}, u32[]{:S(2)}) %collective-permute-start.1) | collective-permute-done | bytes 65568 | tf_op jit(solution)/shard_map/ppermute | solution.py:71
  13.5 2.5 %collective-permute-start.5 = (bf16[2,2,1,16,512]{4,3,2,1,0:T(8,128)(2,1)S(1)}, bf16[2,2,1,16,512]{4,3,2,1,0:T(8,128)(2,1)S(1)}, u32[]{:S(2)}, u32[]{:S(2)}) collective-permute-start(bf16[2,2,1,16,512]{4,3,2,1,0:T(8,128)(2,1)S(1)} %bitcast.546), channel_id=1, source_target_pairs={{0,24},{4,28},{8,16},{12,20},{16,8},{20,12},{24,0},{28,4},{1,25},{... | collective-permute-start | bytes 196616 | tf_op jit(solution)/shard_map/ppermute | solution.py:71
  17.1 1.7 collective-permute-done.5
  21.0 2.8 %collective-permute-start.14 = (bf16[2,48,512]{2,1,0:T(8,128)(2,1)S(1)}, bf16[2,48,512]{2,1,0:T(8,128)(2,1)S(1)}, u32[]{:S(2)}, u32[]{:S(2)}) collective-permute-start(bf16[2,48,512]{2,1,0:T(8,128)(2,1)S(1)} %fusion.117), channel_id=1, source_target_pairs={{0,3},{1,2},{2,1},{3,0},{4,7},{5,6},{6,5},{7,4},{8,11},{9,10},{10,... | collective-permute-start | bytes 294920 | tf_op jit(solution)/shard_map/ppermute | solution.py:71
  23.8 1.7 collective-permute-start.12
  27.7 2.3 %collective-permute-start.7 = (bf16[3,64,1024]{2,1,0:T(8,128)(2,1)S(1)}, bf16[3,64,1024]{2,1,0:T(8,128)(2,1)S(1)}, u32[]{:S(2)}, u32[]{:S(2)}) collective-permute-start(bf16[3,64,1024]{2,1,0:T(8,128)(2,1)S(1)} %pad_maximum_fusion.2), channel_id=1, source_target_pairs={{0,1},{3,2},{4,5},{7,6},{8,9},{11,10},{12,13},{15,14},{16,17},{19,... | collective-permute-start | bytes 1179656 | tf_op jit(solution)/shard_map/ppermute | solution.py:165
  31.3 1.8 collective-permute-done.13
  37.2 1.9 %collective-permute-done.7 = bf16[3,64,1024]{2,1,0:T(8,128)(2,1)S(1)} collective-permute-done((bf16[3,64,1024]{2,1,0:T(8,128)(2,1)S(1)}, bf16[3,64,1024]{2,1,0:T(8,128)(2,1)S(1)}, u32[]{:S(2)}, u32[]{:S(2)}) %collective-permute-start.7) | collective-permute-done | bytes 393248 | tf_op jit(solution)/shard_map/ppermute | solution.py:165
  39.7 4.4 %collective-permute-start.8 = (bf16[3,64,1024]{2,1,0:T(8,128)(2,1)S(1)}, bf16[3,64,1024]{2,1,0:T(8,128)(2,1)S(1)}, u32[]{:S(2)}, u32[]{:S(2)}) collective-permute-start(bf16[3,64,1024]{2,1,0:T(8,128)(2,1)S(1)} %maximum_select_fusion.1), channel_id=1, source_target_pairs={{0,1},{3,2},{4,5},{7,6},{8,9},{11,10},{12,13},{15,14},{16,17},{19,... | collective-permute-start | bytes 1179656 | tf_op jit(solution)/shard_map/ppermute | solution.py:165
  46.4 3.2 %collective-permute-start.21 = (bf16[3,64,1024]{2,1,0:T(8,128)(2,1)S(1)}, bf16[3,64,1024]{2,1,0:T(8,128)(2,1)S(1)}, u32[]{:S(2)}, u32[]{:S(2)}) collective-permute-start(bf16[3,64,1024]{2,1,0:T(8,128)(2,1)S(1)} %pad_maximum_fusion.7), channel_id=1, source_target_pairs={{0,1},{3,2},{4,5},{7,6},{8,9},{11,10},{12,13},{15,14},{16,17},{19,... | collective-permute-start | bytes 1179656 | tf_op jit(solution)/shard_map/ppermute | solution.py:165
  50.3 3.4 %collective-permute-done.8 = bf16[3,64,1024]{2,1,0:T(8,128)(2,1)S(1)} collective-permute-done((bf16[3,64,1024]{2,1,0:T(8,128)(2,1)S(1)}, bf16[3,64,1024]{2,1,0:T(8,128)(2,1)S(1)}, u32[]{:S(2)}, u32[]{:S(2)}) %collective-permute-start.8) | collective-permute-done | bytes 393248 | tf_op jit(solution)/shard_map/ppermute | solution.py:165
  54.8 4.2 %collective-permute-start.20 = (bf16[3,64,1024]{2,1,0:T(8,128)(2,1)S(1)}, bf16[3,64,1024]{2,1,0:T(8,128)(2,1)S(1)}, u32[]{:S(2)}, u32[]{:S(2)}) collective-permute-start(bf16[3,64,1024]{2,1,0:T(8,128)(2,1)S(1)} %get-tuple-element.58), channel_id=1, source_target_pairs={{0,1},{3,2},{1,0},{2,3},{4,5},{7,6},{5,4},{6,7},{8,9},{11,10},{9,8... | collective-permute-start | bytes 1179656 | tf_op jit(solution)/shard_map/ppermute | solution.py:169
  60.2 1.8 collective-permute-done.21
  64.1 6.2 %collective-permute-start.19 = (bf16[3,64,1024]{2,1,0:T(8,128)(2,1)S(1)}, bf16[3,64,1024]{2,1,0:T(8,128)(2,1)S(1)}, u32[]{:S(2)}, u32[]{:S(2)}) collective-permute-start(bf16[3,64,1024]{2,1,0:T(8,128)(2,1)S(1)} %broadcast_select_fusion.9), channel_id=1, source_target_pairs={{0,1},{3,2},{1,0},{2,3},{4,5},{7,6},{5,4},{6,7},{8,9},{11,10},{9,8... | collective-permute-start | bytes 1179656 | tf_op jit(solution)/shard_map/ppermute | solution.py:169
  72.1 8.0 %collective-permute-start.25 = (bf16[3,64,1024]{2,1,0:T(8,128)(2,1)S(1)}, bf16[3,64,1024]{2,1,0:T(8,128)(2,1)S(1)}, u32[]{:S(2)}, u32[]{:S(2)}) collective-permute-start(bf16[3,64,1024]{2,1,0:T(8,128)(2,1)S(1)} %get-tuple-element.56), channel_id=1, source_target_pairs={{0,1},{3,2},{1,0},{2,3},{4,5},{7,6},{5,4},{6,7},{8,9},{11,10},{9,8... | collective-permute-start | bytes 1179656 | tf_op jit(solution)/shard_map/ppermute | solution.py:169
  81.5 7.3 %collective-permute-start.24 = (bf16[3,64,1024]{2,1,0:T(8,128)(2,1)S(1)}, bf16[3,64,1024]{2,1,0:T(8,128)(2,1)S(1)}, u32[]{:S(2)}, u32[]{:S(2)}) collective-permute-start(bf16[3,64,1024]{2,1,0:T(8,128)(2,1)S(1)} %broadcast_select_fusion.3), channel_id=1, source_target_pairs={{0,1},{3,2},{1,0},{2,3},{4,5},{7,6},{5,4},{6,7},{8,9},{11,10},{9,8... | collective-permute-start | bytes 1179656 | tf_op jit(solution)/shard_map/ppermute | solution.py:169
  94.2 2.0 %collective-permute-done.24 = bf16[3,64,1024]{2,1,0:T(8,128)(2,1)S(1)} collective-permute-done((bf16[3,64,1024]{2,1,0:T(8,128)(2,1)S(1)}, bf16[3,64,1024]{2,1,0:T(8,128)(2,1)S(1)}, u32[]{:S(2)}, u32[]{:S(2)}) %collective-permute-start.24) | collective-permute-done | bytes 393248 | tf_op jit(solution)/shard_map/ppermute | solution.py:169
  98.1 7.4 %collective-permute-start.29 = (bf16[3,64,1024]{2,1,0:T(8,128)(2,1)S(1)}, bf16[3,64,1024]{2,1,0:T(8,128)(2,1)S(1)}, u32[]{:S(2)}, u32[]{:S(2)}) collective-permute-start(bf16[3,64,1024]{2,1,0:T(8,128)(2,1)S(1)} %get-tuple-element.54), channel_id=1, source_target_pairs={{0,1},{3,2},{1,0},{2,3},{4,5},{7,6},{5,4},{6,7},{8,9},{11,10},{9,8... | collective-permute-start | bytes 1179656 | tf_op jit(solution)/shard_map/ppermute | solution.py:169
  107.2 9.4 %collective-permute-start.28 = (bf16[3,64,1024]{2,1,0:T(8,128)(2,1)S(1)}, bf16[3,64,1024]{2,1,0:T(8,128)(2,1)S(1)}, u32[]{:S(2)}, u32[]{:S(2)}) collective-permute-start(bf16[3,64,1024]{2,1,0:T(8,128)(2,1)S(1)} %broadcast_select_fusion.8), channel_id=1, source_target_pairs={{0,1},{3,2},{1,0},{2,3},{4,5},{7,6},{5,4},{6,7},{8,9},{11,10},{9,8... | collective-permute-start | bytes 1179656 | tf_op jit(solution)/shard_map/ppermute | solution.py:169
  117.7 6.2 %collective-permute-start.32 = (bf16[3,64,1024]{2,1,0:T(8,128)(2,1)S(1)}, bf16[3,64,1024]{2,1,0:T(8,128)(2,1)S(1)}, u32[]{:S(2)}, u32[]{:S(2)}) collective-permute-start(bf16[3,64,1024]{2,1,0:T(8,128)(2,1)S(1)} %get-tuple-element.50), channel_id=1, source_target_pairs={{0,1},{3,2},{1,0},{2,3},{4,5},{7,6},{5,4},{6,7},{8,9},{11,10},{9,8... | collective-permute-start | bytes 1179656 | tf_op jit(solution)/shard_map/ppermute | solution.py:169
  128.4 2.4 %collective-permute-done.32 = bf16[3,64,1024]{2,1,0:T(8,128)(2,1)S(1)} collective-permute-done((bf16[3,64,1024]{2,1,0:T(8,128)(2,1)S(1)}, bf16[3,64,1024]{2,1,0:T(8,128)(2,1)S(1)}, u32[]{:S(2)}, u32[]{:S(2)}) %collective-permute-start.32) | collective-permute-done | bytes 393248 | tf_op jit(solution)/shard_map/ppermute | solution.py:169
  133.5 1.6 collective-permute-start.38
  135.6 9.5 %collective-permute-done.42 = bf16[3,64,1024]{2,1,0:T(8,128)(2,1)S(1)} collective-permute-done((bf16[3,64,1024]{2,1,0:T(8,128)(2,1)S(1)}, bf16[3,64,1024]{2,1,0:T(8,128)(2,1)S(1)}, u32[]{:S(2)}, u32[]{:S(2)}) %collective-permute-start.42) | collective-permute-done | bytes 393248 | tf_op jit(solution)/shard_map/ppermute | solution.py:167
  149.8 9.5 %collective-permute-done.35 = bf16[3,64,1024]{2,1,0:T(8,128)(2,1)S(1)} collective-permute-done((bf16[3,64,1024]{2,1,0:T(8,128)(2,1)S(1)}, bf16[3,64,1024]{2,1,0:T(8,128)(2,1)S(1)}, u32[]{:S(2)}, u32[]{:S(2)}) %collective-permute-start.35) | collective-permute-done | bytes 393248 | tf_op jit(solution)/shard_map/ppermute | solution.py:167
  162.2 2.0 %multiply_convert_fusion = bf16[1024,512]{1,0:T(8,128)(2,1)} fusion(bf16[3,640,1024]{2,1,0:T(8,128)(2,1)S(1)} %get-tuple-element.10, bf16[2,640,512]{2,1,0:T(8,128)(2,1)S(1)} %maximum_select_fusion), kind=kOutput, calls=%fused_computation | convolution fusion | flops 672137216 | bytes 3014656 | tf_op jit(solution)/shard_map/dot_general | solution.py:37
  164.2 2.9 %collective-permute-done.39 = bf16[2,48,512]{2,1,0:T(8,128)(2,1)S(1)} collective-permute-done((bf16[2,48,512]{2,1,0:T(8,128)(2,1)S(1)}, bf16[2,48,512]{2,1,0:T(8,128)(2,1)S(1)}, u32[]{:S(2)}, u32[]{:S(2)}) %collective-permute-start.39) | collective-permute-done | bytes 98336 | tf_op jit(solution)/shard_map/ppermute | solution.py:71
  168.3 1.6 collective-permute-start.47
  171.8 2.7 %collective-permute-done.40 = bf16[2,48,512]{2,1,0:T(8,128)(2,1)S(1)} collective-permute-done((bf16[2,48,512]{2,1,0:T(8,128)(2,1)S(1)}, bf16[2,48,512]{2,1,0:T(8,128)(2,1)S(1)}, u32[]{:S(2)}, u32[]{:S(2)}) %collective-permute-start.40) | collective-permute-done | bytes 98336 | tf_op jit(solution)/shard_map/ppermute | solution.py:71
  174.7 2.1 %collective-permute-start.50 = (bf16[2,32,512]{2,1,0:T(8,128)(2,1)S(1)}, bf16[2,32,512]{2,1,0:T(8,128)(2,1)S(1)}, u32[]{:S(2)}, u32[]{:S(2)}) collective-permute-start(bf16[2,32,512]{2,1,0:T(8,128)(2,1)S(1)} %bitcast.557), channel_id=1, source_target_pairs={{0,3},{1,2},{2,1},{3,0},{4,7},{5,6},{6,5},{7,4},{8,11},{9,10},{10,... | collective-permute-start | bytes 196616 | tf_op jit(solution)/shard_map/ppermute | solution.py:71
  179.2 2.0 %multiply_convert_fusion.2 = bf16[512,1024]{1,0:T(8,128)(2,1)} fusion(bf16[3,640,1024]{2,1,0:T(8,128)(2,1)S(1)} %get-tuple-element.10, bf16[2,640,512]{2,1,0:T(8,128)(2,1)S(1)} %maximum_select_fusion, pred[512]{0:T(512)(128)(4,1)S(1)} %ne.91, bf16[512]{0:T(512)(128)(2,1)S(1)} %slice_reduce_fusion.1), kind=kOutput, calls=%fused_computation.2 | convolution fusion | flops 672464896 | bytes 3016192 | tf_op jit(solution)/shard_map/dot_general | solution.py:37
  181.2 2.0 %multiply_convert_fusion.1 = bf16[512,1024]{1,0:T(8,128)(2,1)} fusion(bf16[3,640,1024]{2,1,0:T(8,128)(2,1)S(1)} %get-tuple-element.10, bf16[2,640,512]{2,1,0:T(8,128)(2,1)S(1)} %maximum_select_fusion, pred[512]{0:T(512)(128)(4,1)S(1)} %ne.91, bf16[512]{0:T(512)(128)(2,1)S(1)} %slice_reduce_fusion.1), kind=kOutput, calls=%fused_computation.1 | convolution fusion | flops 672464896 | bytes 3016192 | tf_op jit(solution)/shard_map/dot_general | solution.py:37
  (246 shorter events, 59.8 us)
Async XLA Ops:
  1.5 8.7 %collective-permute-start.2 = (bf16[2,32,512]{2,1,0:T(8,128)(2,1)S(1)}, bf16[2,32,512]{2,1,0:T(8,128)(2,1)S(1)}, u32[]{:S(2)}, u32[]{:S(2)}) collective-permute-start(bf16[2,32,512]{2,1,0:T(8,128)(2,1)S(1)} %pad_maximum_fusion.26), channel_id=1, source_target_pairs={{0,3},{1,2},{2,1},{3,0},{4,7},{5,6},{6,5},{7,4},{8,11},{9,10},{10,... | collective-permute-start | bytes 196616 | tf_op jit(solution)/shard_map/ppermute | solution.py:71
  21.0 10.3 %collective-permute-start.14 = (bf16[2,48,512]{2,1,0:T(8,128)(2,1)S(1)}, bf16[2,48,512]{2,1,0:T(8,128)(2,1)S(1)}, u32[]{:S(2)}, u32[]{:S(2)}) collective-permute-start(bf16[2,48,512]{2,1,0:T(8,128)(2,1)S(1)} %fusion.117), channel_id=1, source_target_pairs={{0,3},{1,2},{2,1},{3,0},{4,7},{5,6},{6,5},{7,4},{8,11},{9,10},{10,... | collective-permute-start | bytes 294920 | tf_op jit(solution)/shard_map/ppermute | solution.py:71
  23.7 9.3 %collective-permute-start.13 = (bf16[2,48,512]{2,1,0:T(8,128)(2,1)S(1)}, bf16[2,48,512]{2,1,0:T(8,128)(2,1)S(1)}, u32[]{:S(2)}, u32[]{:S(2)}) collective-permute-start(bf16[2,48,512]{2,1,0:T(8,128)(2,1)S(1)} %fusion.117), channel_id=1, source_target_pairs={{0,2},{1,3},{2,0},{3,1},{4,6},{5,7},{6,4},{7,5},{8,10},{9,11},{10,... | collective-permute-start | bytes 294920 | tf_op jit(solution)/shard_map/ppermute | solution.py:71
  23.8 9.3 %collective-permute-start.12 = (bf16[2,48,512]{2,1,0:T(8,128)(2,1)S(1)}, bf16[2,48,512]{2,1,0:T(8,128)(2,1)S(1)}, u32[]{:S(2)}, u32[]{:S(2)}) collective-permute-start(bf16[2,48,512]{2,1,0:T(8,128)(2,1)S(1)} %fusion.117), channel_id=1, source_target_pairs={{0,1},{1,0},{2,3},{3,2},{4,5},{5,4},{6,7},{7,6},{8,9},{9,8},{10,11... | collective-permute-start | bytes 294920 | tf_op jit(solution)/shard_map/ppermute | solution.py:71
  27.7 11.4 %collective-permute-start.7 = (bf16[3,64,1024]{2,1,0:T(8,128)(2,1)S(1)}, bf16[3,64,1024]{2,1,0:T(8,128)(2,1)S(1)}, u32[]{:S(2)}, u32[]{:S(2)}) collective-permute-start(bf16[3,64,1024]{2,1,0:T(8,128)(2,1)S(1)} %pad_maximum_fusion.2), channel_id=1, source_target_pairs={{0,1},{3,2},{4,5},{7,6},{8,9},{11,10},{12,13},{15,14},{16,17},{19,... | collective-permute-start | bytes 1179656 | tf_op jit(solution)/shard_map/ppermute | solution.py:165
  33.7 12.5 %collective-permute-start.17 = (bf16[2,3,1,16,512]{4,3,2,1,0:T(8,128)(2,1)S(1)}, bf16[2,3,1,16,512]{4,3,2,1,0:T(8,128)(2,1)S(1)}, u32[]{:S(2)}, u32[]{:S(2)}) collective-permute-start(bf16[2,3,1,16,512]{4,3,2,1,0:T(8,128)(2,1)S(1)} %bitcast.553), channel_id=1, source_target_pairs={{0,24},{4,28},{8,16},{12,20},{16,8},{20,12},{24,0},{28,4},{1,25},{... | collective-permute-start | bytes 294920 | tf_op jit(solution)/shard_map/ppermute | solution.py:71
  35.2 10.9 %collective-permute-start.16 = (bf16[2,3,1,16,512]{4,3,2,1,0:T(8,128)(2,1)S(1)}, bf16[2,3,1,16,512]{4,3,2,1,0:T(8,128)(2,1)S(1)}, u32[]{:S(2)}, u32[]{:S(2)}) collective-permute-start(bf16[2,3,1,16,512]{4,3,2,1,0:T(8,128)(2,1)S(1)} %bitcast.554), channel_id=1, source_target_pairs={{0,16},{4,20},{8,24},{12,28},{16,0},{20,4},{24,8},{28,12},{1,17},{... | collective-permute-start | bytes 294920 | tf_op jit(solution)/shard_map/ppermute | solution.py:71
  35.7 10.4 %collective-permute-start.15 = (bf16[2,3,1,16,512]{4,3,2,1,0:T(8,128)(2,1)S(1)}, bf16[2,3,1,16,512]{4,3,2,1,0:T(8,128)(2,1)S(1)}, u32[]{:S(2)}, u32[]{:S(2)}) collective-permute-start(bf16[2,3,1,16,512]{4,3,2,1,0:T(8,128)(2,1)S(1)} %bitcast.555), channel_id=1, source_target_pairs={{0,8},{4,12},{8,0},{12,4},{16,24},{20,28},{24,16},{28,20},{1,9},{5... | collective-permute-start | bytes 294920 | tf_op jit(solution)/shard_map/ppermute | solution.py:71
  39.7 13.9 %collective-permute-start.8 = (bf16[3,64,1024]{2,1,0:T(8,128)(2,1)S(1)}, bf16[3,64,1024]{2,1,0:T(8,128)(2,1)S(1)}, u32[]{:S(2)}, u32[]{:S(2)}) collective-permute-start(bf16[3,64,1024]{2,1,0:T(8,128)(2,1)S(1)} %maximum_select_fusion.1), channel_id=1, source_target_pairs={{0,1},{3,2},{4,5},{7,6},{8,9},{11,10},{12,13},{15,14},{16,17},{19,... | collective-permute-start | bytes 1179656 | tf_op jit(solution)/shard_map/ppermute | solution.py:165
  46.2 12.8 %collective-permute-start.18 = (bf16[2,3,4,16,512]{4,3,2,1,0:T(8,128)(2,1)S(1)}, bf16[2,3,4,16,512]{4,3,2,1,0:T(8,128)(2,1)S(1)}, u32[]{:S(2)}, u32[]{:S(2)}) collective-permute-start(bf16[2,3,4,16,512]{4,3,2,1,0:T(8,128)(2,1)S(1)} %pad_maximum_fusion.4), channel_id=1, source_target_pairs={{0,4},{4,0},{8,12},{12,8},{16,20},{20,16},{24,28},{28,24},{1,5},{5... | collective-permute-start | bytes 1179656 | tf_op jit(solution)/shard_map/ppermute | solution.py:71
  46.4 15.7 %collective-permute-start.21 = (bf16[3,64,1024]{2,1,0:T(8,128)(2,1)S(1)}, bf16[3,64,1024]{2,1,0:T(8,128)(2,1)S(1)}, u32[]{:S(2)}, u32[]{:S(2)}) collective-permute-start(bf16[3,64,1024]{2,1,0:T(8,128)(2,1)S(1)} %pad_maximum_fusion.7), channel_id=1, source_target_pairs={{0,1},{3,2},{4,5},{7,6},{8,9},{11,10},{12,13},{15,14},{16,17},{19,... | collective-permute-start | bytes 1179656 | tf_op jit(solution)/shard_map/ppermute | solution.py:165
  54.1 9.9 %collective-permute-start.10 = (bf16[3,64,1024]{2,1,0:T(8,128)(2,1)S(1)}, bf16[3,64,1024]{2,1,0:T(8,128)(2,1)S(1)}, u32[]{:S(2)}, u32[]{:S(2)}) collective-permute-start(bf16[3,64,1024]{2,1,0:T(8,128)(2,1)S(1)} %get-tuple-element.59), channel_id=1, source_target_pairs={{1,2},{2,1},{5,6},{6,5},{9,10},{10,9},{13,14},{14,13},{17,18},{18,... | collective-permute-start | bytes 1179656 | tf_op jit(solution)/shard_map/ppermute | solution.py:174
  54.8 15.7 %collective-permute-start.20 = (bf16[3,64,1024]{2,1,0:T(8,128)(2,1)S(1)}, bf16[3,64,1024]{2,1,0:T(8,128)(2,1)S(1)}, u32[]{:S(2)}, u32[]{:S(2)}) collective-permute-start(bf16[3,64,1024]{2,1,0:T(8,128)(2,1)S(1)} %get-tuple-element.58), channel_id=1, source_target_pairs={{0,1},{3,2},{1,0},{2,3},{4,5},{7,6},{5,4},{6,7},{8,9},{11,10},{9,8... | collective-permute-start | bytes 1179656 | tf_op jit(solution)/shard_map/ppermute | solution.py:169
  62.2 8.3 %collective-permute-start.22 = (bf16[3,64,1024]{2,1,0:T(8,128)(2,1)S(1)}, bf16[3,64,1024]{2,1,0:T(8,128)(2,1)S(1)}, u32[]{:S(2)}, u32[]{:S(2)}) collective-permute-start(bf16[3,64,1024]{2,1,0:T(8,128)(2,1)S(1)} %add_convert_fusion.3), channel_id=1, source_target_pairs={{1,2},{2,1},{5,6},{6,5},{9,10},{10,9},{13,14},{14,13},{17,18},{18,... | collective-permute-start | bytes 1179656 | tf_op jit(solution)/shard_map/ppermute | solution.py:174
  64.1 16.6 %collective-permute-start.19 = (bf16[3,64,1024]{2,1,0:T(8,128)(2,1)S(1)}, bf16[3,64,1024]{2,1,0:T(8,128)(2,1)S(1)}, u32[]{:S(2)}, u32[]{:S(2)}) collective-permute-start(bf16[3,64,1024]{2,1,0:T(8,128)(2,1)S(1)} %broadcast_select_fusion.9), channel_id=1, source_target_pairs={{0,1},{3,2},{1,0},{2,3},{4,5},{7,6},{5,4},{6,7},{8,9},{11,10},{9,8... | collective-permute-start | bytes 1179656 | tf_op jit(solution)/shard_map/ppermute | solution.py:169
  70.9 10.4 %collective-permute-start.23 = (bf16[3,64,1024]{2,1,0:T(8,128)(2,1)S(1)}, bf16[3,64,1024]{2,1,0:T(8,128)(2,1)S(1)}, u32[]{:S(2)}, u32[]{:S(2)}) collective-permute-start(bf16[3,64,1024]{2,1,0:T(8,128)(2,1)S(1)} %get-tuple-element.57), channel_id=1, source_target_pairs={{1,2},{2,1},{5,6},{6,5},{9,10},{10,9},{13,14},{14,13},{17,18},{18,... | collective-permute-start | bytes 1179656 | tf_op jit(solution)/shard_map/ppermute | solution.py:174
  72.1 19.9 %collective-permute-start.25 = (bf16[3,64,1024]{2,1,0:T(8,128)(2,1)S(1)}, bf16[3,64,1024]{2,1,0:T(8,128)(2,1)S(1)}, u32[]{:S(2)}, u32[]{:S(2)}) collective-permute-start(bf16[3,64,1024]{2,1,0:T(8,128)(2,1)S(1)} %get-tuple-element.56), channel_id=1, source_target_pairs={{0,1},{3,2},{1,0},{2,3},{4,5},{7,6},{5,4},{6,7},{8,9},{11,10},{9,8... | collective-permute-start | bytes 1179656 | tf_op jit(solution)/shard_map/ppermute | solution.py:169
  81.5 14.7 %collective-permute-start.24 = (bf16[3,64,1024]{2,1,0:T(8,128)(2,1)S(1)}, bf16[3,64,1024]{2,1,0:T(8,128)(2,1)S(1)}, u32[]{:S(2)}, u32[]{:S(2)}) collective-permute-start(bf16[3,64,1024]{2,1,0:T(8,128)(2,1)S(1)} %broadcast_select_fusion.3), channel_id=1, source_target_pairs={{0,1},{3,2},{1,0},{2,3},{4,5},{7,6},{5,4},{6,7},{8,9},{11,10},{9,8... | collective-permute-start | bytes 1179656 | tf_op jit(solution)/shard_map/ppermute | solution.py:169
  97.4 9.7 %collective-permute-start.27 = (bf16[3,64,1024]{2,1,0:T(8,128)(2,1)S(1)}, bf16[3,64,1024]{2,1,0:T(8,128)(2,1)S(1)}, u32[]{:S(2)}, u32[]{:S(2)}) collective-permute-start(bf16[3,64,1024]{2,1,0:T(8,128)(2,1)S(1)} %get-tuple-element.55), channel_id=1, source_target_pairs={{1,2},{2,1},{5,6},{6,5},{9,10},{10,9},{13,14},{14,13},{17,18},{18,... | collective-permute-start | bytes 1179656 | tf_op jit(solution)/shard_map/ppermute | solution.py:174
  98.1 18.5 %collective-permute-start.29 = (bf16[3,64,1024]{2,1,0:T(8,128)(2,1)S(1)}, bf16[3,64,1024]{2,1,0:T(8,128)(2,1)S(1)}, u32[]{:S(2)}, u32[]{:S(2)}) collective-permute-start(bf16[3,64,1024]{2,1,0:T(8,128)(2,1)S(1)} %get-tuple-element.54), channel_id=1, source_target_pairs={{0,1},{3,2},{1,0},{2,3},{4,5},{7,6},{5,4},{6,7},{8,9},{11,10},{9,8... | collective-permute-start | bytes 1179656 | tf_op jit(solution)/shard_map/ppermute | solution.py:169
  105.6 11.0 %collective-permute-start.31 = (bf16[3,64,1024]{2,1,0:T(8,128)(2,1)S(1)}, bf16[3,64,1024]{2,1,0:T(8,128)(2,1)S(1)}, u32[]{:S(2)}, u32[]{:S(2)}) collective-permute-start(bf16[3,64,1024]{2,1,0:T(8,128)(2,1)S(1)} %add_convert_fusion.1), channel_id=1, source_target_pairs={{1,2},{2,1},{5,6},{6,5},{9,10},{10,9},{13,14},{14,13},{17,18},{18,... | collective-permute-start | bytes 1179656 | tf_op jit(solution)/shard_map/ppermute | solution.py:174
  107.2 17.1 %collective-permute-start.28 = (bf16[3,64,1024]{2,1,0:T(8,128)(2,1)S(1)}, bf16[3,64,1024]{2,1,0:T(8,128)(2,1)S(1)}, u32[]{:S(2)}, u32[]{:S(2)}) collective-permute-start(bf16[3,64,1024]{2,1,0:T(8,128)(2,1)S(1)} %broadcast_select_fusion.8), channel_id=1, source_target_pairs={{0,1},{3,2},{1,0},{2,3},{4,5},{7,6},{5,4},{6,7},{8,9},{11,10},{9,8... | collective-permute-start | bytes 1179656 | tf_op jit(solution)/shard_map/ppermute | solution.py:169
  117.0 10.0 %collective-permute-start.41 = (bf16[3,64,1024]{2,1,0:T(8,128)(2,1)S(1)}, bf16[3,64,1024]{2,1,0:T(8,128)(2,1)S(1)}, u32[]{:S(2)}, u32[]{:S(2)}) collective-permute-start(bf16[3,64,1024]{2,1,0:T(8,128)(2,1)S(1)} %get-tuple-element.49), channel_id=1, source_target_pairs={{1,2},{2,1},{5,6},{6,5},{9,10},{10,9},{13,14},{14,13},{17,18},{18,... | collective-permute-start | bytes 1179656 | tf_op jit(solution)/shard_map/ppermute | solution.py:174
  117.7 13.0 %collective-permute-start.32 = (bf16[3,64,1024]{2,1,0:T(8,128)(2,1)S(1)}, bf16[3,64,1024]{2,1,0:T(8,128)(2,1)S(1)}, u32[]{:S(2)}, u32[]{:S(2)}) collective-permute-start(bf16[3,64,1024]{2,1,0:T(8,128)(2,1)S(1)} %get-tuple-element.50), channel_id=1, source_target_pairs={{0,1},{3,2},{1,0},{2,3},{4,5},{7,6},{5,4},{6,7},{8,9},{11,10},{9,8... | collective-permute-start | bytes 1179656 | tf_op jit(solution)/shard_map/ppermute | solution.py:169
  127.1 18.1 %collective-permute-start.42 = (bf16[3,64,1024]{2,1,0:T(8,128)(2,1)S(1)}, bf16[3,64,1024]{2,1,0:T(8,128)(2,1)S(1)}, u32[]{:S(2)}, u32[]{:S(2)}) collective-permute-start(bf16[3,64,1024]{2,1,0:T(8,128)(2,1)S(1)} %collective-permute-done.41), channel_id=1, source_target_pairs={{1,0},{2,3},{5,4},{6,7},{9,8},{10,11},{13,12},{14,15},{17,16},{18,... | collective-permute-start | bytes 1179656 | tf_op jit(solution)/shard_map/ppermute | solution.py:167
  131.2 15.9 %collective-permute-start.34 = (bf16[3,64,1024]{2,1,0:T(8,128)(2,1)S(1)}, bf16[3,64,1024]{2,1,0:T(8,128)(2,1)S(1)}, u32[]{:S(2)}, u32[]{:S(2)}) collective-permute-start(bf16[3,64,1024]{2,1,0:T(8,128)(2,1)S(1)} %pad_maximum_fusion.16), channel_id=1, source_target_pairs={{1,2},{2,1},{5,6},{6,5},{9,10},{10,9},{13,14},{14,13},{17,18},{18,... | collective-permute-start | bytes 1179656 | tf_op jit(solution)/shard_map/ppermute | solution.py:174
  131.9 27.6 %collective-permute-start.43 = (bf16[3,64,1024]{2,1,0:T(8,128)(2,1)S(1)}, bf16[3,64,1024]{2,1,0:T(8,128)(2,1)S(1)}, u32[]{:S(2)}, u32[]{:S(2)}) collective-permute-start(bf16[3,64,1024]{2,1,0:T(8,128)(2,1)S(1)} %pad_maximum_fusion.16), channel_id=1, source_target_pairs={{1,0},{2,3},{5,4},{6,7},{9,8},{10,11},{13,12},{14,15},{17,16},{18,... | collective-permute-start | bytes 1179656 | tf_op jit(solution)/shard_map/ppermute | solution.py:167
  133.5 15.5 %collective-permute-start.38 = (bf16[2,3,16,512]{3,2,1,0:T(8,128)(2,1)S(1)}, bf16[2,3,16,512]{3,2,1,0:T(8,128)(2,1)S(1)}, u32[]{:S(2)}, u32[]{:S(2)}) collective-permute-start(bf16[2,3,16,512]{3,2,1,0:T(8,128)(2,1)S(1)} %get-tuple-element.52), channel_id=1, source_target_pairs={{0,24},{4,28},{8,16},{12,20},{16,8},{20,12},{24,0},{28,4},{1,25},{... | collective-permute-start | bytes 294920 | tf_op jit(solution)/shard_map/ppermute | solution.py:71
  135.1 13.9 %collective-permute-start.37 = (bf16[2,3,16,512]{3,2,1,0:T(8,128)(2,1)S(1)}, bf16[2,3,16,512]{3,2,1,0:T(8,128)(2,1)S(1)}, u32[]{:S(2)}, u32[]{:S(2)}) collective-permute-start(bf16[2,3,16,512]{3,2,1,0:T(8,128)(2,1)S(1)} %get-tuple-element.53), channel_id=1, source_target_pairs={{0,16},{4,20},{8,24},{12,28},{16,0},{20,4},{24,8},{28,12},{1,17},{... | collective-permute-start | bytes 294920 | tf_op jit(solution)/shard_map/ppermute | solution.py:71
  147.1 12.2 %collective-permute-start.35 = (bf16[3,64,1024]{2,1,0:T(8,128)(2,1)S(1)}, bf16[3,64,1024]{2,1,0:T(8,128)(2,1)S(1)}, u32[]{:S(2)}, u32[]{:S(2)}) collective-permute-start(bf16[3,64,1024]{2,1,0:T(8,128)(2,1)S(1)} %broadcast_select_fusion), channel_id=1, source_target_pairs={{1,0},{2,3},{5,4},{6,7},{9,8},{10,11},{13,12},{14,15},{17,16},{18,... | collective-permute-start | bytes 1179656 | tf_op jit(solution)/shard_map/ppermute | solution.py:167
  167.1 7.4 %collective-permute-start.40 = (bf16[2,48,512]{2,1,0:T(8,128)(2,1)S(1)}, bf16[2,48,512]{2,1,0:T(8,128)(2,1)S(1)}, u32[]{:S(2)}, u32[]{:S(2)}) collective-permute-start(bf16[2,48,512]{2,1,0:T(8,128)(2,1)S(1)} %fusion.116), channel_id=1, source_target_pairs={{0,2},{1,3},{2,0},{3,1},{4,6},{5,7},{6,4},{7,5},{8,10},{9,11},{10,... | collective-permute-start | bytes 294920 | tf_op jit(solution)/shard_map/ppermute | solution.py:71
  174.7 8.5 %collective-permute-start.50 = (bf16[2,32,512]{2,1,0:T(8,128)(2,1)S(1)}, bf16[2,32,512]{2,1,0:T(8,128)(2,1)S(1)}, u32[]{:S(2)}, u32[]{:S(2)}) collective-permute-start(bf16[2,32,512]{2,1,0:T(8,128)(2,1)S(1)} %bitcast.557), channel_id=1, source_target_pairs={{0,3},{1,2},{2,1},{3,0},{4,7},{5,6},{6,5},{7,4},{8,11},{9,10},{10,... | collective-permute-start | bytes 196616 | tf_op jit(solution)/shard_map/ppermute | solution.py:71
  (24 other events, 192.5 us)

commit v14 on v13

--- a/solution.py
+++ b/solution.py
@@ -88,12 +88,14 @@
     return turn(sum(piece.astype(F32) * sign[:, :width] for piece, sign in zip(pieces, signs)), square)
 
 
-def rotate_by_halves(block, bits, square):
+def rotate_by_halves(block, bits, square, ahead):
     block = turn(block, square)
     for level, bit in enumerate(bits):
-        came = exchange(block.astype(BF16), "tensor", 1 << level)
+        message = block.astype(BF16)
+        message = after(message, ahead) if level else message
+        came = exchange(message, "tensor", 1 << level)
         block = block * bit[:, : block.shape[-1]] + came.astype(F32)
-    return block
+    return block, message
 
 
 def dp_stages():
@@ -266,17 +268,18 @@
                 crossed.append(across(acts[i]))
                 outs += [acts[i], crossed[i]]
     low, high = leave([done(i) for i in range(split, chunks)])
+    sums, _, ahead = scatter_dp(low, high)
     if split > 0:
         first_sums = after(first_sums.reshape(2, -1, width), came[-1])
-        ends.append(rotate_by_halves(first_sums, bits, square))
-    sums, _, ahead = scatter_dp(low, high)
+        block, ahead = rotate_by_halves(first_sums, bits, square, ahead)
+        ends.append(block)
     ends.append(rotate(spread(sums.reshape(2, -1, width).astype(BF16)), signs, square))
     ends = jnp.concatenate(ends, axis=1)
 
     acts = jnp.concatenate([done(i) for i in range(chunks)], axis=1)
     rows = [jnp.stack(group, axis=2).reshape(2, -1, width) for group in groups]
     rows = after(jnp.concatenate(rows, axis=1), high[0, 0, :1])
-    late_rows = after(rows[0], ahead[0, 0, :1])
+    late_rows = after(rows[0], ahead.reshape(-1, width)[:1])
     factor = 1.0 / math.sqrt(rows.shape[1])
     return (
         ends[0],

time: 186 us -> 184 us (0.989)
  transfers between devices with their start and end apart: 51 -> 51, of which waited for: 19 -> 21; matrix products, arithmetic and copies ran while one was open for 17% -> 17% of each run, Pallas kernels for 0% -> 0%
where the time goes in v14:
time: 184 us
  starting transfers between devices  99.5 us (54%)
  waiting for transfers between devices  44.9 us (24%)
  matrix products  24.7 us (13%)
  other arithmetic  11 us (6%)
  between operations  2.02 us (1%)
  local copies, waits for them, and re-layouts  1.84 us (1%)
    ppermute x7, starting transfers between devices, swap(): return lax.ppermute(block, 'tensor', pairs + back)  48.8 us
    ppermute x28, starting transfers between devices, exchange(): return lax.ppermute(block, axis, [(i, i ^ apart) for i in range(count)])  29.6 us
    dot_general x56, matrix products, dot(): lax.dot_general(left, right, (((left_dim,), (right_dim,)), ((), ())), pre...  24.7 us
    ppermute x3, waiting for transfers between devices, swap(): return lax.ppermute(out, 'tensor', back)  19 us
    ppermute x28, waiting for transfers between devices, exchange(): return lax.ppermute(block, axis, [(i, i ^ apart) for i in range(count)])  13.9 us
    ppermute x3, starting transfers between devices, swap(): return lax.ppermute(into, 'tensor', pairs)  9.93 us
    ppermute x3, waiting for transfers between devices, swap(): return lax.ppermute(into, 'tensor', pairs)  7.15 us
    ppermute x10, starting transfers between devices, across(): return lax.ppermute(block, 'tensor', [(half - 1, half), (half, half - 1)])  7.04 us
  transfers between devices with their start and end apart: 51, of which 21 were waited for; matrix products, arithmetic and copies ran while one was open for 17% of the time, Pallas kernels for 0%

profile of v14, /device:TPU:0, one launch (start us, length us, event | category | flops | bytes accessed | tf_op | source)
XLA Modules:
  0.0 183.9 jit_solution(6440293800349643314)
XLA Ops:
  1.5 5.0 %collective-permute-start.2 = (bf16[2,32,512]{2,1,0:T(8,128)(2,1)S(1)}, bf16[2,32,512]{2,1,0:T(8,128)(2,1)S(1)}, u32[]{:S(2)}, u32[]{:S(2)}) collective-permute-start(bf16[2,32,512]{2,1,0:T(8,128)(2,1)S(1)} %pad_maximum_fusion.26), channel_id=1, source_target_pairs={{0,3},{1,2},{2,1},{3,0},{4,7},{5,6},{6,5},{7,4},{8,11},{9,10},{10,... | collective-permute-start | bytes 196616 | tf_op jit(solution)/shard_map/ppermute | solution.py:71
  10.3 1.9 %collective-permute-done.1 = bf16[2,32,512]{2,1,0:T(8,128)(2,1)S(1)} collective-permute-done((bf16[2,32,512]{2,1,0:T(8,128)(2,1)S(1)}, bf16[2,32,512]{2,1,0:T(8,128)(2,1)S(1)}, u32[]{:S(2)}, u32[]{:S(2)}) %collective-permute-start.1) | collective-permute-done | bytes 65568 | tf_op jit(solution)/shard_map/ppermute | solution.py:71
  13.5 2.5 %collective-permute-start.5 = (bf16[2,2,1,16,512]{4,3,2,1,0:T(8,128)(2,1)S(1)}, bf16[2,2,1,16,512]{4,3,2,1,0:T(8,128)(2,1)S(1)}, u32[]{:S(2)}, u32[]{:S(2)}) collective-permute-start(bf16[2,2,1,16,512]{4,3,2,1,0:T(8,128)(2,1)S(1)} %bitcast.548), channel_id=1, source_target_pairs={{0,24},{4,28},{8,16},{12,20},{16,8},{20,12},{24,0},{28,4},{1,25},{... | collective-permute-start | bytes 196616 | tf_op jit(solution)/shard_map/ppermute | solution.py:71
  17.1 1.7 collective-permute-done.5
  21.0 2.8 %collective-permute-start.14 = (bf16[2,48,512]{2,1,0:T(8,128)(2,1)S(1)}, bf16[2,48,512]{2,1,0:T(8,128)(2,1)S(1)}, u32[]{:S(2)}, u32[]{:S(2)}) collective-permute-start(bf16[2,48,512]{2,1,0:T(8,128)(2,1)S(1)} %fusion.118), channel_id=1, source_target_pairs={{0,3},{1,2},{2,1},{3,0},{4,7},{5,6},{6,5},{7,4},{8,11},{9,10},{10,... | collective-permute-start | bytes 294920 | tf_op jit(solution)/shard_map/ppermute | solution.py:71
  23.8 1.7 collective-permute-start.12
  27.7 2.3 %collective-permute-start.7 = (bf16[3,64,1024]{2,1,0:T(8,128)(2,1)S(1)}, bf16[3,64,1024]{2,1,0:T(8,128)(2,1)S(1)}, u32[]{:S(2)}, u32[]{:S(2)}) collective-permute-start(bf16[3,64,1024]{2,1,0:T(8,128)(2,1)S(1)} %pad_maximum_fusion.2), channel_id=1, source_target_pairs={{0,1},{3,2},{4,5},{7,6},{8,9},{11,10},{12,13},{15,14},{16,17},{19,... | collective-permute-start | bytes 1179656 | tf_op jit(solution)/shard_map/ppermute | solution.py:167
  31.3 1.8 collective-permute-done.13
  33.7 1.6 collective-permute-start.17
  37.2 1.9 %collective-permute-done.7 = bf16[3,64,1024]{2,1,0:T(8,128)(2,1)S(1)} collective-permute-done((bf16[3,64,1024]{2,1,0:T(8,128)(2,1)S(1)}, bf16[3,64,1024]{2,1,0:T(8,128)(2,1)S(1)}, u32[]{:S(2)}, u32[]{:S(2)}) %collective-permute-start.7) | collective-permute-done | bytes 393248 | tf_op jit(solution)/shard_map/ppermute | solution.py:167
  39.7 4.4 %collective-permute-start.8 = (bf16[3,64,1024]{2,1,0:T(8,128)(2,1)S(1)}, bf16[3,64,1024]{2,1,0:T(8,128)(2,1)S(1)}, u32[]{:S(2)}, u32[]{:S(2)}) collective-permute-start(bf16[3,64,1024]{2,1,0:T(8,128)(2,1)S(1)} %maximum_select_fusion.1), channel_id=1, source_target_pairs={{0,1},{3,2},{4,5},{7,6},{8,9},{11,10},{12,13},{15,14},{16,17},{19,... | collective-permute-start | bytes 1179656 | tf_op jit(solution)/shard_map/ppermute | solution.py:167
  46.4 3.2 %collective-permute-start.21 = (bf16[3,64,1024]{2,1,0:T(8,128)(2,1)S(1)}, bf16[3,64,1024]{2,1,0:T(8,128)(2,1)S(1)}, u32[]{:S(2)}, u32[]{:S(2)}) collective-permute-start(bf16[3,64,1024]{2,1,0:T(8,128)(2,1)S(1)} %pad_maximum_fusion.7), channel_id=1, source_target_pairs={{0,1},{3,2},{4,5},{7,6},{8,9},{11,10},{12,13},{15,14},{16,17},{19,... | collective-permute-start | bytes 1179656 | tf_op jit(solution)/shard_map/ppermute | solution.py:167
  50.3 3.4 %collective-permute-done.8 = bf16[3,64,1024]{2,1,0:T(8,128)(2,1)S(1)} collective-permute-done((bf16[3,64,1024]{2,1,0:T(8,128)(2,1)S(1)}, bf16[3,64,1024]{2,1,0:T(8,128)(2,1)S(1)}, u32[]{:S(2)}, u32[]{:S(2)}) %collective-permute-start.8) | collective-permute-done | bytes 393248 | tf_op jit(solution)/shard_map/ppermute | solution.py:167
  54.8 4.2 %collective-permute-start.20 = (bf16[3,64,1024]{2,1,0:T(8,128)(2,1)S(1)}, bf16[3,64,1024]{2,1,0:T(8,128)(2,1)S(1)}, u32[]{:S(2)}, u32[]{:S(2)}) collective-permute-start(bf16[3,64,1024]{2,1,0:T(8,128)(2,1)S(1)} %get-tuple-element.58), channel_id=1, source_target_pairs={{0,1},{3,2},{1,0},{2,3},{4,5},{7,6},{5,4},{6,7},{8,9},{11,10},{9,8... | collective-permute-start | bytes 1179656 | tf_op jit(solution)/shard_map/ppermute | solution.py:171
  60.2 1.8 collective-permute-done.21
  64.1 6.2 %collective-permute-start.19 = (bf16[3,64,1024]{2,1,0:T(8,128)(2,1)S(1)}, bf16[3,64,1024]{2,1,0:T(8,128)(2,1)S(1)}, u32[]{:S(2)}, u32[]{:S(2)}) collective-permute-start(bf16[3,64,1024]{2,1,0:T(8,128)(2,1)S(1)} %broadcast_select_fusion.9), channel_id=1, source_target_pairs={{0,1},{3,2},{1,0},{2,3},{4,5},{7,6},{5,4},{6,7},{8,9},{11,10},{9,8... | collective-permute-start | bytes 1179656 | tf_op jit(solution)/shard_map/ppermute | solution.py:171
  72.1 8.0 %collective-permute-start.25 = (bf16[3,64,1024]{2,1,0:T(8,128)(2,1)S(1)}, bf16[3,64,1024]{2,1,0:T(8,128)(2,1)S(1)}, u32[]{:S(2)}, u32[]{:S(2)}) collective-permute-start(bf16[3,64,1024]{2,1,0:T(8,128)(2,1)S(1)} %get-tuple-element.56), channel_id=1, source_target_pairs={{0,1},{3,2},{1,0},{2,3},{4,5},{7,6},{5,4},{6,7},{8,9},{11,10},{9,8... | collective-permute-start | bytes 1179656 | tf_op jit(solution)/shard_map/ppermute | solution.py:171
  81.5 7.3 %collective-permute-start.24 = (bf16[3,64,1024]{2,1,0:T(8,128)(2,1)S(1)}, bf16[3,64,1024]{2,1,0:T(8,128)(2,1)S(1)}, u32[]{:S(2)}, u32[]{:S(2)}) collective-permute-start(bf16[3,64,1024]{2,1,0:T(8,128)(2,1)S(1)} %broadcast_select_fusion.3), channel_id=1, source_target_pairs={{0,1},{3,2},{1,0},{2,3},{4,5},{7,6},{5,4},{6,7},{8,9},{11,10},{9,8... | collective-permute-start | bytes 1179656 | tf_op jit(solution)/shard_map/ppermute | solution.py:171
  94.2 2.0 %collective-permute-done.24 = bf16[3,64,1024]{2,1,0:T(8,128)(2,1)S(1)} collective-permute-done((bf16[3,64,1024]{2,1,0:T(8,128)(2,1)S(1)}, bf16[3,64,1024]{2,1,0:T(8,128)(2,1)S(1)}, u32[]{:S(2)}, u32[]{:S(2)}) %collective-permute-start.24) | collective-permute-done | bytes 393248 | tf_op jit(solution)/shard_map/ppermute | solution.py:171
  98.1 7.4 %collective-permute-start.29 = (bf16[3,64,1024]{2,1,0:T(8,128)(2,1)S(1)}, bf16[3,64,1024]{2,1,0:T(8,128)(2,1)S(1)}, u32[]{:S(2)}, u32[]{:S(2)}) collective-permute-start(bf16[3,64,1024]{2,1,0:T(8,128)(2,1)S(1)} %get-tuple-element.54), channel_id=1, source_target_pairs={{0,1},{3,2},{1,0},{2,3},{4,5},{7,6},{5,4},{6,7},{8,9},{11,10},{9,8... | collective-permute-start | bytes 1179656 | tf_op jit(solution)/shard_map/ppermute | solution.py:171
  107.2 9.4 %collective-permute-start.28 = (bf16[3,64,1024]{2,1,0:T(8,128)(2,1)S(1)}, bf16[3,64,1024]{2,1,0:T(8,128)(2,1)S(1)}, u32[]{:S(2)}, u32[]{:S(2)}) collective-permute-start(bf16[3,64,1024]{2,1,0:T(8,128)(2,1)S(1)} %broadcast_select_fusion.8), channel_id=1, source_target_pairs={{0,1},{3,2},{1,0},{2,3},{4,5},{7,6},{5,4},{6,7},{8,9},{11,10},{9,8... | collective-permute-start | bytes 1179656 | tf_op jit(solution)/shard_map/ppermute | solution.py:171
  117.7 6.2 %collective-permute-start.32 = (bf16[3,64,1024]{2,1,0:T(8,128)(2,1)S(1)}, bf16[3,64,1024]{2,1,0:T(8,128)(2,1)S(1)}, u32[]{:S(2)}, u32[]{:S(2)}) collective-permute-start(bf16[3,64,1024]{2,1,0:T(8,128)(2,1)S(1)} %get-tuple-element.50), channel_id=1, source_target_pairs={{0,1},{3,2},{1,0},{2,3},{4,5},{7,6},{5,4},{6,7},{8,9},{11,10},{9,8... | collective-permute-start | bytes 1179656 | tf_op jit(solution)/shard_map/ppermute | solution.py:171
  128.4 2.4 %collective-permute-done.32 = bf16[3,64,1024]{2,1,0:T(8,128)(2,1)S(1)} collective-permute-done((bf16[3,64,1024]{2,1,0:T(8,128)(2,1)S(1)}, bf16[3,64,1024]{2,1,0:T(8,128)(2,1)S(1)}, u32[]{:S(2)}, u32[]{:S(2)}) %collective-permute-start.32) | collective-permute-done | bytes 393248 | tf_op jit(solution)/shard_map/ppermute | solution.py:171
  133.5 1.6 collective-permute-start.38
  135.6 9.5 %collective-permute-done.41 = bf16[3,64,1024]{2,1,0:T(8,128)(2,1)S(1)} collective-permute-done((bf16[3,64,1024]{2,1,0:T(8,128)(2,1)S(1)}, bf16[3,64,1024]{2,1,0:T(8,128)(2,1)S(1)}, u32[]{:S(2)}, u32[]{:S(2)}) %collective-permute-start.41) | collective-permute-done | bytes 393248 | tf_op jit(solution)/shard_map/ppermute | solution.py:169
  149.8 9.5 %collective-permute-done.35 = bf16[3,64,1024]{2,1,0:T(8,128)(2,1)S(1)} collective-permute-done((bf16[3,64,1024]{2,1,0:T(8,128)(2,1)S(1)}, bf16[3,64,1024]{2,1,0:T(8,128)(2,1)S(1)}, u32[]{:S(2)}, u32[]{:S(2)}) %collective-permute-start.35) | collective-permute-done | bytes 393248 | tf_op jit(solution)/shard_map/ppermute | solution.py:169
  163.0 1.5 collective-permute-start.44
  166.5 2.0 %multiply_convert_fusion = bf16[1024,512]{1,0:T(8,128)(2,1)} fusion(bf16[3,640,1024]{2,1,0:T(8,128)(2,1)S(1)} %get-tuple-element.10, bf16[2,640,512]{2,1,0:T(8,128)(2,1)S(1)} %maximum_select_fusion), kind=kOutput, calls=%fused_computation | convolution fusion | flops 672137216 | bytes 3014656 | tf_op jit(solution)/shard_map/dot_general | solution.py:37
  169.6 2.2 %collective-permute-start.50 = (bf16[2,32,512]{2,1,0:T(8,128)(2,1)S(1)}, bf16[2,32,512]{2,1,0:T(8,128)(2,1)S(1)}, u32[]{:S(2)}, u32[]{:S(2)}) collective-permute-start(bf16[2,32,512]{2,1,0:T(8,128)(2,1)S(1)} %bitcast.559), channel_id=1, source_target_pairs={{0,3},{1,2},{2,1},{3,0},{4,7},{5,6},{6,5},{7,4},{8,11},{9,10},{10,... | collective-permute-start | bytes 196616 | tf_op jit(solution)/shard_map/ppermute | solution.py:71
  175.5 2.0 %multiply_convert_fusion.2 = bf16[512,1024]{1,0:T(8,128)(2,1)} fusion(bf16[3,640,1024]{2,1,0:T(8,128)(2,1)S(1)} %get-tuple-element.10, bf16[2,640,512]{2,1,0:T(8,128)(2,1)S(1)} %maximum_select_fusion, pred[512]{0:T(512)(128)(4,1)S(1)} %compare_reduce_fusion.5, bf16[512]{0:T(512)(128)(2,1)S(1)} %slice_reduce_fusion.3), kind=kOutput, calls=%fused_computation.2 | convolution fusion | flops 672464896 | bytes 3016192 | tf_op jit(solution)/shard_map/dot_general | solution.py:37
  177.5 2.0 %multiply_convert_fusion.1 = bf16[512,1024]{1,0:T(8,128)(2,1)} fusion(bf16[3,640,1024]{2,1,0:T(8,128)(2,1)S(1)} %get-tuple-element.10, bf16[2,640,512]{2,1,0:T(8,128)(2,1)S(1)} %maximum_select_fusion, pred[512]{0:T(512)(128)(4,1)S(1)} %compare_reduce_fusion.5, bf16[512]{0:T(512)(128)(2,1)S(1)} %slice_reduce_fusion.3), kind=kOutput, calls=%fused_computation.1 | convolution fusion | flops 672464896 | bytes 3016192 | tf_op jit(solution)/shard_map/dot_general | solution.py:37
  179.5 2.0 %collective-permute-done.49 = bf16[2,32,512]{2,1,0:T(8,128)(2,1)S(1)} collective-permute-done((bf16[2,32,512]{2,1,0:T(8,128)(2,1)S(1)}, bf16[2,32,512]{2,1,0:T(8,128)(2,1)S(1)}, u32[]{:S(2)}, u32[]{:S(2)}) %collective-permute-start.49) | collective-permute-done | bytes 65568 | tf_op jit(solution)/shard_map/ppermute | solution.py:71
  (248 shorter events, 60.4 us)
Async XLA Ops:
  21.0 10.3 %collective-permute-start.14 = (bf16[2,48,512]{2,1,0:T(8,128)(2,1)S(1)}, bf16[2,48,512]{2,1,0:T(8,128)(2,1)S(1)}, u32[]{:S(2)}, u32[]{:S(2)}) collective-permute-start(bf16[2,48,512]{2,1,0:T(8,128)(2,1)S(1)} %fusion.118), channel_id=1, source_target_pairs={{0,3},{1,2},{2,1},{3,0},{4,7},{5,6},{6,5},{7,4},{8,11},{9,10},{10,... | collective-permute-start | bytes 294920 | tf_op jit(solution)/shard_map/ppermute | solution.py:71
  23.7 9.3 %collective-permute-start.13 = (bf16[2,48,512]{2,1,0:T(8,128)(2,1)S(1)}, bf16[2,48,512]{2,1,0:T(8,128)(2,1)S(1)}, u32[]{:S(2)}, u32[]{:S(2)}) collective-permute-start(bf16[2,48,512]{2,1,0:T(8,128)(2,1)S(1)} %fusion.118), channel_id=1, source_target_pairs={{0,2},{1,3},{2,0},{3,1},{4,6},{5,7},{6,4},{7,5},{8,10},{9,11},{10,... | collective-permute-start | bytes 294920 | tf_op jit(solution)/shard_map/ppermute | solution.py:71
  23.8 9.3 %collective-permute-start.12 = (bf16[2,48,512]{2,1,0:T(8,128)(2,1)S(1)}, bf16[2,48,512]{2,1,0:T(8,128)(2,1)S(1)}, u32[]{:S(2)}, u32[]{:S(2)}) collective-permute-start(bf16[2,48,512]{2,1,0:T(8,128)(2,1)S(1)} %fusion.118), channel_id=1, source_target_pairs={{0,1},{1,0},{2,3},{3,2},{4,5},{5,4},{6,7},{7,6},{8,9},{9,8},{10,11... | collective-permute-start | bytes 294920 | tf_op jit(solution)/shard_map/ppermute | solution.py:71
  27.7 11.4 %collective-permute-start.7 = (bf16[3,64,1024]{2,1,0:T(8,128)(2,1)S(1)}, bf16[3,64,1024]{2,1,0:T(8,128)(2,1)S(1)}, u32[]{:S(2)}, u32[]{:S(2)}) collective-permute-start(bf16[3,64,1024]{2,1,0:T(8,128)(2,1)S(1)} %pad_maximum_fusion.2), channel_id=1, source_target_pairs={{0,1},{3,2},{4,5},{7,6},{8,9},{11,10},{12,13},{15,14},{16,17},{19,... | collective-permute-start | bytes 1179656 | tf_op jit(solution)/shard_map/ppermute | solution.py:167
  33.7 12.5 %collective-permute-start.17 = (bf16[2,3,1,16,512]{4,3,2,1,0:T(8,128)(2,1)S(1)}, bf16[2,3,1,16,512]{4,3,2,1,0:T(8,128)(2,1)S(1)}, u32[]{:S(2)}, u32[]{:S(2)}) collective-permute-start(bf16[2,3,1,16,512]{4,3,2,1,0:T(8,128)(2,1)S(1)} %bitcast.555), channel_id=1, source_target_pairs={{0,24},{4,28},{8,16},{12,20},{16,8},{20,12},{24,0},{28,4},{1,25},{... | collective-permute-start | bytes 294920 | tf_op jit(solution)/shard_map/ppermute | solution.py:71
  35.2 10.9 %collective-permute-start.16 = (bf16[2,3,1,16,512]{4,3,2,1,0:T(8,128)(2,1)S(1)}, bf16[2,3,1,16,512]{4,3,2,1,0:T(8,128)(2,1)S(1)}, u32[]{:S(2)}, u32[]{:S(2)}) collective-permute-start(bf16[2,3,1,16,512]{4,3,2,1,0:T(8,128)(2,1)S(1)} %bitcast.556), channel_id=1, source_target_pairs={{0,16},{4,20},{8,24},{12,28},{16,0},{20,4},{24,8},{28,12},{1,17},{... | collective-permute-start | bytes 294920 | tf_op jit(solution)/shard_map/ppermute | solution.py:71
  35.7 10.4 %collective-permute-start.15 = (bf16[2,3,1,16,512]{4,3,2,1,0:T(8,128)(2,1)S(1)}, bf16[2,3,1,16,512]{4,3,2,1,0:T(8,128)(2,1)S(1)}, u32[]{:S(2)}, u32[]{:S(2)}) collective-permute-start(bf16[2,3,1,16,512]{4,3,2,1,0:T(8,128)(2,1)S(1)} %bitcast.557), channel_id=1, source_target_pairs={{0,8},{4,12},{8,0},{12,4},{16,24},{20,28},{24,16},{28,20},{1,9},{5... | collective-permute-start | bytes 294920 | tf_op jit(solution)/shard_map/ppermute | solution.py:71
  39.7 13.9 %collective-permute-start.8 = (bf16[3,64,1024]{2,1,0:T(8,128)(2,1)S(1)}, bf16[3,64,1024]{2,1,0:T(8,128)(2,1)S(1)}, u32[]{:S(2)}, u32[]{:S(2)}) collective-permute-start(bf16[3,64,1024]{2,1,0:T(8,128)(2,1)S(1)} %maximum_select_fusion.1), channel_id=1, source_target_pairs={{0,1},{3,2},{4,5},{7,6},{8,9},{11,10},{12,13},{15,14},{16,17},{19,... | collective-permute-start | bytes 1179656 | tf_op jit(solution)/shard_map/ppermute | solution.py:167
  46.2 12.8 %collective-permute-start.18 = (bf16[2,3,4,16,512]{4,3,2,1,0:T(8,128)(2,1)S(1)}, bf16[2,3,4,16,512]{4,3,2,1,0:T(8,128)(2,1)S(1)}, u32[]{:S(2)}, u32[]{:S(2)}) collective-permute-start(bf16[2,3,4,16,512]{4,3,2,1,0:T(8,128)(2,1)S(1)} %pad_maximum_fusion.4), channel_id=1, source_target_pairs={{0,4},{4,0},{8,12},{12,8},{16,20},{20,16},{24,28},{28,24},{1,5},{5... | collective-permute-start | bytes 1179656 | tf_op jit(solution)/shard_map/ppermute | solution.py:71
  46.4 15.7 %collective-permute-start.21 = (bf16[3,64,1024]{2,1,0:T(8,128)(2,1)S(1)}, bf16[3,64,1024]{2,1,0:T(8,128)(2,1)S(1)}, u32[]{:S(2)}, u32[]{:S(2)}) collective-permute-start(bf16[3,64,1024]{2,1,0:T(8,128)(2,1)S(1)} %pad_maximum_fusion.7), channel_id=1, source_target_pairs={{0,1},{3,2},{4,5},{7,6},{8,9},{11,10},{12,13},{15,14},{16,17},{19,... | collective-permute-start | bytes 1179656 | tf_op jit(solution)/shard_map/ppermute | solution.py:167
  54.1 9.9 %collective-permute-start.10 = (bf16[3,64,1024]{2,1,0:T(8,128)(2,1)S(1)}, bf16[3,64,1024]{2,1,0:T(8,128)(2,1)S(1)}, u32[]{:S(2)}, u32[]{:S(2)}) collective-permute-start(bf16[3,64,1024]{2,1,0:T(8,128)(2,1)S(1)} %get-tuple-element.59), channel_id=1, source_target_pairs={{1,2},{2,1},{5,6},{6,5},{9,10},{10,9},{13,14},{14,13},{17,18},{18,... | collective-permute-start | bytes 1179656 | tf_op jit(solution)/shard_map/ppermute | solution.py:176
  54.8 15.7 %collective-permute-start.20 = (bf16[3,64,1024]{2,1,0:T(8,128)(2,1)S(1)}, bf16[3,64,1024]{2,1,0:T(8,128)(2,1)S(1)}, u32[]{:S(2)}, u32[]{:S(2)}) collective-permute-start(bf16[3,64,1024]{2,1,0:T(8,128)(2,1)S(1)} %get-tuple-element.58), channel_id=1, source_target_pairs={{0,1},{3,2},{1,0},{2,3},{4,5},{7,6},{5,4},{6,7},{8,9},{11,10},{9,8... | collective-permute-start | bytes 1179656 | tf_op jit(solution)/shard_map/ppermute | solution.py:171
  64.1 16.6 %collective-permute-start.19 = (bf16[3,64,1024]{2,1,0:T(8,128)(2,1)S(1)}, bf16[3,64,1024]{2,1,0:T(8,128)(2,1)S(1)}, u32[]{:S(2)}, u32[]{:S(2)}) collective-permute-start(bf16[3,64,1024]{2,1,0:T(8,128)(2,1)S(1)} %broadcast_select_fusion.9), channel_id=1, source_target_pairs={{0,1},{3,2},{1,0},{2,3},{4,5},{7,6},{5,4},{6,7},{8,9},{11,10},{9,8... | collective-permute-start | bytes 1179656 | tf_op jit(solution)/shard_map/ppermute | solution.py:171
  70.9 10.4 %collective-permute-start.23 = (bf16[3,64,1024]{2,1,0:T(8,128)(2,1)S(1)}, bf16[3,64,1024]{2,1,0:T(8,128)(2,1)S(1)}, u32[]{:S(2)}, u32[]{:S(2)}) collective-permute-start(bf16[3,64,1024]{2,1,0:T(8,128)(2,1)S(1)} %get-tuple-element.57), channel_id=1, source_target_pairs={{1,2},{2,1},{5,6},{6,5},{9,10},{10,9},{13,14},{14,13},{17,18},{18,... | collective-permute-start | bytes 1179656 | tf_op jit(solution)/shard_map/ppermute | solution.py:176
  72.1 19.9 %collective-permute-start.25 = (bf16[3,64,1024]{2,1,0:T(8,128)(2,1)S(1)}, bf16[3,64,1024]{2,1,0:T(8,128)(2,1)S(1)}, u32[]{:S(2)}, u32[]{:S(2)}) collective-permute-start(bf16[3,64,1024]{2,1,0:T(8,128)(2,1)S(1)} %get-tuple-element.56), channel_id=1, source_target_pairs={{0,1},{3,2},{1,0},{2,3},{4,5},{7,6},{5,4},{6,7},{8,9},{11,10},{9,8... | collective-permute-start | bytes 1179656 | tf_op jit(solution)/shard_map/ppermute | solution.py:171
  81.5 14.7 %collective-permute-start.24 = (bf16[3,64,1024]{2,1,0:T(8,128)(2,1)S(1)}, bf16[3,64,1024]{2,1,0:T(8,128)(2,1)S(1)}, u32[]{:S(2)}, u32[]{:S(2)}) collective-permute-start(bf16[3,64,1024]{2,1,0:T(8,128)(2,1)S(1)} %broadcast_select_fusion.3), channel_id=1, source_target_pairs={{0,1},{3,2},{1,0},{2,3},{4,5},{7,6},{5,4},{6,7},{8,9},{11,10},{9,8... | collective-permute-start | bytes 1179656 | tf_op jit(solution)/shard_map/ppermute | solution.py:171
  97.4 9.7 %collective-permute-start.27 = (bf16[3,64,1024]{2,1,0:T(8,128)(2,1)S(1)}, bf16[3,64,1024]{2,1,0:T(8,128)(2,1)S(1)}, u32[]{:S(2)}, u32[]{:S(2)}) collective-permute-start(bf16[3,64,1024]{2,1,0:T(8,128)(2,1)S(1)} %get-tuple-element.55), channel_id=1, source_target_pairs={{1,2},{2,1},{5,6},{6,5},{9,10},{10,9},{13,14},{14,13},{17,18},{18,... | collective-permute-start | bytes 1179656 | tf_op jit(solution)/shard_map/ppermute | solution.py:176
  98.1 18.5 %collective-permute-start.29 = (bf16[3,64,1024]{2,1,0:T(8,128)(2,1)S(1)}, bf16[3,64,1024]{2,1,0:T(8,128)(2,1)S(1)}, u32[]{:S(2)}, u32[]{:S(2)}) collective-permute-start(bf16[3,64,1024]{2,1,0:T(8,128)(2,1)S(1)} %get-tuple-element.54), channel_id=1, source_target_pairs={{0,1},{3,2},{1,0},{2,3},{4,5},{7,6},{5,4},{6,7},{8,9},{11,10},{9,8... | collective-permute-start | bytes 1179656 | tf_op jit(solution)/shard_map/ppermute | solution.py:171
  105.6 11.0 %collective-permute-start.31 = (bf16[3,64,1024]{2,1,0:T(8,128)(2,1)S(1)}, bf16[3,64,1024]{2,1,0:T(8,128)(2,1)S(1)}, u32[]{:S(2)}, u32[]{:S(2)}) collective-permute-start(bf16[3,64,1024]{2,1,0:T(8,128)(2,1)S(1)} %add_convert_fusion.1), channel_id=1, source_target_pairs={{1,2},{2,1},{5,6},{6,5},{9,10},{10,9},{13,14},{14,13},{17,18},{18,... | collective-permute-start | bytes 1179656 | tf_op jit(solution)/shard_map/ppermute | solution.py:176
  107.2 17.1 %collective-permute-start.28 = (bf16[3,64,1024]{2,1,0:T(8,128)(2,1)S(1)}, bf16[3,64,1024]{2,1,0:T(8,128)(2,1)S(1)}, u32[]{:S(2)}, u32[]{:S(2)}) collective-permute-start(bf16[3,64,1024]{2,1,0:T(8,128)(2,1)S(1)} %broadcast_select_fusion.8), channel_id=1, source_target_pairs={{0,1},{3,2},{1,0},{2,3},{4,5},{7,6},{5,4},{6,7},{8,9},{11,10},{9,8... | collective-permute-start | bytes 1179656 | tf_op jit(solution)/shard_map/ppermute | solution.py:171
  117.0 10.0 %collective-permute-start.40 = (bf16[3,64,1024]{2,1,0:T(8,128)(2,1)S(1)}, bf16[3,64,1024]{2,1,0:T(8,128)(2,1)S(1)}, u32[]{:S(2)}, u32[]{:S(2)}) collective-permute-start(bf16[3,64,1024]{2,1,0:T(8,128)(2,1)S(1)} %get-tuple-element.49), channel_id=1, source_target_pairs={{1,2},{2,1},{5,6},{6,5},{9,10},{10,9},{13,14},{14,13},{17,18},{18,... | collective-permute-start | bytes 1179656 | tf_op jit(solution)/shard_map/ppermute | solution.py:176
  117.7 13.0 %collective-permute-start.32 = (bf16[3,64,1024]{2,1,0:T(8,128)(2,1)S(1)}, bf16[3,64,1024]{2,1,0:T(8,128)(2,1)S(1)}, u32[]{:S(2)}, u32[]{:S(2)}) collective-permute-start(bf16[3,64,1024]{2,1,0:T(8,128)(2,1)S(1)} %get-tuple-element.50), channel_id=1, source_target_pairs={{0,1},{3,2},{1,0},{2,3},{4,5},{7,6},{5,4},{6,7},{8,9},{11,10},{9,8... | collective-permute-start | bytes 1179656 | tf_op jit(solution)/shard_map/ppermute | solution.py:171
  127.1 18.1 %collective-permute-start.41 = (bf16[3,64,1024]{2,1,0:T(8,128)(2,1)S(1)}, bf16[3,64,1024]{2,1,0:T(8,128)(2,1)S(1)}, u32[]{:S(2)}, u32[]{:S(2)}) collective-permute-start(bf16[3,64,1024]{2,1,0:T(8,128)(2,1)S(1)} %collective-permute-done.40), channel_id=1, source_target_pairs={{1,0},{2,3},{5,4},{6,7},{9,8},{10,11},{13,12},{14,15},{17,16},{18,... | collective-permute-start | bytes 1179656 | tf_op jit(solution)/shard_map/ppermute | solution.py:169
  131.2 15.9 %collective-permute-start.34 = (bf16[3,64,1024]{2,1,0:T(8,128)(2,1)S(1)}, bf16[3,64,1024]{2,1,0:T(8,128)(2,1)S(1)}, u32[]{:S(2)}, u32[]{:S(2)}) collective-permute-start(bf16[3,64,1024]{2,1,0:T(8,128)(2,1)S(1)} %pad_maximum_fusion.16), channel_id=1, source_target_pairs={{1,2},{2,1},{5,6},{6,5},{9,10},{10,9},{13,14},{14,13},{17,18},{18,... | collective-permute-start | bytes 1179656 | tf_op jit(solution)/shard_map/ppermute | solution.py:176
  131.9 27.6 %collective-permute-start.42 = (bf16[3,64,1024]{2,1,0:T(8,128)(2,1)S(1)}, bf16[3,64,1024]{2,1,0:T(8,128)(2,1)S(1)}, u32[]{:S(2)}, u32[]{:S(2)}) collective-permute-start(bf16[3,64,1024]{2,1,0:T(8,128)(2,1)S(1)} %pad_maximum_fusion.16), channel_id=1, source_target_pairs={{1,0},{2,3},{5,4},{6,7},{9,8},{10,11},{13,12},{14,15},{17,16},{18,... | collective-permute-start | bytes 1179656 | tf_op jit(solution)/shard_map/ppermute | solution.py:169
  133.5 15.5 %collective-permute-start.38 = (bf16[2,3,16,512]{3,2,1,0:T(8,128)(2,1)S(1)}, bf16[2,3,16,512]{3,2,1,0:T(8,128)(2,1)S(1)}, u32[]{:S(2)}, u32[]{:S(2)}) collective-permute-start(bf16[2,3,16,512]{3,2,1,0:T(8,128)(2,1)S(1)} %get-tuple-element.52), channel_id=1, source_target_pairs={{0,24},{4,28},{8,16},{12,20},{16,8},{20,12},{24,0},{28,4},{1,25},{... | collective-permute-start | bytes 294920 | tf_op jit(solution)/shard_map/ppermute | solution.py:71
  135.1 13.9 %collective-permute-start.37 = (bf16[2,3,16,512]{3,2,1,0:T(8,128)(2,1)S(1)}, bf16[2,3,16,512]{3,2,1,0:T(8,128)(2,1)S(1)}, u32[]{:S(2)}, u32[]{:S(2)}) collective-permute-start(bf16[2,3,16,512]{3,2,1,0:T(8,128)(2,1)S(1)} %get-tuple-element.53), channel_id=1, source_target_pairs={{0,16},{4,20},{8,24},{12,28},{16,0},{20,4},{24,8},{28,12},{1,17},{... | collective-permute-start | bytes 294920 | tf_op jit(solution)/shard_map/ppermute | solution.py:71
  147.1 12.2 %collective-permute-start.35 = (bf16[3,64,1024]{2,1,0:T(8,128)(2,1)S(1)}, bf16[3,64,1024]{2,1,0:T(8,128)(2,1)S(1)}, u32[]{:S(2)}, u32[]{:S(2)}) collective-permute-start(bf16[3,64,1024]{2,1,0:T(8,128)(2,1)S(1)} %broadcast_select_fusion), channel_id=1, source_target_pairs={{1,0},{2,3},{5,4},{6,7},{9,8},{10,11},{13,12},{14,15},{17,16},{18,... | collective-permute-start | bytes 1179656 | tf_op jit(solution)/shard_map/ppermute | solution.py:169
  161.8 12.2 %collective-permute-start.39 = (bf16[2,48,512]{2,1,0:T(8,128)(2,1)S(1)}, bf16[2,48,512]{2,1,0:T(8,128)(2,1)S(1)}, u32[]{:S(2)}, u32[]{:S(2)}) collective-permute-start(bf16[2,48,512]{2,1,0:T(8,128)(2,1)S(1)} %convert_element_type.342), channel_id=1, source_target_pairs={{0,1},{1,0},{2,3},{3,2},{4,5},{5,4},{6,7},{7,6},{8,9},{9,8},{10,11... | collective-permute-start | bytes 294920 | tf_op jit(solution)/shard_map/ppermute | solution.py:71
  169.6 9.9 %collective-permute-start.50 = (bf16[2,32,512]{2,1,0:T(8,128)(2,1)S(1)}, bf16[2,32,512]{2,1,0:T(8,128)(2,1)S(1)}, u32[]{:S(2)}, u32[]{:S(2)}) collective-permute-start(bf16[2,32,512]{2,1,0:T(8,128)(2,1)S(1)} %bitcast.559), channel_id=1, source_target_pairs={{0,3},{1,2},{2,1},{3,0},{4,7},{5,6},{6,5},{7,4},{8,11},{9,10},{10,... | collective-permute-start | bytes 196616 | tf_op jit(solution)/shard_map/ppermute | solution.py:71
  171.7 9.7 %collective-permute-start.49 = (bf16[2,32,512]{2,1,0:T(8,128)(2,1)S(1)}, bf16[2,32,512]{2,1,0:T(8,128)(2,1)S(1)}, u32[]{:S(2)}, u32[]{:S(2)}) collective-permute-start(bf16[2,32,512]{2,1,0:T(8,128)(2,1)S(1)} %bitcast.560), channel_id=1, source_target_pairs={{0,2},{1,3},{2,0},{3,1},{4,6},{5,7},{6,4},{7,5},{8,10},{9,11},{10,... | collective-permute-start | bytes 196616 | tf_op jit(solution)/shard_map/ppermute | solution.py:71
  174.1 8.9 %collective-permute-start.45 = (bf16[2,48,512]{2,1,0:T(8,128)(2,1)S(1)}, bf16[2,48,512]{2,1,0:T(8,128)(2,1)S(1)}, u32[]{:S(2)}, u32[]{:S(2)}) collective-permute-start(bf16[2,48,512]{2,1,0:T(8,128)(2,1)S(1)} %fusion.117), channel_id=1, source_target_pairs={{0,2},{1,3},{2,0},{3,1},{4,6},{5,7},{6,4},{7,5},{8,10},{9,11},{10,... | collective-permute-start | bytes 294920 | tf_op jit(solution)/shard_map/ppermute | solution.py:71
  (24 other events, 194.2 us)

commit v15 on v14

--- a/solution.py
+++ b/solution.py
@@ -236,7 +236,7 @@
             group, place = (groups[0], i) if i < first else (groups[1], i - first)
             x, g = group[which][0, place], group[which][1, place]
             if s > 0:
-                other = acts[i - 2] if i > 3 else came[max(s - LAG, 0)] if s > 1 else messages[0][2:]
+                other = middle if s == 6 else acts[i - 2] if i > 3 else came[max(s - LAG, 0)] if s > 1 else messages[0][2:]
                 x, g = after(x, other), after(g, other)
             parts = [dot(x, gate_weight, 1, 0), dot(x, up_weight, 1, 0), dot(g, down_weight, 1, 1)]
             message = jnp.stack(parts).astype(BF16)

time: 184 us -> 183 us (level)
  transfers between devices with their start and end apart: 51 -> 51, of which waited for: 21 -> 20; matrix products, arithmetic and copies ran while one was open for 17% -> 17% of each run, Pallas kernels for 0% -> 0%
where the time goes in v15:
time: 183 us; the launch traced here: 182 us
  starting transfers between devices  98.2 us (54%)
  waiting for transfers between devices  44.1 us (24%)
  matrix products  24.7 us (13%)
  other arithmetic  11 us (6%)
  between operations  2.01 us (1%)
  local copies, waits for them, and re-layouts  1.84 us (1%)
    ppermute x7, starting transfers between devices, swap(): return lax.ppermute(block, 'tensor', pairs + back)  47.9 us
    ppermute x28, starting transfers between devices, exchange(): return lax.ppermute(block, axis, [(i, i ^ apart) for i in range(count)])  29.3 us
    dot_general x56, matrix products, dot(): lax.dot_general(left, right, (((left_dim,), (right_dim,)), ((), ())), pre...  24.7 us
    ppermute x3, waiting for transfers between devices, swap(): return lax.ppermute(out, 'tensor', back)  19 us
    ppermute x28, waiting for transfers between devices, exchange(): return lax.ppermute(block, axis, [(i, i ^ apart) for i in range(count)])  14.2 us
    ppermute x3, starting transfers between devices, swap(): return lax.ppermute(into, 'tensor', pairs)  9.93 us
    ppermute x3, waiting for transfers between devices, swap(): return lax.ppermute(into, 'tensor', pairs)  7.14 us
    ppermute x10, starting transfers between devices, across(): return lax.ppermute(block, 'tensor', [(half - 1, half), (half, half - 1)])  7.04 us
  transfers between devices with their start and end apart: 51, of which 20 were waited for; matrix products, arithmetic and copies ran while one was open for 17% of the time, Pallas kernels for 0%

profile of v15, /device:TPU:0, one launch (start us, length us, event | category | flops | bytes accessed | tf_op | source)
XLA Modules:
  0.0 181.9 jit_solution(13881387603151953548)
XLA Ops:
  1.5 5.0 %collective-permute-start.2 = (bf16[2,32,512]{2,1,0:T(8,128)(2,1)S(1)}, bf16[2,32,512]{2,1,0:T(8,128)(2,1)S(1)}, u32[]{:S(2)}, u32[]{:S(2)}) collective-permute-start(bf16[2,32,512]{2,1,0:T(8,128)(2,1)S(1)} %pad_maximum_fusion.26), channel_id=1, source_target_pairs={{0,3},{1,2},{2,1},{3,0},{4,7},{5,6},{6,5},{7,4},{8,11},{9,10},{10,... | collective-permute-start | bytes 196616 | tf_op jit(solution)/shard_map/ppermute | solution.py:71
  10.3 1.9 %collective-permute-done.1 = bf16[2,32,512]{2,1,0:T(8,128)(2,1)S(1)} collective-permute-done((bf16[2,32,512]{2,1,0:T(8,128)(2,1)S(1)}, bf16[2,32,512]{2,1,0:T(8,128)(2,1)S(1)}, u32[]{:S(2)}, u32[]{:S(2)}) %collective-permute-start.1) | collective-permute-done | bytes 65568 | tf_op jit(solution)/shard_map/ppermute | solution.py:71
  13.5 2.5 %collective-permute-start.5 = (bf16[2,2,1,16,512]{4,3,2,1,0:T(8,128)(2,1)S(1)}, bf16[2,2,1,16,512]{4,3,2,1,0:T(8,128)(2,1)S(1)}, u32[]{:S(2)}, u32[]{:S(2)}) collective-permute-start(bf16[2,2,1,16,512]{4,3,2,1,0:T(8,128)(2,1)S(1)} %bitcast.548), channel_id=1, source_target_pairs={{0,24},{4,28},{8,16},{12,20},{16,8},{20,12},{24,0},{28,4},{1,25},{... | collective-permute-start | bytes 196616 | tf_op jit(solution)/shard_map/ppermute | solution.py:71
  17.1 1.7 collective-permute-done.5
  21.0 2.8 %collective-permute-start.14 = (bf16[2,48,512]{2,1,0:T(8,128)(2,1)S(1)}, bf16[2,48,512]{2,1,0:T(8,128)(2,1)S(1)}, u32[]{:S(2)}, u32[]{:S(2)}) collective-permute-start(bf16[2,48,512]{2,1,0:T(8,128)(2,1)S(1)} %fusion.118), channel_id=1, source_target_pairs={{0,3},{1,2},{2,1},{3,0},{4,7},{5,6},{6,5},{7,4},{8,11},{9,10},{10,... | collective-permute-start | bytes 294920 | tf_op jit(solution)/shard_map/ppermute | solution.py:71
  23.8 1.7 collective-permute-start.12
  27.7 2.3 %collective-permute-start.7 = (bf16[3,64,1024]{2,1,0:T(8,128)(2,1)S(1)}, bf16[3,64,1024]{2,1,0:T(8,128)(2,1)S(1)}, u32[]{:S(2)}, u32[]{:S(2)}) collective-permute-start(bf16[3,64,1024]{2,1,0:T(8,128)(2,1)S(1)} %pad_maximum_fusion.2), channel_id=1, source_target_pairs={{0,1},{3,2},{4,5},{7,6},{8,9},{11,10},{12,13},{15,14},{16,17},{19,... | collective-permute-start | bytes 1179656 | tf_op jit(solution)/shard_map/ppermute | solution.py:167
  31.3 1.8 collective-permute-done.13
  33.7 1.6 collective-permute-start.17
  37.2 1.9 %collective-permute-done.7 = bf16[3,64,1024]{2,1,0:T(8,128)(2,1)S(1)} collective-permute-done((bf16[3,64,1024]{2,1,0:T(8,128)(2,1)S(1)}, bf16[3,64,1024]{2,1,0:T(8,128)(2,1)S(1)}, u32[]{:S(2)}, u32[]{:S(2)}) %collective-permute-start.7) | collective-permute-done | bytes 393248 | tf_op jit(solution)/shard_map/ppermute | solution.py:167
  39.7 4.4 %collective-permute-start.8 = (bf16[3,64,1024]{2,1,0:T(8,128)(2,1)S(1)}, bf16[3,64,1024]{2,1,0:T(8,128)(2,1)S(1)}, u32[]{:S(2)}, u32[]{:S(2)}) collective-permute-start(bf16[3,64,1024]{2,1,0:T(8,128)(2,1)S(1)} %maximum_select_fusion.1), channel_id=1, source_target_pairs={{0,1},{3,2},{4,5},{7,6},{8,9},{11,10},{12,13},{15,14},{16,17},{19,... | collective-permute-start | bytes 1179656 | tf_op jit(solution)/shard_map/ppermute | solution.py:167
  46.4 3.2 %collective-permute-start.21 = (bf16[3,64,1024]{2,1,0:T(8,128)(2,1)S(1)}, bf16[3,64,1024]{2,1,0:T(8,128)(2,1)S(1)}, u32[]{:S(2)}, u32[]{:S(2)}) collective-permute-start(bf16[3,64,1024]{2,1,0:T(8,128)(2,1)S(1)} %pad_maximum_fusion.7), channel_id=1, source_target_pairs={{0,1},{3,2},{4,5},{7,6},{8,9},{11,10},{12,13},{15,14},{16,17},{19,... | collective-permute-start | bytes 1179656 | tf_op jit(solution)/shard_map/ppermute | solution.py:167
  50.3 3.4 %collective-permute-done.8 = bf16[3,64,1024]{2,1,0:T(8,128)(2,1)S(1)} collective-permute-done((bf16[3,64,1024]{2,1,0:T(8,128)(2,1)S(1)}, bf16[3,64,1024]{2,1,0:T(8,128)(2,1)S(1)}, u32[]{:S(2)}, u32[]{:S(2)}) %collective-permute-start.8) | collective-permute-done | bytes 393248 | tf_op jit(solution)/shard_map/ppermute | solution.py:167
  54.8 4.2 %collective-permute-start.20 = (bf16[3,64,1024]{2,1,0:T(8,128)(2,1)S(1)}, bf16[3,64,1024]{2,1,0:T(8,128)(2,1)S(1)}, u32[]{:S(2)}, u32[]{:S(2)}) collective-permute-start(bf16[3,64,1024]{2,1,0:T(8,128)(2,1)S(1)} %get-tuple-element.58), channel_id=1, source_target_pairs={{0,1},{3,2},{1,0},{2,3},{4,5},{7,6},{5,4},{6,7},{8,9},{11,10},{9,8... | collective-permute-start | bytes 1179656 | tf_op jit(solution)/shard_map/ppermute | solution.py:171
  60.2 1.8 %collective-permute-done.21 = bf16[3,64,1024]{2,1,0:T(8,128)(2,1)S(1)} collective-permute-done((bf16[3,64,1024]{2,1,0:T(8,128)(2,1)S(1)}, bf16[3,64,1024]{2,1,0:T(8,128)(2,1)S(1)}, u32[]{:S(2)}, u32[]{:S(2)}) %collective-permute-start.21) | collective-permute-done | bytes 393248 | tf_op jit(solution)/shard_map/ppermute | solution.py:167
  64.1 6.2 %collective-permute-start.19 = (bf16[3,64,1024]{2,1,0:T(8,128)(2,1)S(1)}, bf16[3,64,1024]{2,1,0:T(8,128)(2,1)S(1)}, u32[]{:S(2)}, u32[]{:S(2)}) collective-permute-start(bf16[3,64,1024]{2,1,0:T(8,128)(2,1)S(1)} %broadcast_select_fusion.9), channel_id=1, source_target_pairs={{0,1},{3,2},{1,0},{2,3},{4,5},{7,6},{5,4},{6,7},{8,9},{11,10},{9,8... | collective-permute-start | bytes 1179656 | tf_op jit(solution)/shard_map/ppermute | solution.py:171
  71.6 8.0 %collective-permute-start.25 = (bf16[3,64,1024]{2,1,0:T(8,128)(2,1)S(1)}, bf16[3,64,1024]{2,1,0:T(8,128)(2,1)S(1)}, u32[]{:S(2)}, u32[]{:S(2)}) collective-permute-start(bf16[3,64,1024]{2,1,0:T(8,128)(2,1)S(1)} %get-tuple-element.56), channel_id=1, source_target_pairs={{0,1},{3,2},{1,0},{2,3},{4,5},{7,6},{5,4},{6,7},{8,9},{11,10},{9,8... | collective-permute-start | bytes 1179656 | tf_op jit(solution)/shard_map/ppermute | solution.py:171
  82.5 9.0 %collective-permute-start.24 = (bf16[3,64,1024]{2,1,0:T(8,128)(2,1)S(1)}, bf16[3,64,1024]{2,1,0:T(8,128)(2,1)S(1)}, u32[]{:S(2)}, u32[]{:S(2)}) collective-permute-start(bf16[3,64,1024]{2,1,0:T(8,128)(2,1)S(1)} %broadcast_select_fusion.3), channel_id=1, source_target_pairs={{0,1},{3,2},{1,0},{2,3},{4,5},{7,6},{5,4},{6,7},{8,9},{11,10},{9,8... | collective-permute-start | bytes 1179656 | tf_op jit(solution)/shard_map/ppermute | solution.py:171
  99.2 3.8 %collective-permute-start.29 = (bf16[3,64,1024]{2,1,0:T(8,128)(2,1)S(1)}, bf16[3,64,1024]{2,1,0:T(8,128)(2,1)S(1)}, u32[]{:S(2)}, u32[]{:S(2)}) collective-permute-start(bf16[3,64,1024]{2,1,0:T(8,128)(2,1)S(1)} %get-tuple-element.54), channel_id=1, source_target_pairs={{0,1},{3,2},{1,0},{2,3},{4,5},{7,6},{5,4},{6,7},{8,9},{11,10},{9,8... | collective-permute-start | bytes 1179656 | tf_op jit(solution)/shard_map/ppermute | solution.py:171
  104.8 9.9 %collective-permute-start.28 = (bf16[3,64,1024]{2,1,0:T(8,128)(2,1)S(1)}, bf16[3,64,1024]{2,1,0:T(8,128)(2,1)S(1)}, u32[]{:S(2)}, u32[]{:S(2)}) collective-permute-start(bf16[3,64,1024]{2,1,0:T(8,128)(2,1)S(1)} %broadcast_select_fusion.8), channel_id=1, source_target_pairs={{0,1},{3,2},{1,0},{2,3},{4,5},{7,6},{5,4},{6,7},{8,9},{11,10},{9,8... | collective-permute-start | bytes 1179656 | tf_op jit(solution)/shard_map/ppermute | solution.py:171
  115.8 6.7 %collective-permute-start.32 = (bf16[3,64,1024]{2,1,0:T(8,128)(2,1)S(1)}, bf16[3,64,1024]{2,1,0:T(8,128)(2,1)S(1)}, u32[]{:S(2)}, u32[]{:S(2)}) collective-permute-start(bf16[3,64,1024]{2,1,0:T(8,128)(2,1)S(1)} %get-tuple-element.50), channel_id=1, source_target_pairs={{0,1},{3,2},{1,0},{2,3},{4,5},{7,6},{5,4},{6,7},{8,9},{11,10},{9,8... | collective-permute-start | bytes 1179656 | tf_op jit(solution)/shard_map/ppermute | solution.py:171
  126.6 2.2 %collective-permute-done.32 = bf16[3,64,1024]{2,1,0:T(8,128)(2,1)S(1)} collective-permute-done((bf16[3,64,1024]{2,1,0:T(8,128)(2,1)S(1)}, bf16[3,64,1024]{2,1,0:T(8,128)(2,1)S(1)}, u32[]{:S(2)}, u32[]{:S(2)}) %collective-permute-start.32) | collective-permute-done | bytes 393248 | tf_op jit(solution)/shard_map/ppermute | solution.py:171
  131.6 1.6 collective-permute-start.38
  133.7 8.7 %collective-permute-done.41 = bf16[3,64,1024]{2,1,0:T(8,128)(2,1)S(1)} collective-permute-done((bf16[3,64,1024]{2,1,0:T(8,128)(2,1)S(1)}, bf16[3,64,1024]{2,1,0:T(8,128)(2,1)S(1)}, u32[]{:S(2)}, u32[]{:S(2)}) %collective-permute-start.41) | collective-permute-done | bytes 393248 | tf_op jit(solution)/shard_map/ppermute | solution.py:169
  144.4 1.5 collective-permute-start.35
  147.0 10.3 %collective-permute-done.35 = bf16[3,64,1024]{2,1,0:T(8,128)(2,1)S(1)} collective-permute-done((bf16[3,64,1024]{2,1,0:T(8,128)(2,1)S(1)}, bf16[3,64,1024]{2,1,0:T(8,128)(2,1)S(1)}, u32[]{:S(2)}, u32[]{:S(2)}) %collective-permute-start.35) | collective-permute-done | bytes 393248 | tf_op jit(solution)/shard_map/ppermute | solution.py:169
  161.0 1.6 collective-permute-start.44
  164.6 2.0 %multiply_convert_fusion = bf16[1024,512]{1,0:T(8,128)(2,1)} fusion(bf16[3,640,1024]{2,1,0:T(8,128)(2,1)S(1)} %get-tuple-element.10, bf16[2,640,512]{2,1,0:T(8,128)(2,1)S(1)} %maximum_select_fusion), kind=kOutput, calls=%fused_computation | convolution fusion | flops 672137216 | bytes 3014656 | tf_op jit(solution)/shard_map/dot_general | solution.py:37
  167.6 1.9 %collective-permute-start.50 = (bf16[2,32,512]{2,1,0:T(8,128)(2,1)S(1)}, bf16[2,32,512]{2,1,0:T(8,128)(2,1)S(1)}, u32[]{:S(2)}, u32[]{:S(2)}) collective-permute-start(bf16[2,32,512]{2,1,0:T(8,128)(2,1)S(1)} %bitcast.559), channel_id=1, source_target_pairs={{0,3},{1,2},{2,1},{3,0},{4,7},{5,6},{6,5},{7,4},{8,11},{9,10},{10,... | collective-permute-start | bytes 196616 | tf_op jit(solution)/shard_map/ppermute | solution.py:71
  173.2 2.0 %multiply_convert_fusion.2 = bf16[512,1024]{1,0:T(8,128)(2,1)} fusion(bf16[3,640,1024]{2,1,0:T(8,128)(2,1)S(1)} %get-tuple-element.10, bf16[2,640,512]{2,1,0:T(8,128)(2,1)S(1)} %maximum_select_fusion, pred[512]{0:T(512)(128)(4,1)S(1)} %compare_reduce_fusion.5, bf16[512]{0:T(512)(128)(2,1)S(1)} %slice_reduce_fusion.3), kind=kOutput, calls=%fused_computation.2 | convolution fusion | flops 672464896 | bytes 3016192 | tf_op jit(solution)/shard_map/dot_general | solution.py:37
  175.2 2.0 %multiply_convert_fusion.1 = bf16[512,1024]{1,0:T(8,128)(2,1)} fusion(bf16[3,640,1024]{2,1,0:T(8,128)(2,1)S(1)} %get-tuple-element.10, bf16[2,640,512]{2,1,0:T(8,128)(2,1)S(1)} %maximum_select_fusion, pred[512]{0:T(512)(128)(4,1)S(1)} %compare_reduce_fusion.5, bf16[512]{0:T(512)(128)(2,1)S(1)} %slice_reduce_fusion.3), kind=kOutput, calls=%fused_computation.1 | convolution fusion | flops 672464896 | bytes 3016192 | tf_op jit(solution)/shard_map/dot_general | solution.py:37
  177.2 2.5 %collective-permute-done.49 = bf16[2,32,512]{2,1,0:T(8,128)(2,1)S(1)} collective-permute-done((bf16[2,32,512]{2,1,0:T(8,128)(2,1)S(1)}, bf16[2,32,512]{2,1,0:T(8,128)(2,1)S(1)}, u32[]{:S(2)}, u32[]{:S(2)}) %collective-permute-start.49) | collective-permute-done | bytes 65568 | tf_op jit(solution)/shard_map/ppermute | solution.py:71
  (248 shorter events, 59.8 us)
Async XLA Ops:
  21.0 10.3 %collective-permute-start.14 = (bf16[2,48,512]{2,1,0:T(8,128)(2,1)S(1)}, bf16[2,48,512]{2,1,0:T(8,128)(2,1)S(1)}, u32[]{:S(2)}, u32[]{:S(2)}) collective-permute-start(bf16[2,48,512]{2,1,0:T(8,128)(2,1)S(1)} %fusion.118), channel_id=1, source_target_pairs={{0,3},{1,2},{2,1},{3,0},{4,7},{5,6},{6,5},{7,4},{8,11},{9,10},{10,... | collective-permute-start | bytes 294920 | tf_op jit(solution)/shard_map/ppermute | solution.py:71
  23.7 9.3 %collective-permute-start.13 = (bf16[2,48,512]{2,1,0:T(8,128)(2,1)S(1)}, bf16[2,48,512]{2,1,0:T(8,128)(2,1)S(1)}, u32[]{:S(2)}, u32[]{:S(2)}) collective-permute-start(bf16[2,48,512]{2,1,0:T(8,128)(2,1)S(1)} %fusion.118), channel_id=1, source_target_pairs={{0,2},{1,3},{2,0},{3,1},{4,6},{5,7},{6,4},{7,5},{8,10},{9,11},{10,... | collective-permute-start | bytes 294920 | tf_op jit(solution)/shard_map/ppermute | solution.py:71
  23.8 9.3 %collective-permute-start.12 = (bf16[2,48,512]{2,1,0:T(8,128)(2,1)S(1)}, bf16[2,48,512]{2,1,0:T(8,128)(2,1)S(1)}, u32[]{:S(2)}, u32[]{:S(2)}) collective-permute-start(bf16[2,48,512]{2,1,0:T(8,128)(2,1)S(1)} %fusion.118), channel_id=1, source_target_pairs={{0,1},{1,0},{2,3},{3,2},{4,5},{5,4},{6,7},{7,6},{8,9},{9,8},{10,11... | collective-permute-start | bytes 294920 | tf_op jit(solution)/shard_map/ppermute | solution.py:71
  27.7 11.4 %collective-permute-start.7 = (bf16[3,64,1024]{2,1,0:T(8,128)(2,1)S(1)}, bf16[3,64,1024]{2,1,0:T(8,128)(2,1)S(1)}, u32[]{:S(2)}, u32[]{:S(2)}) collective-permute-start(bf16[3,64,1024]{2,1,0:T(8,128)(2,1)S(1)} %pad_maximum_fusion.2), channel_id=1, source_target_pairs={{0,1},{3,2},{4,5},{7,6},{8,9},{11,10},{12,13},{15,14},{16,17},{19,... | collective-permute-start | bytes 1179656 | tf_op jit(solution)/shard_map/ppermute | solution.py:167
  33.7 12.5 %collective-permute-start.17 = (bf16[2,3,1,16,512]{4,3,2,1,0:T(8,128)(2,1)S(1)}, bf16[2,3,1,16,512]{4,3,2,1,0:T(8,128)(2,1)S(1)}, u32[]{:S(2)}, u32[]{:S(2)}) collective-permute-start(bf16[2,3,1,16,512]{4,3,2,1,0:T(8,128)(2,1)S(1)} %bitcast.555), channel_id=1, source_target_pairs={{0,24},{4,28},{8,16},{12,20},{16,8},{20,12},{24,0},{28,4},{1,25},{... | collective-permute-start | bytes 294920 | tf_op jit(solution)/shard_map/ppermute | solution.py:71
  35.2 10.9 %collective-permute-start.16 = (bf16[2,3,1,16,512]{4,3,2,1,0:T(8,128)(2,1)S(1)}, bf16[2,3,1,16,512]{4,3,2,1,0:T(8,128)(2,1)S(1)}, u32[]{:S(2)}, u32[]{:S(2)}) collective-permute-start(bf16[2,3,1,16,512]{4,3,2,1,0:T(8,128)(2,1)S(1)} %bitcast.556), channel_id=1, source_target_pairs={{0,16},{4,20},{8,24},{12,28},{16,0},{20,4},{24,8},{28,12},{1,17},{... | collective-permute-start | bytes 294920 | tf_op jit(solution)/shard_map/ppermute | solution.py:71
  35.7 10.4 %collective-permute-start.15 = (bf16[2,3,1,16,512]{4,3,2,1,0:T(8,128)(2,1)S(1)}, bf16[2,3,1,16,512]{4,3,2,1,0:T(8,128)(2,1)S(1)}, u32[]{:S(2)}, u32[]{:S(2)}) collective-permute-start(bf16[2,3,1,16,512]{4,3,2,1,0:T(8,128)(2,1)S(1)} %bitcast.557), channel_id=1, source_target_pairs={{0,8},{4,12},{8,0},{12,4},{16,24},{20,28},{24,16},{28,20},{1,9},{5... | collective-permute-start | bytes 294920 | tf_op jit(solution)/shard_map/ppermute | solution.py:71
  39.7 13.9 %collective-permute-start.8 = (bf16[3,64,1024]{2,1,0:T(8,128)(2,1)S(1)}, bf16[3,64,1024]{2,1,0:T(8,128)(2,1)S(1)}, u32[]{:S(2)}, u32[]{:S(2)}) collective-permute-start(bf16[3,64,1024]{2,1,0:T(8,128)(2,1)S(1)} %maximum_select_fusion.1), channel_id=1, source_target_pairs={{0,1},{3,2},{4,5},{7,6},{8,9},{11,10},{12,13},{15,14},{16,17},{19,... | collective-permute-start | bytes 1179656 | tf_op jit(solution)/shard_map/ppermute | solution.py:167
  46.2 12.8 %collective-permute-start.18 = (bf16[2,3,4,16,512]{4,3,2,1,0:T(8,128)(2,1)S(1)}, bf16[2,3,4,16,512]{4,3,2,1,0:T(8,128)(2,1)S(1)}, u32[]{:S(2)}, u32[]{:S(2)}) collective-permute-start(bf16[2,3,4,16,512]{4,3,2,1,0:T(8,128)(2,1)S(1)} %pad_maximum_fusion.4), channel_id=1, source_target_pairs={{0,4},{4,0},{8,12},{12,8},{16,20},{20,16},{24,28},{28,24},{1,5},{5... | collective-permute-start | bytes 1179656 | tf_op jit(solution)/shard_map/ppermute | solution.py:71
  46.4 15.7 %collective-permute-start.21 = (bf16[3,64,1024]{2,1,0:T(8,128)(2,1)S(1)}, bf16[3,64,1024]{2,1,0:T(8,128)(2,1)S(1)}, u32[]{:S(2)}, u32[]{:S(2)}) collective-permute-start(bf16[3,64,1024]{2,1,0:T(8,128)(2,1)S(1)} %pad_maximum_fusion.7), channel_id=1, source_target_pairs={{0,1},{3,2},{4,5},{7,6},{8,9},{11,10},{12,13},{15,14},{16,17},{19,... | collective-permute-start | bytes 1179656 | tf_op jit(solution)/shard_map/ppermute | solution.py:167
  54.1 9.9 %collective-permute-start.10 = (bf16[3,64,1024]{2,1,0:T(8,128)(2,1)S(1)}, bf16[3,64,1024]{2,1,0:T(8,128)(2,1)S(1)}, u32[]{:S(2)}, u32[]{:S(2)}) collective-permute-start(bf16[3,64,1024]{2,1,0:T(8,128)(2,1)S(1)} %get-tuple-element.59), channel_id=1, source_target_pairs={{1,2},{2,1},{5,6},{6,5},{9,10},{10,9},{13,14},{14,13},{17,18},{18,... | collective-permute-start | bytes 1179656 | tf_op jit(solution)/shard_map/ppermute | solution.py:176
  54.8 15.7 %collective-permute-start.20 = (bf16[3,64,1024]{2,1,0:T(8,128)(2,1)S(1)}, bf16[3,64,1024]{2,1,0:T(8,128)(2,1)S(1)}, u32[]{:S(2)}, u32[]{:S(2)}) collective-permute-start(bf16[3,64,1024]{2,1,0:T(8,128)(2,1)S(1)} %get-tuple-element.58), channel_id=1, source_target_pairs={{0,1},{3,2},{1,0},{2,3},{4,5},{7,6},{5,4},{6,7},{8,9},{11,10},{9,8... | collective-permute-start | bytes 1179656 | tf_op jit(solution)/shard_map/ppermute | solution.py:171
  64.1 15.5 %collective-permute-start.19 = (bf16[3,64,1024]{2,1,0:T(8,128)(2,1)S(1)}, bf16[3,64,1024]{2,1,0:T(8,128)(2,1)S(1)}, u32[]{:S(2)}, u32[]{:S(2)}) collective-permute-start(bf16[3,64,1024]{2,1,0:T(8,128)(2,1)S(1)} %broadcast_select_fusion.9), channel_id=1, source_target_pairs={{0,1},{3,2},{1,0},{2,3},{4,5},{7,6},{5,4},{6,7},{8,9},{11,10},{9,8... | collective-permute-start | bytes 1179656 | tf_op jit(solution)/shard_map/ppermute | solution.py:171
  70.9 11.5 %collective-permute-start.23 = (bf16[3,64,1024]{2,1,0:T(8,128)(2,1)S(1)}, bf16[3,64,1024]{2,1,0:T(8,128)(2,1)S(1)}, u32[]{:S(2)}, u32[]{:S(2)}) collective-permute-start(bf16[3,64,1024]{2,1,0:T(8,128)(2,1)S(1)} %get-tuple-element.57), channel_id=1, source_target_pairs={{1,2},{2,1},{5,6},{6,5},{9,10},{10,9},{13,14},{14,13},{17,18},{18,... | collective-permute-start | bytes 1179656 | tf_op jit(solution)/shard_map/ppermute | solution.py:176
  71.6 22.0 %collective-permute-start.25 = (bf16[3,64,1024]{2,1,0:T(8,128)(2,1)S(1)}, bf16[3,64,1024]{2,1,0:T(8,128)(2,1)S(1)}, u32[]{:S(2)}, u32[]{:S(2)}) collective-permute-start(bf16[3,64,1024]{2,1,0:T(8,128)(2,1)S(1)} %get-tuple-element.56), channel_id=1, source_target_pairs={{0,1},{3,2},{1,0},{2,3},{4,5},{7,6},{5,4},{6,7},{8,9},{11,10},{9,8... | collective-permute-start | bytes 1179656 | tf_op jit(solution)/shard_map/ppermute | solution.py:171
  80.9 12.7 %collective-permute-start.26 = (bf16[3,64,1024]{2,1,0:T(8,128)(2,1)S(1)}, bf16[3,64,1024]{2,1,0:T(8,128)(2,1)S(1)}, u32[]{:S(2)}, u32[]{:S(2)}) collective-permute-start(bf16[3,64,1024]{2,1,0:T(8,128)(2,1)S(1)} %add_convert_fusion.2), channel_id=1, source_target_pairs={{1,2},{2,1},{5,6},{6,5},{9,10},{10,9},{13,14},{14,13},{17,18},{18,... | collective-permute-start | bytes 1179656 | tf_op jit(solution)/shard_map/ppermute | solution.py:176
  82.5 14.7 %collective-permute-start.24 = (bf16[3,64,1024]{2,1,0:T(8,128)(2,1)S(1)}, bf16[3,64,1024]{2,1,0:T(8,128)(2,1)S(1)}, u32[]{:S(2)}, u32[]{:S(2)}) collective-permute-start(bf16[3,64,1024]{2,1,0:T(8,128)(2,1)S(1)} %broadcast_select_fusion.3), channel_id=1, source_target_pairs={{0,1},{3,2},{1,0},{2,3},{4,5},{7,6},{5,4},{6,7},{8,9},{11,10},{9,8... | collective-permute-start | bytes 1179656 | tf_op jit(solution)/shard_map/ppermute | solution.py:171
  99.2 15.5 %collective-permute-start.29 = (bf16[3,64,1024]{2,1,0:T(8,128)(2,1)S(1)}, bf16[3,64,1024]{2,1,0:T(8,128)(2,1)S(1)}, u32[]{:S(2)}, u32[]{:S(2)}) collective-permute-start(bf16[3,64,1024]{2,1,0:T(8,128)(2,1)S(1)} %get-tuple-element.54), channel_id=1, source_target_pairs={{0,1},{3,2},{1,0},{2,3},{4,5},{7,6},{5,4},{6,7},{8,9},{11,10},{9,8... | collective-permute-start | bytes 1179656 | tf_op jit(solution)/shard_map/ppermute | solution.py:171
  103.2 11.5 %collective-permute-start.31 = (bf16[3,64,1024]{2,1,0:T(8,128)(2,1)S(1)}, bf16[3,64,1024]{2,1,0:T(8,128)(2,1)S(1)}, u32[]{:S(2)}, u32[]{:S(2)}) collective-permute-start(bf16[3,64,1024]{2,1,0:T(8,128)(2,1)S(1)} %add_convert_fusion.1), channel_id=1, source_target_pairs={{1,2},{2,1},{5,6},{6,5},{9,10},{10,9},{13,14},{14,13},{17,18},{18,... | collective-permute-start | bytes 1179656 | tf_op jit(solution)/shard_map/ppermute | solution.py:176
  104.8 17.7 %collective-permute-start.28 = (bf16[3,64,1024]{2,1,0:T(8,128)(2,1)S(1)}, bf16[3,64,1024]{2,1,0:T(8,128)(2,1)S(1)}, u32[]{:S(2)}, u32[]{:S(2)}) collective-permute-start(bf16[3,64,1024]{2,1,0:T(8,128)(2,1)S(1)} %broadcast_select_fusion.8), channel_id=1, source_target_pairs={{0,1},{3,2},{1,0},{2,3},{4,5},{7,6},{5,4},{6,7},{8,9},{11,10},{9,8... | collective-permute-start | bytes 1179656 | tf_op jit(solution)/shard_map/ppermute | solution.py:171
  115.1 10.2 %collective-permute-start.40 = (bf16[3,64,1024]{2,1,0:T(8,128)(2,1)S(1)}, bf16[3,64,1024]{2,1,0:T(8,128)(2,1)S(1)}, u32[]{:S(2)}, u32[]{:S(2)}) collective-permute-start(bf16[3,64,1024]{2,1,0:T(8,128)(2,1)S(1)} %get-tuple-element.49), channel_id=1, source_target_pairs={{1,2},{2,1},{5,6},{6,5},{9,10},{10,9},{13,14},{14,13},{17,18},{18,... | collective-permute-start | bytes 1179656 | tf_op jit(solution)/shard_map/ppermute | solution.py:176
  115.8 13.0 %collective-permute-start.32 = (bf16[3,64,1024]{2,1,0:T(8,128)(2,1)S(1)}, bf16[3,64,1024]{2,1,0:T(8,128)(2,1)S(1)}, u32[]{:S(2)}, u32[]{:S(2)}) collective-permute-start(bf16[3,64,1024]{2,1,0:T(8,128)(2,1)S(1)} %get-tuple-element.50), channel_id=1, source_target_pairs={{0,1},{3,2},{1,0},{2,3},{4,5},{7,6},{5,4},{6,7},{8,9},{11,10},{9,8... | collective-permute-start | bytes 1179656 | tf_op jit(solution)/shard_map/ppermute | solution.py:171
  125.3 17.0 %collective-permute-start.41 = (bf16[3,64,1024]{2,1,0:T(8,128)(2,1)S(1)}, bf16[3,64,1024]{2,1,0:T(8,128)(2,1)S(1)}, u32[]{:S(2)}, u32[]{:S(2)}) collective-permute-start(bf16[3,64,1024]{2,1,0:T(8,128)(2,1)S(1)} %collective-permute-done.40), channel_id=1, source_target_pairs={{1,0},{2,3},{5,4},{6,7},{9,8},{10,11},{13,12},{14,15},{17,16},{18,... | collective-permute-start | bytes 1179656 | tf_op jit(solution)/shard_map/ppermute | solution.py:169
  129.3 15.0 %collective-permute-start.34 = (bf16[3,64,1024]{2,1,0:T(8,128)(2,1)S(1)}, bf16[3,64,1024]{2,1,0:T(8,128)(2,1)S(1)}, u32[]{:S(2)}, u32[]{:S(2)}) collective-permute-start(bf16[3,64,1024]{2,1,0:T(8,128)(2,1)S(1)} %pad_maximum_fusion.16), channel_id=1, source_target_pairs={{1,2},{2,1},{5,6},{6,5},{9,10},{10,9},{13,14},{14,13},{17,18},{18,... | collective-permute-start | bytes 1179656 | tf_op jit(solution)/shard_map/ppermute | solution.py:176
  129.9 27.6 %collective-permute-start.42 = (bf16[3,64,1024]{2,1,0:T(8,128)(2,1)S(1)}, bf16[3,64,1024]{2,1,0:T(8,128)(2,1)S(1)}, u32[]{:S(2)}, u32[]{:S(2)}) collective-permute-start(bf16[3,64,1024]{2,1,0:T(8,128)(2,1)S(1)} %pad_maximum_fusion.16), channel_id=1, source_target_pairs={{1,0},{2,3},{5,4},{6,7},{9,8},{10,11},{13,12},{14,15},{17,16},{18,... | collective-permute-start | bytes 1179656 | tf_op jit(solution)/shard_map/ppermute | solution.py:169
  131.6 14.6 %collective-permute-start.38 = (bf16[2,3,16,512]{3,2,1,0:T(8,128)(2,1)S(1)}, bf16[2,3,16,512]{3,2,1,0:T(8,128)(2,1)S(1)}, u32[]{:S(2)}, u32[]{:S(2)}) collective-permute-start(bf16[2,3,16,512]{3,2,1,0:T(8,128)(2,1)S(1)} %get-tuple-element.52), channel_id=1, source_target_pairs={{0,24},{4,28},{8,16},{12,20},{16,8},{20,12},{24,0},{28,4},{1,25},{... | collective-permute-start | bytes 294920 | tf_op jit(solution)/shard_map/ppermute | solution.py:71
  133.1 13.1 %collective-permute-start.37 = (bf16[2,3,16,512]{3,2,1,0:T(8,128)(2,1)S(1)}, bf16[2,3,16,512]{3,2,1,0:T(8,128)(2,1)S(1)}, u32[]{:S(2)}, u32[]{:S(2)}) collective-permute-start(bf16[2,3,16,512]{3,2,1,0:T(8,128)(2,1)S(1)} %get-tuple-element.53), channel_id=1, source_target_pairs={{0,16},{4,20},{8,24},{12,28},{16,0},{20,4},{24,8},{28,12},{1,17},{... | collective-permute-start | bytes 294920 | tf_op jit(solution)/shard_map/ppermute | solution.py:71
  144.4 13.0 %collective-permute-start.35 = (bf16[3,64,1024]{2,1,0:T(8,128)(2,1)S(1)}, bf16[3,64,1024]{2,1,0:T(8,128)(2,1)S(1)}, u32[]{:S(2)}, u32[]{:S(2)}) collective-permute-start(bf16[3,64,1024]{2,1,0:T(8,128)(2,1)S(1)} %broadcast_select_fusion), channel_id=1, source_target_pairs={{1,0},{2,3},{5,4},{6,7},{9,8},{10,11},{13,12},{14,15},{17,16},{18,... | collective-permute-start | bytes 1179656 | tf_op jit(solution)/shard_map/ppermute | solution.py:169
  159.9 12.2 %collective-permute-start.39 = (bf16[2,48,512]{2,1,0:T(8,128)(2,1)S(1)}, bf16[2,48,512]{2,1,0:T(8,128)(2,1)S(1)}, u32[]{:S(2)}, u32[]{:S(2)}) collective-permute-start(bf16[2,48,512]{2,1,0:T(8,128)(2,1)S(1)} %convert_element_type.342), channel_id=1, source_target_pairs={{0,1},{1,0},{2,3},{3,2},{4,5},{5,4},{6,7},{7,6},{8,9},{9,8},{10,11... | collective-permute-start | bytes 294920 | tf_op jit(solution)/shard_map/ppermute | solution.py:71
  167.6 9.6 %collective-permute-start.50 = (bf16[2,32,512]{2,1,0:T(8,128)(2,1)S(1)}, bf16[2,32,512]{2,1,0:T(8,128)(2,1)S(1)}, u32[]{:S(2)}, u32[]{:S(2)}) collective-permute-start(bf16[2,32,512]{2,1,0:T(8,128)(2,1)S(1)} %bitcast.559), channel_id=1, source_target_pairs={{0,3},{1,2},{2,1},{3,0},{4,7},{5,6},{6,5},{7,4},{8,11},{9,10},{10,... | collective-permute-start | bytes 196616 | tf_op jit(solution)/shard_map/ppermute | solution.py:71
  169.5 10.2 %collective-permute-start.49 = (bf16[2,32,512]{2,1,0:T(8,128)(2,1)S(1)}, bf16[2,32,512]{2,1,0:T(8,128)(2,1)S(1)}, u32[]{:S(2)}, u32[]{:S(2)}) collective-permute-start(bf16[2,32,512]{2,1,0:T(8,128)(2,1)S(1)} %bitcast.560), channel_id=1, source_target_pairs={{0,2},{1,3},{2,0},{3,1},{4,6},{5,7},{6,4},{7,5},{8,10},{9,11},{10,... | collective-permute-start | bytes 196616 | tf_op jit(solution)/shard_map/ppermute | solution.py:71
  170.7 9.0 %collective-permute-start.48 = (bf16[2,32,512]{2,1,0:T(8,128)(2,1)S(1)}, bf16[2,32,512]{2,1,0:T(8,128)(2,1)S(1)}, u32[]{:S(2)}, u32[]{:S(2)}) collective-permute-start(bf16[2,32,512]{2,1,0:T(8,128)(2,1)S(1)} %bitcast.561), channel_id=1, source_target_pairs={{0,1},{1,0},{2,3},{3,2},{4,5},{5,4},{6,7},{7,6},{8,9},{9,8},{10,11... | collective-permute-start | bytes 196616 | tf_op jit(solution)/shard_map/ppermute | solution.py:71
  (24 other events, 197.1 us)

commit v16 on v15

--- a/solution.py
+++ b/solution.py
@@ -229,14 +229,14 @@
 
     steps = 2 * chunks
     split, ends = max(chunks - 2, 0), []
-    messages, came, crossed, acts, outs = [], [], [], [], []
+    messages, came, mids, crossed, acts, outs = [], [], [], [], [], []
     for s in range(steps + LAG):
         if s < steps:
             i, which = divmod(s, 2)
             group, place = (groups[0], i) if i < first else (groups[1], i - first)
             x, g = group[which][0, place], group[which][1, place]
             if s > 0:
-                other = middle if s == 6 else acts[i - 2] if i > 3 else came[max(s - LAG, 0)] if s > 1 else messages[0][2:]
+                other = middle if s == 6 else mids[i - 2] if i > 3 else came[max(s - LAG, 0)] if s > 1 else messages[0][2:]
                 x, g = after(x, other), after(g, other)
             parts = [dot(x, gate_weight, 1, 0), dot(x, up_weight, 1, 0), dot(g, down_weight, 1, 1)]
             message = jnp.stack(parts).astype(BF16)
@@ -261,6 +261,7 @@
             total = messages[s].astype(F32) + came[s].astype(F32)
             if which == 0:
                 middle = total.astype(BF16)
+                mids.append(middle)
                 other_sums = across(middle)
             else:
                 gate, up, grad_hidden = total + other_sums.astype(F32)

time: 183 us -> 180 us (0.984)
  transfers between devices with their start and end apart: 51 -> 51, of which waited for: 20 -> 19; matrix products, arithmetic and copies ran while one was open for 17% -> 18% of each run, Pallas kernels for 0% -> 0%
where the time goes in v16:
time: 180 us; the launch traced here: 179 us
  starting transfers between devices  96.6 us (54%)
  waiting for transfers between devices  42.7 us (24%)
  matrix products  24.7 us (14%)
  other arithmetic  11 us (6%)
  between operations  2.01 us (1%)
  local copies, waits for them, and re-layouts  1.84 us (1%)
    ppermute x7, starting transfers between devices, swap(): return lax.ppermute(block, 'tensor', pairs + back)  46.3 us
    ppermute x28, starting transfers between devices, exchange(): return lax.ppermute(block, axis, [(i, i ^ apart) for i in range(count)])  29.3 us
    dot_general x56, matrix products, dot(): lax.dot_general(left, right, (((left_dim,), (right_dim,)), ((), ())), pre...  24.7 us
    ppermute x3, waiting for transfers between devices, swap(): return lax.ppermute(out, 'tensor', back)  19 us
    ppermute x28, waiting for transfers between devices, exchange(): return lax.ppermute(block, axis, [(i, i ^ apart) for i in range(count)])  14.2 us
    ppermute x3, starting transfers between devices, swap(): return lax.ppermute(into, 'tensor', pairs)  9.93 us
    ppermute x3, waiting for transfers between devices, swap(): return lax.ppermute(into, 'tensor', pairs)  7.15 us
    ppermute x10, starting transfers between devices, across(): return lax.ppermute(block, 'tensor', [(half - 1, half), (half, half - 1)])  7.04 us
  transfers between devices with their start and end apart: 51, of which 19 were waited for; matrix products, arithmetic and copies ran while one was open for 18% of the time, Pallas kernels for 0%

profile of v16, /device:TPU:0, one launch (start us, length us, event | category | flops | bytes accessed | tf_op | source)
XLA Modules:
  0.0 178.9 jit_solution(3627551282693504139)
XLA Ops:
  1.5 5.0 %collective-permute-start.2 = (bf16[2,32,512]{2,1,0:T(8,128)(2,1)S(1)}, bf16[2,32,512]{2,1,0:T(8,128)(2,1)S(1)}, u32[]{:S(2)}, u32[]{:S(2)}) collective-permute-start(bf16[2,32,512]{2,1,0:T(8,128)(2,1)S(1)} %pad_maximum_fusion.26), channel_id=1, source_target_pairs={{0,3},{1,2},{2,1},{3,0},{4,7},{5,6},{6,5},{7,4},{8,11},{9,10},{10,... | collective-permute-start | bytes 196616 | tf_op jit(solution)/shard_map/ppermute | solution.py:71
  10.3 1.9 %collective-permute-done.1 = bf16[2,32,512]{2,1,0:T(8,128)(2,1)S(1)} collective-permute-done((bf16[2,32,512]{2,1,0:T(8,128)(2,1)S(1)}, bf16[2,32,512]{2,1,0:T(8,128)(2,1)S(1)}, u32[]{:S(2)}, u32[]{:S(2)}) %collective-permute-start.1) | collective-permute-done | bytes 65568 | tf_op jit(solution)/shard_map/ppermute | solution.py:71
  13.5 2.5 %collective-permute-start.5 = (bf16[2,2,1,16,512]{4,3,2,1,0:T(8,128)(2,1)S(1)}, bf16[2,2,1,16,512]{4,3,2,1,0:T(8,128)(2,1)S(1)}, u32[]{:S(2)}, u32[]{:S(2)}) collective-permute-start(bf16[2,2,1,16,512]{4,3,2,1,0:T(8,128)(2,1)S(1)} %bitcast.541), channel_id=1, source_target_pairs={{0,24},{4,28},{8,16},{12,20},{16,8},{20,12},{24,0},{28,4},{1,25},{... | collective-permute-start | bytes 196616 | tf_op jit(solution)/shard_map/ppermute | solution.py:71
  17.1 1.7 collective-permute-done.5
  21.0 2.8 %collective-permute-start.14 = (bf16[2,48,512]{2,1,0:T(8,128)(2,1)S(1)}, bf16[2,48,512]{2,1,0:T(8,128)(2,1)S(1)}, u32[]{:S(2)}, u32[]{:S(2)}) collective-permute-start(bf16[2,48,512]{2,1,0:T(8,128)(2,1)S(1)} %fusion.118), channel_id=1, source_target_pairs={{0,3},{1,2},{2,1},{3,0},{4,7},{5,6},{6,5},{7,4},{8,11},{9,10},{10,... | collective-permute-start | bytes 294920 | tf_op jit(solution)/shard_map/ppermute | solution.py:71
  23.8 1.7 collective-permute-start.12
  27.7 2.3 %collective-permute-start.7 = (bf16[3,64,1024]{2,1,0:T(8,128)(2,1)S(1)}, bf16[3,64,1024]{2,1,0:T(8,128)(2,1)S(1)}, u32[]{:S(2)}, u32[]{:S(2)}) collective-permute-start(bf16[3,64,1024]{2,1,0:T(8,128)(2,1)S(1)} %pad_maximum_fusion.2), channel_id=1, source_target_pairs={{0,1},{3,2},{4,5},{7,6},{8,9},{11,10},{12,13},{15,14},{16,17},{19,... | collective-permute-start | bytes 1179656 | tf_op jit(solution)/shard_map/ppermute | solution.py:167
  31.3 1.8 collective-permute-done.13
  33.7 1.6 collective-permute-start.17
  37.2 1.9 %collective-permute-done.7 = bf16[3,64,1024]{2,1,0:T(8,128)(2,1)S(1)} collective-permute-done((bf16[3,64,1024]{2,1,0:T(8,128)(2,1)S(1)}, bf16[3,64,1024]{2,1,0:T(8,128)(2,1)S(1)}, u32[]{:S(2)}, u32[]{:S(2)}) %collective-permute-start.7) | collective-permute-done | bytes 393248 | tf_op jit(solution)/shard_map/ppermute | solution.py:167
  39.7 4.4 %collective-permute-start.8 = (bf16[3,64,1024]{2,1,0:T(8,128)(2,1)S(1)}, bf16[3,64,1024]{2,1,0:T(8,128)(2,1)S(1)}, u32[]{:S(2)}, u32[]{:S(2)}) collective-permute-start(bf16[3,64,1024]{2,1,0:T(8,128)(2,1)S(1)} %maximum_select_fusion.1), channel_id=1, source_target_pairs={{0,1},{3,2},{4,5},{7,6},{8,9},{11,10},{12,13},{15,14},{16,17},{19,... | collective-permute-start | bytes 1179656 | tf_op jit(solution)/shard_map/ppermute | solution.py:167
  46.4 3.2 %collective-permute-start.21 = (bf16[3,64,1024]{2,1,0:T(8,128)(2,1)S(1)}, bf16[3,64,1024]{2,1,0:T(8,128)(2,1)S(1)}, u32[]{:S(2)}, u32[]{:S(2)}) collective-permute-start(bf16[3,64,1024]{2,1,0:T(8,128)(2,1)S(1)} %pad_maximum_fusion.7), channel_id=1, source_target_pairs={{0,1},{3,2},{4,5},{7,6},{8,9},{11,10},{12,13},{15,14},{16,17},{19,... | collective-permute-start | bytes 1179656 | tf_op jit(solution)/shard_map/ppermute | solution.py:167
  50.3 3.4 %collective-permute-done.8 = bf16[3,64,1024]{2,1,0:T(8,128)(2,1)S(1)} collective-permute-done((bf16[3,64,1024]{2,1,0:T(8,128)(2,1)S(1)}, bf16[3,64,1024]{2,1,0:T(8,128)(2,1)S(1)}, u32[]{:S(2)}, u32[]{:S(2)}) %collective-permute-start.8) | collective-permute-done | bytes 393248 | tf_op jit(solution)/shard_map/ppermute | solution.py:167
  54.8 4.2 %collective-permute-start.20 = (bf16[3,64,1024]{2,1,0:T(8,128)(2,1)S(1)}, bf16[3,64,1024]{2,1,0:T(8,128)(2,1)S(1)}, u32[]{:S(2)}, u32[]{:S(2)}) collective-permute-start(bf16[3,64,1024]{2,1,0:T(8,128)(2,1)S(1)} %get-tuple-element.58), channel_id=1, source_target_pairs={{0,1},{3,2},{1,0},{2,3},{4,5},{7,6},{5,4},{6,7},{8,9},{11,10},{9,8... | collective-permute-start | bytes 1179656 | tf_op jit(solution)/shard_map/ppermute | solution.py:171
  60.2 1.8 %collective-permute-done.21 = bf16[3,64,1024]{2,1,0:T(8,128)(2,1)S(1)} collective-permute-done((bf16[3,64,1024]{2,1,0:T(8,128)(2,1)S(1)}, bf16[3,64,1024]{2,1,0:T(8,128)(2,1)S(1)}, u32[]{:S(2)}, u32[]{:S(2)}) %collective-permute-start.21) | collective-permute-done | bytes 393248 | tf_op jit(solution)/shard_map/ppermute | solution.py:167
  64.1 6.2 %collective-permute-start.19 = (bf16[3,64,1024]{2,1,0:T(8,128)(2,1)S(1)}, bf16[3,64,1024]{2,1,0:T(8,128)(2,1)S(1)}, u32[]{:S(2)}, u32[]{:S(2)}) collective-permute-start(bf16[3,64,1024]{2,1,0:T(8,128)(2,1)S(1)} %broadcast_select_fusion.9), channel_id=1, source_target_pairs={{0,1},{3,2},{1,0},{2,3},{4,5},{7,6},{5,4},{6,7},{8,9},{11,10},{9,8... | collective-permute-start | bytes 1179656 | tf_op jit(solution)/shard_map/ppermute | solution.py:171
  71.6 8.0 %collective-permute-start.25 = (bf16[3,64,1024]{2,1,0:T(8,128)(2,1)S(1)}, bf16[3,64,1024]{2,1,0:T(8,128)(2,1)S(1)}, u32[]{:S(2)}, u32[]{:S(2)}) collective-permute-start(bf16[3,64,1024]{2,1,0:T(8,128)(2,1)S(1)} %get-tuple-element.56), channel_id=1, source_target_pairs={{0,1},{3,2},{1,0},{2,3},{4,5},{7,6},{5,4},{6,7},{8,9},{11,10},{9,8... | collective-permute-start | bytes 1179656 | tf_op jit(solution)/shard_map/ppermute | solution.py:171
  84.8 6.7 %collective-permute-start.24 = (bf16[3,64,1024]{2,1,0:T(8,128)(2,1)S(1)}, bf16[3,64,1024]{2,1,0:T(8,128)(2,1)S(1)}, u32[]{:S(2)}, u32[]{:S(2)}) collective-permute-start(bf16[3,64,1024]{2,1,0:T(8,128)(2,1)S(1)} %broadcast_select_fusion.3), channel_id=1, source_target_pairs={{0,1},{3,2},{1,0},{2,3},{4,5},{7,6},{5,4},{6,7},{8,9},{11,10},{9,8... | collective-permute-start | bytes 1179656 | tf_op jit(solution)/shard_map/ppermute | solution.py:171
  94.6 5.4 %collective-permute-start.29 = (bf16[3,64,1024]{2,1,0:T(8,128)(2,1)S(1)}, bf16[3,64,1024]{2,1,0:T(8,128)(2,1)S(1)}, u32[]{:S(2)}, u32[]{:S(2)}) collective-permute-start(bf16[3,64,1024]{2,1,0:T(8,128)(2,1)S(1)} %get-tuple-element.54), channel_id=1, source_target_pairs={{0,1},{3,2},{1,0},{2,3},{4,5},{7,6},{5,4},{6,7},{8,9},{11,10},{9,8... | collective-permute-start | bytes 1179656 | tf_op jit(solution)/shard_map/ppermute | solution.py:171
  102.6 9.0 %collective-permute-start.28 = (bf16[3,64,1024]{2,1,0:T(8,128)(2,1)S(1)}, bf16[3,64,1024]{2,1,0:T(8,128)(2,1)S(1)}, u32[]{:S(2)}, u32[]{:S(2)}) collective-permute-start(bf16[3,64,1024]{2,1,0:T(8,128)(2,1)S(1)} %broadcast_select_fusion.8), channel_id=1, source_target_pairs={{0,1},{3,2},{1,0},{2,3},{4,5},{7,6},{5,4},{6,7},{8,9},{11,10},{9,8... | collective-permute-start | bytes 1179656 | tf_op jit(solution)/shard_map/ppermute | solution.py:171
  112.8 6.7 %collective-permute-start.32 = (bf16[3,64,1024]{2,1,0:T(8,128)(2,1)S(1)}, bf16[3,64,1024]{2,1,0:T(8,128)(2,1)S(1)}, u32[]{:S(2)}, u32[]{:S(2)}) collective-permute-start(bf16[3,64,1024]{2,1,0:T(8,128)(2,1)S(1)} %get-tuple-element.50), channel_id=1, source_target_pairs={{0,1},{3,2},{1,0},{2,3},{4,5},{7,6},{5,4},{6,7},{8,9},{11,10},{9,8... | collective-permute-start | bytes 1179656 | tf_op jit(solution)/shard_map/ppermute | solution.py:171
  123.6 2.2 %collective-permute-done.32 = bf16[3,64,1024]{2,1,0:T(8,128)(2,1)S(1)} collective-permute-done((bf16[3,64,1024]{2,1,0:T(8,128)(2,1)S(1)}, bf16[3,64,1024]{2,1,0:T(8,128)(2,1)S(1)}, u32[]{:S(2)}, u32[]{:S(2)}) %collective-permute-start.32) | collective-permute-done | bytes 393248 | tf_op jit(solution)/shard_map/ppermute | solution.py:171
  128.6 1.6 collective-permute-start.38
  130.7 8.7 %collective-permute-done.41 = bf16[3,64,1024]{2,1,0:T(8,128)(2,1)S(1)} collective-permute-done((bf16[3,64,1024]{2,1,0:T(8,128)(2,1)S(1)}, bf16[3,64,1024]{2,1,0:T(8,128)(2,1)S(1)}, u32[]{:S(2)}, u32[]{:S(2)}) %collective-permute-start.41) | collective-permute-done | bytes 393248 | tf_op jit(solution)/shard_map/ppermute | solution.py:169
  141.4 1.5 collective-permute-start.35
  144.0 10.3 %collective-permute-done.35 = bf16[3,64,1024]{2,1,0:T(8,128)(2,1)S(1)} collective-permute-done((bf16[3,64,1024]{2,1,0:T(8,128)(2,1)S(1)}, bf16[3,64,1024]{2,1,0:T(8,128)(2,1)S(1)}, u32[]{:S(2)}, u32[]{:S(2)}) %collective-permute-start.35) | collective-permute-done | bytes 393248 | tf_op jit(solution)/shard_map/ppermute | solution.py:169
  158.0 1.6 collective-permute-start.44
  161.6 2.0 %multiply_convert_fusion = bf16[1024,512]{1,0:T(8,128)(2,1)} fusion(bf16[3,640,1024]{2,1,0:T(8,128)(2,1)S(1)} %get-tuple-element.10, bf16[2,640,512]{2,1,0:T(8,128)(2,1)S(1)} %maximum_select_fusion), kind=kOutput, calls=%fused_computation | convolution fusion | flops 672137216 | bytes 3014656 | tf_op jit(solution)/shard_map/dot_general | solution.py:37
  164.6 1.9 %collective-permute-start.50 = (bf16[2,32,512]{2,1,0:T(8,128)(2,1)S(1)}, bf16[2,32,512]{2,1,0:T(8,128)(2,1)S(1)}, u32[]{:S(2)}, u32[]{:S(2)}) collective-permute-start(bf16[2,32,512]{2,1,0:T(8,128)(2,1)S(1)} %bitcast.552), channel_id=1, source_target_pairs={{0,3},{1,2},{2,1},{3,0},{4,7},{5,6},{6,5},{7,4},{8,11},{9,10},{10,... | collective-permute-start | bytes 196616 | tf_op jit(solution)/shard_map/ppermute | solution.py:71
  170.2 2.0 %multiply_convert_fusion.2 = bf16[512,1024]{1,0:T(8,128)(2,1)} fusion(bf16[3,640,1024]{2,1,0:T(8,128)(2,1)S(1)} %get-tuple-element.10, bf16[2,640,512]{2,1,0:T(8,128)(2,1)S(1)} %maximum_select_fusion, pred[512]{0:T(512)(128)(4,1)S(1)} %compare_reduce_fusion.5, bf16[512]{0:T(512)(128)(2,1)S(1)} %slice_reduce_fusion.3), kind=kOutput, calls=%fused_computation.2 | convolution fusion | flops 672464896 | bytes 3016192 | tf_op jit(solution)/shard_map/dot_general | solution.py:37
  172.2 2.0 %multiply_convert_fusion.1 = bf16[512,1024]{1,0:T(8,128)(2,1)} fusion(bf16[3,640,1024]{2,1,0:T(8,128)(2,1)S(1)} %get-tuple-element.10, bf16[2,640,512]{2,1,0:T(8,128)(2,1)S(1)} %maximum_select_fusion, pred[512]{0:T(512)(128)(4,1)S(1)} %compare_reduce_fusion.5, bf16[512]{0:T(512)(128)(2,1)S(1)} %slice_reduce_fusion.3), kind=kOutput, calls=%fused_computation.1 | convolution fusion | flops 672464896 | bytes 3016192 | tf_op jit(solution)/shard_map/dot_general | solution.py:37
  174.2 2.5 %collective-permute-done.49 = bf16[2,32,512]{2,1,0:T(8,128)(2,1)S(1)} collective-permute-done((bf16[2,32,512]{2,1,0:T(8,128)(2,1)S(1)}, bf16[2,32,512]{2,1,0:T(8,128)(2,1)S(1)}, u32[]{:S(2)}, u32[]{:S(2)}) %collective-permute-start.49) | collective-permute-done | bytes 65568 | tf_op jit(solution)/shard_map/ppermute | solution.py:71
  (248 shorter events, 58.4 us)
Async XLA Ops:
  21.0 10.3 %collective-permute-start.14 = (bf16[2,48,512]{2,1,0:T(8,128)(2,1)S(1)}, bf16[2,48,512]{2,1,0:T(8,128)(2,1)S(1)}, u32[]{:S(2)}, u32[]{:S(2)}) collective-permute-start(bf16[2,48,512]{2,1,0:T(8,128)(2,1)S(1)} %fusion.118), channel_id=1, source_target_pairs={{0,3},{1,2},{2,1},{3,0},{4,7},{5,6},{6,5},{7,4},{8,11},{9,10},{10,... | collective-permute-start | bytes 294920 | tf_op jit(solution)/shard_map/ppermute | solution.py:71
  23.7 9.3 %collective-permute-start.13 = (bf16[2,48,512]{2,1,0:T(8,128)(2,1)S(1)}, bf16[2,48,512]{2,1,0:T(8,128)(2,1)S(1)}, u32[]{:S(2)}, u32[]{:S(2)}) collective-permute-start(bf16[2,48,512]{2,1,0:T(8,128)(2,1)S(1)} %fusion.118), channel_id=1, source_target_pairs={{0,2},{1,3},{2,0},{3,1},{4,6},{5,7},{6,4},{7,5},{8,10},{9,11},{10,... | collective-permute-start | bytes 294920 | tf_op jit(solution)/shard_map/ppermute | solution.py:71
  23.8 9.3 %collective-permute-start.12 = (bf16[2,48,512]{2,1,0:T(8,128)(2,1)S(1)}, bf16[2,48,512]{2,1,0:T(8,128)(2,1)S(1)}, u32[]{:S(2)}, u32[]{:S(2)}) collective-permute-start(bf16[2,48,512]{2,1,0:T(8,128)(2,1)S(1)} %fusion.118), channel_id=1, source_target_pairs={{0,1},{1,0},{2,3},{3,2},{4,5},{5,4},{6,7},{7,6},{8,9},{9,8},{10,11... | collective-permute-start | bytes 294920 | tf_op jit(solution)/shard_map/ppermute | solution.py:71
  27.7 11.4 %collective-permute-start.7 = (bf16[3,64,1024]{2,1,0:T(8,128)(2,1)S(1)}, bf16[3,64,1024]{2,1,0:T(8,128)(2,1)S(1)}, u32[]{:S(2)}, u32[]{:S(2)}) collective-permute-start(bf16[3,64,1024]{2,1,0:T(8,128)(2,1)S(1)} %pad_maximum_fusion.2), channel_id=1, source_target_pairs={{0,1},{3,2},{4,5},{7,6},{8,9},{11,10},{12,13},{15,14},{16,17},{19,... | collective-permute-start | bytes 1179656 | tf_op jit(solution)/shard_map/ppermute | solution.py:167
  33.7 12.5 %collective-permute-start.17 = (bf16[2,3,1,16,512]{4,3,2,1,0:T(8,128)(2,1)S(1)}, bf16[2,3,1,16,512]{4,3,2,1,0:T(8,128)(2,1)S(1)}, u32[]{:S(2)}, u32[]{:S(2)}) collective-permute-start(bf16[2,3,1,16,512]{4,3,2,1,0:T(8,128)(2,1)S(1)} %bitcast.548), channel_id=1, source_target_pairs={{0,24},{4,28},{8,16},{12,20},{16,8},{20,12},{24,0},{28,4},{1,25},{... | collective-permute-start | bytes 294920 | tf_op jit(solution)/shard_map/ppermute | solution.py:71
  35.2 10.9 %collective-permute-start.16 = (bf16[2,3,1,16,512]{4,3,2,1,0:T(8,128)(2,1)S(1)}, bf16[2,3,1,16,512]{4,3,2,1,0:T(8,128)(2,1)S(1)}, u32[]{:S(2)}, u32[]{:S(2)}) collective-permute-start(bf16[2,3,1,16,512]{4,3,2,1,0:T(8,128)(2,1)S(1)} %bitcast.549), channel_id=1, source_target_pairs={{0,16},{4,20},{8,24},{12,28},{16,0},{20,4},{24,8},{28,12},{1,17},{... | collective-permute-start | bytes 294920 | tf_op jit(solution)/shard_map/ppermute | solution.py:71
  35.7 10.4 %collective-permute-start.15 = (bf16[2,3,1,16,512]{4,3,2,1,0:T(8,128)(2,1)S(1)}, bf16[2,3,1,16,512]{4,3,2,1,0:T(8,128)(2,1)S(1)}, u32[]{:S(2)}, u32[]{:S(2)}) collective-permute-start(bf16[2,3,1,16,512]{4,3,2,1,0:T(8,128)(2,1)S(1)} %bitcast.550), channel_id=1, source_target_pairs={{0,8},{4,12},{8,0},{12,4},{16,24},{20,28},{24,16},{28,20},{1,9},{5... | collective-permute-start | bytes 294920 | tf_op jit(solution)/shard_map/ppermute | solution.py:71
  39.7 13.9 %collective-permute-start.8 = (bf16[3,64,1024]{2,1,0:T(8,128)(2,1)S(1)}, bf16[3,64,1024]{2,1,0:T(8,128)(2,1)S(1)}, u32[]{:S(2)}, u32[]{:S(2)}) collective-permute-start(bf16[3,64,1024]{2,1,0:T(8,128)(2,1)S(1)} %maximum_select_fusion.1), channel_id=1, source_target_pairs={{0,1},{3,2},{4,5},{7,6},{8,9},{11,10},{12,13},{15,14},{16,17},{19,... | collective-permute-start | bytes 1179656 | tf_op jit(solution)/shard_map/ppermute | solution.py:167
  46.2 12.8 %collective-permute-start.18 = (bf16[2,3,4,16,512]{4,3,2,1,0:T(8,128)(2,1)S(1)}, bf16[2,3,4,16,512]{4,3,2,1,0:T(8,128)(2,1)S(1)}, u32[]{:S(2)}, u32[]{:S(2)}) collective-permute-start(bf16[2,3,4,16,512]{4,3,2,1,0:T(8,128)(2,1)S(1)} %pad_maximum_fusion.4), channel_id=1, source_target_pairs={{0,4},{4,0},{8,12},{12,8},{16,20},{20,16},{24,28},{28,24},{1,5},{5... | collective-permute-start | bytes 1179656 | tf_op jit(solution)/shard_map/ppermute | solution.py:71
  46.4 15.7 %collective-permute-start.21 = (bf16[3,64,1024]{2,1,0:T(8,128)(2,1)S(1)}, bf16[3,64,1024]{2,1,0:T(8,128)(2,1)S(1)}, u32[]{:S(2)}, u32[]{:S(2)}) collective-permute-start(bf16[3,64,1024]{2,1,0:T(8,128)(2,1)S(1)} %pad_maximum_fusion.7), channel_id=1, source_target_pairs={{0,1},{3,2},{4,5},{7,6},{8,9},{11,10},{12,13},{15,14},{16,17},{19,... | collective-permute-start | bytes 1179656 | tf_op jit(solution)/shard_map/ppermute | solution.py:167
  54.1 9.9 %collective-permute-start.10 = (bf16[3,64,1024]{2,1,0:T(8,128)(2,1)S(1)}, bf16[3,64,1024]{2,1,0:T(8,128)(2,1)S(1)}, u32[]{:S(2)}, u32[]{:S(2)}) collective-permute-start(bf16[3,64,1024]{2,1,0:T(8,128)(2,1)S(1)} %get-tuple-element.59), channel_id=1, source_target_pairs={{1,2},{2,1},{5,6},{6,5},{9,10},{10,9},{13,14},{14,13},{17,18},{18,... | collective-permute-start | bytes 1179656 | tf_op jit(solution)/shard_map/ppermute | solution.py:176
  54.8 15.7 %collective-permute-start.20 = (bf16[3,64,1024]{2,1,0:T(8,128)(2,1)S(1)}, bf16[3,64,1024]{2,1,0:T(8,128)(2,1)S(1)}, u32[]{:S(2)}, u32[]{:S(2)}) collective-permute-start(bf16[3,64,1024]{2,1,0:T(8,128)(2,1)S(1)} %get-tuple-element.58), channel_id=1, source_target_pairs={{0,1},{3,2},{1,0},{2,3},{4,5},{7,6},{5,4},{6,7},{8,9},{11,10},{9,8... | collective-permute-start | bytes 1179656 | tf_op jit(solution)/shard_map/ppermute | solution.py:171
  64.1 15.5 %collective-permute-start.19 = (bf16[3,64,1024]{2,1,0:T(8,128)(2,1)S(1)}, bf16[3,64,1024]{2,1,0:T(8,128)(2,1)S(1)}, u32[]{:S(2)}, u32[]{:S(2)}) collective-permute-start(bf16[3,64,1024]{2,1,0:T(8,128)(2,1)S(1)} %broadcast_select_fusion.9), channel_id=1, source_target_pairs={{0,1},{3,2},{1,0},{2,3},{4,5},{7,6},{5,4},{6,7},{8,9},{11,10},{9,8... | collective-permute-start | bytes 1179656 | tf_op jit(solution)/shard_map/ppermute | solution.py:171
  70.9 13.7 %collective-permute-start.23 = (bf16[3,64,1024]{2,1,0:T(8,128)(2,1)S(1)}, bf16[3,64,1024]{2,1,0:T(8,128)(2,1)S(1)}, u32[]{:S(2)}, u32[]{:S(2)}) collective-permute-start(bf16[3,64,1024]{2,1,0:T(8,128)(2,1)S(1)} %get-tuple-element.57), channel_id=1, source_target_pairs={{1,2},{2,1},{5,6},{6,5},{9,10},{10,9},{13,14},{14,13},{17,18},{18,... | collective-permute-start | bytes 1179656 | tf_op jit(solution)/shard_map/ppermute | solution.py:176
  71.6 21.8 %collective-permute-start.25 = (bf16[3,64,1024]{2,1,0:T(8,128)(2,1)S(1)}, bf16[3,64,1024]{2,1,0:T(8,128)(2,1)S(1)}, u32[]{:S(2)}, u32[]{:S(2)}) collective-permute-start(bf16[3,64,1024]{2,1,0:T(8,128)(2,1)S(1)} %get-tuple-element.56), channel_id=1, source_target_pairs={{0,1},{3,2},{1,0},{2,3},{4,5},{7,6},{5,4},{6,7},{8,9},{11,10},{9,8... | collective-permute-start | bytes 1179656 | tf_op jit(solution)/shard_map/ppermute | solution.py:171
  82.0 11.5 %collective-permute-start.26 = (bf16[3,64,1024]{2,1,0:T(8,128)(2,1)S(1)}, bf16[3,64,1024]{2,1,0:T(8,128)(2,1)S(1)}, u32[]{:S(2)}, u32[]{:S(2)}) collective-permute-start(bf16[3,64,1024]{2,1,0:T(8,128)(2,1)S(1)} %add_convert_fusion.2), channel_id=1, source_target_pairs={{1,2},{2,1},{5,6},{6,5},{9,10},{10,9},{13,14},{14,13},{17,18},{18,... | collective-permute-start | bytes 1179656 | tf_op jit(solution)/shard_map/ppermute | solution.py:176
  84.8 15.3 %collective-permute-start.24 = (bf16[3,64,1024]{2,1,0:T(8,128)(2,1)S(1)}, bf16[3,64,1024]{2,1,0:T(8,128)(2,1)S(1)}, u32[]{:S(2)}, u32[]{:S(2)}) collective-permute-start(bf16[3,64,1024]{2,1,0:T(8,128)(2,1)S(1)} %broadcast_select_fusion.3), channel_id=1, source_target_pairs={{0,1},{3,2},{1,0},{2,3},{4,5},{7,6},{5,4},{6,7},{8,9},{11,10},{9,8... | collective-permute-start | bytes 1179656 | tf_op jit(solution)/shard_map/ppermute | solution.py:171
  94.6 17.0 %collective-permute-start.29 = (bf16[3,64,1024]{2,1,0:T(8,128)(2,1)S(1)}, bf16[3,64,1024]{2,1,0:T(8,128)(2,1)S(1)}, u32[]{:S(2)}, u32[]{:S(2)}) collective-permute-start(bf16[3,64,1024]{2,1,0:T(8,128)(2,1)S(1)} %get-tuple-element.54), channel_id=1, source_target_pairs={{0,1},{3,2},{1,0},{2,3},{4,5},{7,6},{5,4},{6,7},{8,9},{11,10},{9,8... | collective-permute-start | bytes 1179656 | tf_op jit(solution)/shard_map/ppermute | solution.py:171
  100.2 11.5 %collective-permute-start.31 = (bf16[3,64,1024]{2,1,0:T(8,128)(2,1)S(1)}, bf16[3,64,1024]{2,1,0:T(8,128)(2,1)S(1)}, u32[]{:S(2)}, u32[]{:S(2)}) collective-permute-start(bf16[3,64,1024]{2,1,0:T(8,128)(2,1)S(1)} %add_convert_fusion.1), channel_id=1, source_target_pairs={{1,2},{2,1},{5,6},{6,5},{9,10},{10,9},{13,14},{14,13},{17,18},{18,... | collective-permute-start | bytes 1179656 | tf_op jit(solution)/shard_map/ppermute | solution.py:176
  102.6 16.9 %collective-permute-start.28 = (bf16[3,64,1024]{2,1,0:T(8,128)(2,1)S(1)}, bf16[3,64,1024]{2,1,0:T(8,128)(2,1)S(1)}, u32[]{:S(2)}, u32[]{:S(2)}) collective-permute-start(bf16[3,64,1024]{2,1,0:T(8,128)(2,1)S(1)} %broadcast_select_fusion.8), channel_id=1, source_target_pairs={{0,1},{3,2},{1,0},{2,3},{4,5},{7,6},{5,4},{6,7},{8,9},{11,10},{9,8... | collective-permute-start | bytes 1179656 | tf_op jit(solution)/shard_map/ppermute | solution.py:171
  112.1 10.2 %collective-permute-start.40 = (bf16[3,64,1024]{2,1,0:T(8,128)(2,1)S(1)}, bf16[3,64,1024]{2,1,0:T(8,128)(2,1)S(1)}, u32[]{:S(2)}, u32[]{:S(2)}) collective-permute-start(bf16[3,64,1024]{2,1,0:T(8,128)(2,1)S(1)} %get-tuple-element.49), channel_id=1, source_target_pairs={{1,2},{2,1},{5,6},{6,5},{9,10},{10,9},{13,14},{14,13},{17,18},{18,... | collective-permute-start | bytes 1179656 | tf_op jit(solution)/shard_map/ppermute | solution.py:176
  112.8 13.0 %collective-permute-start.32 = (bf16[3,64,1024]{2,1,0:T(8,128)(2,1)S(1)}, bf16[3,64,1024]{2,1,0:T(8,128)(2,1)S(1)}, u32[]{:S(2)}, u32[]{:S(2)}) collective-permute-start(bf16[3,64,1024]{2,1,0:T(8,128)(2,1)S(1)} %get-tuple-element.50), channel_id=1, source_target_pairs={{0,1},{3,2},{1,0},{2,3},{4,5},{7,6},{5,4},{6,7},{8,9},{11,10},{9,8... | collective-permute-start | bytes 1179656 | tf_op jit(solution)/shard_map/ppermute | solution.py:171
  122.3 17.1 %collective-permute-start.41 = (bf16[3,64,1024]{2,1,0:T(8,128)(2,1)S(1)}, bf16[3,64,1024]{2,1,0:T(8,128)(2,1)S(1)}, u32[]{:S(2)}, u32[]{:S(2)}) collective-permute-start(bf16[3,64,1024]{2,1,0:T(8,128)(2,1)S(1)} %collective-permute-done.40), channel_id=1, source_target_pairs={{1,0},{2,3},{5,4},{6,7},{9,8},{10,11},{13,12},{14,15},{17,16},{18,... | collective-permute-start | bytes 1179656 | tf_op jit(solution)/shard_map/ppermute | solution.py:169
  126.2 15.1 %collective-permute-start.34 = (bf16[3,64,1024]{2,1,0:T(8,128)(2,1)S(1)}, bf16[3,64,1024]{2,1,0:T(8,128)(2,1)S(1)}, u32[]{:S(2)}, u32[]{:S(2)}) collective-permute-start(bf16[3,64,1024]{2,1,0:T(8,128)(2,1)S(1)} %pad_maximum_fusion.16), channel_id=1, source_target_pairs={{1,2},{2,1},{5,6},{6,5},{9,10},{10,9},{13,14},{14,13},{17,18},{18,... | collective-permute-start | bytes 1179656 | tf_op jit(solution)/shard_map/ppermute | solution.py:176
  126.9 27.6 %collective-permute-start.42 = (bf16[3,64,1024]{2,1,0:T(8,128)(2,1)S(1)}, bf16[3,64,1024]{2,1,0:T(8,128)(2,1)S(1)}, u32[]{:S(2)}, u32[]{:S(2)}) collective-permute-start(bf16[3,64,1024]{2,1,0:T(8,128)(2,1)S(1)} %pad_maximum_fusion.16), channel_id=1, source_target_pairs={{1,0},{2,3},{5,4},{6,7},{9,8},{10,11},{13,12},{14,15},{17,16},{18,... | collective-permute-start | bytes 1179656 | tf_op jit(solution)/shard_map/ppermute | solution.py:169
  128.6 14.6 %collective-permute-start.38 = (bf16[2,3,16,512]{3,2,1,0:T(8,128)(2,1)S(1)}, bf16[2,3,16,512]{3,2,1,0:T(8,128)(2,1)S(1)}, u32[]{:S(2)}, u32[]{:S(2)}) collective-permute-start(bf16[2,3,16,512]{3,2,1,0:T(8,128)(2,1)S(1)} %get-tuple-element.52), channel_id=1, source_target_pairs={{0,24},{4,28},{8,16},{12,20},{16,8},{20,12},{24,0},{28,4},{1,25},{... | collective-permute-start | bytes 294920 | tf_op jit(solution)/shard_map/ppermute | solution.py:71
  130.1 13.1 %collective-permute-start.37 = (bf16[2,3,16,512]{3,2,1,0:T(8,128)(2,1)S(1)}, bf16[2,3,16,512]{3,2,1,0:T(8,128)(2,1)S(1)}, u32[]{:S(2)}, u32[]{:S(2)}) collective-permute-start(bf16[2,3,16,512]{3,2,1,0:T(8,128)(2,1)S(1)} %get-tuple-element.53), channel_id=1, source_target_pairs={{0,16},{4,20},{8,24},{12,28},{16,0},{20,4},{24,8},{28,12},{1,17},{... | collective-permute-start | bytes 294920 | tf_op jit(solution)/shard_map/ppermute | solution.py:71
  141.4 13.0 %collective-permute-start.35 = (bf16[3,64,1024]{2,1,0:T(8,128)(2,1)S(1)}, bf16[3,64,1024]{2,1,0:T(8,128)(2,1)S(1)}, u32[]{:S(2)}, u32[]{:S(2)}) collective-permute-start(bf16[3,64,1024]{2,1,0:T(8,128)(2,1)S(1)} %broadcast_select_fusion), channel_id=1, source_target_pairs={{1,0},{2,3},{5,4},{6,7},{9,8},{10,11},{13,12},{14,15},{17,16},{18,... | collective-permute-start | bytes 1179656 | tf_op jit(solution)/shard_map/ppermute | solution.py:169
  156.9 12.2 %collective-permute-start.39 = (bf16[2,48,512]{2,1,0:T(8,128)(2,1)S(1)}, bf16[2,48,512]{2,1,0:T(8,128)(2,1)S(1)}, u32[]{:S(2)}, u32[]{:S(2)}) collective-permute-start(bf16[2,48,512]{2,1,0:T(8,128)(2,1)S(1)} %convert_element_type.342), channel_id=1, source_target_pairs={{0,1},{1,0},{2,3},{3,2},{4,5},{5,4},{6,7},{7,6},{8,9},{9,8},{10,11... | collective-permute-start | bytes 294920 | tf_op jit(solution)/shard_map/ppermute | solution.py:71
  164.6 9.6 %collective-permute-start.50 = (bf16[2,32,512]{2,1,0:T(8,128)(2,1)S(1)}, bf16[2,32,512]{2,1,0:T(8,128)(2,1)S(1)}, u32[]{:S(2)}, u32[]{:S(2)}) collective-permute-start(bf16[2,32,512]{2,1,0:T(8,128)(2,1)S(1)} %bitcast.552), channel_id=1, source_target_pairs={{0,3},{1,2},{2,1},{3,0},{4,7},{5,6},{6,5},{7,4},{8,11},{9,10},{10,... | collective-permute-start | bytes 196616 | tf_op jit(solution)/shard_map/ppermute | solution.py:71
  166.5 10.2 %collective-permute-start.49 = (bf16[2,32,512]{2,1,0:T(8,128)(2,1)S(1)}, bf16[2,32,512]{2,1,0:T(8,128)(2,1)S(1)}, u32[]{:S(2)}, u32[]{:S(2)}) collective-permute-start(bf16[2,32,512]{2,1,0:T(8,128)(2,1)S(1)} %bitcast.553), channel_id=1, source_target_pairs={{0,2},{1,3},{2,0},{3,1},{4,6},{5,7},{6,4},{7,5},{8,10},{9,11},{10,... | collective-permute-start | bytes 196616 | tf_op jit(solution)/shard_map/ppermute | solution.py:71
  167.7 9.0 %collective-permute-start.48 = (bf16[2,32,512]{2,1,0:T(8,128)(2,1)S(1)}, bf16[2,32,512]{2,1,0:T(8,128)(2,1)S(1)}, u32[]{:S(2)}, u32[]{:S(2)}) collective-permute-start(bf16[2,32,512]{2,1,0:T(8,128)(2,1)S(1)} %bitcast.554), channel_id=1, source_target_pairs={{0,1},{1,0},{2,3},{3,2},{4,5},{5,4},{6,7},{7,6},{8,9},{9,8},{10,11... | collective-permute-start | bytes 196616 | tf_op jit(solution)/shard_map/ppermute | solution.py:71
  (24 other events, 199.5 us)
